TPU v7x, 32 devices: a whole 2x2x4 slice. The times are simulated.
32 devices in a mesh: node: 8 (over z, core), dev: 4 (over y, x).
Axes of the slice: x: 2, y: 2, z: 4, core: 2. Of those that a mesh axis runs over, the one named last changes fastest.
Arguments:
- density: float32 [192, 64, 4096], P(('node', 'dev')), may hold values from -18 to 18
- owner_counts: int32 [32], P(('node', 'dev')), may hold values from 1 to 6, as said below
Outputs:
- coefficients: float32 [192, 64, 4096], P(('node', 'dev'))
Inputs may be any that keep to these rules, and one draw needn't show every extreme that they name: `owner_counts`: every device holds at least one block, the counts sum to 96, and some device holds exactly 6.
All inputs are finite; a program needn't handle non-finite values.
Results may differ from a plain program's by a relative error of at most 0.00002.
Values sent between devices are 32-bit elements; how exact they have to be, the bound alone decides.
No kernel may reach another device: no remote copies, remote signals or barrier semaphores. Data moves between devices by JAX's collectives and lax.ppermute only.
A program may use at most 128 MiB of HBM per device.

v0:
```python
import jax
import jax.numpy as jnp
from jax import lax
from jax.sharding import PartitionSpec as P

ALPHA_LIFT = -1.586134342059924
BETA_LIFT = -0.052980118572961
GAMMA_LIFT = 0.882911075530934
DELTA_LIFT = 0.443506852043971
SCALE_LIFT = 1.230174104914001
INVERSE_SCALE = 1.0 / SCALE_LIFT


def passed_along(value, axis, steps):
    count = lax.axis_size(axis)
    initial, last = (max(0, -steps), min(count, count - steps))
    return lax.ppermute(value, axis, [(source, source + steps) for source in range(initial, last)])


def lift_rows(values):
    slot_count, length, others = values.shape
    paired = values.reshape(slot_count, length // 2, 2, others)
    low_part = paired[:, :, 0]
    high_part = paired[:, :, 1]
    high_part = high_part + ALPHA_LIFT * (
        low_part + jnp.concatenate([low_part[:, 1:], low_part[:, -1:]], 1)
    )
    low_part = low_part + BETA_LIFT * (
        jnp.concatenate([high_part[:, :1], high_part[:, :-1]], 1) + high_part
    )
    high_part = high_part + GAMMA_LIFT * (
        low_part + jnp.concatenate([low_part[:, 1:], low_part[:, -1:]], 1)
    )
    low_part = low_part + DELTA_LIFT * (
        jnp.concatenate([high_part[:, :1], high_part[:, :-1]], 1) + high_part
    )
    return jnp.concatenate([low_part * INVERSE_SCALE, high_part * SCALE_LIFT], 1)


def one_level(volume):
    slot_count, length = (volume.shape[0], volume.shape[1])
    for axis_number in range(3):
        lifted = lift_rows(volume.reshape(slot_count, length, length * length))
        volume = jnp.transpose(lifted.reshape(slot_count, length, length, length), (0, 2, 3, 1))
    return volume


def corner_level(volume, corner_edge):
    inner = one_level(volume[:, :corner_edge, :corner_edge, :corner_edge])
    return volume.at[:, :corner_edge, :corner_edge, :corner_edge].set(inner)


def per_device(density, owner_counts):
    slot_total = density.shape[0]
    block_edge = density.shape[1]
    half_edge = block_edge // 2
    quarter = block_edge // 4
    cube_size = quarter * quarter * quarter
    octet_cap = (slot_total - 1) // 8 + 1
    all_counts = lax.all_gather(owner_counts, ("node", "dev"), axis=0, tiled=True)
    starts = jnp.cumsum(all_counts) - all_counts
    my_index = lax.axis_index(("node", "dev"))
    my_start = starts[my_index]
    my_count = all_counts[my_index]
    fine_coeffs = corner_level(
        one_level(density.reshape(slot_total, block_edge, block_edge, block_edge)), half_edge
    )
    lowpass = fine_coeffs[:, :quarter, :quarter, :quarter].reshape(slot_total, cube_size)
    received = [lowpass[None]]
    for offset in range(1, 8):
        received.append(passed_along(lowpass, ("node", "dev"), -offset)[None])
    window = jnp.concatenate(received, 0)
    first_octet = (my_start + 7) // 8
    octet_ids = first_octet + jnp.arange(octet_cap, dtype=jnp.int32)
    child_blocks = octet_ids[:, None] * 8 + jnp.arange(8, dtype=jnp.int32)[None, :]
    owners = (
        jnp.sum((starts[None, None, :] <= child_blocks[:, :, None]).astype(jnp.int32), axis=2) - 1
    )
    row_index = (owners - my_index) * slot_total + child_blocks - starts[owners]
    row_index = jnp.clip(row_index, 0, 8 * slot_total - 1)
    pieces = jnp.take(window.reshape(8 * slot_total, cube_size), row_index.reshape(-1), axis=0)
    pieces = pieces.reshape(octet_cap, 2, 2, 2, quarter, quarter, quarter)
    merged = jnp.transpose(pieces, (0, 3, 4, 2, 5, 1, 6)).reshape(
        octet_cap, half_edge, half_edge, half_edge
    )
    coarse = corner_level(corner_level(one_level(merged), half_edge // 2), half_edge // 4)
    results = coarse.reshape(octet_cap, 2, quarter, 2, quarter, 2, quarter)
    results = jnp.transpose(results, (0, 5, 3, 1, 2, 4, 6)).reshape(octet_cap * 8, cube_size)
    returned = [results[None]]
    for offset in range(1, 8):
        returned.append(passed_along(results, ("node", "dev"), offset)[None])
    result_table = jnp.concatenate(returned, 0)
    slot_ids = jnp.arange(slot_total, dtype=jnp.int32)
    live_slots = slot_ids < my_count
    block_ids = my_start + slot_ids
    octet_of = block_ids // 8
    child_of = block_ids % 8
    merge_owner = (
        jnp.sum((starts[None, :] <= (octet_of * 8)[:, None]).astype(jnp.int32), axis=1) - 1
    )
    distance = my_index - merge_owner
    within = octet_of - (starts[merge_owner] + 7) // 8
    flat_index = distance * (octet_cap * 8) + within * 8 + child_of
    flat_index = jnp.clip(flat_index, 0, 8 * octet_cap * 8 - 1)
    corners = jnp.take(result_table.reshape(8 * octet_cap * 8, cube_size), flat_index, axis=0)
    corners = corners.reshape(slot_total, quarter, quarter, quarter)
    fine_coeffs = fine_coeffs.at[:, :quarter, :quarter, :quarter].set(corners)
    fine_coeffs = jnp.where(
        live_slots[:, None, None, None], fine_coeffs, jnp.zeros_like(fine_coeffs)
    )
    return fine_coeffs.reshape(slot_total, block_edge, block_edge * block_edge)


def solution(mesh):
    in_specs = (P(("node", "dev"), None, None), P(("node", "dev")))
    out_specs = P(("node", "dev"), None, None)
    return jax.shard_map(
        per_device, mesh=mesh, in_specs=in_specs, out_specs=out_specs, check_vma=False
    )
```

profile of v0, /device:TPU:0, one launch (start us, length us, event | category | flops | bytes accessed | tf_op | source)
XLA Modules:
  0.0 706.2 jit_solution(5605951726942663808)
XLA Ops:
  0.0 8.2 %reshape_reshape_reshape.6 = f32[6,32,2,4096]{3,2,1,0:T(2,128)} reshape(f32[6,64,4096]{2,1,0:T(8,128)} %param.10) | data formatting | bytes 12582912 | tf_op jit(solution)/shard_map/reshape;reshape;reshape | solution.py:22
  8.2 18.8 %slice_reduce_fusion.96 = (f32[6,32,4096]{2,1,0:T(8,128)}, f32[6,32,1,4096]{3,2,1,0:T(1,128)S(1)}, f32[6,32,1,4096]{3,2,1,0:T(1,128)S(1)}) fusion(f32[6,32,2,4096]{3,2,1,0:T(2,128)} %reshape_reshape_reshape.6), kind=kLoop, calls=%fused_computation.545 | loop fusion | bytes 15728640 | tf_op jit(solution)/shard_map/slice | solution.py:24
  32.6 6.3 fusion.28
  63.7 6.1 concatenate.1394
  75.4 6.3 concatenate.1392
  90.4 19.0 %fusion.6 = (f32[6,32,64,64]{3,2,1,0:T(8,128)}, f32[6,32,64,64]{3,2,1,0:T(8,128)}) fusion(f32[6,31,64,64]{3,2,1,0:T(8,128)} %concatenate.1392, f32[6,1,64,64]{3,2,1,0:T(8,128)S(1)} %concatenate.1391, f32[6,1,64,64]{3,2,1,0:T(8,128)S(1)} %concatenate.1395, f32[6,31,64,64]{3,2,1,0:T(8,128)} %concatenate.1394, f32[6,32,64,64]{3,2,1,0:T(8,128)} %squeeze.157, ...), kind=kLoop, calls=%fused_computation.16 | loop fusion | flops 14155776 | bytes 25165824 | tf_op jit(solution)/shard_map/mul | solution.py:37
  109.4 12.2 %maximum_bitcast_fusion = f32[6,64,64,64]{2,1,3,0:T(8,128)} fusion(f32[6,32,64,64]{3,2,1,0:T(8,128)} %get-tuple-element.68, f32[6,32,64,64]{3,2,1,0:T(8,128)} %get-tuple-element.67), kind=kLoop, calls=%fused_computation.4 | loop fusion | flops 1572864 | bytes 12582912 | tf_op jit(solution)/shard_map/transpose | solution.py:44
  121.6 13.2 %copy.666 = f32[6,64,64,64]{3,2,1,0:T(8,128)} copy(f32[6,64,64,64]{2,1,3,0:T(8,128)} %maximum_bitcast_fusion) | data formatting | bytes 12582912 | tf_op jit(solution)/shard_map/transpose | solution.py:44
  134.8 12.4 %reshape_reshape.39 = f32[6,32,2,4096]{3,2,1,0:T(2,128)} reshape(f32[6,64,64,64]{3,2,1,0:T(8,128)} %copy.666) | data formatting | bytes 12582912 | tf_op jit(solution)/shard_map/reshape;reshape | solution.py:22
  147.2 13.0 %fusion.236 = (f32[6,32,1,4096]{3,2,1,0:T(1,128)}, f32[6,32,1,4096]{3,2,1,0:T(1,128)S(1)}) fusion(f32[6,32,2,4096]{3,2,1,0:T(2,128)} %reshape_reshape.39), kind=kLoop, calls=%fused_computation.547 | loop fusion | bytes 12582912 | tf_op jit(solution)/shard_map/slice | solution.py:24
  168.1 6.5 fusion.34
  193.0 6.5 squeeze.161
  199.4 6.2 copy.750
  205.7 6.1 concatenate.1410
  217.4 6.3 concatenate.1408
  231.8 18.9 %fusion.15 = (f32[6,32,64,64]{3,2,1,0:T(8,128)}, f32[6,32,64,64]{3,2,1,0:T(8,128)}) fusion(f32[6,31,64,64]{3,2,1,0:T(8,128)} %concatenate.1408, f32[6,1,64,64]{3,2,1,0:T(8,128)S(1)} %concatenate.1407, f32[6,1,64,64]{3,2,1,0:T(8,128)S(1)} %concatenate.1411, f32[6,31,64,64]{3,2,1,0:T(8,128)} %concatenate.1410, f32[6,32,64,64]{3,2,1,0:T(8,128)} %squeeze.161, ...), kind=kLoop, calls=%fused_computation.29 | loop fusion | flops 14155776 | bytes 25165824 | tf_op jit(solution)/shard_map/mul | solution.py:37
  250.7 12.2 %maximum_bitcast_fusion.1 = f32[6,64,64,64]{2,1,3,0:T(8,128)} fusion(f32[6,32,64,64]{3,2,1,0:T(8,128)} %get-tuple-element.66, f32[6,32,64,64]{3,2,1,0:T(8,128)} %get-tuple-element.65), kind=kLoop, calls=%fused_computation.5 | loop fusion | flops 1572864 | bytes 12582912 | tf_op jit(solution)/shard_map/transpose | solution.py:44
  262.9 13.2 %copy.669 = f32[6,64,64,64]{3,2,1,0:T(8,128)} copy(f32[6,64,64,64]{2,1,3,0:T(8,128)} %maximum_bitcast_fusion.1) | data formatting | bytes 12582912 | tf_op jit(solution)/shard_map/transpose | solution.py:44
  276.1 12.4 %reshape_reshape.40 = f32[6,32,2,4096]{3,2,1,0:T(2,128)} reshape(f32[6,64,64,64]{3,2,1,0:T(8,128)} %copy.669) | data formatting | bytes 12582912 | tf_op jit(solution)/shard_map/reshape;reshape | solution.py:22
  288.5 13.0 %fusion.235 = (f32[6,32,1,4096]{3,2,1,0:T(1,128)}, f32[6,32,1,4096]{3,2,1,0:T(1,128)S(1)}) fusion(f32[6,32,2,4096]{3,2,1,0:T(2,128)} %reshape_reshape.40), kind=kLoop, calls=%fused_computation.546 | loop fusion | bytes 12582912 | tf_op jit(solution)/shard_map/slice | solution.py:24
  309.4 6.5 fusion.40
  334.2 6.5 squeeze.165
  340.7 6.2 copy.752
  358.7 6.3 concatenate.1424
  373.0 18.9 %fusion.24 = (f32[6,32,64,64]{3,2,1,0:T(8,128)}, f32[6,32,64,64]{3,2,1,0:T(8,128)}) fusion(f32[6,31,64,64]{3,2,1,0:T(8,128)} %concatenate.1424, f32[6,1,64,64]{3,2,1,0:T(8,128)S(1)} %concatenate.1423, f32[6,1,64,64]{3,2,1,0:T(8,128)S(1)} %concatenate.1427, f32[6,31,64,64]{3,2,1,0:T(8,128)} %concatenate.1426, f32[6,32,64,64]{3,2,1,0:T(8,128)} %squeeze.165, ...), kind=kLoop, calls=%fused_computation.42 | loop fusion | flops 14155776 | bytes 25165824 | tf_op jit(solution)/shard_map/mul | solution.py:37
  392.0 12.2 %maximum_bitcast_fusion.2 = f32[6,64,64,64]{2,1,3,0:T(8,128)} fusion(f32[6,32,64,64]{3,2,1,0:T(8,128)} %get-tuple-element.64, f32[6,32,64,64]{3,2,1,0:T(8,128)} %get-tuple-element.63), kind=kLoop, calls=%fused_computation.6 | loop fusion | flops 1572864 | bytes 12582912 | tf_op jit(solution)/shard_map/transpose | solution.py:44
  500.0 49.7 %all-reduce = s32[32]{0:T(128)S(1)} all-reduce(s32[32]{0:T(128)S(1)} %dynamic-update-slice.12), channel_id=1, replica_groups=mesh['node'=8,'dev'=4] {'node','dev'}, use_global_device_ids=true, to_apply=%add | all-reduce | flops 32 | bytes 256
  561.9 31.6 %scatter.14 = f32[6,64,64,64]{2,1,3,0:T(8,128)} dynamic-update-slice(f32[6,64,64,64]{2,1,3,0:T(8,128)} %maximum_bitcast_fusion.2, f32[6,32,32,32]{2,1,3,0:T(8,128)S(1)} %maximum_bitcast_fusion.5, s32[]{:T(128)} %constant.233.clone.1, s32[]{:T(128)} %constant.233.clone.1, s32[]{:T(128)} %constant.233.clone.1, s32[]{:T(128)} %constant.233.clone.1) | dynamic-update-slice | bytes 1572868 | tf_op jit(solution)/shard_map/scatter | solution.py:50
  660.7 9.1 %scatter.19 = f32[6,64,64,64]{2,1,3,0:T(8,128)} dynamic-update-slice(f32[6,64,64,64]{2,1,3,0:T(8,128)} %scatter.14, f32[6,16,16,16]{2,1,3,0:T(8,128)S(1)} %broadcast_select_fusion.1, s32[]{:T(128)} %constant.233.clone.1, s32[]{:T(128)} %constant.233.clone.1, s32[]{:T(128)} %constant.233.clone.1, s32[]{:T(128)} %constant.233.clone.1) | dynamic-update-slice | bytes 196612 | tf_op jit(solution)/shard_map/scatter | solution.py:107
  669.8 12.1 %broadcast_select_fusion = f32[6,64,64,64]{2,1,3,0:T(8,128)} fusion(f32[6,64,64,64]{2,1,3,0:T(8,128)} %scatter.19, pred[6]{0:T(512)(128)(4,1)S(1)} %iota_compare_fusion), kind=kLoop, calls=%fused_computation.46 | loop fusion | flops 1572864 | bytes 12582918 | tf_op jit(solution)/shard_map/jit(_where)/select_n | solution.py:108
  681.9 13.3 %copy.745 = f32[6,64,64,64]{3,2,1,0:T(8,128)} copy(f32[6,64,64,64]{2,1,3,0:T(8,128)} %broadcast_select_fusion) | data formatting | bytes 12582912 | tf_op jit(solution)/shard_map/jit(_where)/select_n | solution.py:108
  695.2 10.8 %reshape.5025 = f32[6,64,4096]{2,1,0:T(8,128)} reshape(f32[6,64,64,64]{3,2,1,0:T(8,128)} %copy.745) | data formatting | bytes 12582912 | tf_op jit(solution)/shard_map/reshape | solution.py:111
  (501 shorter events, 302.8 us)
Async XLA Ops:
  31.4 7.5 %copy-start.12 = (f32[6,31,4096]{2,1,0:T(8,128)}, f32[6,31,4096]{2,1,0:T(8,128)S(1)}, u32[]{:S(2)}) copy-start(f32[6,31,4096]{2,1,0:T(8,128)S(1)} %slice.764) | copy-start | bytes 9142276
  43.6 2.7 copy-start.9
  75.4 10.8 %copy-start.20 = (f32[6,32,4096]{2,1,0:T(8,128)S(1)}, f32[6,32,4096]{2,1,0:T(8,128)}, u32[]{:S(2)}) copy-start(f32[6,32,4096]{2,1,0:T(8,128)} %get-tuple-element.79) | copy-start | bytes 9437188
  160.2 2.8 copy-start
  163.0 4.1 copy-start.1
  163.0 5.1 copy-start.10
  164.6 10.0 %copy-start.13 = (f32[6,31,4096]{2,1,0:T(8,128)}, f32[6,31,4096]{2,1,0:T(8,128)S(1)}, u32[]{:S(2)}) copy-start(f32[6,31,4096]{2,1,0:T(8,128)S(1)} %slice.774) | copy-start | bytes 9142276
  179.0 2.7 copy-start.7
  217.4 9.1 %copy-start.18 = (f32[6,32,1,4096]{3,1,0,2:T(8,128)S(1)}, f32[6,32,1,4096]{3,1,0,2:T(8,128)}, u32[]{:S(2)}) copy-start(f32[6,32,1,4096]{3,1,0,2:T(8,128)} %copy.750) | copy-start | bytes 9437188
  301.5 2.8 copy-start.2
  304.2 4.1 copy-start.3
  304.3 5.1 copy-start.11
  305.9 10.0 %copy-start.14 = (f32[6,31,4096]{2,1,0:T(8,128)}, f32[6,31,4096]{2,1,0:T(8,128)S(1)}, u32[]{:S(2)}) copy-start(f32[6,31,4096]{2,1,0:T(8,128)S(1)} %slice.784) | copy-start | bytes 9142276
  320.2 2.7 copy-start.8
  358.7 9.1 %copy-start.19 = (f32[6,32,1,4096]{3,1,0,2:T(8,128)S(1)}, f32[6,32,1,4096]{3,1,0,2:T(8,128)}, u32[]{:S(2)}) copy-start(f32[6,32,1,4096]{3,1,0,2:T(8,128)} %copy.752) | copy-start | bytes 9437188
  491.2 105.2 %collective-permute-start = (f32[6,4096]{1,0:T(8,128)S(1)}, f32[6,4096]{1,0:T(8,128)}, u32[]{:S(2)}, u32[]{:S(2)}) collective-permute-start(f32[6,4096]{1,0:T(8,128)S(1)} %reshape.5020), channel_id=1, source_target_pairs={{1,0},{2,1},{3,2},{4,3},{5,4},{6,5},{7,6},{8,7},{9,8},{10,9},{11,1... | collective-permute-start | bytes 294920 | tf_op jit(solution)/shard_map/ppermute | solution.py:17
  492.5 106.1 %collective-permute-start.1 = (f32[6,4096]{1,0:T(8,128)S(1)}, f32[6,4096]{1,0:T(8,128)}, u32[]{:S(2)}, u32[]{:S(2)}) collective-permute-start(f32[6,4096]{1,0:T(8,128)S(1)} %reshape.5020), channel_id=1, source_target_pairs={{2,0},{3,1},{4,2},{5,3},{6,4},{7,5},{8,6},{9,7},{10,8},{11,9},{12,... | collective-permute-start | bytes 294920 | tf_op jit(solution)/shard_map/ppermute | solution.py:17
  493.8 107.2 %collective-permute-start.2 = (f32[6,4096]{1,0:T(8,128)S(1)}, f32[6,4096]{1,0:T(8,128)}, u32[]{:S(2)}, u32[]{:S(2)}) collective-permute-start(f32[6,4096]{1,0:T(8,128)S(1)} %reshape.5020), channel_id=1, source_target_pairs={{3,0},{4,1},{5,2},{6,3},{7,4},{8,5},{9,6},{10,7},{11,8},{12,9},{13... | collective-permute-start | bytes 294920 | tf_op jit(solution)/shard_map/ppermute | solution.py:17
  495.1 106.8 %collective-permute-start.3 = (f32[6,4096]{1,0:T(8,128)S(1)}, f32[6,4096]{1,0:T(8,128)}, u32[]{:S(2)}, u32[]{:S(2)}) collective-permute-start(f32[6,4096]{1,0:T(8,128)S(1)} %reshape.5020), channel_id=1, source_target_pairs={{4,0},{5,1},{6,2},{7,3},{8,4},{9,5},{10,6},{11,7},{12,8},{13,9},{1... | collective-permute-start | bytes 294920 | tf_op jit(solution)/shard_map/ppermute | solution.py:17
  496.4 106.5 %collective-permute-start.4 = (f32[6,4096]{1,0:T(8,128)S(1)}, f32[6,4096]{1,0:T(8,128)S(1)}, u32[]{:S(2)}, u32[]{:S(2)}) collective-permute-start(f32[6,4096]{1,0:T(8,128)S(1)} %reshape.5020), channel_id=1, source_target_pairs={{5,0},{6,1},{7,2},{8,3},{9,4},{10,5},{11,6},{12,7},{13,8},{14,9},{... | collective-permute-start | bytes 294920 | tf_op jit(solution)/shard_map/ppermute | solution.py:17
  549.7 5.8 copy-start.24
  561.9 32.9 %copy-start.23 = (s32[8]{0:T(128)S(1)}, s32[8]{0:T(128)}, u32[]{:S(2)}) copy-start(s32[8]{0:T(128)} %get-tuple-element.61) | copy-start | bytes 100
  561.9 33.8 %copy-start.21 = (s32[6]{0:T(128)S(1)}, s32[6]{0:T(128)}, u32[]{:S(2)}) copy-start(s32[6]{0:T(128)} %fusion.231) | copy-start | bytes 76
  596.3 6.5 collective-permute-start.5
  598.6 10.0 %collective-permute-start.6 = (f32[6,4096]{1,0:T(8,128)S(1)}, f32[6,4096]{1,0:T(8,128)S(1)}, u32[]{:S(2)}, u32[]{:S(2)}) collective-permute-start(f32[6,4096]{1,0:T(8,128)S(1)} %reshape.5020), channel_id=1, source_target_pairs={{7,0},{8,1},{9,2},{10,3},{11,4},{12,5},{13,6},{14,7},{15,8},{16,9}... | collective-permute-start | bytes 294920 | tf_op jit(solution)/shard_map/ppermute | solution.py:17
  633.9 15.3 %collective-permute-start.7 = (f32[8,4096]{1,0:T(8,128)S(1)}, f32[8,4096]{1,0:T(8,128)S(1)}, u32[]{:S(2)}, u32[]{:S(2)}) collective-permute-start(f32[8,4096]{1,0:T(8,128)S(1)} %reshape.5023), channel_id=1, source_target_pairs={{0,1},{1,2},{2,3},{3,4},{4,5},{5,6},{6,7},{7,8},{8,9},{9,10},{10,1... | collective-permute-start | bytes 393224 | tf_op jit(solution)/shard_map/ppermute | solution.py:17
  636.4 16.4 %collective-permute-start.8 = (f32[8,4096]{1,0:T(8,128)S(1)}, f32[8,4096]{1,0:T(8,128)S(1)}, u32[]{:S(2)}, u32[]{:S(2)}) collective-permute-start(f32[8,4096]{1,0:T(8,128)S(1)} %reshape.5023), channel_id=1, source_target_pairs={{0,2},{1,3},{2,4},{3,5},{4,6},{5,7},{6,8},{7,9},{8,10},{9,11},{10,... | collective-permute-start | bytes 393224 | tf_op jit(solution)/shard_map/ppermute | solution.py:17
  639.6 17.3 %collective-permute-start.9 = (f32[8,4096]{1,0:T(8,128)S(1)}, f32[8,4096]{1,0:T(8,128)S(1)}, u32[]{:S(2)}, u32[]{:S(2)}) collective-permute-start(f32[8,4096]{1,0:T(8,128)S(1)} %reshape.5023), channel_id=1, source_target_pairs={{0,3},{1,4},{2,5},{3,6},{4,7},{5,8},{6,9},{7,10},{8,11},{9,12},{10... | collective-permute-start | bytes 393224 | tf_op jit(solution)/shard_map/ppermute | solution.py:17
  643.1 13.8 %collective-permute-start.10 = (f32[8,4096]{1,0:T(8,128)S(1)}, f32[8,4096]{1,0:T(8,128)S(1)}, u32[]{:S(2)}, u32[]{:S(2)}) collective-permute-start(f32[8,4096]{1,0:T(8,128)S(1)} %reshape.5023), channel_id=1, source_target_pairs={{0,4},{1,5},{2,6},{3,7},{4,8},{5,9},{6,10},{7,11},{8,12},{9,13},{1... | collective-permute-start | bytes 393224 | tf_op jit(solution)/shard_map/ppermute | solution.py:17
  647.1 9.8 %collective-permute-start.11 = (f32[8,4096]{1,0:T(8,128)S(1)}, f32[8,4096]{1,0:T(8,128)S(1)}, u32[]{:S(2)}, u32[]{:S(2)}) collective-permute-start(f32[8,4096]{1,0:T(8,128)S(1)} %reshape.5023), channel_id=1, source_target_pairs={{0,5},{1,6},{2,7},{3,8},{4,9},{5,10},{6,11},{7,12},{8,13},{9,14},{... | collective-permute-start | bytes 393224 | tf_op jit(solution)/shard_map/ppermute | solution.py:17
  649.2 7.7 %collective-permute-start.12 = (f32[8,4096]{1,0:T(8,128)S(1)}, f32[8,4096]{1,0:T(8,128)S(1)}, u32[]{:S(2)}, u32[]{:S(2)}) collective-permute-start(f32[8,4096]{1,0:T(8,128)S(1)} %reshape.5023), channel_id=1, source_target_pairs={{0,6},{1,7},{2,8},{3,9},{4,10},{5,11},{6,12},{7,13},{8,14},{9,15},... | collective-permute-start | bytes 393224 | tf_op jit(solution)/shard_map/ppermute | solution.py:17
  652.9 6.5 collective-permute-start.13
  (8 other events, 11.0 us)
where the time goes:
time: 714 us; the launch traced here: 706 us
  local copies, waits for them, and re-layouts  438 us (61%)
  other arithmetic  175 us (25%)
  blocking collectives  49.7 us (7%)
  starting transfers between devices  32 us (4%)
  waiting for transfers between devices  8.11 us (1%)
    mul x15, other arithmetic, lift_rows(): low_part * INVERSE_SCALE  69.8 us
    concatenate x60, local copies, waits for them, and re-layouts, lift_rows(): jnp.concatenate([low_part[:, 1:], low_part[:, -1:]], 1)  60.3 us
    concatenate x60, local copies, waits for them, and re-layouts, lift_rows(): jnp.concatenate([high_part[:, :1], high_part[:, :-1]], 1) + high_part  52.5 us
    slice x15, local copies, waits for them, and re-layouts, lift_rows(): high_part = paired[:, :, 1]  49.7 us
    unnamed x1, blocking collectives  49.7 us
    another operation x15, local copies, waits for them, and re-layouts, lift_rows(): paired = values.reshape(slot_count, length // 2, 2, others)  45.5 us
    unnamed x78, local copies, waits for them, and re-layouts  42.4 us
    transpose x12, other arithmetic, one_level(): jnp.transpose(lifted.reshape(slot_count, length, length, length), (0, 2,...  37.4 us
  transfers between devices with their start and end apart: 14, of which 2 were waited for; matrix products, arithmetic and copies ran while one was open for 7% of the time, Pallas kernels for 0%

commit v1 on v0

v1 whole, which is shorter than its diff:
```python
import functools

import jax
import jax.numpy as jnp
import numpy as np
from jax import lax
from jax.experimental import pallas as pl
from jax.experimental.pallas import tpu as pltpu
from jax.sharding import PartitionSpec as P

ALPHA = -1.586134342059924
BETA = -0.052980118572961
GAMMA = 0.882911075530934
DELTA = 0.443506852043971
SCALE = 1.230174104914001
SQUARE = SCALE * SCALE
F32 = jnp.float32
BF16 = jnp.bfloat16
AXES = ("node", "dev")
MIB = 1 << 20


def pass_matrix(n):
    low, high = np.eye(n)[0::2], np.eye(n)[1::2]

    def after(v):
        return np.concatenate([v[1:], v[-1:]], 0)

    def before(v):
        return np.concatenate([v[:1], v[:-1]], 0)

    high = high + ALPHA * (low + after(low))
    low = low + BETA * (before(high) + high)
    high = high + GAMMA * (low + after(low))
    low = low + DELTA * (before(high) + high)
    return np.concatenate([low / SCALE, high * SCALE], 0)


def two_terms(matrix):
    matrix = np.asarray(matrix, np.float32)
    first = matrix.astype(BF16)
    return first, (matrix - first.astype(np.float32)).astype(BF16)


def left_terms(matrix):
    first, second = two_terms(matrix)
    return np.concatenate([first, second, first], 1)


def split(value):
    first = value.astype(BF16)
    return first, (value - first.astype(F32)).astype(BF16)


def dot(left, right):
    return jnp.dot(left, right, preferred_element_type=F32)


def times(value, first, second):
    high, low = split(value)
    return dot(high, first) + dot(low, first) + dot(high, second)


def times_left(terms, value):
    high, low = split(value)
    return dot(terms, jnp.concatenate([high, high, low], 0))


def lowpass_kernel(x_ref, wh_ref, wl_ref, ax_ref, out_ref, acc_ref):
    step = pl.program_id(0)
    slots, edge, width = x_ref.shape
    part = times(x_ref[...].reshape(slots * edge, width), wh_ref[...], wl_ref[...])

    @pl.when(step == 0)
    def _():
        acc_ref[...] = part

    @pl.when(step > 0)
    def _():
        acc_ref[...] += part

    @pl.when(step == pl.num_programs(0) - 1)
    def _():
        for slot in range(slots):
            out_ref[slot] = times_left(ax_ref[...], acc_ref[pl.ds(slot * edge, edge), :])


def lowpass_call(density):
    slots, edge, plane = density.shape
    quarter = edge // 4
    two_levels = pass_matrix(edge // 2)[:quarter] @ pass_matrix(edge)[: edge // 2]
    first, second = two_terms(np.kron(two_levels.T, two_levels.T))
    terms = left_terms(two_levels)
    steps = 8
    width = plane // steps
    cols = quarter * quarter
    return pl.pallas_call(
        lowpass_kernel,
        grid=(steps,),
        in_specs=[
            pl.BlockSpec((slots, edge, width), lambda j: (0, 0, j)),
            pl.BlockSpec((width, cols), lambda j: (j, 0)),
            pl.BlockSpec((width, cols), lambda j: (j, 0)),
            pl.BlockSpec(terms.shape, lambda j: (0, 0)),
        ],
        out_specs=pl.BlockSpec((slots, quarter, cols), lambda j: (0, 0, 0)),
        out_shape=jax.ShapeDtypeStruct((slots, quarter, cols), F32),
        scratch_shapes=[pltpu.VMEM((slots * edge, cols), F32)],
        compiler_params=pltpu.CompilerParams(vmem_limit_bytes=24 * MIB),
        cost_estimate=pl.CostEstimate(
            flops=6 * slots * edge * plane * cols, bytes_accessed=10 * MIB, transcendentals=0
        ),
        name="lowpass",
    )(density, first, second, terms)


def lift(low, high, low_end, high_end, scaled):
    up = SQUARE if scaled else 1.0
    count = len(low)

    def raise_high(factor):
        last = low_end(low)
        for i in range(count):
            follow = low[i + 1] if i + 1 < count else last
            high[i] = high[i] + (factor * up) * (low[i] + follow)

    def raise_low(factor):
        previous = high_end(high)
        for i in range(count):
            low[i] = low[i] + (factor / up) * (previous + high[i])
            previous = high[i]

    raise_high(ALPHA)
    raise_low(BETA)
    raise_high(GAMMA)
    raise_low(DELTA)


def fine_kernel(
    count_ref, x_ref, w1h_ref, w1l_ref, w2h_ref, w2l_ref, out_ref, xh_ref, xl_ref, y_ref, z_ref, c_ref, d_ref
):
    slot = pl.program_id(0)
    edge = x_ref.shape[1]
    pairs = x_ref.shape[2] // 256
    half = edge // 2
    lane = lax.broadcasted_iota(jnp.int32, (8, 128), 1)
    row = lax.broadcasted_iota(jnp.int32, (8, 128), 0)
    front = lane < 64
    inner = (lane & 63) < half

    def turn(value):
        return pltpu.roll(value, 64, 1)

    def low_end_lanes(low):
        return jnp.where(front, turn(low[0]), low[-1])

    def high_end_lanes(high):
        return jnp.where(front, high[0], turn(high[-1]))

    def low_end_rows(low):
        return jnp.where(row < 7, pltpu.roll(low[0], 7, 0), low[-1])

    def high_end_rows(high):
        return jnp.where(row > 0, pltpu.roll(high[-1], 1, 0), high[0])

    @pl.when(slot >= count_ref[0])
    def _():
        out_ref[...] = jnp.zeros_like(out_ref)

    @pl.when(slot < count_ref[0])
    def _():
        for j in range(pairs):
            for q in range(2):
                tile = x_ref[0, :, pl.ds((j + q * pairs) * 128, 128)]
                high, low = split(tile)
                xh_ref[pl.ds(j * edge, edge), pl.ds(q * 128, 128)] = high
                xl_ref[pl.ds(j * edge, edge), pl.ds(q * 128, 128)] = low
        lifted = (
            dot(xh_ref[...], w1h_ref[...])
            + dot(xl_ref[...], w1h_ref[...])
            + dot(xh_ref[...], w1l_ref[...])
        )
        y_ref[0] = lifted[:, :128].reshape(pairs, edge, 128)
        y_ref[1] = lifted[:, 128:].reshape(pairs, edge, 128)

        @pl.loop(0, edge // 8)
        def _(r):
            rows = pl.ds(pl.multiple_of(r * 8, 8), 8)
            low = [y_ref[0, j, rows, :] for j in range(pairs)]
            high = [y_ref[1, j, rows, :] for j in range(pairs)]
            lift(low, high, low_end_lanes, high_end_lanes, True)
            for j in range(pairs):
                y_ref[0, j, rows, :] = low[j]
                y_ref[1, j, rows, :] = high[j]

        for part in range(2):

            @pl.loop(0, pairs // 2)
            def _(t):
                made = []
                for u in range(2):
                    j = 2 * t + u
                    low = [y_ref[part, j, pl.ds(2 * m, 8, stride=8), :] for m in range(4)]
                    high = [y_ref[part, j, pl.ds(2 * m + 1, 8, stride=8), :] for m in range(4)]
                    lift(low, high, low_end_rows, high_end_rows, False)
                    low = [v * (1.0 / SCALE) for v in low]
                    high = [v * SCALE for v in high]
                    if part == 0:
                        for m in range(4):
                            c_ref[u, t, pl.ds(8 * m, 8), :] = low[m]
                    made.append(low + high)
                for m in range(8):
                    a, b = made[0][m], made[1][m]
                    rows = pl.ds((m % 4) + half * (m // 4), 8, stride=4)
                    z_ref[part * pairs + t, rows, :] = jnp.where(front, a, turn(b))
                    z_ref[part * pairs + pairs // 2 + t, rows, :] = jnp.where(front, turn(a), b)

        corner = jnp.concatenate(
            [c_ref[0].reshape(pairs // 2 * 32, 128), c_ref[1].reshape(pairs // 2 * 32, 128)], 1
        )
        lifted = times(corner, w2h_ref[...], w2l_ref[...])
        c_ref[0] = lifted[:, :128].reshape(pairs // 2, 32, 128)
        c_ref[1] = lifted[:, 128:].reshape(pairs // 2, 32, 128)

        @pl.loop(0, 4)
        def _(r):
            rows = pl.ds(pl.multiple_of(r * 8, 8), 8)
            low = [c_ref[0, j, rows, :] for j in range(pairs // 2)]
            high = [c_ref[1, j, rows, :] for j in range(pairs // 2)]
            lift(low, high, low_end_lanes, high_end_lanes, True)
            for j in range(pairs // 2):
                c_ref[0, j, rows, :] = low[j]
                c_ref[1, j, rows, :] = high[j]

        for part in range(2):

            @pl.loop(0, pairs // 4)
            def _(t):
                made = []
                for u in range(2):
                    j = 2 * t + u
                    low = [c_ref[part, j, pl.ds(16 * m, 8), :] for m in range(2)]
                    high = [c_ref[part, j, pl.ds(16 * m + 8, 8), :] for m in range(2)]
                    lift(low, high, low_end_rows, high_end_rows, False)
                    low = [v * (1.0 / SCALE) for v in low]
                    high = [v * SCALE for v in high]
                    made.append(low + high)
                for m in range(4):
                    a, b = made[0][m], made[1][m]
                    rows = pl.ds((m % 2) + half // 2 * (m // 2), 8, stride=2)
                    d_ref[part * (pairs // 2) + t, rows, :] = jnp.where(front, a, turn(b))
                    d_ref[part * (pairs // 2) + pairs // 4 + t, rows, :] = jnp.where(front, turn(a), b)

        for t in range(2 * pairs):
            for r in range(edge // 8):
                rows = pl.ds(8 * r, 8)
                value = z_ref[t, rows, :]
                if t < pairs and r < half // 8:
                    value = jnp.where(inner, d_ref[t, rows, :], value)
                out_ref[0, rows, pl.ds(t * 128, 128)] = value


def fine_call(owner_counts, density):
    slots, edge, plane = density.shape
    half = edge // 2
    pairs = plane // 256
    one = pass_matrix(edge).T
    zero = np.zeros_like(one)
    w1 = np.block(
        [
            [one / SCALE, zero, zero, zero],
            [zero, zero, one * SCALE, zero],
            [zero, one / SCALE, zero, zero],
            [zero, zero, zero, one * SCALE],
        ]
    )
    two = np.zeros_like(one)
    two[:half, :half] = pass_matrix(half).T
    w2 = np.kron(np.diag([1 / SCALE, 1 / SCALE, SCALE, SCALE]), two)
    w1h, w1l = two_terms(w1)
    w2h, w2l = two_terms(w2)
    fixed = pl.BlockSpec((256, 256), lambda s: (0, 0))
    return pl.pallas_call(
        fine_kernel,
        grid=(slots,),
        in_specs=[
            pl.BlockSpec(memory_space=pltpu.SMEM),
            pl.BlockSpec((1, edge, plane), lambda s: (s, 0, 0)),
            fixed,
            fixed,
            fixed,
            fixed,
        ],
        out_specs=pl.BlockSpec((1, edge, plane), lambda s: (s, 0, 0)),
        out_shape=jax.ShapeDtypeStruct(density.shape, F32),
        scratch_shapes=[
            pltpu.VMEM((pairs * edge, 256), BF16),
            pltpu.VMEM((pairs * edge, 256), BF16),
            pltpu.VMEM((2, pairs, edge, 128), F32),
            pltpu.VMEM((2 * pairs, edge, 128), F32),
            pltpu.VMEM((2, pairs // 2, 32, 128), F32),
            pltpu.VMEM((pairs, 32, 128), F32),
        ],
        compiler_params=pltpu.CompilerParams(vmem_limit_bytes=32 * MIB),
        cost_estimate=pl.CostEstimate(
            flops=6 * slots * edge * plane * 256, bytes_accessed=12 * MIB, transcendentals=0
        ),
        name="fine",
    )(owner_counts, density, w1h, w1l, w2h, w2l)


def coarse_kernel(
    index_ref,
    table_ref,
    wx_ref,
    wzh_ref,
    wzl_ref,
    wyh_ref,
    wyl_ref,
    w23h_ref,
    w23l_ref,
    wx2_ref,
    wx3_ref,
    fine_ref,
    out_ref,
    piece_ref,
    block_ref,
    corner_ref,
    piece_sem,
    corner_sem,
    out_sem,
):
    slots = corner_ref.shape[0]
    lane = lax.broadcasted_iota(jnp.int32, (16, 128), 1)

    def piece_copy(i):
        return pltpu.make_async_copy(table_ref.at[index_ref[i]], piece_ref.at[i], piece_sem.at[i])

    def window(s):
        return out_ref.at[s, pl.ds(0, 16), pl.ds(0, 1024)]

    for i in range(16):
        piece_copy(i).start()
    for s in range(slots):
        pltpu.make_async_copy(window(s), corner_ref.at[s], corner_sem.at[s]).start()
    for i in range(16):
        piece_copy(i).wait()

    first = [
        [times_left(wx_ref[...], piece_ref[pl.ds(o * 8 + 2 * q, 2)].reshape(32, 256)) for q in range(4)]
        for o in range(2)
    ]
    stacked = []
    for o in range(2):
        for cy in range(2):
            for yh in range(2):
                part = slice(yh * 128, yh * 128 + 128)
                stacked.append(jnp.concatenate([first[o][cy][:, part], first[o][2 + cy][:, part]], 1))
    lifted = times(jnp.concatenate(stacked, 0), wzh_ref[...], wzl_ref[...])
    stacked = []
    for o in range(2):
        for tz in range(2):
            stacked.append(
                jnp.concatenate(
                    [lifted[(o * 4 + u) * 32 : (o * 4 + u + 1) * 32, tz * 128 : tz * 128 + 128] for u in range(4)],
                    1,
                )
            )
    lifted = times(jnp.concatenate(stacked, 0), wyh_ref[...], wyl_ref[...])
    corner = []
    for o in range(2):
        for tz in range(2):
            for ty in range(2):
                for tx in range(2):
                    at = (o * 2 + tz) * 32 + tx * 16
                    value = lifted[at : at + 16, ty * 256 : ty * 256 + 256]
                    if tx + ty + tz == 0:
                        corner.append(value)
                    else:
                        block_ref[o * 8 + tx + 2 * ty + 4 * tz] = value
    both = times(jnp.concatenate(corner, 0), w23h_ref[...], w23l_ref[...])
    spot = lax.broadcasted_iota(jnp.int32, (16, 256), 1)
    depth = lax.broadcasted_iota(jnp.int32, (16, 256), 0)
    small = (depth < 8) & (spot < 128) & ((spot & 15) < 8)
    for o in range(2):
        mine = both[o * 16 : o * 16 + 16]
        second = times_left(wx2_ref[...], mine[:, :256])
        third = times_left(wx3_ref[...], mine[:, 256:])
        block_ref[o * 8] = jnp.where(small, third, second)

    for s in range(slots):
        pltpu.make_async_copy(window(s), corner_ref.at[s], corner_sem.at[s]).wait()
    for s in range(slots):

        @pl.when(index_ref[16 + slots + s] > 0)
        def _():
            value = block_ref[index_ref[16 + s]]
            for t in range(8):
                tile = value[:, (t // 4) * 128 : (t // 4) * 128 + 128]
                near = pltpu.roll(tile, (128 - 32 * (t % 4)) % 128, 1)
                far = pltpu.roll(tile, (64 - 16 - 32 * (t % 4)) % 128, 1)
                old = corner_ref[s, :, pl.ds(t * 128, 128)]
                new = jnp.where(lane < 16, near, jnp.where((lane >= 64) & (lane < 80), far, old))
                corner_ref[s, :, pl.ds(t * 128, 128)] = new
            pltpu.make_async_copy(corner_ref.at[s], window(s), out_sem.at[s]).start()

    for s in range(slots):

        @pl.when(index_ref[16 + slots + s] > 0)
        def _():
            pltpu.make_async_copy(corner_ref.at[s], window(s), out_sem.at[s]).wait()


def coarse_call(index, table, fine):
    slots, edge, plane = fine.shape
    m32, m16, m8 = pass_matrix(32), pass_matrix(16), pass_matrix(8)
    deep = np.zeros((16, 16))
    deep[:8] = m8 @ m16[:8]
    eye8, eye16 = np.eye(8), np.eye(16)
    wz = np.zeros((256, 256))
    for cz in range(2):
        for tz in range(2):
            wz[cz * 128 : cz * 128 + 128, tz * 128 : tz * 128 + 128] = np.kron(
                eye8, m32[tz * 16 : tz * 16 + 16, cz * 16 : cz * 16 + 16].T
            )
    w23 = np.concatenate([np.kron(m16.T, m16.T), np.kron(deep.T, deep.T)], 1)
    weights = [
        left_terms(m32),
        *two_terms(wz),
        *two_terms(np.kron(m32.T, eye16)),
        *two_terms(w23),
        left_terms(m16),
        left_terms(deep),
    ]
    anywhere = pl.BlockSpec(memory_space=pl.ANY)
    vmem = pl.BlockSpec(memory_space=pltpu.VMEM)
    return pl.pallas_call(
        coarse_kernel,
        in_specs=[pl.BlockSpec(memory_space=pltpu.SMEM), anywhere] + [vmem] * len(weights) + [anywhere],
        out_specs=anywhere,
        out_shape=jax.ShapeDtypeStruct(fine.shape, F32),
        scratch_shapes=[
            pltpu.VMEM((16, 16, 256), F32),
            pltpu.VMEM((16, 16, 256), F32),
            pltpu.VMEM((slots, 16, 1024), F32),
            pltpu.SemaphoreType.DMA((16,)),
            pltpu.SemaphoreType.DMA((slots,)),
            pltpu.SemaphoreType.DMA((slots,)),
        ],
        input_output_aliases={2 + len(weights): 0},
        compiler_params=pltpu.CompilerParams(vmem_limit_bytes=16 * MIB),
        name="coarse",
    )(index, table, *weights, fine)


def find_pieces(counts, me, slots):
    starts = jnp.cumsum(counts) - counts
    devices = jnp.arange(counts.shape[0], dtype=jnp.int32)
    start = jnp.sum(jnp.where(devices < me, counts, 0))
    count = jnp.sum(jnp.where(devices == me, counts, 0))
    base = start // 8 * 8
    blocks = base + jnp.arange(16, dtype=jnp.int32)
    inside = (starts[None, :] <= blocks[:, None]) & (blocks[:, None] < (starts + counts)[None, :])
    rows = jnp.sum(
        jnp.where(inside, devices[None, :] * slots + blocks[:, None] - starts[None, :], 0), axis=1
    )
    slot_ids = jnp.arange(slots, dtype=jnp.int32)
    return jnp.concatenate([rows, start - base + slot_ids, (slot_ids < count).astype(jnp.int32)])


def gather_counts(owner_counts):
    sent = lax.optimization_barrier(jnp.broadcast_to(owner_counts[0], (8, 128)))
    every = lax.all_gather(sent, AXES, axis=0, tiled=True)
    return every.reshape(-1, 8, 128)[:, 0, 0]


def per_device(density, owner_counts):
    slots = density.shape[0]
    counts = gather_counts(owner_counts)
    index = find_pieces(counts, lax.axis_index(AXES), slots)
    lowpass = lowpass_call(density)
    table = lax.all_gather(lowpass, AXES, axis=0, tiled=True)
    fine = fine_call(owner_counts, density)
    return coarse_call(index, table, fine)


def solution(mesh):
    in_specs = (P(AXES, None, None), P(AXES))
    out_specs = P(AXES, None, None)
    return jax.shard_map(per_device, mesh=mesh, in_specs=in_specs, out_specs=out_specs, check_vma=False)
```

time: 714 us -> 155 us (0.22); the launches traced: 706 us -> 154 us
  local copies, waits for them, and re-layouts: 438 us -> 12 us
  other arithmetic: 175 us -> 1.72 us
  Pallas kernels: 0 us -> 52.4 us
  starting transfers between devices: 32 us -> 0.01 us
  blocking collectives: 49.7 us -> 70.8 us
  between operations: 3.62 us -> 17.5 us
  waiting for transfers between devices: 8.11 us -> 0.02 us
    concatenate x122 -> x0, local copies, waits for them, and re-layouts: 113 us -> none  [the longest x60 60.3 us: lift_rows(): jnp.concatenate([low_part[:, 1:], low_part[:, -1:]], 1)]
    slice x127 -> x1, local copies, waits for them, and re-layouts: 86.1 us -> 0.66 us  [gather_counts(): return every.reshape(-1, 8, 128)[:, 0, 0]]
    all_gather x0 -> x1, blocking collectives: none -> 70.8 us  [gather_counts(): every = lax.all_gather(sent, AXES, axis=0, tiled=True)]
    mul x16 -> x0, other arithmetic: 70.5 us -> none  [the longest x15 69.8 us: lift_rows(): low_part * INVERSE_SCALE]
    pallas_call x0 -> x3, Pallas kernels: none -> 52.4 us  [the longest x1 43.1 us: fine_call(): pl.pallas_call(fine_kernel, grid=(slots,), in_specs=[pl.BlockSpec(memory_...]
    unnamed x1 -> x0, blocking collectives: 49.7 us -> none
    another operation x18 -> x0, local copies, waits for them, and re-layouts: 48.4 us -> none  [the longest x15 45.5 us: lift_rows(): paired = values.reshape(slot_count, length // 2, 2, others)]
    add x46 -> x2, other arithmetic: 45.4 us -> 0.01 us  [the longest x1 0.01 us: find_pieces(): start - base + slot_ids]
  transfers between devices with their start and end apart: 14 -> 1, of which waited for: 2 -> 0; matrix products, arithmetic and copies ran while one was open for 7% -> 2% of each run, Pallas kernels for 0% -> 28%
where the time goes in v1:
time: 155 us; the launch traced here: 154 us
  blocking collectives  70.8 us (46%)
  Pallas kernels  52.4 us (34%)
  between operations  17.5 us (11%)
  local copies, waits for them, and re-layouts  12 us (8%)
  other arithmetic  1.72 us (1%)
    all_gather x1, blocking collectives, gather_counts(): every = lax.all_gather(sent, AXES, axis=0, tiled=True)  70.8 us
    pallas_call x1, Pallas kernels, fine_call(): pl.pallas_call(fine_kernel, grid=(slots,), in_specs=[pl.BlockSpec(memory_...  43.1 us
    unnamed x38, local copies, waits for them, and re-layouts  11.4 us
    pallas_call x1, Pallas kernels, lowpass_call(): pl.pallas_call(lowpass_kernel, grid=(steps,), in_specs=[pl.BlockSpec((slo...  5.56 us
    pallas_call x1, Pallas kernels, coarse_call(): pl.pallas_call(coarse_kernel, in_specs=[pl.BlockSpec(memory_space=pltpu.S...  3.74 us
  transfers between devices with their start and end apart: 1, of which 0 were waited for; matrix products, arithmetic and copies ran while one was open for 2% of the time, Pallas kernels for 28%

profile of v1, /device:TPU:0, one launch (start us, length us, event | category | flops | bytes accessed | tf_op | source)
XLA Modules:
  0.0 154.4 jit_solution(4962865345008501391)
XLA Ops:
  6.5 0.0 all-gather.2.cloned.1.call-start
  6.5 2.8 %copy-done = f32[6,64,4096]{2,1,0:T(8,128)S(1)} copy-done((f32[6,64,4096]{2,1,0:T(8,128)S(1)}, f32[6,64,4096]{2,1,0:T(8,128)}, u32[]{:S(2)}) %copy-start) | copy-done | bytes 6291480
  9.3 1.6 %copy-done.3 = bf16[4096,256]{1,0:T(8,128)(2,1)S(1)} copy-done((bf16[4096,256]{1,0:T(8,128)(2,1)S(1)}, bf16[4096,256]{1,0:T(8,128)(2,1)}, u32[]{:S(2)}) %copy-start.3) | copy-done | bytes 2097176
  10.9 1.6 %copy-done.4 = bf16[4096,256]{1,0:T(8,128)(2,1)S(1)} copy-done((bf16[4096,256]{1,0:T(8,128)(2,1)S(1)}, bf16[4096,256]{1,0:T(8,128)(2,1)}, u32[]{:S(2)}) %copy-start.4) | copy-done | bytes 2097176
  12.5 0.7 copy-done.16
  13.2 5.6 %lowpass.1 = f32[6,16,256]{2,1,0:T(8,128)} custom-call(f32[6,64,4096]{2,1,0:T(8,128)S(1)} %copy-done, bf16[4096,256]{1,0:T(8,128)(2,1)S(1)} %copy-done.4, bf16[4096,256]{1,0:T(8,128)(2,1)S(1)} %copy-done.3, bf16[16,192]{1,0:T(8,128)(2,1)S(1)} %copy-done.16), custom_call_target="tpu_custom_call" | custom-call | flops 2415919104 | bytes 10485760 | tf_op jit(solution)/shard_map/lowpass/pallas_call | solution.py:97
  18.8 0.0 all-gather.2.cloned.1.call-update
  19.5 70.8 %all_gather.6 = s32[256,128]{1,0:T(8,128)S(1)} all-gather(s32[8,128]{1,0:T(8,128)S(1)} %broadcast_in_dim.10), channel_id=1, replica_groups=mesh['node'=8,'dev'=4] {'node','dev'}, dimensions={0}, use_global_device_ids=true | all-gather | bytes 135168 | tf_op jit(solution)/shard_map/all_gather | solution.py:473
  90.2 0.7 fusion.2
  90.9 0.1 reduce-window.7
  90.9 0.1 reduce
  91.1 0.7 fusion
  95.0 0.6 compare_convert_fusion
  95.6 0.2 select_reduce_fusion
  95.8 0.1 pad_add_fusion.index_ref
  95.9 0.0 copy-done.11
  95.9 0.0 copy-done.12
  95.9 0.0 copy-done.13
  95.9 0.0 copy-done.14
  95.9 0.0 copy-start.1
  95.9 2.8 %copy-done.1 = f32[6,64,4096]{2,1,0:T(8,128)S(1)} copy-done((f32[6,64,4096]{2,1,0:T(8,128)S(1)}, f32[6,64,4096]{2,1,0:T(8,128)}, u32[]{:S(2)}) %copy-start.1) | copy-done | bytes 6291480
  98.7 0.0 copy-start.9
  98.7 0.0 copy-start.10
  98.7 0.0 copy-start.15
  98.8 0.0 copy-start.17
  98.8 0.0 copy-start.18
  98.8 43.1 %fine.1.fine_ref = f32[6,64,4096]{2,1,0:T(8,128)} custom-call(s32[1]{0:T(128)} %copy.26.count_ref, f32[6,64,4096]{2,1,0:T(8,128)S(1)} %copy-done.1, bf16[256,256]{1,0:T(8,128)(2,1)S(1)} %copy-done.14, bf16[256,256]{1,0:T(8,128)(2,1)S(1)} %copy-done.13, bf16[256,256]{1,0:T(8,128)(2,1)S(1)} %copy-done.12, bf16[256,256]{1,0:T(8,128)(2,1)S(1)} %copy-done.11), custom_call_target="tpu_custom_call" | custom-call | flops 2415919104 | bytes 12582912 | tf_op jit(solution)/shard_map/fine/pallas_call | solution.py:283
  141.9 0.0 copy-done.5
  141.9 0.0 copy-done.6
  141.9 0.0 copy-done.7
  142.0 1.9 %copy-done.2 = f32[192,16,256]{2,1,0:T(8,128)S(1)} copy-done((f32[192,16,256]{2,1,0:T(8,128)S(1)}, f32[192,16,256]{2,1,0:T(8,128)}, u32[]{:S(2)}) %copy-start.2) | copy-done | bytes 3145752
  143.8 3.7 %coarse.1 = f32[6,64,4096]{2,1,0:T(8,128)} custom-call(s32[28]{0:T(128)S(1)} %pad_add_fusion.index_ref, f32[192,16,256]{2,1,0:T(8,128)S(1)} %copy-done.2, bf16[32,96]{1,0:T(8,128)(2,1)S(1)} %copy-done.15, bf16[256,256]{1,0:T(8,128)(2,1)S(1)} %copy-done.10, bf16[256,256]{1,0:T(8,128)(2,1)S(1)} %copy-done.9, ...), custom_call_target="tpu_custom_call", output_to_operand_aliasing={{}: (11, {})} | custom-call | tf_op jit(solution)/shard_map/coarse/pallas_call | solution.py:437
  (23 shorter events, 0.0 us)
Async XLA Ops:
  6.5 135.3 %all-gather.2.cloned.1.call-start = ((), (), s32[]{:S(2)}) async-start(), calls=%async_computation | async-start | bytes 3244032 | tf_op jit(solution)/shard_map/all_gather | solution.py:482
  6.5 2.8 %copy-start = (f32[6,64,4096]{2,1,0:T(8,128)S(1)}, f32[6,64,4096]{2,1,0:T(8,128)}, u32[]{:S(2)}) copy-start(f32[6,64,4096]{2,1,0:T(8,128)} %x_ref.3) | copy-start | bytes 18874372
  9.3 1.6 %copy-start.3 = (bf16[4096,256]{1,0:T(8,128)(2,1)S(1)}, bf16[4096,256]{1,0:T(8,128)(2,1)}, u32[]{:S(2)}) copy-start(bf16[4096,256]{1,0:T(8,128)(2,1)} %constant.67.clone.wl_ref) | copy-start | bytes 6291460
  10.9 1.6 %copy-start.4 = (bf16[4096,256]{1,0:T(8,128)(2,1)S(1)}, bf16[4096,256]{1,0:T(8,128)(2,1)}, u32[]{:S(2)}) copy-start(bf16[4096,256]{1,0:T(8,128)(2,1)} %constant.66.clone.wh_ref) | copy-start | bytes 6291460
  12.5 0.7 copy-start.16
  13.2 82.7 %copy-start.11 = (bf16[256,256]{1,0:T(8,128)(2,1)S(1)}, bf16[256,256]{1,0:T(8,128)(2,1)}, u32[]{:S(2)}) copy-start(bf16[256,256]{1,0:T(8,128)(2,1)} %constant.72.clone.w2l_ref) | copy-start | bytes 393220
  13.2 82.7 %copy-start.12 = (bf16[256,256]{1,0:T(8,128)(2,1)S(1)}, bf16[256,256]{1,0:T(8,128)(2,1)}, u32[]{:S(2)}) copy-start(bf16[256,256]{1,0:T(8,128)(2,1)} %constant.71.clone.w2h_ref) | copy-start | bytes 393220
  13.2 82.7 %copy-start.13 = (bf16[256,256]{1,0:T(8,128)(2,1)S(1)}, bf16[256,256]{1,0:T(8,128)(2,1)}, u32[]{:S(2)}) copy-start(bf16[256,256]{1,0:T(8,128)(2,1)} %constant.70.clone.w1l_ref) | copy-start | bytes 393220
  13.2 82.7 %copy-start.14 = (bf16[256,256]{1,0:T(8,128)(2,1)S(1)}, bf16[256,256]{1,0:T(8,128)(2,1)}, u32[]{:S(2)}) copy-start(bf16[256,256]{1,0:T(8,128)(2,1)} %constant.69.clone.w1h_ref) | copy-start | bytes 393220
  95.9 2.8 %copy-start.1 = (f32[6,64,4096]{2,1,0:T(8,128)S(1)}, f32[6,64,4096]{2,1,0:T(8,128)}, u32[]{:S(2)}) copy-start(f32[6,64,4096]{2,1,0:T(8,128)} %x_ref.3) | copy-start | bytes 18874372
  98.7 43.2 %copy-start.5 = (bf16[512,512]{1,0:T(8,128)(2,1)S(1)}, bf16[512,512]{1,0:T(8,128)(2,1)}, u32[]{:S(2)}) copy-start(bf16[512,512]{1,0:T(8,128)(2,1)} %constant.77.clone.wyl_ref) | copy-start | bytes 1572868
  98.7 43.2 %copy-start.6 = (bf16[512,512]{1,0:T(8,128)(2,1)S(1)}, bf16[512,512]{1,0:T(8,128)(2,1)}, u32[]{:S(2)}) copy-start(bf16[512,512]{1,0:T(8,128)(2,1)} %constant.76.clone.wyh_ref) | copy-start | bytes 1572868
  98.7 43.2 %copy-start.7 = (bf16[256,512]{1,0:T(8,128)(2,1)S(1)}, bf16[256,512]{1,0:T(8,128)(2,1)}, u32[]{:S(2)}) copy-start(bf16[256,512]{1,0:T(8,128)(2,1)} %constant.79.clone.w23l_ref) | copy-start | bytes 786436
  98.7 43.2 %copy-start.8 = (bf16[256,512]{1,0:T(8,128)(2,1)S(1)}, bf16[256,512]{1,0:T(8,128)(2,1)}, u32[]{:S(2)}) copy-start(bf16[256,512]{1,0:T(8,128)(2,1)} %constant.78.clone.w23h_ref) | copy-start | bytes 786436
  98.7 43.2 %copy-start.9 = (bf16[256,256]{1,0:T(8,128)(2,1)S(1)}, bf16[256,256]{1,0:T(8,128)(2,1)}, u32[]{:S(2)}) copy-start(bf16[256,256]{1,0:T(8,128)(2,1)} %constant.75.clone.wzl_ref) | copy-start | bytes 393220
  98.7 43.2 %copy-start.10 = (bf16[256,256]{1,0:T(8,128)(2,1)S(1)}, bf16[256,256]{1,0:T(8,128)(2,1)}, u32[]{:S(2)}) copy-start(bf16[256,256]{1,0:T(8,128)(2,1)} %constant.74.clone.wzh_ref) | copy-start | bytes 393220
  98.7 43.2 %copy-start.15 = (bf16[32,96]{1,0:T(8,128)(2,1)S(1)}, bf16[32,96]{1,0:T(8,128)(2,1)}, u32[]{:S(2)}) copy-start(bf16[32,96]{1,0:T(8,128)(2,1)} %constant.73.clone.wx_ref) | copy-start | bytes 18436
  98.8 43.2 %copy-start.17 = (bf16[16,48]{1,0:T(8,128)(2,1)S(1)}, bf16[16,48]{1,0:T(8,128)(2,1)}, u32[]{:S(2)}) copy-start(bf16[16,48]{1,0:T(8,128)(2,1)} %constant.81.clone.wx3_ref) | copy-start | bytes 4612
  98.8 43.2 %copy-start.18 = (bf16[16,48]{1,0:T(8,128)(2,1)S(1)}, bf16[16,48]{1,0:T(8,128)(2,1)}, u32[]{:S(2)}) copy-start(bf16[16,48]{1,0:T(8,128)(2,1)} %constant.80.clone.wx2_ref) | copy-start | bytes 4612
  141.9 1.9 %copy-start.2 = (f32[192,16,256]{2,1,0:T(8,128)S(1)}, f32[192,16,256]{2,1,0:T(8,128)}, u32[]{:S(2)}) copy-start(f32[192,16,256]{2,1,0:T(8,128)} %all-gather.2.cloned.1.call-done.table_ref) | copy-start | bytes 9437188
Sparse Core Ops, SparseCore 0:
  18.9 62.1 all-gather.1

commit v2 on v1

v2 whole, which is shorter than its diff:
```python
import functools

import jax
import jax.numpy as jnp
import numpy as np
from jax import lax
from jax.experimental import pallas as pl
from jax.experimental.pallas import tpu as pltpu
from jax.sharding import PartitionSpec as P

ALPHA = -1.586134342059924
BETA = -0.052980118572961
GAMMA = 0.882911075530934
DELTA = 0.443506852043971
SCALE = 1.230174104914001
SQUARE = SCALE * SCALE
F32 = jnp.float32
BF16 = jnp.bfloat16
AXES = ("node", "dev")
MIB = 1 << 20
VMEM_LIMIT = 56 * MIB


def pass_matrix(n):
    low, high = np.eye(n)[0::2], np.eye(n)[1::2]

    def after(v):
        return np.concatenate([v[1:], v[-1:]], 0)

    def before(v):
        return np.concatenate([v[:1], v[:-1]], 0)

    high = high + ALPHA * (low + after(low))
    low = low + BETA * (before(high) + high)
    high = high + GAMMA * (low + after(low))
    low = low + DELTA * (before(high) + high)
    return np.concatenate([low / SCALE, high * SCALE], 0)


def two_terms(matrix):
    matrix = np.asarray(matrix, np.float32)
    first = matrix.astype(BF16)
    return first, (matrix - first.astype(np.float32)).astype(BF16)


def left_terms(matrix):
    first, second = two_terms(matrix)
    return np.concatenate([first, second, first], 1)


def split(value):
    first = value.astype(BF16)
    return first, (value - first.astype(F32)).astype(BF16)


def dot(left, right):
    return jnp.dot(left, right, preferred_element_type=F32)


def times(value, first, second):
    high, low = split(value)
    return dot(high, first) + dot(low, first) + dot(high, second)


def times_left(terms, value):
    high, low = split(value)
    return dot(terms, jnp.concatenate([high, high, low], 0))


def lowpass_kernel(count_ref, x_ref, wh_ref, wl_ref, ax_ref, out_ref, acc_ref):
    step = pl.program_id(0)
    slots, edge, width = x_ref.shape
    part = times(x_ref[...].reshape(slots * edge, width), wh_ref[...], wl_ref[...])

    @pl.when(step == 0)
    def _():
        acc_ref[...] = part

    @pl.when(step > 0)
    def _():
        acc_ref[...] += part

    @pl.when(step == pl.num_programs(0) - 1)
    def _():
        out_ref[...] = jnp.full(out_ref.shape, count_ref[0].astype(F32))
        for slot in range(slots):
            made = times_left(ax_ref[...], acc_ref[pl.ds(slot * edge, edge), :])
            for h in range(2):
                out_ref[pl.ds(8 * h + slot, edge // 4, stride=16), :] = made[:, h * 128 : h * 128 + 128]


def lowpass_call(owner_counts, density):
    slots, edge, plane = density.shape
    quarter = edge // 4
    two_levels = pass_matrix(edge // 2)[:quarter] @ pass_matrix(edge)[: edge // 2]
    first, second = two_terms(np.kron(two_levels.T, two_levels.T))
    terms = left_terms(two_levels)
    steps = 8
    width = plane // steps
    cols = quarter * quarter
    pieces = pl.pallas_call(
        lowpass_kernel,
        grid=(steps,),
        in_specs=[
            pl.BlockSpec(memory_space=pltpu.SMEM),
            pl.BlockSpec((slots, edge, width), lambda j: (0, 0, j)),
            pl.BlockSpec((width, cols), lambda j: (j, 0)),
            pl.BlockSpec((width, cols), lambda j: (j, 0)),
            pl.BlockSpec(terms.shape, lambda j: (0, 0)),
        ],
        out_specs=pl.BlockSpec((16 * quarter, 128), lambda j: (0, 0)),
        out_shape=jax.ShapeDtypeStruct((16 * quarter, 128), F32),
        scratch_shapes=[pltpu.VMEM((slots * edge, cols), F32)],
        compiler_params=pltpu.CompilerParams(vmem_limit_bytes=VMEM_LIMIT),
        cost_estimate=pl.CostEstimate(
            flops=6 * slots * edge * plane * cols, bytes_accessed=10 * MIB, transcendentals=0
        ),
        name="lowpass",
    )(owner_counts, density, first, second, terms)
    return pieces.reshape(2 * quarter, 8, 128)


def route_kernel(me_ref, got_ref, send_ref, index_ref, order_ref, count_ref, sem):
    devices = got_ref.shape[0]
    copy = pltpu.make_async_copy(got_ref.at[:, 7, :], count_ref, sem)
    copy.start()
    order_ref[...] = jnp.zeros_like(order_ref)
    copy.wait()
    start, my_start, my_count = 0, 0, 0
    starts = []
    for d in range(devices):
        count = count_ref[d, 0].astype(jnp.int32)
        starts.append(start)
        my_start = jnp.where(me_ref[0] == d, start, my_start)
        my_count = jnp.where(me_ref[0] == d, count, my_count)
        order_ref[pl.ds(start, 8), :] = got_ref[d]
        start = start + count
    for d in range(devices):
        at = pl.multiple_of(starts[d] // 8 * 8, 8) if d else 0
        send_ref[d] = order_ref[pl.ds(at, 16), :]
    index_ref[0] = my_start % 8
    index_ref[1] = my_count


def route_call(me, got, slots):
    devices = got.shape[0]
    return pl.pallas_call(
        route_kernel,
        in_specs=[
            pl.BlockSpec(memory_space=pltpu.SMEM),
            pl.BlockSpec(memory_space=pltpu.VMEM),
        ],
        out_specs=[pl.BlockSpec(memory_space=pltpu.VMEM), pl.BlockSpec(memory_space=pltpu.SMEM)],
        out_shape=[
            jax.ShapeDtypeStruct((devices, 16, 128), F32),
            jax.ShapeDtypeStruct((2,), jnp.int32),
        ],
        scratch_shapes=[
            pltpu.VMEM((devices * slots + 16, 128), F32),
            pltpu.SMEM((devices, 128), F32),
            pltpu.SemaphoreType.DMA,
        ],
        compiler_params=pltpu.CompilerParams(vmem_limit_bytes=VMEM_LIMIT),
        name="route",
    )(me, got)


def lift(low, high, n, halo, scaled):
    up = SQUARE if scaled else 1.0
    at = 2 if halo else 0
    first, second, third, fourth = ({} for _ in range(4))

    def get(values, i, is_low):
        if halo:
            return values[i]
        return values[min(i, n - 1)] if is_low else values[max(i, 0)]

    lows = {i - at: low[i] for i in range(len(low))}
    highs = {i - at: high[i] for i in range(len(high))}

    def make_first(i):
        first[i] = highs[i] + (ALPHA * up) * (lows[i] + get(lows, i + 1, True))

    def make_second(i):
        second[i] = lows[i] + (BETA / up) * (get(first, i - 1, False) + first[i])

    def make_third(i):
        third[i] = first[i] + (GAMMA * up) * (second[i] + get(second, i + 1, True))

    def make_fourth(i):
        fourth[i] = second[i] + (DELTA / up) * (get(third, i - 1, False) + third[i])

    if halo:
        for i in range(-2, n + 1):
            make_first(i)
            if i >= -1:
                make_second(i)
            if i >= 0:
                make_third(i - 1)
            if i >= 1:
                make_fourth(i - 1)
    else:
        for i in range(n):
            make_first(i)
            make_second(i)
            if i >= 1:
                make_third(i - 1)
                make_fourth(i - 1)
        make_third(n - 1)
        make_fourth(n - 1)
    return [fourth[i] for i in range(n)], [third[i] for i in range(n)]


def fine_kernel(
    count_ref, x_ref, w1_ref, w2_ref, out_ref, l_ref, y_ref, z_ref, c_ref, d_ref, e_ref
):
    slot = pl.program_id(0)
    edge = x_ref.shape[1]
    pairs = x_ref.shape[2] // 256
    half = edge // 2
    lane = lax.broadcasted_iota(jnp.int32, (8, 128), 1)
    front = lane < 64
    inner = (lane & 63) < half

    def turn(value):
        return pltpu.roll(value, 64, 1)

    def with_halo(low, high):
        def left(values, i):
            return jnp.where(front, values[i[0]], turn(values[i[1]]))

        def right(values, i):
            return jnp.where(front, turn(values[i[0]]), values[i[1]])

        low_all = [left(low, (2, -2)), left(low, (1, -1))] + low + [right(low, (0, -1)), right(low, (1, -2))]
        high_all = [left(high, (1, -2)), left(high, (0, -1))] + high + [right(high, (0, -2))]
        return low_all, high_all

    @pl.when(slot >= count_ref[0])
    def _():
        out_ref[...] = jnp.zeros_like(out_ref)

    @pl.when(slot < count_ref[0])
    def _():
        for j in range(pairs):
            for q in range(2):
                high, low = split(x_ref[0, :, pl.ds((j + q * pairs) * 128, 128)])
                rows = pl.ds(j * edge, edge)
                l_ref[rows, pl.ds(q * 128, 128)] = high
                l_ref[rows, pl.ds(256 + q * 128, 128)] = low
                l_ref[rows, pl.ds(512 + q * 128, 128)] = high
        lifted = dot(l_ref[...], w1_ref[...])
        y_ref[pl.ds(0, pairs * edge), :] = lifted[:, :128]
        y_ref[pl.ds(pairs * edge, pairs * edge), :] = lifted[:, 128:]

        for r in range(edge // 8):
            low = [y_ref[pl.ds(j * edge + r * 8, 8), :] for j in range(pairs)]
            high = [y_ref[pl.ds((pairs + j) * edge + r * 8, 8), :] for j in range(pairs)]
            low, high = lift(*with_halo(low, high), pairs, True, True)
            for j in range(pairs):
                y_ref[pl.ds(j * edge + r * 8, 8), :] = low[j]
                y_ref[pl.ds((pairs + j) * edge + r * 8, 8), :] = high[j]

        for part in range(2):
            made = []
            for u in range(2):
                at = (part * pairs + u) * edge
                rows = [y_ref[pl.ds(at + x, 8, stride=2 * edge), :] for x in range(edge)]
                low, high = lift(rows[0::2], rows[1::2], half, False, False)
                low = [v * (1.0 / SCALE) for v in low]
                high = [v * SCALE for v in high]
                if part == 0:
                    for x in range(half):
                        c_ref[pl.ds(8 * x, 8), pl.ds(u * 128, 128)] = low[x]
                made.append(low + high)
            for x in range(edge):
                a, b = made[0][x], made[1][x]
                at = part * pairs * edge + x
                z_ref[pl.ds(at, 8, stride=edge), :] = jnp.where(front, a, turn(b))
                z_ref[pl.ds(at + pairs // 2 * edge, 8, stride=edge), :] = jnp.where(front, turn(a), b)

        high, low = split(c_ref[...])
        lifted = dot(jnp.concatenate([high, low, high], 1), w2_ref[...])
        d_ref[pl.ds(0, 8 * half), :] = lifted[:, :128]
        d_ref[pl.ds(8 * half, 8 * half), :] = lifted[:, 128:]

        for r in range(half // 8):
            low = [d_ref[pl.ds(64 * r + i, 8, stride=8), :] for i in range(8)]
            high = [d_ref[pl.ds(8 * half + 64 * r + i, 8, stride=8), :] for i in range(8)]
            low, high = lift(*with_halo(low, high), 8, True, True)
            for i in range(8):
                d_ref[pl.ds(64 * r + i, 8, stride=8), :] = low[i]
                d_ref[pl.ds(8 * half + 64 * r + i, 8, stride=8), :] = high[i]

        for u in range(2):
            rows = [d_ref[pl.ds(8 * (u * half + x), 8), :] for x in range(half)]
            low, high = lift(rows[0::2], rows[1::2], half // 2, False, False)
            for x in range(half // 2):
                e_ref[pl.ds(u * 8 * half + x, 8, stride=half), :] = low[x] * (1.0 / SCALE)
                e_ref[pl.ds(u * 8 * half + half // 2 + x, 8, stride=half), :] = high[x] * SCALE

        for u in range(2):
            for t in range(4):
                for r in range(half // 8):
                    a = e_ref[pl.ds((u * 8 + 2 * t) * half + 8 * r, 8), :]
                    b = e_ref[pl.ds((u * 8 + 2 * t + 1) * half + 8 * r, 8), :]
                    for tile, value in (
                        (u * 8 + t, jnp.where(front, a, turn(b))),
                        (u * 8 + 4 + t, jnp.where(front, turn(a), b)),
                    ):
                        old = z_ref[pl.ds(tile * edge + 8 * r, 8), :]
                        out_ref[0, pl.ds(8 * r, 8), pl.ds(tile * 128, 128)] = jnp.where(inner, value, old)
        for t in range(2 * pairs):
            first = half if t < pairs else 0
            out_ref[0, pl.ds(first, edge - first), pl.ds(t * 128, 128)] = z_ref[
                pl.ds(t * edge + first, edge - first), :
            ]


def fine_call(owner_counts, density):
    slots, edge, plane = density.shape
    half = edge // 2
    pairs = plane // 256
    one = pass_matrix(edge).T
    zero = np.zeros_like(one)
    w1 = np.block(
        [
            [one / SCALE, zero, zero, zero],
            [zero, zero, one * SCALE, zero],
            [zero, one / SCALE, zero, zero],
            [zero, zero, zero, one * SCALE],
        ]
    )
    two = np.zeros_like(one)
    two[:half, :half] = pass_matrix(half).T
    w2 = np.kron(np.diag([1 / SCALE, 1 / SCALE, SCALE, SCALE]), two)
    def stacked(matrix):
        first, second = two_terms(matrix)
        return np.concatenate([first, first, second], 0)

    fixed = pl.BlockSpec((768, 256), lambda s: (0, 0))
    return pl.pallas_call(
        fine_kernel,
        grid=(slots,),
        in_specs=[
            pl.BlockSpec(memory_space=pltpu.SMEM),
            pl.BlockSpec((1, edge, plane), lambda s: (s, 0, 0)),
            fixed,
            fixed,
        ],
        out_specs=pl.BlockSpec((1, edge, plane), lambda s: (s, 0, 0)),
        out_shape=jax.ShapeDtypeStruct(density.shape, F32),
        scratch_shapes=[
            pltpu.VMEM((pairs * edge, 768), BF16),
            pltpu.VMEM((2 * pairs * edge, 128), F32),
            pltpu.VMEM((2 * pairs * edge, 128), F32),
            pltpu.VMEM((8 * half, 256), F32),
            pltpu.VMEM((16 * half, 128), F32),
            pltpu.VMEM((16 * half, 128), F32),
        ],
        compiler_params=pltpu.CompilerParams(vmem_limit_bytes=VMEM_LIMIT),
        cost_estimate=pl.CostEstimate(
            flops=6 * slots * edge * plane * 256, bytes_accessed=12 * MIB, transcendentals=0
        ),
        name="fine",
    )(owner_counts, density, stacked(w1), stacked(w2))


def coarse_kernel(
    index_ref,
    piece_ref,
    wx_ref,
    wzh_ref,
    wzl_ref,
    wyh_ref,
    wyl_ref,
    w23h_ref,
    w23l_ref,
    wx2_ref,
    wx3_ref,
    fine_ref,
    out_ref,
    block_ref,
    corner_ref,
    corner_sem,
    out_sem,
):
    slots = corner_ref.shape[0]
    lane = lax.broadcasted_iota(jnp.int32, (16, 128), 1)

    def window(s):
        return out_ref.at[s, pl.ds(0, 16), pl.ds(0, 1024)]

    def piece(i):
        return jnp.concatenate([piece_ref[pl.ds(16 * h + i, 16, stride=32), :] for h in range(2)], 1)

    for s in range(slots):
        pltpu.make_async_copy(window(s), corner_ref.at[s], corner_sem.at[s]).start()

    first = [
        [
            times_left(wx_ref[...], jnp.concatenate([piece(o * 8 + 2 * q), piece(o * 8 + 2 * q + 1)], 0))
            for q in range(4)
        ]
        for o in range(2)
    ]
    stacked = []
    for o in range(2):
        for cy in range(2):
            for yh in range(2):
                part = slice(yh * 128, yh * 128 + 128)
                stacked.append(jnp.concatenate([first[o][cy][:, part], first[o][2 + cy][:, part]], 1))
    lifted = times(jnp.concatenate(stacked, 0), wzh_ref[...], wzl_ref[...])
    stacked = []
    for o in range(2):
        for tz in range(2):
            stacked.append(
                jnp.concatenate(
                    [lifted[(o * 4 + u) * 32 : (o * 4 + u + 1) * 32, tz * 128 : tz * 128 + 128] for u in range(4)],
                    1,
                )
            )
    lifted = times(jnp.concatenate(stacked, 0), wyh_ref[...], wyl_ref[...])
    corner = []
    for o in range(2):
        for tz in range(2):
            for ty in range(2):
                for tx in range(2):
                    at = (o * 2 + tz) * 32 + tx * 16
                    value = lifted[at : at + 16, ty * 256 : ty * 256 + 256]
                    if tx + ty + tz == 0:
                        corner.append(value)
                    else:
                        block_ref[o * 8 + tx + 2 * ty + 4 * tz] = value
    both = times(jnp.concatenate(corner, 0), w23h_ref[...], w23l_ref[...])
    spot = lax.broadcasted_iota(jnp.int32, (16, 256), 1)
    depth = lax.broadcasted_iota(jnp.int32, (16, 256), 0)
    small = (depth < 8) & (spot < 128) & ((spot & 15) < 8)
    for o in range(2):
        mine = both[o * 16 : o * 16 + 16]
        second = times_left(wx2_ref[...], mine[:, :256])
        third = times_left(wx3_ref[...], mine[:, 256:])
        block_ref[o * 8] = jnp.where(small, third, second)

    for s in range(slots):
        pltpu.make_async_copy(window(s), corner_ref.at[s], corner_sem.at[s]).wait()
    for s in range(slots):

        @pl.when(s < index_ref[1])
        def _():
            value = block_ref[index_ref[0] + s]
            for t in range(8):
                tile = value[:, (t // 4) * 128 : (t // 4) * 128 + 128]
                near = pltpu.roll(tile, (128 - 32 * (t % 4)) % 128, 1)
                far = pltpu.roll(tile, (64 - 16 - 32 * (t % 4)) % 128, 1)
                old = corner_ref[s, :, pl.ds(t * 128, 128)]
                new = jnp.where(lane < 16, near, jnp.where((lane >= 64) & (lane < 80), far, old))
                corner_ref[s, :, pl.ds(t * 128, 128)] = new
            pltpu.make_async_copy(corner_ref.at[s], window(s), out_sem.at[s]).start()

    for s in range(slots):

        @pl.when(s < index_ref[1])
        def _():
            pltpu.make_async_copy(corner_ref.at[s], window(s), out_sem.at[s]).wait()


def coarse_call(index, pieces, fine):
    slots, edge, plane = fine.shape
    m32, m16, m8 = pass_matrix(32), pass_matrix(16), pass_matrix(8)
    deep = np.zeros((16, 16))
    deep[:8] = m8 @ m16[:8]
    eye8, eye16 = np.eye(8), np.eye(16)
    wz = np.zeros((256, 256))
    for cz in range(2):
        for tz in range(2):
            wz[cz * 128 : cz * 128 + 128, tz * 128 : tz * 128 + 128] = np.kron(
                eye8, m32[tz * 16 : tz * 16 + 16, cz * 16 : cz * 16 + 16].T
            )
    w23 = np.concatenate([np.kron(m16.T, m16.T), np.kron(deep.T, deep.T)], 1)
    weights = [
        left_terms(m32),
        *two_terms(wz),
        *two_terms(np.kron(m32.T, eye16)),
        *two_terms(w23),
        left_terms(m16),
        left_terms(deep),
    ]
    anywhere = pl.BlockSpec(memory_space=pl.ANY)
    vmem = pl.BlockSpec(memory_space=pltpu.VMEM)
    return pl.pallas_call(
        coarse_kernel,
        in_specs=[pl.BlockSpec(memory_space=pltpu.SMEM), vmem] + [vmem] * len(weights) + [anywhere],
        out_specs=anywhere,
        out_shape=jax.ShapeDtypeStruct(fine.shape, F32),
        scratch_shapes=[
            pltpu.VMEM((16, 16, 256), F32),
            pltpu.VMEM((slots, 16, 1024), F32),
            pltpu.SemaphoreType.DMA((slots,)),
            pltpu.SemaphoreType.DMA((slots,)),
        ],
        input_output_aliases={2 + len(weights): 0},
        compiler_params=pltpu.CompilerParams(vmem_limit_bytes=VMEM_LIMIT),
        name="coarse",
    )(index, pieces.reshape(-1, 128), *weights, fine)


def exchange(lowpass, slots):
    me = lax.axis_index(AXES)
    devices = lax.axis_size(AXES)
    if devices == lowpass.shape[0]:
        got = lax.all_to_all(lowpass, AXES, 0, 0, tiled=True)
        sent, index = route_call(me.reshape(1), got, slots)
        return lax.all_to_all(sent, AXES, 0, 0, tiled=True), index
    every = lax.all_gather(lowpass, AXES, axis=0)
    counts = every[:, 0, 7, 0].astype(jnp.int32)
    starts = jnp.cumsum(counts) - counts
    blocks = starts[me] // 8 * 8 + jnp.arange(16, dtype=jnp.int32)
    owners = jnp.sum((starts[None, :] <= blocks[:, None]).astype(jnp.int32), axis=1) - 1
    place = jnp.minimum(blocks - starts[owners], slots - 1)
    pieces = jnp.transpose(every[owners, :, place], (1, 0, 2))
    return pieces, jnp.stack([starts[me] % 8, counts[me]])


def per_device(density, owner_counts):
    lowpass = lowpass_call(owner_counts, density)
    pieces, index = exchange(lowpass, density.shape[0])
    fine = fine_call(owner_counts, density)
    return coarse_call(index, pieces, fine)


def solution(mesh):
    in_specs = (P(AXES, None, None), P(AXES))
    out_specs = P(AXES, None, None)
    return jax.shard_map(per_device, mesh=mesh, in_specs=in_specs, out_specs=out_specs, check_vma=False)
```

time: 155 us -> 56.4 us (0.36)
  blocking collectives: 70.8 us -> 0 us
  Pallas kernels: 52.4 us -> 35.5 us
  between operations: 17.5 us -> 0.69 us
  local copies, waits for them, and re-layouts: 12 us -> 1.36 us
  starting transfers between devices: 0.01 us -> 9.9 us
  waiting for transfers between devices: 0.02 us -> 8.4 us
  other arithmetic: 1.72 us -> 0 us
    all_gather x1 -> x0, blocking collectives: 70.8 us -> none  [gather_counts(): every = lax.all_gather(sent, AXES, axis=0, tiled=True)]
    pallas_call x1, Pallas kernels: 43.1 us -> 19.7 us  [fine_call(): pl.pallas_call(fine_kernel, grid=(slots,), in_specs=[pl.BlockSpec(memory_...]
    unnamed x38 -> x4, local copies, waits for them, and re-layouts: 11.4 us -> 1.36 us
    all_to_all x0 -> x2, starting transfers between devices: none -> 9.9 us  [the longest x1 7.3 us: exchange(): got = lax.all_to_all(lowpass, AXES, 0, 0, tiled=True)]
    all_to_all x0 -> x2, waiting for transfers between devices: none -> 8.4 us  [the longest x1 8.4 us: exchange(): got = lax.all_to_all(lowpass, AXES, 0, 0, tiled=True)]
    pallas_call x1 -> x2, Pallas kernels: 5.56 us -> 11.5 us  [the longest x1 8.83 us: lowpass_call(): pl.pallas_call(lowpass_kernel, grid=(steps,), in_specs=[pl.BlockSpec(memo...]
  transfers between devices with their start and end apart: 1 -> 2, of which waited for: 0 -> 1; matrix products, arithmetic and copies ran while one was open for 2% -> 0% of each run, Pallas kernels for 28% -> 35%
where the time goes in v2:
time: 56.4 us; the launch traced here: 55.9 us
  Pallas kernels  35.5 us (63%)
  starting transfers between devices  9.9 us (18%)
  waiting for transfers between devices  8.4 us (15%)
  local copies, waits for them, and re-layouts  1.36 us (2%)
  between operations  0.69 us (1%)
    pallas_call x1, Pallas kernels, fine_call(): pl.pallas_call(fine_kernel, grid=(slots,), in_specs=[pl.BlockSpec(memory_...  19.7 us
    pallas_call x1, Pallas kernels, lowpass_call(): pl.pallas_call(lowpass_kernel, grid=(steps,), in_specs=[pl.BlockSpec(memo...  8.83 us
    all_to_all x1, waiting for transfers between devices, exchange(): got = lax.all_to_all(lowpass, AXES, 0, 0, tiled=True)  8.4 us
    all_to_all x1, starting transfers between devices, exchange(): got = lax.all_to_all(lowpass, AXES, 0, 0, tiled=True)  7.3 us
    pallas_call x1, Pallas kernels, coarse_call(): pl.pallas_call(coarse_kernel, in_specs=[pl.BlockSpec(memory_space=pltpu.S...  4.26 us
    pallas_call x1, Pallas kernels, route_call(): pl.pallas_call(route_kernel, in_specs=[pl.BlockSpec(memory_space=pltpu.SM...  2.69 us
    all_to_all x1, starting transfers between devices, exchange(): return (lax.all_to_all(sent, AXES, 0, 0, tiled=True), index)  2.6 us
    unnamed x4, local copies, waits for them, and re-layouts  1.36 us
  transfers between devices with their start and end apart: 2, of which 1 were waited for; matrix products, arithmetic and copies ran while one was open for 0% of the time, Pallas kernels for 35%

profile of v2, /device:TPU:0, one launch (start us, length us, event | category | flops | bytes accessed | tf_op | source)
XLA Modules:
  0.0 55.9 jit_solution(8047613066304681810)
XLA Ops:
  0.7 8.8 %lowpass.1 = f32[256,128]{1,0:T(8,128)} custom-call(s32[1]{0:T(128)S(6)} %copy.19.count_ref, f32[6,64,4096]{2,1,0:T(8,128)} %x_ref.3, bf16[4096,256]{1,0:T(8,128)(2,1)} %constant.39.clone.wh_ref, bf16[4096,256]{1,0:T(8,128)(2,1)} %constant.40.clone.wl_ref, bf16[16,192]{1,0:T(8,128)(2,1)} %constant.41.clone.ax_ref), custom_call_target="tpu_custom_call" | custom-call | flops 2415919104 | bytes 10485760 | tf_op jit(solution)/shard_map/lowpass/pallas_call | solution.py:101
  9.5 7.3 %all-to-all-start = ((f32[32,8,128]{2,1,0:T(8,128)}), f32[32,8,128]{2,1,0:T(8,128)S(1)}, u32[]{:S(2)}, u32[]{:S(2)}) async-start(f32[32,8,128]{2,1,0:T(8,128)} %bitcast.4), calls=%async_computation | async-start | bytes 262144 | tf_op jit(solution)/shard_map/all_to_all | solution.py:512
  16.8 8.4 %all-to-all-done.got_ref = f32[32,8,128]{2,1,0:T(8,128)S(1)} async-done(((f32[32,8,128]{2,1,0:T(8,128)}), f32[32,8,128]{2,1,0:T(8,128)S(1)}, u32[]{:S(2)}, u32[]{:S(2)}) %all-to-all-start) | async-done | bytes 131104 | tf_op jit(solution)/shard_map/all_to_all | solution.py:512
  25.2 0.0 copy-start.1
  25.2 0.7 %copy-done.1 = f32[32,8,128]{2,1,0:T(8,128)} copy-done((f32[32,8,128]{2,1,0:T(8,128)}, f32[32,8,128]{2,1,0:T(8,128)S(1)}, u32[]{:S(2)}) %copy-start.1) | copy-done | bytes 131096
  25.9 2.7 %route.1 = (f32[32,16,128]{2,1,0:T(8,128)}, s32[2]{0:T(128)}) custom-call(s32[1]{0:T(128)} %bitcast.me_ref, f32[32,8,128]{2,1,0:T(8,128)} %copy-done.1), custom_call_target="tpu_custom_call" | custom-call | tf_op jit(solution)/shard_map/route/pallas_call | solution.py:147
  28.6 2.6 %all-to-all-start.1 = ((f32[32,16,128]{2,1,0:T(8,128)}), f32[32,16,128]{2,1,0:T(8,128)S(1)}, u32[]{:S(2)}, u32[]{:S(2)}) async-start(f32[32,16,128]{2,1,0:T(8,128)} %get-tuple-element.8), calls=%async_computation.1 | async-start | bytes 524288 | tf_op jit(solution)/shard_map/all_to_all | solution.py:514
  31.2 19.7 %fine.1.fine_ref = f32[6,64,4096]{2,1,0:T(8,128)} custom-call(s32[1]{0:T(128)S(6)} %copy.19.count_ref, f32[6,64,4096]{2,1,0:T(8,128)} %x_ref.3, bf16[768,256]{1,0:T(8,128)(2,1)} %constant.42.clone.w1_ref, bf16[768,256]{1,0:T(8,128)(2,1)} %constant.43.clone.w2_ref), custom_call_target="tpu_custom_call" | custom-call | flops 2415919104 | bytes 12582912 | tf_op jit(solution)/shard_map/fine/pallas_call | solution.py:342
  50.9 0.0 all-to-all-done.1
  50.9 0.0 copy-start
  50.9 0.7 %copy-done = f32[32,16,128]{2,1,0:T(8,128)} copy-done((f32[32,16,128]{2,1,0:T(8,128)}, f32[32,16,128]{2,1,0:T(8,128)S(1)}, u32[]{:S(2)}) %copy-start) | copy-done | bytes 262168
  51.6 4.3 %coarse.1 = f32[6,64,4096]{2,1,0:T(8,128)} custom-call(s32[2]{0:T(128)} %get-tuple-element.7.index_ref, f32[512,128]{1,0:T(8,128)} %bitcast.3, bf16[32,96]{1,0:T(8,128)(2,1)} %constant.44.clone.wx_ref, bf16[256,256]{1,0:T(8,128)(2,1)} %constant.45.clone.wzh_ref, bf16[256,256]{1,0:T(8,128)(2,1)} %constant.46.clone.wzl_ref, ...), custom_call_target="tpu_custom_call", output_to_operand_aliasing={{}: (11, {})} | custom-call | tf_op jit(solution)/shard_map/coarse/pallas_call | solution.py:491
Async XLA Ops:
  9.5 15.7 %all-to-all-start = ((f32[32,8,128]{2,1,0:T(8,128)}), f32[32,8,128]{2,1,0:T(8,128)S(1)}, u32[]{:S(2)}, u32[]{:S(2)}) async-start(f32[32,8,128]{2,1,0:T(8,128)} %bitcast.4), calls=%async_computation | async-start | bytes 262144 | tf_op jit(solution)/shard_map/all_to_all | solution.py:512
  25.2 0.7 %copy-start.1 = (f32[32,8,128]{2,1,0:T(8,128)}, f32[32,8,128]{2,1,0:T(8,128)S(1)}, u32[]{:S(2)}) copy-start(f32[32,8,128]{2,1,0:T(8,128)S(1)} %all-to-all-done.got_ref) | copy-start | bytes 393220
  28.6 22.3 %all-to-all-start.1 = ((f32[32,16,128]{2,1,0:T(8,128)}), f32[32,16,128]{2,1,0:T(8,128)S(1)}, u32[]{:S(2)}, u32[]{:S(2)}) async-start(f32[32,16,128]{2,1,0:T(8,128)} %get-tuple-element.8), calls=%async_computation.1 | async-start | bytes 524288 | tf_op jit(solution)/shard_map/all_to_all | solution.py:514
  50.9 0.7 %copy-start = (f32[32,16,128]{2,1,0:T(8,128)}, f32[32,16,128]{2,1,0:T(8,128)S(1)}, u32[]{:S(2)}) copy-start(f32[32,16,128]{2,1,0:T(8,128)S(1)} %all-to-all-done.1) | copy-start | bytes 786436

commit v3 on v2

--- a/solution.py
+++ b/solution.py
@@ -67,60 +67,95 @@
     return dot(terms, jnp.concatenate([high, high, low], 0))
 
 
-def lowpass_kernel(count_ref, x_ref, wh_ref, wl_ref, ax_ref, out_ref, acc_ref):
-    step = pl.program_id(0)
-    slots, edge, width = x_ref.shape
-    part = times(x_ref[...].reshape(slots * edge, width), wh_ref[...], wl_ref[...])
-
-    @pl.when(step == 0)
-    def _():
-        acc_ref[...] = part
-
-    @pl.when(step > 0)
-    def _():
-        acc_ref[...] += part
-
-    @pl.when(step == pl.num_programs(0) - 1)
-    def _():
-        out_ref[...] = jnp.full(out_ref.shape, count_ref[0].astype(F32))
-        for slot in range(slots):
-            made = times_left(ax_ref[...], acc_ref[pl.ds(slot * edge, edge), :])
-            for h in range(2):
-                out_ref[pl.ds(8 * h + slot, edge // 4, stride=16), :] = made[:, h * 128 : h * 128 + 128]
+def start_tiles(src_ref, dst_ref, sem, tiles):
+    for t in tiles:
+        pltpu.make_async_copy(src_ref.at[..., pl.ds(t * 128, 128)], dst_ref.at[..., t, :], sem).start()
+
+
+def split_rows(rows):
+    return [split(jnp.concatenate(rows[m : m + 2], 0)) for m in range(0, len(rows), 2)]
+
+
+def lowpass_kernel(
+    count_ref, x_ref, wz_any, wyh_any, wyl_any, out_ref, x_buf, wz_ref, wyh_ref, wyl_ref, l_ref, z_ref, sems, w_sems
+):
+    slots, edge = x_ref.shape[:2]
+    quarter = edge // 4
+    order = (0, 2, 1, 3)
+    for g in order:
+        start_tiles(x_ref, x_buf, sems.at[g], range(8 * g, 8 * g + 8))
+    weights = [
+        pltpu.make_async_copy(src, dst, w_sems.at[i])
+        for i, (src, dst) in enumerate(((wz_any, wz_ref), (wyh_any, wyh_ref), (wyl_any, wyl_ref)))
+    ]
+    for copy in weights:
+        copy.start()
+    for g in order:
+        part = x_buf.at[:, :, pl.ds(8 * g, 8), :]
+        pltpu.make_async_copy(part, part, sems.at[g]).wait()
+        at = (g % 2) * 256 + (g // 2) * 128
+
+        @pl.loop(0, slots)
+        def _(s):
+            rows = [x_buf[s, x, pl.ds(8 * g, 8), :] for x in range(edge)]
+            rows, _ = lift(rows[0::2], rows[1::2], edge // 2, False, False)
+            rows, _ = lift(rows[0::2], rows[1::2], quarter, False, False)
+            for m, (high, low) in enumerate(split_rows(rows)):
+                place = pl.ds(pl.multiple_of(s * 8 * quarter + 16 * m, 16), 16)
+                l_ref[place, pl.ds(at, 128)] = high
+                l_ref[place, pl.ds(512 + at, 128)] = low
+                l_ref[place, pl.ds(1024 + at, 128)] = high
+
+    for copy in weights:
+        copy.wait()
+    z_ref[...] = dot(l_ref[...], wz_ref[...])
+    wide = jnp.concatenate([z_ref[pl.ds(i, slots * quarter, stride=8), :] for i in range(8)], 1)
+    made = times(wide, wyh_ref[...], wyl_ref[...])
+    out_ref[...] = jnp.full(out_ref.shape, count_ref[0].astype(F32))
+    for slot in range(slots):
+        for h in range(2):
+            out_ref[pl.ds(8 * h + slot, quarter, stride=16), :] = made[
+                slot * quarter : (slot + 1) * quarter, h * 128 : h * 128 + 128
+            ]
+
+
+def stacked(matrix):
+    first, second = two_terms(matrix)
+    return np.concatenate([first, first, second], 0)
 
 
 def lowpass_call(owner_counts, density):
     slots, edge, plane = density.shape
     quarter = edge // 4
     two_levels = pass_matrix(edge // 2)[:quarter] @ pass_matrix(edge)[: edge // 2]
-    first, second = two_terms(np.kron(two_levels.T, two_levels.T))
-    terms = left_terms(two_levels)
-    steps = 8
-    width = plane // steps
-    cols = quarter * quarter
+    wz = stacked(np.kron(np.eye(8), two_levels.T))
+    i, gp, q, p = np.meshgrid(np.arange(8), np.arange(2), np.arange(2), np.arange(2), indexing="ij")
+    entry = (2 * (8 * gp + i) + p + 32 * q).reshape(-1)
+    wy = np.kron(two_levels.T[entry] / SQUARE, np.eye(quarter))
+    wyh, wyl = two_terms(wy)
+    anywhere = pl.BlockSpec(memory_space=pl.ANY)
     pieces = pl.pallas_call(
         lowpass_kernel,
-        grid=(steps,),
-        in_specs=[
-            pl.BlockSpec(memory_space=pltpu.SMEM),
-            pl.BlockSpec((slots, edge, width), lambda j: (0, 0, j)),
-            pl.BlockSpec((width, cols), lambda j: (j, 0)),
-            pl.BlockSpec((width, cols), lambda j: (j, 0)),
-            pl.BlockSpec(terms.shape, lambda j: (0, 0)),
+        in_specs=[pl.BlockSpec(memory_space=pltpu.SMEM)] + [anywhere] * 4,
+        out_specs=pl.BlockSpec(memory_space=pltpu.VMEM),
+        out_shape=jax.ShapeDtypeStruct((16 * quarter, 128), F32),
+        scratch_shapes=[
+            pltpu.VMEM((slots, edge, plane // 128, 128), F32),
+            pltpu.VMEM(wz.shape, BF16),
+            pltpu.VMEM(wyh.shape, BF16),
+            pltpu.VMEM(wyl.shape, BF16),
+            pltpu.VMEM((slots * 8 * quarter, 1536), BF16),
+            pltpu.VMEM((slots * 8 * quarter, 128), F32),
+            pltpu.SemaphoreType.DMA((4,)),
+            pltpu.SemaphoreType.DMA((3,)),
         ],
-        out_specs=pl.BlockSpec((16 * quarter, 128), lambda j: (0, 0)),
-        out_shape=jax.ShapeDtypeStruct((16 * quarter, 128), F32),
-        scratch_shapes=[pltpu.VMEM((slots * edge, cols), F32)],
         compiler_params=pltpu.CompilerParams(vmem_limit_bytes=VMEM_LIMIT),
-        cost_estimate=pl.CostEstimate(
-            flops=6 * slots * edge * plane * cols, bytes_accessed=10 * MIB, transcendentals=0
-        ),
         name="lowpass",
-    )(owner_counts, density, first, second, terms)
+    )(owner_counts, density, wz, wyh, wyl)
     return pieces.reshape(2 * quarter, 8, 128)
 
 
-def route_kernel(me_ref, got_ref, send_ref, index_ref, order_ref, count_ref, sem):
+def route_kernel(me_ref, got_ref, _, send_ref, index_ref, order_ref, count_ref, sem):
     devices = got_ref.shape[0]
     copy = pltpu.make_async_copy(got_ref.at[:, 7, :], count_ref, sem)
     copy.start()
@@ -142,13 +177,14 @@
     index_ref[1] = my_count
 
 
-def route_call(me, got, slots):
+def route_call(me, got, meanwhile, slots):
     devices = got.shape[0]
     return pl.pallas_call(
         route_kernel,
         in_specs=[
             pl.BlockSpec(memory_space=pltpu.SMEM),
             pl.BlockSpec(memory_space=pltpu.VMEM),
+            pl.BlockSpec(memory_space=pl.ANY),
         ],
         out_specs=[pl.BlockSpec(memory_space=pltpu.VMEM), pl.BlockSpec(memory_space=pltpu.SMEM)],
         out_shape=[
@@ -162,7 +198,7 @@
         ],
         compiler_params=pltpu.CompilerParams(vmem_limit_bytes=VMEM_LIMIT),
         name="route",
-    )(me, got)
+    )(me, got, meanwhile)
 
 
 def lift(low, high, n, halo, scaled):
@@ -211,12 +247,13 @@
     return [fourth[i] for i in range(n)], [third[i] for i in range(n)]
 
 
-def fine_kernel(
-    count_ref, x_ref, w1_ref, w2_ref, out_ref, l_ref, y_ref, z_ref, c_ref, d_ref, e_ref
-):
-    slot = pl.program_id(0)
+def fine_kernel(count_ref, x_ref, w1_ref, w2_ref, *refs, offset):
+    out_ref, x_buf, l_ref, y_ref, c_ref, m_ref, d_ref, sems = refs[-8:]
+    step = pl.program_id(0)
+    slot = step + offset
     edge = x_ref.shape[1]
-    pairs = x_ref.shape[2] // 256
+    tiles = x_ref.shape[2] // 128
+    pairs = tiles // 2
     half = edge // 2
     lane = lax.broadcasted_iota(jnp.int32, (8, 128), 1)
     front = lane < 64
@@ -236,88 +273,83 @@
         high_all = [left(high, (1, -2)), left(high, (0, -1))] + high + [right(high, (0, -2))]
         return low_all, high_all
 
+    def fetch(which, place):
+        start_tiles(x_ref.at[which], x_buf.at[place], sems.at[place], range(tiles))
+
+    def scaled_rows(rows):
+        low, high = lift(rows[0::2], rows[1::2], len(rows) // 2, False, False)
+        return [v * (1.0 / SCALE) for v in low] + [v * SCALE for v in high]
+
+    def store_terms(ref, row, col, rows):
+        for m, (high, low) in enumerate(split_rows(rows)):
+            place = pl.ds(row + 16 * m, 16)
+            ref[place, pl.ds(col, 128)] = high
+            ref[place, pl.ds(256 + col, 128)] = low
+            ref[place, pl.ds(512 + col, 128)] = high
+
+    @pl.when((step == 0) & (slot < count_ref[0]))
+    def _():
+        fetch(slot, 0)
+
+    @pl.when((step + 1 < pl.num_programs(0)) & (slot + 1 < count_ref[0]))
+    def _():
+        fetch(slot + 1, (step + 1) % 2)
+
     @pl.when(slot >= count_ref[0])
     def _():
         out_ref[...] = jnp.zeros_like(out_ref)
 
     @pl.when(slot < count_ref[0])
     def _():
-        for j in range(pairs):
-            for q in range(2):
-                high, low = split(x_ref[0, :, pl.ds((j + q * pairs) * 128, 128)])
-                rows = pl.ds(j * edge, edge)
-                l_ref[rows, pl.ds(q * 128, 128)] = high
-                l_ref[rows, pl.ds(256 + q * 128, 128)] = low
-                l_ref[rows, pl.ds(512 + q * 128, 128)] = high
+        x = x_buf.at[step % 2]
+        pltpu.make_async_copy(x, x, sems.at[step % 2]).wait()
+        for g in range(4):
+            rows = scaled_rows([x[i, pl.ds(8 * g, 8), :] for i in range(edge)])
+            store_terms(l_ref, (g % 2) * 8 * edge, (g // 2) * 128, rows)
         lifted = dot(l_ref[...], w1_ref[...])
         y_ref[pl.ds(0, pairs * edge), :] = lifted[:, :128]
         y_ref[pl.ds(pairs * edge, pairs * edge), :] = lifted[:, 128:]
-
         for r in range(edge // 8):
-            low = [y_ref[pl.ds(j * edge + r * 8, 8), :] for j in range(pairs)]
-            high = [y_ref[pl.ds((pairs + j) * edge + r * 8, 8), :] for j in range(pairs)]
+            rows = pl.ds(8 * r, 8)
+
+            def tile(part, j):
+                at = (part * 2 + j // 8) * 8 * edge + 64 * r + j % 8
+                return y_ref[pl.ds(at, 8, stride=8), :]
+
+            low = [tile(0, j) for j in range(pairs)]
+            high = [tile(1, j) for j in range(pairs)]
             low, high = lift(*with_halo(low, high), pairs, True, True)
-            for j in range(pairs):
-                y_ref[pl.ds(j * edge + r * 8, 8), :] = low[j]
-                y_ref[pl.ds((pairs + j) * edge + r * 8, 8), :] = high[j]
-
-        for part in range(2):
-            made = []
-            for u in range(2):
-                at = (part * pairs + u) * edge
-                rows = [y_ref[pl.ds(at + x, 8, stride=2 * edge), :] for x in range(edge)]
-                low, high = lift(rows[0::2], rows[1::2], half, False, False)
-                low = [v * (1.0 / SCALE) for v in low]
-                high = [v * SCALE for v in high]
-                if part == 0:
-                    for x in range(half):
-                        c_ref[pl.ds(8 * x, 8), pl.ds(u * 128, 128)] = low[x]
-                made.append(low + high)
-            for x in range(edge):
-                a, b = made[0][x], made[1][x]
-                at = part * pairs * edge + x
-                z_ref[pl.ds(at, 8, stride=edge), :] = jnp.where(front, a, turn(b))
-                z_ref[pl.ds(at + pairs // 2 * edge, 8, stride=edge), :] = jnp.where(front, turn(a), b)
-
-        high, low = split(c_ref[...])
-        lifted = dot(jnp.concatenate([high, low, high], 1), w2_ref[...])
+            for part, values in enumerate((low, high)):
+                for t in range(pairs // 2):
+                    a, b = values[2 * t], values[2 * t + 1]
+                    at = part * pairs + t
+                    out_ref[0, rows, pl.ds(at * 128, 128)] = jnp.where(front, a, turn(b))
+                    out_ref[0, rows, pl.ds((at + pairs // 2) * 128, 128)] = jnp.where(front, turn(a), b)
+            if r < half // 8:
+                low, high = lift(*with_halo(low[0::2], low[1::2]), 8, True, False)
+                for i in range(8):
+                    c_ref[pl.ds(i * half + 8 * r, 8), :] = low[i]
+                    c_ref[pl.ds((8 + i) * half + 8 * r, 8), :] = high[i]
+        for u in range(2):
+            rows = scaled_rows([c_ref[pl.ds(u * 8 * half + i, 8, stride=half), :] for i in range(half)])
+            store_terms(m_ref, 0, u * 128, rows)
+        lifted = dot(m_ref[...], w2_ref[...])
         d_ref[pl.ds(0, 8 * half), :] = lifted[:, :128]
         d_ref[pl.ds(8 * half, 8 * half), :] = lifted[:, 128:]
-
-        for r in range(half // 8):
-            low = [d_ref[pl.ds(64 * r + i, 8, stride=8), :] for i in range(8)]
-            high = [d_ref[pl.ds(8 * half + 64 * r + i, 8, stride=8), :] for i in range(8)]
-            low, high = lift(*with_halo(low, high), 8, True, True)
-            for i in range(8):
-                d_ref[pl.ds(64 * r + i, 8, stride=8), :] = low[i]
-                d_ref[pl.ds(8 * half + 64 * r + i, 8, stride=8), :] = high[i]
-
-        for u in range(2):
-            rows = [d_ref[pl.ds(8 * (u * half + x), 8), :] for x in range(half)]
-            low, high = lift(rows[0::2], rows[1::2], half // 2, False, False)
-            for x in range(half // 2):
-                e_ref[pl.ds(u * 8 * half + x, 8, stride=half), :] = low[x] * (1.0 / SCALE)
-                e_ref[pl.ds(u * 8 * half + half // 2 + x, 8, stride=half), :] = high[x] * SCALE
-
         for u in range(2):
             for t in range(4):
                 for r in range(half // 8):
-                    a = e_ref[pl.ds((u * 8 + 2 * t) * half + 8 * r, 8), :]
-                    b = e_ref[pl.ds((u * 8 + 2 * t + 1) * half + 8 * r, 8), :]
-                    for tile, value in (
+                    a = d_ref[pl.ds(u * 8 * half + 64 * r + 2 * t, 8, stride=8), :]
+                    b = d_ref[pl.ds(u * 8 * half + 64 * r + 2 * t + 1, 8, stride=8), :]
+                    for at, value in (
                         (u * 8 + t, jnp.where(front, a, turn(b))),
                         (u * 8 + 4 + t, jnp.where(front, turn(a), b)),
                     ):
-                        old = z_ref[pl.ds(tile * edge + 8 * r, 8), :]
-                        out_ref[0, pl.ds(8 * r, 8), pl.ds(tile * 128, 128)] = jnp.where(inner, value, old)
-        for t in range(2 * pairs):
-            first = half if t < pairs else 0
-            out_ref[0, pl.ds(first, edge - first), pl.ds(t * 128, 128)] = z_ref[
-                pl.ds(t * edge + first, edge - first), :
-            ]
-
-
-def fine_call(owner_counts, density):
+                        rows, cols = pl.ds(8 * r, 8), pl.ds(at * 128, 128)
+                        out_ref[0, rows, cols] = jnp.where(inner, value, out_ref[0, rows, cols])
+
+
+def fine_call(owner_counts, density, first, last, before=None, after=None):
     slots, edge, plane = density.shape
     half = edge // 2
     pairs = plane // 256
@@ -334,36 +366,33 @@
     two = np.zeros_like(one)
     two[:half, :half] = pass_matrix(half).T
     w2 = np.kron(np.diag([1 / SCALE, 1 / SCALE, SCALE, SCALE]), two)
-    def stacked(matrix):
-        first, second = two_terms(matrix)
-        return np.concatenate([first, first, second], 0)
-
+    anywhere = pl.BlockSpec(memory_space=pl.ANY)
     fixed = pl.BlockSpec((768, 256), lambda s: (0, 0))
+    old = [after] if before is None else [before]
     return pl.pallas_call(
-        fine_kernel,
-        grid=(slots,),
-        in_specs=[
-            pl.BlockSpec(memory_space=pltpu.SMEM),
-            pl.BlockSpec((1, edge, plane), lambda s: (s, 0, 0)),
-            fixed,
-            fixed,
-        ],
-        out_specs=pl.BlockSpec((1, edge, plane), lambda s: (s, 0, 0)),
+        functools.partial(fine_kernel, offset=first),
+        grid=(last - first,),
+        in_specs=[pl.BlockSpec(memory_space=pltpu.SMEM), anywhere, fixed, fixed] + [anywhere] * len(old),
+        out_specs=pl.BlockSpec((1, edge, plane), lambda s: (s + first, 0, 0)),
         out_shape=jax.ShapeDtypeStruct(density.shape, F32),
         scratch_shapes=[
+            pltpu.VMEM((2, edge, plane // 128, 128), F32),
             pltpu.VMEM((pairs * edge, 768), BF16),
             pltpu.VMEM((2 * pairs * edge, 128), F32),
-            pltpu.VMEM((2 * pairs * edge, 128), F32),
-            pltpu.VMEM((8 * half, 256), F32),
             pltpu.VMEM((16 * half, 128), F32),
+            pltpu.VMEM((8 * half, 768), BF16),
             pltpu.VMEM((16 * half, 128), F32),
+            pltpu.SemaphoreType.DMA((2,)),
         ],
+        input_output_aliases={} if before is None else {4: 0},
         compiler_params=pltpu.CompilerParams(vmem_limit_bytes=VMEM_LIMIT),
         cost_estimate=pl.CostEstimate(
-            flops=6 * slots * edge * plane * 256, bytes_accessed=12 * MIB, transcendentals=0
+            flops=6 * (last - first) * edge * plane * 256,
+            bytes_accessed=2 * (last - first) * MIB,
+            transcendentals=0,
         ),
         name="fine",
-    )(owner_counts, density, stacked(w1), stacked(w2))
+    )(owner_counts, density, stacked(w1), stacked(w2), *old)
 
 
 def coarse_kernel(
@@ -505,12 +534,12 @@
     )(index, pieces.reshape(-1, 128), *weights, fine)
 
 
-def exchange(lowpass, slots):
+def exchange(lowpass, slots, meanwhile):
     me = lax.axis_index(AXES)
     devices = lax.axis_size(AXES)
     if devices == lowpass.shape[0]:
         got = lax.all_to_all(lowpass, AXES, 0, 0, tiled=True)
-        sent, index = route_call(me.reshape(1), got, slots)
+        sent, index = route_call(me.reshape(1), got, meanwhile, slots)
         return lax.all_to_all(sent, AXES, 0, 0, tiled=True), index
     every = lax.all_gather(lowpass, AXES, axis=0)
     counts = every[:, 0, 7, 0].astype(jnp.int32)
@@ -524,8 +553,10 @@
 
 def per_device(density, owner_counts):
     lowpass = lowpass_call(owner_counts, density)
-    pieces, index = exchange(lowpass, density.shape[0])
-    fine = fine_call(owner_counts, density)
+    slots = density.shape[0]
+    fine = fine_call(owner_counts, density, 0, slots // 2, after=lowpass)
+    pieces, index = exchange(lowpass, slots, fine)
+    fine = fine_call(owner_counts, density, slots // 2, slots, fine)
     return coarse_call(index, pieces, fine)
 
 

time: 56.4 us -> 48.9 us (0.87)
  waiting for transfers between devices: 8.4 us -> 1.8 us
  Pallas kernels: 35.5 us -> 31.4 us
  starting transfers between devices: 9.9 us -> 13.1 us
    all_to_all x1, waiting for transfers between devices: 8.4 us -> 0.01 us  [exchange(): got = lax.all_to_all(lowpass, AXES, 0, 0, tiled=True)]
    pallas_call x2 -> x3, Pallas kernels: 28.6 us -> 24.4 us  [the longest x2 18.3 us: fine_call(): pl.pallas_call(functools.partial(fine_kernel, offset=first), grid=(last -...]
    all_to_all x1, starting transfers between devices: 2.6 us -> 5.84 us  [exchange(): return (lax.all_to_all(sent, AXES, 0, 0, tiled=True), index)]
    all_to_all x1, waiting for transfers between devices: 0.01 us -> 1.8 us  [exchange(): return (lax.all_to_all(sent, AXES, 0, 0, tiled=True), index)]
  transfers between devices with their start and end apart: 2 -> 2, of which waited for: 1 -> 1; matrix products, arithmetic and copies ran while one was open for 0% -> 0% of each run, Pallas kernels for 35% -> 38%
where the time goes in v3:
time: 48.9 us; the launch traced here: 48.4 us
  Pallas kernels  31.4 us (64%)
  starting transfers between devices  13.1 us (27%)
  waiting for transfers between devices  1.8 us (4%)
  local copies, waits for them, and re-layouts  1.34 us (3%)
  between operations  0.72 us (1%)
    pallas_call x2, Pallas kernels, fine_call(): pl.pallas_call(functools.partial(fine_kernel, offset=first), grid=(last -...  18.3 us
    all_to_all x1, starting transfers between devices, exchange(): got = lax.all_to_all(lowpass, AXES, 0, 0, tiled=True)  7.3 us
    pallas_call x1, Pallas kernels, lowpass_call(): pl.pallas_call(lowpass_kernel, in_specs=[pl.BlockSpec(memory_space=pltpu....  6.11 us
    all_to_all x1, starting transfers between devices, exchange(): return (lax.all_to_all(sent, AXES, 0, 0, tiled=True), index)  5.84 us
    pallas_call x1, Pallas kernels, coarse_call(): pl.pallas_call(coarse_kernel, in_specs=[pl.BlockSpec(memory_space=pltpu.S...  4.26 us
    pallas_call x1, Pallas kernels, route_call(): pl.pallas_call(route_kernel, in_specs=[pl.BlockSpec(memory_space=pltpu.SM...  2.69 us
    all_to_all x1, waiting for transfers between devices, exchange(): return (lax.all_to_all(sent, AXES, 0, 0, tiled=True), index)  1.8 us
    unnamed x4, local copies, waits for them, and re-layouts  1.34 us
  transfers between devices with their start and end apart: 2, of which 1 were waited for; matrix products, arithmetic and copies ran while one was open for 0% of the time, Pallas kernels for 38%

profile of v3, /device:TPU:0, one launch (start us, length us, event | category | flops | bytes accessed | tf_op | source)
XLA Modules:
  0.0 48.4 jit_solution(15587041386843788767)
XLA Ops:
  0.7 6.1 %lowpass.1 = f32[256,128]{1,0:T(8,128)} custom-call(s32[1]{0:T(128)S(6)} %copy.23.count_ref, f32[6,64,4096]{2,1,0:T(8,128)} %x_ref.5, bf16[1536,128]{1,0:T(8,128)(2,1)} %constant.39.clone.wz_any, bf16[1024,256]{1,0:T(8,128)(2,1)} %constant.40.clone.wyh_any, bf16[1024,256]{1,0:T(8,128)(2,1)} %constant.41.clone.wyl_any), custom_call_target="tpu_custom_call" | custom-call | tf_op jit(solution)/shard_map/lowpass/pallas_call | solution.py:137
  6.8 7.3 %all-to-all-start = ((f32[32,8,128]{2,1,0:T(8,128)}), f32[32,8,128]{2,1,0:T(8,128)S(1)}, u32[]{:S(2)}, u32[]{:S(2)}) async-start(f32[32,8,128]{2,1,0:T(8,128)} %bitcast.3), calls=%async_computation | async-start | bytes 262144 | tf_op jit(solution)/shard_map/all_to_all | solution.py:541
  14.1 9.2 %fine.2._.refs_0_ = f32[6,64,4096]{2,1,0:T(8,128)} custom-call(s32[1]{0:T(128)S(6)} %copy.23.count_ref, f32[6,64,4096]{2,1,0:T(8,128)} %x_ref.5, bf16[768,256]{1,0:T(8,128)(2,1)} %constant.42.clone.w1_ref, bf16[768,256]{1,0:T(8,128)(2,1)} %constant.43.clone.w2_ref, f32[32,8,128]{2,1,0:T(8,128)} %bitcast.4), custom_call_target="tpu_custom_call" | custom-call | flops 1207959552 | bytes 6291456 | tf_op jit(solution)/shard_map/fine/pallas_call | solution.py:372
  23.3 0.0 all-to-all-done.got_ref
  23.3 0.0 copy-start.1
  23.3 0.6 %copy-done.1 = f32[32,8,128]{2,1,0:T(8,128)} copy-done((f32[32,8,128]{2,1,0:T(8,128)}, f32[32,8,128]{2,1,0:T(8,128)S(1)}, u32[]{:S(2)}) %copy-start.1) | copy-done | bytes 131096
  23.9 2.7 %route.1 = (f32[32,16,128]{2,1,0:T(8,128)}, s32[2]{0:T(128)}) custom-call(s32[1]{0:T(128)} %bitcast.me_ref, f32[32,8,128]{2,1,0:T(8,128)} %copy-done.1, f32[6,64,4096]{2,1,0:T(8,128)} %fine.2._.refs_0_), custom_call_target="tpu_custom_call" | custom-call | tf_op jit(solution)/shard_map/route/pallas_call | solution.py:182
  26.6 5.8 %all-to-all-start.1 = ((f32[32,16,128]{2,1,0:T(8,128)}), f32[32,16,128]{2,1,0:T(8,128)S(1)}, u32[]{:S(2)}, u32[]{:S(2)}) async-start(f32[32,16,128]{2,1,0:T(8,128)} %get-tuple-element.8), calls=%async_computation.1 | async-start | bytes 524288 | tf_op jit(solution)/shard_map/all_to_all | solution.py:543
  32.5 9.1 %fine.3.fine_ref = f32[6,64,4096]{2,1,0:T(8,128)} custom-call(s32[1]{0:T(128)S(6)} %copy.23.count_ref, f32[6,64,4096]{2,1,0:T(8,128)} %x_ref.5, bf16[768,256]{1,0:T(8,128)(2,1)} %constant.42.clone.w1_ref, bf16[768,256]{1,0:T(8,128)(2,1)} %constant.43.clone.w2_ref, f32[6,64,4096]{2,1,0:T(8,128)} %fine.2._.refs_0_), custom_call_target="tpu_custom_call", output_to_operand_aliasing={{}: (4, {})} | custom-call | flops 1207959552 | bytes 6291456 | tf_op jit(solution)/shard_map/fine/pallas_call | solution.py:372
  41.6 1.8 %all-to-all-done.1 = f32[32,16,128]{2,1,0:T(8,128)S(1)} async-done(((f32[32,16,128]{2,1,0:T(8,128)}), f32[32,16,128]{2,1,0:T(8,128)S(1)}, u32[]{:S(2)}, u32[]{:S(2)}) %all-to-all-start.1) | async-done | bytes 262176 | tf_op jit(solution)/shard_map/all_to_all | solution.py:543
  43.4 0.0 copy-start
  43.4 0.7 %copy-done = f32[32,16,128]{2,1,0:T(8,128)} copy-done((f32[32,16,128]{2,1,0:T(8,128)}, f32[32,16,128]{2,1,0:T(8,128)S(1)}, u32[]{:S(2)}) %copy-start) | copy-done | bytes 262168
  44.1 4.3 %coarse.1 = f32[6,64,4096]{2,1,0:T(8,128)} custom-call(s32[2]{0:T(128)} %get-tuple-element.7.index_ref, f32[512,128]{1,0:T(8,128)} %bitcast.5, bf16[32,96]{1,0:T(8,128)(2,1)} %constant.44.clone.wx_ref, bf16[256,256]{1,0:T(8,128)(2,1)} %constant.45.clone.wzh_ref, bf16[256,256]{1,0:T(8,128)(2,1)} %constant.46.clone.wzl_ref, ...), custom_call_target="tpu_custom_call", output_to_operand_aliasing={{}: (11, {})} | custom-call | tf_op jit(solution)/shard_map/coarse/pallas_call | solution.py:520
Async XLA Ops:
  6.8 16.5 %all-to-all-start = ((f32[32,8,128]{2,1,0:T(8,128)}), f32[32,8,128]{2,1,0:T(8,128)S(1)}, u32[]{:S(2)}, u32[]{:S(2)}) async-start(f32[32,8,128]{2,1,0:T(8,128)} %bitcast.3), calls=%async_computation | async-start | bytes 262144 | tf_op jit(solution)/shard_map/all_to_all | solution.py:541
  23.3 0.7 %copy-start.1 = (f32[32,8,128]{2,1,0:T(8,128)}, f32[32,8,128]{2,1,0:T(8,128)S(1)}, u32[]{:S(2)}) copy-start(f32[32,8,128]{2,1,0:T(8,128)S(1)} %all-to-all-done.got_ref) | copy-start | bytes 393220
  26.6 16.8 %all-to-all-start.1 = ((f32[32,16,128]{2,1,0:T(8,128)}), f32[32,16,128]{2,1,0:T(8,128)S(1)}, u32[]{:S(2)}, u32[]{:S(2)}) async-start(f32[32,16,128]{2,1,0:T(8,128)} %get-tuple-element.8), calls=%async_computation.1 | async-start | bytes 524288 | tf_op jit(solution)/shard_map/all_to_all | solution.py:543
  43.4 0.7 %copy-start = (f32[32,16,128]{2,1,0:T(8,128)}, f32[32,16,128]{2,1,0:T(8,128)S(1)}, u32[]{:S(2)}) copy-start(f32[32,16,128]{2,1,0:T(8,128)S(1)} %all-to-all-done.1) | copy-start | bytes 786436

commit v4 on v3

--- a/solution.py
+++ b/solution.py
@@ -81,34 +81,57 @@
 ):
     slots, edge = x_ref.shape[:2]
     quarter = edge // 4
-    order = (0, 2, 1, 3)
-    for g in order:
-        start_tiles(x_ref, x_buf, sems.at[g], range(8 * g, 8 * g + 8))
+
+    def copies(g):
+        return [
+            pltpu.make_async_copy(
+                x_ref.at[:, :, pl.ds(t * 128, 128)],
+                x_buf.at[pl.ds(t * slots, slots)],
+                sems.at[g],
+            )
+            for t in range(8 * g, 8 * g + 8)
+        ]
+
     weights = [
         pltpu.make_async_copy(src, dst, w_sems.at[i])
         for i, (src, dst) in enumerate(((wz_any, wz_ref), (wyh_any, wyh_ref), (wyl_any, wyl_ref)))
     ]
-    for copy in weights:
-        copy.start()
-    for g in order:
-        part = x_buf.at[:, :, pl.ds(8 * g, 8), :]
+    order = (0, 2, 1, 3)
+    for g in order[:2]:
+        for copy in copies(g):
+            copy.start()
+    rows_ref = x_buf.reshape(x_buf.shape[0] * edge, 128)
+    for n, g in enumerate(order):
+        part = x_buf.at[pl.ds(8 * g * slots, 8 * slots)]
         pltpu.make_async_copy(part, part, sems.at[g]).wait()
-        at = (g % 2) * 256 + (g // 2) * 128
+        if n + 2 < len(order):
+            for copy in copies(order[n + 2]):
+                copy.start()
+        if n == 0:
+            for copy in weights:
+                copy.start()
+        at = (g // 2) * 128
 
         @pl.loop(0, slots)
         def _(s):
-            rows = [x_buf[s, x, pl.ds(8 * g, 8), :] for x in range(edge)]
+            base = (8 * g * slots + s) * edge
+            rows = [rows_ref[pl.ds(base + x, 8, stride=slots * edge), :] for x in range(edge)]
             rows, _ = lift(rows[0::2], rows[1::2], edge // 2, False, False)
             rows, _ = lift(rows[0::2], rows[1::2], quarter, False, False)
             for m, (high, low) in enumerate(split_rows(rows)):
                 place = pl.ds(pl.multiple_of(s * 8 * quarter + 16 * m, 16), 16)
-                l_ref[place, pl.ds(at, 128)] = high
-                l_ref[place, pl.ds(512 + at, 128)] = low
-                l_ref[place, pl.ds(1024 + at, 128)] = high
-
-    for copy in weights:
+                l_ref[g % 2, place, pl.ds(at, 128)] = high
+                l_ref[g % 2, place, pl.ds(256 + at, 128)] = low
+                l_ref[g % 2, place, pl.ds(512 + at, 128)] = high
+
+        if n == 1:
+            weights[0].wait()
+            z_ref[...] = dot(l_ref[0], wz_ref[0])
+        if n == 3:
+            z_ref[...] += dot(l_ref[1], wz_ref[1])
+
+    for copy in weights[1:]:
         copy.wait()
-    z_ref[...] = dot(l_ref[...], wz_ref[...])
     wide = jnp.concatenate([z_ref[pl.ds(i, slots * quarter, stride=8), :] for i in range(8)], 1)
     made = times(wide, wyh_ref[...], wyl_ref[...])
     out_ref[...] = jnp.full(out_ref.shape, count_ref[0].astype(F32))
@@ -128,7 +151,8 @@
     slots, edge, plane = density.shape
     quarter = edge // 4
     two_levels = pass_matrix(edge // 2)[:quarter] @ pass_matrix(edge)[: edge // 2]
-    wz = stacked(np.kron(np.eye(8), two_levels.T))
+    wide = np.kron(np.eye(8), two_levels.T)
+    wz = np.stack([stacked(wide[:256]), stacked(wide[256:])])
     i, gp, q, p = np.meshgrid(np.arange(8), np.arange(2), np.arange(2), np.arange(2), indexing="ij")
     entry = (2 * (8 * gp + i) + p + 32 * q).reshape(-1)
     wy = np.kron(two_levels.T[entry] / SQUARE, np.eye(quarter))
@@ -140,11 +164,11 @@
         out_specs=pl.BlockSpec(memory_space=pltpu.VMEM),
         out_shape=jax.ShapeDtypeStruct((16 * quarter, 128), F32),
         scratch_shapes=[
-            pltpu.VMEM((slots, edge, plane // 128, 128), F32),
+            pltpu.VMEM((plane // 128 * slots, edge, 128), F32),
             pltpu.VMEM(wz.shape, BF16),
             pltpu.VMEM(wyh.shape, BF16),
             pltpu.VMEM(wyl.shape, BF16),
-            pltpu.VMEM((slots * 8 * quarter, 1536), BF16),
+            pltpu.VMEM((2, slots * 8 * quarter, 768), BF16),
             pltpu.VMEM((slots * 8 * quarter, 128), F32),
             pltpu.SemaphoreType.DMA((4,)),
             pltpu.SemaphoreType.DMA((3,)),
@@ -155,12 +179,17 @@
     return pieces.reshape(2 * quarter, 8, 128)
 
 
-def route_kernel(me_ref, got_ref, _, send_ref, index_ref, order_ref, count_ref, sem):
+def route_kernel(me_ref, got_any, _, send_ref, index_ref, got_ref, order_ref, count_ref, sems):
     devices = got_ref.shape[0]
-    copy = pltpu.make_async_copy(got_ref.at[:, 7, :], count_ref, sem)
-    copy.start()
+    copies = [
+        pltpu.make_async_copy(got_any.at[:, 7, :], count_ref, sems.at[0]),
+        pltpu.make_async_copy(got_any, got_ref, sems.at[1]),
+    ]
+    for copy in copies:
+        copy.start()
     order_ref[...] = jnp.zeros_like(order_ref)
-    copy.wait()
+    for copy in copies:
+        copy.wait()
     start, my_start, my_count = 0, 0, 0
     starts = []
     for d in range(devices):
@@ -183,7 +212,7 @@
         route_kernel,
         in_specs=[
             pl.BlockSpec(memory_space=pltpu.SMEM),
-            pl.BlockSpec(memory_space=pltpu.VMEM),
+            pl.BlockSpec(memory_space=pl.ANY),
             pl.BlockSpec(memory_space=pl.ANY),
         ],
         out_specs=[pl.BlockSpec(memory_space=pltpu.VMEM), pl.BlockSpec(memory_space=pltpu.SMEM)],
@@ -192,9 +221,10 @@
             jax.ShapeDtypeStruct((2,), jnp.int32),
         ],
         scratch_shapes=[
+            pltpu.VMEM(got.shape, F32),
             pltpu.VMEM((devices * slots + 16, 128), F32),
             pltpu.SMEM((devices, 128), F32),
-            pltpu.SemaphoreType.DMA,
+            pltpu.SemaphoreType.DMA((2,)),
         ],
         compiler_params=pltpu.CompilerParams(vmem_limit_bytes=VMEM_LIMIT),
         name="route",
@@ -273,8 +303,13 @@
         high_all = [left(high, (1, -2)), left(high, (0, -1))] + high + [right(high, (0, -2))]
         return low_all, high_all
 
-    def fetch(which, place):
-        start_tiles(x_ref.at[which], x_buf.at[place], sems.at[place], range(tiles))
+    def fetch(which, place, which_tiles):
+        start_tiles(x_ref.at[which], x_buf.at[place], sems.at[place], which_tiles)
+
+    def fetch_next(phase):
+        @pl.when((step + 1 < pl.num_programs(0)) & (slot + 1 < count_ref[0]))
+        def _():
+            fetch(slot + 1, (step + 1) % 2, range(2 * phase, 2 * phase + 2))
 
     def scaled_rows(rows):
         low, high = lift(rows[0::2], rows[1::2], len(rows) // 2, False, False)
@@ -289,11 +324,7 @@
 
     @pl.when((step == 0) & (slot < count_ref[0]))
     def _():
-        fetch(slot, 0)
-
-    @pl.when((step + 1 < pl.num_programs(0)) & (slot + 1 < count_ref[0]))
-    def _():
-        fetch(slot + 1, (step + 1) % 2)
+        fetch(slot, 0, range(tiles))
 
     @pl.when(slot >= count_ref[0])
     def _():
@@ -306,6 +337,8 @@
         for g in range(4):
             rows = scaled_rows([x[i, pl.ds(8 * g, 8), :] for i in range(edge)])
             store_terms(l_ref, (g % 2) * 8 * edge, (g // 2) * 128, rows)
+            fetch_next(2 * g)
+            fetch_next(2 * g + 1)
         lifted = dot(l_ref[...], w1_ref[...])
         y_ref[pl.ds(0, pairs * edge), :] = lifted[:, :128]
         y_ref[pl.ds(pairs * edge, pairs * edge), :] = lifted[:, 128:]
@@ -330,6 +363,7 @@
                 for i in range(8):
                     c_ref[pl.ds(i * half + 8 * r, 8), :] = low[i]
                     c_ref[pl.ds((8 + i) * half + 8 * r, 8), :] = high[i]
+            fetch_next(8 + r)
         for u in range(2):
             rows = scaled_rows([c_ref[pl.ds(u * 8 * half + i, 8, stride=half), :] for i in range(half)])
             store_terms(m_ref, 0, u * 128, rows)
@@ -397,20 +431,23 @@
 
 def coarse_kernel(
     index_ref,
-    piece_ref,
+    piece_any,
     wx_ref,
-    wzh_ref,
-    wzl_ref,
-    wyh_ref,
-    wyl_ref,
-    w23h_ref,
-    w23l_ref,
     wx2_ref,
     wx3_ref,
+    wz_any,
+    wy_any,
+    w23_any,
     fine_ref,
     out_ref,
+    wz_ref,
+    wy_ref,
+    w23_ref,
+    piece_ref,
     block_ref,
     corner_ref,
+    piece_sem,
+    weight_sem,
     corner_sem,
     out_sem,
 ):
@@ -423,8 +460,17 @@
     def piece(i):
         return jnp.concatenate([piece_ref[pl.ds(16 * h + i, 16, stride=32), :] for h in range(2)], 1)
 
+    pieces = pltpu.make_async_copy(piece_any, piece_ref, piece_sem)
+    pieces.start()
+    weights = [
+        pltpu.make_async_copy(src, dst, weight_sem.at[i])
+        for i, (src, dst) in enumerate(((wz_any, wz_ref), (wy_any, wy_ref), (w23_any, w23_ref)))
+    ]
+    for copy in weights:
+        copy.start()
     for s in range(slots):
         pltpu.make_async_copy(window(s), corner_ref.at[s], corner_sem.at[s]).start()
+    pieces.wait()
 
     first = [
         [
@@ -439,7 +485,8 @@
             for yh in range(2):
                 part = slice(yh * 128, yh * 128 + 128)
                 stacked.append(jnp.concatenate([first[o][cy][:, part], first[o][2 + cy][:, part]], 1))
-    lifted = times(jnp.concatenate(stacked, 0), wzh_ref[...], wzl_ref[...])
+    weights[0].wait()
+    lifted = times(jnp.concatenate(stacked, 0), wz_ref[0], wz_ref[1])
     stacked = []
     for o in range(2):
         for tz in range(2):
@@ -449,7 +496,8 @@
                     1,
                 )
             )
-    lifted = times(jnp.concatenate(stacked, 0), wyh_ref[...], wyl_ref[...])
+    weights[1].wait()
+    lifted = times(jnp.concatenate(stacked, 0), wy_ref[0], wy_ref[1])
     corner = []
     for o in range(2):
         for tz in range(2):
@@ -461,7 +509,8 @@
                         corner.append(value)
                     else:
                         block_ref[o * 8 + tx + 2 * ty + 4 * tz] = value
-    both = times(jnp.concatenate(corner, 0), w23h_ref[...], w23l_ref[...])
+    weights[2].wait()
+    both = times(jnp.concatenate(corner, 0), w23_ref[0], w23_ref[1])
     spot = lax.broadcasted_iota(jnp.int32, (16, 256), 1)
     depth = lax.broadcasted_iota(jnp.int32, (16, 256), 0)
     small = (depth < 8) & (spot < 128) & ((spot & 15) < 8)
@@ -507,24 +556,23 @@
                 eye8, m32[tz * 16 : tz * 16 + 16, cz * 16 : cz * 16 + 16].T
             )
     w23 = np.concatenate([np.kron(m16.T, m16.T), np.kron(deep.T, deep.T)], 1)
-    weights = [
-        left_terms(m32),
-        *two_terms(wz),
-        *two_terms(np.kron(m32.T, eye16)),
-        *two_terms(w23),
-        left_terms(m16),
-        left_terms(deep),
-    ]
+    small = [left_terms(m32), left_terms(m16), left_terms(deep)]
+    large = [np.stack(two_terms(w)) for w in (wz, np.kron(m32.T, eye16), w23)]
+    weights = small + large
     anywhere = pl.BlockSpec(memory_space=pl.ANY)
     vmem = pl.BlockSpec(memory_space=pltpu.VMEM)
     return pl.pallas_call(
         coarse_kernel,
-        in_specs=[pl.BlockSpec(memory_space=pltpu.SMEM), vmem] + [vmem] * len(weights) + [anywhere],
+        in_specs=[pl.BlockSpec(memory_space=pltpu.SMEM), anywhere] + [vmem] * len(small) + [anywhere] * (len(large) + 1),
         out_specs=anywhere,
         out_shape=jax.ShapeDtypeStruct(fine.shape, F32),
         scratch_shapes=[
+            *[pltpu.VMEM(w.shape, BF16) for w in large],
+            pltpu.VMEM((32 * 16, 128), F32),
             pltpu.VMEM((16, 16, 256), F32),
             pltpu.VMEM((slots, 16, 1024), F32),
+            pltpu.SemaphoreType.DMA,
+            pltpu.SemaphoreType.DMA((3,)),
             pltpu.SemaphoreType.DMA((slots,)),
             pltpu.SemaphoreType.DMA((slots,)),
         ],
@@ -554,9 +602,10 @@
 def per_device(density, owner_counts):
     lowpass = lowpass_call(owner_counts, density)
     slots = density.shape[0]
-    fine = fine_call(owner_counts, density, 0, slots // 2, after=lowpass)
+    early = slots // 3
+    fine = fine_call(owner_counts, density, 0, early, after=lowpass)
     pieces, index = exchange(lowpass, slots, fine)
-    fine = fine_call(owner_counts, density, slots // 2, slots, fine)
+    fine = fine_call(owner_counts, density, early, slots, fine)
     return coarse_call(index, pieces, fine)
 
 

time: 48.9 us -> 58.6 us (1.20)
  Pallas kernels: 31.4 us -> 42.5 us
  waiting for transfers between devices: 1.8 us -> 0.01 us
    pallas_call x2, Pallas kernels: 18.3 us -> 25.6 us  [fine_call(): pl.pallas_call(functools.partial(fine_kernel, offset=first), grid=(last -...]
    pallas_call x1, Pallas kernels: 6.11 us -> 9.63 us  [lowpass_call(): pl.pallas_call(lowpass_kernel, in_specs=[pl.BlockSpec(memory_space=pltpu....]
    all_to_all x1, waiting for transfers between devices: 1.8 us -> 0.01 us  [exchange(): return (lax.all_to_all(sent, AXES, 0, 0, tiled=True), index)]
    pallas_call x1, Pallas kernels: 4.26 us -> 5.33 us  [coarse_call(): pl.pallas_call(coarse_kernel, in_specs=[pl.BlockSpec(memory_space=pltpu.S...]
    pallas_call x1, Pallas kernels: 2.69 us -> 1.92 us  [route_call(): pl.pallas_call(route_kernel, in_specs=[pl.BlockSpec(memory_space=pltpu.SM...]
  transfers between devices with their start and end apart: 2 -> 2, of which waited for: 1 -> 0; matrix products, arithmetic and copies ran while one was open for 0% -> 0% of each run, Pallas kernels for 38% -> 44%
where the time goes in v4:
time: 58.6 us; the launch traced here: 57.7 us
  Pallas kernels  42.5 us (73%)
  starting transfers between devices  13.1 us (22%)
  local copies, waits for them, and re-layouts  1.34 us (2%)
  between operations  0.74 us (1%)
    pallas_call x2, Pallas kernels, fine_call(): pl.pallas_call(functools.partial(fine_kernel, offset=first), grid=(last -...  25.6 us
    pallas_call x1, Pallas kernels, lowpass_call(): pl.pallas_call(lowpass_kernel, in_specs=[pl.BlockSpec(memory_space=pltpu....  9.63 us
    all_to_all x1, starting transfers between devices, exchange(): got = lax.all_to_all(lowpass, AXES, 0, 0, tiled=True)  7.3 us
    all_to_all x1, starting transfers between devices, exchange(): return (lax.all_to_all(sent, AXES, 0, 0, tiled=True), index)  5.84 us
    pallas_call x1, Pallas kernels, coarse_call(): pl.pallas_call(coarse_kernel, in_specs=[pl.BlockSpec(memory_space=pltpu.S...  5.33 us
    pallas_call x1, Pallas kernels, route_call(): pl.pallas_call(route_kernel, in_specs=[pl.BlockSpec(memory_space=pltpu.SM...  1.92 us
    unnamed x4, local copies, waits for them, and re-layouts  1.34 us
  transfers between devices with their start and end apart: 2, of which 0 were waited for; matrix products, arithmetic and copies ran while one was open for 0% of the time, Pallas kernels for 44%

profile of v4, /device:TPU:0, one launch (start us, length us, event | category | flops | bytes accessed | tf_op | source)
XLA Modules:
  0.0 57.7 jit_solution(9732195155055264805)
XLA Ops:
  0.7 9.6 %lowpass.1 = f32[256,128]{1,0:T(8,128)} custom-call(s32[1]{0:T(128)S(6)} %copy.20.count_ref, f32[6,64,4096]{2,1,0:T(8,128)} %x_ref.5, bf16[2,768,128]{2,1,0:T(8,128)(2,1)} %constant.33.clone.wz_any, bf16[1024,256]{1,0:T(8,128)(2,1)} %constant.34.clone.wyh_any, bf16[1024,256]{1,0:T(8,128)(2,1)} %constant.35.clone.wyl_any), custom_call_target="tpu_custom_call" | custom-call | tf_op jit(solution)/shard_map/lowpass/pallas_call | solution.py:161
  10.3 7.3 %all-to-all-start = ((f32[32,8,128]{2,1,0:T(8,128)}), f32[32,8,128]{2,1,0:T(8,128)S(1)}, u32[]{:S(2)}, u32[]{:S(2)}) async-start(f32[32,8,128]{2,1,0:T(8,128)} %bitcast.3), calls=%async_computation | async-start | bytes 262144 | tf_op jit(solution)/shard_map/all_to_all | solution.py:589
  17.6 9.6 %fine.2._.refs_0_ = f32[6,64,4096]{2,1,0:T(8,128)} custom-call(s32[1]{0:T(128)S(6)} %copy.20.count_ref, f32[6,64,4096]{2,1,0:T(8,128)} %x_ref.5, bf16[768,256]{1,0:T(8,128)(2,1)} %constant.36.clone.w1_ref, bf16[768,256]{1,0:T(8,128)(2,1)} %constant.37.clone.w2_ref, f32[32,8,128]{2,1,0:T(8,128)} %bitcast.4), custom_call_target="tpu_custom_call" | custom-call | flops 805306368 | bytes 4194304 | tf_op jit(solution)/shard_map/fine/pallas_call | solution.py:406
  27.2 0.0 all-to-all-done.got_any
  27.2 0.0 copy-start.1
  27.2 0.6 %copy-done.1 = f32[32,8,128]{2,1,0:T(8,128)} copy-done((f32[32,8,128]{2,1,0:T(8,128)}, f32[32,8,128]{2,1,0:T(8,128)S(1)}, u32[]{:S(2)}) %copy-start.1) | copy-done | bytes 131096
  27.9 1.9 %route.1 = (f32[32,16,128]{2,1,0:T(8,128)}, s32[2]{0:T(128)}) custom-call(s32[1]{0:T(128)} %bitcast.me_ref, f32[32,8,128]{2,1,0:T(8,128)} %copy-done.1, f32[6,64,4096]{2,1,0:T(8,128)} %fine.2._.refs_0_), custom_call_target="tpu_custom_call" | custom-call | tf_op jit(solution)/shard_map/route/pallas_call | solution.py:211
  29.8 5.8 %all-to-all-start.1 = ((f32[32,16,128]{2,1,0:T(8,128)}), f32[32,16,128]{2,1,0:T(8,128)S(1)}, u32[]{:S(2)}, u32[]{:S(2)}) async-start(f32[32,16,128]{2,1,0:T(8,128)} %get-tuple-element.8), calls=%async_computation.1 | async-start | bytes 524288 | tf_op jit(solution)/shard_map/all_to_all | solution.py:591
  35.6 16.0 %fine.3.fine_ref = f32[6,64,4096]{2,1,0:T(8,128)} custom-call(s32[1]{0:T(128)S(6)} %copy.20.count_ref, f32[6,64,4096]{2,1,0:T(8,128)} %x_ref.5, bf16[768,256]{1,0:T(8,128)(2,1)} %constant.36.clone.w1_ref, bf16[768,256]{1,0:T(8,128)(2,1)} %constant.37.clone.w2_ref, f32[6,64,4096]{2,1,0:T(8,128)} %fine.2._.refs_0_), custom_call_target="tpu_custom_call", output_to_operand_aliasing={{}: (4, {})} | custom-call | flops 1610612736 | bytes 8388608 | tf_op jit(solution)/shard_map/fine/pallas_call | solution.py:406
  51.7 0.0 all-to-all-done.1
  51.7 0.0 copy-start
  51.7 0.7 %copy-done = f32[32,16,128]{2,1,0:T(8,128)} copy-done((f32[32,16,128]{2,1,0:T(8,128)}, f32[32,16,128]{2,1,0:T(8,128)S(1)}, u32[]{:S(2)}) %copy-start) | copy-done | bytes 262168
  52.4 5.3 %coarse.1 = f32[6,64,4096]{2,1,0:T(8,128)} custom-call(s32[2]{0:T(128)} %get-tuple-element.7.index_ref, f32[512,128]{1,0:T(8,128)} %bitcast.5, bf16[32,96]{1,0:T(8,128)(2,1)} %constant.38.clone.wx_ref, bf16[16,48]{1,0:T(8,128)(2,1)} %constant.39.clone.wx2_ref, bf16[16,48]{1,0:T(8,128)(2,1)} %constant.40.clone.wx3_ref, ...), custom_call_target="tpu_custom_call", output_to_operand_aliasing={{}: (8, {})} | custom-call | tf_op jit(solution)/shard_map/coarse/pallas_call | solution.py:564
Async XLA Ops:
  10.3 16.9 %all-to-all-start = ((f32[32,8,128]{2,1,0:T(8,128)}), f32[32,8,128]{2,1,0:T(8,128)S(1)}, u32[]{:S(2)}, u32[]{:S(2)}) async-start(f32[32,8,128]{2,1,0:T(8,128)} %bitcast.3), calls=%async_computation | async-start | bytes 262144 | tf_op jit(solution)/shard_map/all_to_all | solution.py:589
  27.2 0.7 %copy-start.1 = (f32[32,8,128]{2,1,0:T(8,128)}, f32[32,8,128]{2,1,0:T(8,128)S(1)}, u32[]{:S(2)}) copy-start(f32[32,8,128]{2,1,0:T(8,128)S(1)} %all-to-all-done.got_any) | copy-start | bytes 393220
  29.8 21.9 %all-to-all-start.1 = ((f32[32,16,128]{2,1,0:T(8,128)}), f32[32,16,128]{2,1,0:T(8,128)S(1)}, u32[]{:S(2)}, u32[]{:S(2)}) async-start(f32[32,16,128]{2,1,0:T(8,128)} %get-tuple-element.8), calls=%async_computation.1 | async-start | bytes 524288 | tf_op jit(solution)/shard_map/all_to_all | solution.py:591
  51.7 0.7 %copy-start = (f32[32,16,128]{2,1,0:T(8,128)}, f32[32,16,128]{2,1,0:T(8,128)S(1)}, u32[]{:S(2)}) copy-start(f32[32,16,128]{2,1,0:T(8,128)S(1)} %all-to-all-done.1) | copy-start | bytes 786436

commit v5 on v3

--- a/solution.py
+++ b/solution.py
@@ -18,7 +18,9 @@
 BF16 = jnp.bfloat16
 AXES = ("node", "dev")
 MIB = 1 << 20
-VMEM_LIMIT = 56 * MIB
+VMEM_LIMIT = 40 * MIB
+VMEM_SMALL = 16 * MIB
+VMEM_LARGE = 45 * MIB
 
 
 def pass_matrix(n):
@@ -59,7 +61,9 @@
 
 def times(value, first, second):
     high, low = split(value)
-    return dot(high, first) + dot(low, first) + dot(high, second)
+    both = dot(jnp.concatenate([high, low], 0), first)
+    count = value.shape[0]
+    return both[:count] + both[count:] + dot(high, second)
 
 
 def times_left(terms, value):
@@ -67,48 +71,45 @@
     return dot(terms, jnp.concatenate([high, high, low], 0))
 
 
-def start_tiles(src_ref, dst_ref, sem, tiles):
-    for t in tiles:
-        pltpu.make_async_copy(src_ref.at[..., pl.ds(t * 128, 128)], dst_ref.at[..., t, :], sem).start()
-
-
 def split_rows(rows):
     return [split(jnp.concatenate(rows[m : m + 2], 0)) for m in range(0, len(rows), 2)]
 
 
 def lowpass_kernel(
-    count_ref, x_ref, wz_any, wyh_any, wyl_any, out_ref, x_buf, wz_ref, wyh_ref, wyl_ref, l_ref, z_ref, sems, w_sems
+    count_ref, x_any, wz_any, wyh_any, wyl_any, out_ref, x_ref, wz_ref, wyh_ref, wyl_ref, l_ref, z_ref, sems, w_sems
 ):
-    slots, edge = x_ref.shape[:2]
+    slots, edge = x_any.shape[:2]
     quarter = edge // 4
-    order = (0, 2, 1, 3)
-    for g in order:
-        start_tiles(x_ref, x_buf, sems.at[g], range(8 * g, 8 * g + 8))
+    rows_all = slots * 8 * quarter
+    for t in range(x_ref.shape[2]):
+        pltpu.make_async_copy(
+            x_any.at[:, :, pl.ds(t * 128, 128)], x_ref.at[:, :, t, :], sems.at[t // 8]
+        ).start()
     weights = [
         pltpu.make_async_copy(src, dst, w_sems.at[i])
         for i, (src, dst) in enumerate(((wz_any, wz_ref), (wyh_any, wyh_ref), (wyl_any, wyl_ref)))
     ]
     for copy in weights:
         copy.start()
-    for g in order:
-        part = x_buf.at[:, :, pl.ds(8 * g, 8), :]
+    for g in range(4):
+        part = x_ref.at[:, :, pl.ds(8 * g, 8), :]
         pltpu.make_async_copy(part, part, sems.at[g]).wait()
-        at = (g % 2) * 256 + (g // 2) * 128
 
         @pl.loop(0, slots)
         def _(s):
-            rows = [x_buf[s, x, pl.ds(8 * g, 8), :] for x in range(edge)]
+            rows = [x_ref[s, x, pl.ds(8 * g, 8), :] for x in range(edge)]
             rows, _ = lift(rows[0::2], rows[1::2], edge // 2, False, False)
             rows, _ = lift(rows[0::2], rows[1::2], quarter, False, False)
             for m, (high, low) in enumerate(split_rows(rows)):
-                place = pl.ds(pl.multiple_of(s * 8 * quarter + 16 * m, 16), 16)
-                l_ref[place, pl.ds(at, 128)] = high
-                l_ref[place, pl.ds(512 + at, 128)] = low
-                l_ref[place, pl.ds(1024 + at, 128)] = high
+                at = pl.multiple_of(s * 8 * quarter + 16 * m, 16)
+                cols = pl.ds((g // 2) * 128, 128)
+                l_ref[g % 2, pl.ds(at, 16), cols] = high
+                l_ref[g % 2, pl.ds(rows_all + at, 16), cols] = low
 
     for copy in weights:
         copy.wait()
-    z_ref[...] = dot(l_ref[...], wz_ref[...])
+    made = dot(l_ref[0], wz_ref[0]) + dot(l_ref[1], wz_ref[1])
+    z_ref[...] = (made[:rows_all, :128] + made[rows_all:, :128]) + made[:rows_all, 128:]
     wide = jnp.concatenate([z_ref[pl.ds(i, slots * quarter, stride=8), :] for i in range(8)], 1)
     made = times(wide, wyh_ref[...], wyl_ref[...])
     out_ref[...] = jnp.full(out_ref.shape, count_ref[0].astype(F32))
@@ -128,39 +129,49 @@
     slots, edge, plane = density.shape
     quarter = edge // 4
     two_levels = pass_matrix(edge // 2)[:quarter] @ pass_matrix(edge)[: edge // 2]
-    wz = stacked(np.kron(np.eye(8), two_levels.T))
+    wide = np.kron(np.eye(8), two_levels.T)
+    wz = np.stack([np.concatenate(two_terms(w), 1) for w in (wide[:256], wide[256:])])
     i, gp, q, p = np.meshgrid(np.arange(8), np.arange(2), np.arange(2), np.arange(2), indexing="ij")
     entry = (2 * (8 * gp + i) + p + 32 * q).reshape(-1)
     wy = np.kron(two_levels.T[entry] / SQUARE, np.eye(quarter))
     wyh, wyl = two_terms(wy)
     anywhere = pl.BlockSpec(memory_space=pl.ANY)
-    pieces = pl.pallas_call(
+    vmem = pl.BlockSpec(memory_space=pltpu.VMEM)
+    rows_all = slots * 8 * quarter
+    pieces, held = pl.pallas_call(
         lowpass_kernel,
         in_specs=[pl.BlockSpec(memory_space=pltpu.SMEM)] + [anywhere] * 4,
-        out_specs=pl.BlockSpec(memory_space=pltpu.VMEM),
-        out_shape=jax.ShapeDtypeStruct((16 * quarter, 128), F32),
+        out_specs=[vmem, vmem],
+        out_shape=[
+            jax.ShapeDtypeStruct((16 * quarter, 128), F32),
+            jax.ShapeDtypeStruct((slots, edge, plane // 128, 128), F32),
+        ],
         scratch_shapes=[
-            pltpu.VMEM((slots, edge, plane // 128, 128), F32),
             pltpu.VMEM(wz.shape, BF16),
             pltpu.VMEM(wyh.shape, BF16),
             pltpu.VMEM(wyl.shape, BF16),
-            pltpu.VMEM((slots * 8 * quarter, 1536), BF16),
-            pltpu.VMEM((slots * 8 * quarter, 128), F32),
+            pltpu.VMEM((2, 2 * rows_all, 256), BF16),
+            pltpu.VMEM((rows_all, 128), F32),
             pltpu.SemaphoreType.DMA((4,)),
             pltpu.SemaphoreType.DMA((3,)),
         ],
-        compiler_params=pltpu.CompilerParams(vmem_limit_bytes=VMEM_LIMIT),
+        compiler_params=pltpu.CompilerParams(vmem_limit_bytes=VMEM_LARGE),
         name="lowpass",
     )(owner_counts, density, wz, wyh, wyl)
-    return pieces.reshape(2 * quarter, 8, 128)
-
-
-def route_kernel(me_ref, got_ref, _, send_ref, index_ref, order_ref, count_ref, sem):
+    return pieces.reshape(2 * quarter, 8, 128), held
+
+
+def route_kernel(me_ref, got_any, _, send_ref, index_ref, got_ref, order_ref, count_ref, sems):
     devices = got_ref.shape[0]
-    copy = pltpu.make_async_copy(got_ref.at[:, 7, :], count_ref, sem)
-    copy.start()
+    copies = [
+        pltpu.make_async_copy(got_any.at[:, 7, :], count_ref, sems.at[0]),
+        pltpu.make_async_copy(got_any, got_ref, sems.at[1]),
+    ]
+    for copy in copies:
+        copy.start()
     order_ref[...] = jnp.zeros_like(order_ref)
-    copy.wait()
+    for copy in copies:
+        copy.wait()
     start, my_start, my_count = 0, 0, 0
     starts = []
     for d in range(devices):
@@ -177,14 +188,14 @@
     index_ref[1] = my_count
 
 
-def route_call(me, got, meanwhile, slots):
+def route_call(me, got, token, slots):
     devices = got.shape[0]
     return pl.pallas_call(
         route_kernel,
         in_specs=[
             pl.BlockSpec(memory_space=pltpu.SMEM),
-            pl.BlockSpec(memory_space=pltpu.VMEM),
             pl.BlockSpec(memory_space=pl.ANY),
+            pl.BlockSpec(memory_space=pltpu.SMEM),
         ],
         out_specs=[pl.BlockSpec(memory_space=pltpu.VMEM), pl.BlockSpec(memory_space=pltpu.SMEM)],
         out_shape=[
@@ -192,13 +203,14 @@
             jax.ShapeDtypeStruct((2,), jnp.int32),
         ],
         scratch_shapes=[
+            pltpu.VMEM(got.shape, F32),
             pltpu.VMEM((devices * slots + 16, 128), F32),
             pltpu.SMEM((devices, 128), F32),
-            pltpu.SemaphoreType.DMA,
-        ],
-        compiler_params=pltpu.CompilerParams(vmem_limit_bytes=VMEM_LIMIT),
+            pltpu.SemaphoreType.DMA((2,)),
+        ],
+        compiler_params=pltpu.CompilerParams(vmem_limit_bytes=VMEM_SMALL),
         name="route",
-    )(me, got, meanwhile)
+    )(me, got, token)
 
 
 def lift(low, high, n, halo, scaled):
@@ -247,17 +259,19 @@
     return [fourth[i] for i in range(n)], [third[i] for i in range(n)]
 
 
-def fine_kernel(count_ref, x_ref, w1_ref, w2_ref, *refs, offset):
-    out_ref, x_buf, l_ref, y_ref, c_ref, m_ref, d_ref, sems = refs[-8:]
-    step = pl.program_id(0)
-    slot = step + offset
-    edge = x_ref.shape[1]
-    tiles = x_ref.shape[2] // 128
+def fine_kernel(count_ref, _, x_ref, w1_ref, w2_ref, *refs, first):
+    out_ref, token_ref, l_ref, y_ref, c_ref, m_ref, d_ref, o_ref, sems = refs[-9:]
+    slots, edge = o_ref.shape[:2]
+    tiles = x_ref.shape[2]
     pairs = tiles // 2
     half = edge // 2
+    block = pairs * edge
+    corner = 8 * half
+    live = jnp.clip(count_ref[0] - first, 0, slots)
     lane = lax.broadcasted_iota(jnp.int32, (8, 128), 1)
     front = lane < 64
     inner = (lane & 63) < half
+    token_ref[0] = live
 
     def turn(value):
         return pltpu.roll(value, 64, 1)
@@ -273,48 +287,42 @@
         high_all = [left(high, (1, -2)), left(high, (0, -1))] + high + [right(high, (0, -2))]
         return low_all, high_all
 
-    def fetch(which, place):
-        start_tiles(x_ref.at[which], x_buf.at[place], sems.at[place], range(tiles))
-
     def scaled_rows(rows):
         low, high = lift(rows[0::2], rows[1::2], len(rows) // 2, False, False)
         return [v * (1.0 / SCALE) for v in low] + [v * SCALE for v in high]
 
     def store_terms(ref, row, col, rows):
         for m, (high, low) in enumerate(split_rows(rows)):
-            place = pl.ds(row + 16 * m, 16)
+            place = pl.ds(pl.multiple_of(row + 16 * m, 16), 16)
             ref[place, pl.ds(col, 128)] = high
             ref[place, pl.ds(256 + col, 128)] = low
             ref[place, pl.ds(512 + col, 128)] = high
 
-    @pl.when((step == 0) & (slot < count_ref[0]))
-    def _():
-        fetch(slot, 0)
-
-    @pl.when((step + 1 < pl.num_programs(0)) & (slot + 1 < count_ref[0]))
-    def _():
-        fetch(slot + 1, (step + 1) % 2)
-
-    @pl.when(slot >= count_ref[0])
-    def _():
-        out_ref[...] = jnp.zeros_like(out_ref)
-
-    @pl.when(slot < count_ref[0])
-    def _():
-        x = x_buf.at[step % 2]
-        pltpu.make_async_copy(x, x, sems.at[step % 2]).wait()
+    def write(s):
+        return pltpu.make_async_copy(o_ref.at[s], out_ref.at[first + s], sems.at[s])
+
+    @pl.loop(live, slots)
+    def _(s):
+        o_ref[s] = jnp.zeros(o_ref.shape[1:], F32)
+        write(s).start()
+
+    @pl.loop(0, live)
+    def _(s):
         for g in range(4):
-            rows = scaled_rows([x[i, pl.ds(8 * g, 8), :] for i in range(edge)])
-            store_terms(l_ref, (g % 2) * 8 * edge, (g // 2) * 128, rows)
-        lifted = dot(l_ref[...], w1_ref[...])
-        y_ref[pl.ds(0, pairs * edge), :] = lifted[:, :128]
-        y_ref[pl.ds(pairs * edge, pairs * edge), :] = lifted[:, 128:]
+            rows = scaled_rows([x_ref[first + s, i, pl.ds(8 * g, 8), :] for i in range(edge)])
+            store_terms(l_ref, s * block + (g % 2) * 8 * edge, (g // 2) * 128, rows)
+
+    lifted = dot(l_ref[...], w1_ref[...])
+    y_ref[0] = lifted[:, :128]
+    y_ref[1] = lifted[:, 128:]
+
+    @pl.loop(0, live)
+    def _(s):
         for r in range(edge // 8):
             rows = pl.ds(8 * r, 8)
 
             def tile(part, j):
-                at = (part * 2 + j // 8) * 8 * edge + 64 * r + j % 8
-                return y_ref[pl.ds(at, 8, stride=8), :]
+                return y_ref[part, pl.ds(s * block + (j // 8) * 8 * edge + 64 * r + j % 8, 8, stride=8), :]
 
             low = [tile(0, j) for j in range(pairs)]
             high = [tile(1, j) for j in range(pairs)]
@@ -323,36 +331,46 @@
                 for t in range(pairs // 2):
                     a, b = values[2 * t], values[2 * t + 1]
                     at = part * pairs + t
-                    out_ref[0, rows, pl.ds(at * 128, 128)] = jnp.where(front, a, turn(b))
-                    out_ref[0, rows, pl.ds((at + pairs // 2) * 128, 128)] = jnp.where(front, turn(a), b)
+                    o_ref[s, rows, pl.ds(at * 128, 128)] = jnp.where(front, a, turn(b))
+                    o_ref[s, rows, pl.ds((at + pairs // 2) * 128, 128)] = jnp.where(front, turn(a), b)
             if r < half // 8:
                 low, high = lift(*with_halo(low[0::2], low[1::2]), 8, True, False)
                 for i in range(8):
-                    c_ref[pl.ds(i * half + 8 * r, 8), :] = low[i]
-                    c_ref[pl.ds((8 + i) * half + 8 * r, 8), :] = high[i]
+                    c_ref[pl.ds(64 * r + i, 8, stride=8), :] = low[i]
+                    c_ref[pl.ds(corner + 64 * r + i, 8, stride=8), :] = high[i]
         for u in range(2):
-            rows = scaled_rows([c_ref[pl.ds(u * 8 * half + i, 8, stride=half), :] for i in range(half)])
-            store_terms(m_ref, 0, u * 128, rows)
-        lifted = dot(m_ref[...], w2_ref[...])
-        d_ref[pl.ds(0, 8 * half), :] = lifted[:, :128]
-        d_ref[pl.ds(8 * half, 8 * half), :] = lifted[:, 128:]
+            rows = scaled_rows([c_ref[pl.ds(u * corner + 8 * i, 8), :] for i in range(half)])
+            store_terms(m_ref, s * corner, u * 128, rows)
+
+    lifted = dot(m_ref[...], w2_ref[...])
+    d_ref[0] = lifted[:, :128]
+    d_ref[1] = lifted[:, 128:]
+
+    @pl.loop(0, live)
+    def _(s):
         for u in range(2):
             for t in range(4):
                 for r in range(half // 8):
-                    a = d_ref[pl.ds(u * 8 * half + 64 * r + 2 * t, 8, stride=8), :]
-                    b = d_ref[pl.ds(u * 8 * half + 64 * r + 2 * t + 1, 8, stride=8), :]
+                    base = s * corner + 64 * r + 2 * t
+                    a = d_ref[u, pl.ds(base, 8, stride=8), :]
+                    b = d_ref[u, pl.ds(base + 1, 8, stride=8), :]
                     for at, value in (
                         (u * 8 + t, jnp.where(front, a, turn(b))),
                         (u * 8 + 4 + t, jnp.where(front, turn(a), b)),
                     ):
                         rows, cols = pl.ds(8 * r, 8), pl.ds(at * 128, 128)
-                        out_ref[0, rows, cols] = jnp.where(inner, value, out_ref[0, rows, cols])
-
-
-def fine_call(owner_counts, density, first, last, before=None, after=None):
-    slots, edge, plane = density.shape
+                        o_ref[s, rows, cols] = jnp.where(inner, value, o_ref[s, rows, cols])
+        write(s).start()
+
+    for s in range(slots):
+        write(s).wait()
+
+
+def fine_call(owner_counts, token, held, first, last, before=None):
+    slots, edge, tiles, _ = held.shape
     half = edge // 2
-    pairs = plane // 256
+    pairs = tiles // 2
+    count = last - first
     one = pass_matrix(edge).T
     zero = np.zeros_like(one)
     w1 = np.block(
@@ -367,32 +385,33 @@
     two[:half, :half] = pass_matrix(half).T
     w2 = np.kron(np.diag([1 / SCALE, 1 / SCALE, SCALE, SCALE]), two)
     anywhere = pl.BlockSpec(memory_space=pl.ANY)
-    fixed = pl.BlockSpec((768, 256), lambda s: (0, 0))
-    old = [after] if before is None else [before]
+    smem = pl.BlockSpec(memory_space=pltpu.SMEM)
+    vmem = pl.BlockSpec(memory_space=pltpu.VMEM)
+    old = [] if before is None else [before]
     return pl.pallas_call(
-        functools.partial(fine_kernel, offset=first),
-        grid=(last - first,),
-        in_specs=[pl.BlockSpec(memory_space=pltpu.SMEM), anywhere, fixed, fixed] + [anywhere] * len(old),
-        out_specs=pl.BlockSpec((1, edge, plane), lambda s: (s + first, 0, 0)),
-        out_shape=jax.ShapeDtypeStruct(density.shape, F32),
+        functools.partial(fine_kernel, first=first),
+        in_specs=[smem, smem, vmem, vmem, vmem] + [anywhere] * len(old),
+        out_specs=[anywhere, smem],
+        out_shape=[
+            jax.ShapeDtypeStruct((slots, edge, tiles * 128), F32),
+            jax.ShapeDtypeStruct((1,), jnp.int32),
+        ],
         scratch_shapes=[
-            pltpu.VMEM((2, edge, plane // 128, 128), F32),
-            pltpu.VMEM((pairs * edge, 768), BF16),
-            pltpu.VMEM((2 * pairs * edge, 128), F32),
+            pltpu.VMEM((count * pairs * edge, 768), BF16),
+            pltpu.VMEM((2, count * pairs * edge, 128), F32),
             pltpu.VMEM((16 * half, 128), F32),
-            pltpu.VMEM((8 * half, 768), BF16),
-            pltpu.VMEM((16 * half, 128), F32),
-            pltpu.SemaphoreType.DMA((2,)),
-        ],
-        input_output_aliases={} if before is None else {4: 0},
+            pltpu.VMEM((count * 8 * half, 768), BF16),
+            pltpu.VMEM((2, count * 8 * half, 128), F32),
+            pltpu.VMEM((count, edge, tiles * 128), F32),
+            pltpu.SemaphoreType.DMA((count,)),
+        ],
+        input_output_aliases={5: 0} if old else {},
         compiler_params=pltpu.CompilerParams(vmem_limit_bytes=VMEM_LIMIT),
         cost_estimate=pl.CostEstimate(
-            flops=6 * (last - first) * edge * plane * 256,
-            bytes_accessed=2 * (last - first) * MIB,
-            transcendentals=0,
+            flops=6 * count * edge * tiles * 128 * 256, bytes_accessed=2 * count * MIB, transcendentals=0
         ),
         name="fine",
-    )(owner_counts, density, stacked(w1), stacked(w2), *old)
+    )(owner_counts, token, held, stacked(w1), stacked(w2), *old)
 
 
 def coarse_kernel(
@@ -462,14 +481,15 @@
                     else:
                         block_ref[o * 8 + tx + 2 * ty + 4 * tz] = value
     both = times(jnp.concatenate(corner, 0), w23h_ref[...], w23l_ref[...])
-    spot = lax.broadcasted_iota(jnp.int32, (16, 256), 1)
-    depth = lax.broadcasted_iota(jnp.int32, (16, 256), 0)
-    small = (depth < 8) & (spot < 128) & ((spot & 15) < 8)
+    depth = lax.broadcasted_iota(jnp.int32, (16, 128), 0)
+    small = (depth < 8) & ((lane & 15) < 8)
     for o in range(2):
         mine = both[o * 16 : o * 16 + 16]
         second = times_left(wx2_ref[...], mine[:, :256])
         third = times_left(wx3_ref[...], mine[:, 256:])
-        block_ref[o * 8] = jnp.where(small, third, second)
+        block_ref[o * 8] = jnp.concatenate(
+            [jnp.where(small, third, second[:, :128]), second[:, 128:]], 1
+        )
 
     for s in range(slots):
         pltpu.make_async_copy(window(s), corner_ref.at[s], corner_sem.at[s]).wait()
@@ -506,7 +526,7 @@
             wz[cz * 128 : cz * 128 + 128, tz * 128 : tz * 128 + 128] = np.kron(
                 eye8, m32[tz * 16 : tz * 16 + 16, cz * 16 : cz * 16 + 16].T
             )
-    w23 = np.concatenate([np.kron(m16.T, m16.T), np.kron(deep.T, deep.T)], 1)
+    w23 = np.concatenate([np.kron(m16.T, m16.T), np.kron(deep.T, deep.T)[:, :128]], 1)
     weights = [
         left_terms(m32),
         *two_terms(wz),
@@ -529,17 +549,17 @@
             pltpu.SemaphoreType.DMA((slots,)),
         ],
         input_output_aliases={2 + len(weights): 0},
-        compiler_params=pltpu.CompilerParams(vmem_limit_bytes=VMEM_LIMIT),
+        compiler_params=pltpu.CompilerParams(vmem_limit_bytes=VMEM_SMALL),
         name="coarse",
     )(index, pieces.reshape(-1, 128), *weights, fine)
 
 
-def exchange(lowpass, slots, meanwhile):
+def exchange(lowpass, slots, token):
     me = lax.axis_index(AXES)
     devices = lax.axis_size(AXES)
     if devices == lowpass.shape[0]:
         got = lax.all_to_all(lowpass, AXES, 0, 0, tiled=True)
-        sent, index = route_call(me.reshape(1), got, meanwhile, slots)
+        sent, index = route_call(me.reshape(1), got, token, slots)
         return lax.all_to_all(sent, AXES, 0, 0, tiled=True), index
     every = lax.all_gather(lowpass, AXES, axis=0)
     counts = every[:, 0, 7, 0].astype(jnp.int32)
@@ -552,11 +572,12 @@
 
 
 def per_device(density, owner_counts):
-    lowpass = lowpass_call(owner_counts, density)
     slots = density.shape[0]
-    fine = fine_call(owner_counts, density, 0, slots // 2, after=lowpass)
-    pieces, index = exchange(lowpass, slots, fine)
-    fine = fine_call(owner_counts, density, slots // 2, slots, fine)
+    early = slots // 3
+    lowpass, held = lowpass_call(owner_counts, density)
+    fine, token = fine_call(owner_counts, owner_counts, held, 0, early)
+    pieces, index = exchange(lowpass, slots, token)
+    fine, _ = fine_call(owner_counts, index, held, early, slots, fine)
     return coarse_call(index, pieces, fine)
 
 

time: 48.9 us -> 57.4 us (1.17)
  local copies, waits for them, and re-layouts: 1.34 us -> 11.3 us
  waiting for transfers between devices: 1.8 us -> 0.01 us
    unnamed x4 -> x34, local copies, waits for them, and re-layouts: 1.34 us -> 11.3 us
    all_to_all x1, waiting for transfers between devices: 1.8 us -> 0.01 us  [exchange(): return (lax.all_to_all(sent, AXES, 0, 0, tiled=True), index)]
    pallas_call x2, Pallas kernels: 18.3 us -> 19.5 us  [fine_call(): pl.pallas_call(functools.partial(fine_kernel, first=first), in_specs=[sme...]
  transfers between devices with their start and end apart: 2 -> 2, of which waited for: 1 -> 0; matrix products, arithmetic and copies ran while one was open for 0% -> 0% of each run, Pallas kernels for 38% -> 34%
where the time goes in v5:
time: 57.4 us; the launch traced here: 56.9 us
  Pallas kernels  31.5 us (55%)
  starting transfers between devices  13.1 us (23%)
  local copies, waits for them, and re-layouts  11.3 us (20%)
  between operations  0.96 us (2%)
    pallas_call x2, Pallas kernels, fine_call(): pl.pallas_call(functools.partial(fine_kernel, first=first), in_specs=[sme...  19.5 us
    unnamed x34, local copies, waits for them, and re-layouts  11.3 us
    all_to_all x1, starting transfers between devices, exchange(): got = lax.all_to_all(lowpass, AXES, 0, 0, tiled=True)  7.3 us
    all_to_all x1, starting transfers between devices, exchange(): return (lax.all_to_all(sent, AXES, 0, 0, tiled=True), index)  5.84 us
    pallas_call x1, Pallas kernels, lowpass_call(): pl.pallas_call(lowpass_kernel, in_specs=[pl.BlockSpec(memory_space=pltpu....  5.69 us
    pallas_call x1, Pallas kernels, coarse_call(): pl.pallas_call(coarse_kernel, in_specs=[pl.BlockSpec(memory_space=pltpu.S...  3.9 us
    pallas_call x1, Pallas kernels, route_call(): pl.pallas_call(route_kernel, in_specs=[pl.BlockSpec(memory_space=pltpu.SM...  2.44 us
  transfers between devices with their start and end apart: 2, of which 0 were waited for; matrix products, arithmetic and copies ran while one was open for 0% of the time, Pallas kernels for 34%

profile of v5, /device:TPU:0, one launch (start us, length us, event | category | flops | bytes accessed | tf_op | source)
XLA Modules:
  0.0 56.9 jit_solution(15403583282561794240)
XLA Ops:
  0.7 0.0 copy-start.7
  0.7 1.0 %copy-done.7 = bf16[1024,256]{1,0:T(8,128)(2,1)S(1)} copy-done((bf16[1024,256]{1,0:T(8,128)(2,1)S(1)}, bf16[1024,256]{1,0:T(8,128)(2,1)}, u32[]{:S(2)}) %copy-start.7) | copy-done | bytes 524312
  1.8 1.0 %copy-done.8 = bf16[1024,256]{1,0:T(8,128)(2,1)S(1)} copy-done((bf16[1024,256]{1,0:T(8,128)(2,1)S(1)}, bf16[1024,256]{1,0:T(8,128)(2,1)}, u32[]{:S(2)}) %copy-start.8) | copy-done | bytes 524312
  2.8 0.9 %copy-done.9 = bf16[2,256,256]{2,1,0:T(8,128)(2,1)S(1)} copy-done((bf16[2,256,256]{2,1,0:T(8,128)(2,1)S(1)}, bf16[2,256,256]{2,1,0:T(8,128)(2,1)}, u32[]{:S(2)}) %copy-start.9) | copy-done | bytes 262168
  3.8 5.7 %lowpass.1 = (f32[256,128]{1,0:T(8,128)}, f32[6,64,32,128]{3,2,1,0:T(8,128)S(1)}) custom-call(s32[1]{0:T(128)S(6)} %copy.23.count_ref._, f32[6,64,4096]{2,1,0:T(8,128)} %x_any.1, bf16[2,256,256]{2,1,0:T(8,128)(2,1)S(1)} %copy-done.9, bf16[1024,256]{1,0:T(8,128)(2,1)S(1)} %copy-done.7, bf16[1024,256]{1,0:T(8,128)(2,1)S(1)} %copy-done.8), custom_call_target="tpu_custom_call" | custom-call | tf_op jit(solution)/shard_map/lowpass/pallas_call | solution.py:141
  9.5 0.0 copy-start
  9.5 2.7 %copy-done = f32[6,64,32,128]{3,2,1,0:T(8,128)} copy-done((f32[6,64,32,128]{3,2,1,0:T(8,128)}, f32[6,64,32,128]{3,2,1,0:T(8,128)S(1)}, u32[]{:S(2)}) %copy-start) | copy-done | bytes 6291480
  12.1 7.3 %all-to-all-start = ((f32[32,8,128]{2,1,0:T(8,128)}), f32[32,8,128]{2,1,0:T(8,128)S(1)}, u32[]{:S(2)}, u32[]{:S(2)}) async-start(f32[32,8,128]{2,1,0:T(8,128)} %bitcast.1), calls=%async_computation | async-start | bytes 262144 | tf_op jit(solution)/shard_map/all_to_all | solution.py:561
  19.4 0.0 copy-done.3
  19.5 0.0 copy-done.4
  19.5 0.0 copy-start.1
  19.5 2.8 %copy-done.1 = f32[6,64,32,128]{3,2,1,0:T(8,128)S(1)} copy-done((f32[6,64,32,128]{3,2,1,0:T(8,128)S(1)}, f32[6,64,32,128]{3,2,1,0:T(8,128)}, u32[]{:S(2)}) %copy-start.1) | copy-done | bytes 6291480
  22.3 6.9 %fine.2 = (f32[6,64,4096]{2,1,0:T(8,128)}, s32[1]{0:T(128)}) custom-call(s32[1]{0:T(128)S(6)} %copy.23.count_ref._, s32[1]{0:T(128)S(6)} %copy.23.count_ref._, f32[6,64,32,128]{3,2,1,0:T(8,128)S(1)} %copy-done.1, bf16[768,256]{1,0:T(8,128)(2,1)S(1)} %copy-done.3, bf16[768,256]{1,0:T(8,128)(2,1)S(1)} %copy-done.4), custom_call_target="tpu_custom_call" | custom-call | flops 805306368 | bytes 4194304 | tf_op jit(solution)/shard_map/fine/pallas_call | solution.py:391
  29.1 0.0 all-to-all-done.got_any
  29.1 2.4 %route.1 = (f32[32,16,128]{2,1,0:T(8,128)}, s32[2]{0:T(128)S(1)}) custom-call(s32[1]{0:T(128)} %bitcast.me_ref, f32[32,8,128]{2,1,0:T(8,128)S(1)} %all-to-all-done.got_any, s32[1]{0:T(128)} %get-tuple-element.14._), custom_call_target="tpu_custom_call" | custom-call | tf_op jit(solution)/shard_map/route/pallas_call | solution.py:193
  31.6 5.8 %all-to-all-start.1 = ((f32[32,16,128]{2,1,0:T(8,128)}), f32[32,16,128]{2,1,0:T(8,128)S(1)}, u32[]{:S(2)}, u32[]{:S(2)}) async-start(f32[32,16,128]{2,1,0:T(8,128)} %get-tuple-element.16), calls=%async_computation.1 | async-start | bytes 524288 | tf_op jit(solution)/shard_map/all_to_all | solution.py:563
  37.4 0.0 copy-start.2
  37.4 2.8 %copy-done.2 = f32[6,64,32,128]{3,2,1,0:T(8,128)S(1)} copy-done((f32[6,64,32,128]{3,2,1,0:T(8,128)S(1)}, f32[6,64,32,128]{3,2,1,0:T(8,128)}, u32[]{:S(2)}) %copy-start.2) | copy-done | bytes 6291480
  40.2 0.0 copy-start.12
  40.2 0.0 copy-start.13
  40.2 0.0 copy-start.14
  40.3 0.0 copy-start.15
  40.3 0.0 copy-start.16
  40.3 12.7 %fine.3 = (f32[6,64,4096]{2,1,0:T(8,128)}, s32[1]{0:T(128)}) custom-call(s32[1]{0:T(128)S(6)} %copy.23.count_ref._, s32[2]{0:T(128)S(1)} %get-tuple-element.15._.index_ref, f32[6,64,32,128]{3,2,1,0:T(8,128)S(1)} %copy-done.2, bf16[768,256]{1,0:T(8,128)(2,1)S(1)} %copy-done.3, bf16[768,256]{1,0:T(8,128)(2,1)S(1)} %copy-done.4, ...), custom_call_target="tpu_custom_call", output_to_operand_aliasing={{0}: (5, {})} | custom-call | flops 1610612736 | bytes 8388608 | tf_op jit(solution)/shard_map/fine/pallas_call | solution.py:391
  52.9 0.0 all-to-all-done.1
  53.0 0.0 copy-done.5
  53.0 0.0 copy-done.6
  53.0 0.0 copy-done.10
  53.0 0.0 copy-done.11
  53.0 0.0 copy-done.12
  53.0 0.0 copy-done.13
  53.0 3.9 %coarse.1 = f32[6,64,4096]{2,1,0:T(8,128)} custom-call(s32[2]{0:T(128)S(1)} %get-tuple-element.15._.index_ref, f32[512,128]{1,0:T(8,128)S(1)} %bitcast.3, bf16[32,96]{1,0:T(8,128)(2,1)S(1)} %copy-done.14, bf16[256,256]{1,0:T(8,128)(2,1)S(1)} %copy-done.12, bf16[256,256]{1,0:T(8,128)(2,1)S(1)} %copy-done.13, ...), custom_call_target="tpu_custom_call", output_to_operand_aliasing={{}: (11, {})} | custom-call | tf_op jit(solution)/shard_map/coarse/pallas_call | solution.py:540
  (11 shorter events, 0.0 us)
Async XLA Ops:
  0.0 19.4 %copy-start.3 = (bf16[768,256]{1,0:T(8,128)(2,1)S(1)}, bf16[768,256]{1,0:T(8,128)(2,1)}, u32[]{:S(2)}) copy-start(bf16[768,256]{1,0:T(8,128)(2,1)} %constant.42.clone.w1_ref) | copy-start | bytes 1179652
  0.0 19.5 %copy-start.4 = (bf16[768,256]{1,0:T(8,128)(2,1)S(1)}, bf16[768,256]{1,0:T(8,128)(2,1)}, u32[]{:S(2)}) copy-start(bf16[768,256]{1,0:T(8,128)(2,1)} %constant.43.clone.w2_ref) | copy-start | bytes 1179652
  0.7 1.0 %copy-start.7 = (bf16[1024,256]{1,0:T(8,128)(2,1)S(1)}, bf16[1024,256]{1,0:T(8,128)(2,1)}, u32[]{:S(2)}) copy-start(bf16[1024,256]{1,0:T(8,128)(2,1)} %constant.40.clone.wyh_any) | copy-start | bytes 1572868
  1.8 1.0 %copy-start.8 = (bf16[1024,256]{1,0:T(8,128)(2,1)S(1)}, bf16[1024,256]{1,0:T(8,128)(2,1)}, u32[]{:S(2)}) copy-start(bf16[1024,256]{1,0:T(8,128)(2,1)} %constant.41.clone.wyl_any) | copy-start | bytes 1572868
  2.8 0.9 %copy-start.9 = (bf16[2,256,256]{2,1,0:T(8,128)(2,1)S(1)}, bf16[2,256,256]{2,1,0:T(8,128)(2,1)}, u32[]{:S(2)}) copy-start(bf16[2,256,256]{2,1,0:T(8,128)(2,1)} %constant.39.clone.wz_any) | copy-start | bytes 786436
  9.5 2.7 %copy-start = (f32[6,64,32,128]{3,2,1,0:T(8,128)}, f32[6,64,32,128]{3,2,1,0:T(8,128)S(1)}, u32[]{:S(2)}) copy-start(f32[6,64,32,128]{3,2,1,0:T(8,128)S(1)} %get-tuple-element.13.x_ref) | copy-start | bytes 18874372
  12.1 17.0 %all-to-all-start = ((f32[32,8,128]{2,1,0:T(8,128)}), f32[32,8,128]{2,1,0:T(8,128)S(1)}, u32[]{:S(2)}, u32[]{:S(2)}) async-start(f32[32,8,128]{2,1,0:T(8,128)} %bitcast.1), calls=%async_computation | async-start | bytes 262144 | tf_op jit(solution)/shard_map/all_to_all | solution.py:561
  19.5 2.8 %copy-start.1 = (f32[6,64,32,128]{3,2,1,0:T(8,128)S(1)}, f32[6,64,32,128]{3,2,1,0:T(8,128)}, u32[]{:S(2)}) copy-start(f32[6,64,32,128]{3,2,1,0:T(8,128)} %copy-done) | copy-start | bytes 18874372
  31.6 21.4 %all-to-all-start.1 = ((f32[32,16,128]{2,1,0:T(8,128)}), f32[32,16,128]{2,1,0:T(8,128)S(1)}, u32[]{:S(2)}, u32[]{:S(2)}) async-start(f32[32,16,128]{2,1,0:T(8,128)} %get-tuple-element.16), calls=%async_computation.1 | async-start | bytes 524288 | tf_op jit(solution)/shard_map/all_to_all | solution.py:563
  37.4 2.8 %copy-start.2 = (f32[6,64,32,128]{3,2,1,0:T(8,128)S(1)}, f32[6,64,32,128]{3,2,1,0:T(8,128)}, u32[]{:S(2)}) copy-start(f32[6,64,32,128]{3,2,1,0:T(8,128)} %copy-done) | copy-start | bytes 18874372
  40.2 12.8 %copy-start.5 = (bf16[512,512]{1,0:T(8,128)(2,1)S(1)}, bf16[512,512]{1,0:T(8,128)(2,1)}, u32[]{:S(2)}) copy-start(bf16[512,512]{1,0:T(8,128)(2,1)} %constant.47.clone.wyh_ref) | copy-start | bytes 1572868
  40.2 12.8 %copy-start.6 = (bf16[512,512]{1,0:T(8,128)(2,1)S(1)}, bf16[512,512]{1,0:T(8,128)(2,1)}, u32[]{:S(2)}) copy-start(bf16[512,512]{1,0:T(8,128)(2,1)} %constant.48.clone.wyl_ref) | copy-start | bytes 1572868
  40.2 12.8 %copy-start.10 = (bf16[256,384]{1,0:T(8,128)(2,1)S(1)}, bf16[256,384]{1,0:T(8,128)(2,1)}, u32[]{:S(2)}) copy-start(bf16[256,384]{1,0:T(8,128)(2,1)} %constant.49.clone.w23h_ref) | copy-start | bytes 589828
  40.2 12.8 %copy-start.11 = (bf16[256,384]{1,0:T(8,128)(2,1)S(1)}, bf16[256,384]{1,0:T(8,128)(2,1)}, u32[]{:S(2)}) copy-start(bf16[256,384]{1,0:T(8,128)(2,1)} %constant.50.clone.w23l_ref) | copy-start | bytes 589828
  40.2 12.8 %copy-start.12 = (bf16[256,256]{1,0:T(8,128)(2,1)S(1)}, bf16[256,256]{1,0:T(8,128)(2,1)}, u32[]{:S(2)}) copy-start(bf16[256,256]{1,0:T(8,128)(2,1)} %constant.45.clone.wzh_ref) | copy-start | bytes 393220
  40.2 12.8 %copy-start.13 = (bf16[256,256]{1,0:T(8,128)(2,1)S(1)}, bf16[256,256]{1,0:T(8,128)(2,1)}, u32[]{:S(2)}) copy-start(bf16[256,256]{1,0:T(8,128)(2,1)} %constant.46.clone.wzl_ref) | copy-start | bytes 393220
  40.2 12.8 %copy-start.14 = (bf16[32,96]{1,0:T(8,128)(2,1)S(1)}, bf16[32,96]{1,0:T(8,128)(2,1)}, u32[]{:S(2)}) copy-start(bf16[32,96]{1,0:T(8,128)(2,1)} %constant.44.clone.wx_ref) | copy-start | bytes 18436
  40.3 12.8 %copy-start.15 = (bf16[16,48]{1,0:T(8,128)(2,1)S(1)}, bf16[16,48]{1,0:T(8,128)(2,1)}, u32[]{:S(2)}) copy-start(bf16[16,48]{1,0:T(8,128)(2,1)} %constant.51.clone.wx2_ref) | copy-start | bytes 4612
  40.3 12.8 %copy-start.16 = (bf16[16,48]{1,0:T(8,128)(2,1)S(1)}, bf16[16,48]{1,0:T(8,128)(2,1)}, u32[]{:S(2)}) copy-start(bf16[16,48]{1,0:T(8,128)(2,1)} %constant.52.clone.wx3_ref) | copy-start | bytes 4612

commit v6 on v5

--- a/solution.py
+++ b/solution.py
@@ -18,9 +18,9 @@
 BF16 = jnp.bfloat16
 AXES = ("node", "dev")
 MIB = 1 << 20
-VMEM_LIMIT = 40 * MIB
+VMEM_LIMIT = 48 * MIB
 VMEM_SMALL = 16 * MIB
-VMEM_LARGE = 45 * MIB
+VMEM_LARGE = 56 * MIB
 
 
 def pass_matrix(n):
@@ -75,16 +75,26 @@
     return [split(jnp.concatenate(rows[m : m + 2], 0)) for m in range(0, len(rows), 2)]
 
 
+def start_tiles(src_ref, dst_ref, sems):
+    for t in range(dst_ref.shape[2]):
+        pltpu.make_async_copy(
+            src_ref.at[:, :, pl.ds(t * 128, 128)], dst_ref.at[:, :, t, :], sems.at[t // 8]
+        ).start()
+
+
+def wait_tiles(dst_ref, sems, group):
+    part = dst_ref.at[:, :, pl.ds(8 * group, 8), :]
+    pltpu.make_async_copy(part, part, sems.at[group]).wait()
+
+
 def lowpass_kernel(
-    count_ref, x_any, wz_any, wyh_any, wyl_any, out_ref, x_ref, wz_ref, wyh_ref, wyl_ref, l_ref, z_ref, sems, w_sems
+    count_ref, x_any, wz_any, wyh_any, wyl_any, out_ref, token_ref, x_ref, wz_ref, wyh_ref, wyl_ref, l_ref, z_ref, sems, w_sems
 ):
     slots, edge = x_any.shape[:2]
     quarter = edge // 4
     rows_all = slots * 8 * quarter
-    for t in range(x_ref.shape[2]):
-        pltpu.make_async_copy(
-            x_any.at[:, :, pl.ds(t * 128, 128)], x_ref.at[:, :, t, :], sems.at[t // 8]
-        ).start()
+    token_ref[0] = count_ref[0]
+    start_tiles(x_any, x_ref, sems)
     weights = [
         pltpu.make_async_copy(src, dst, w_sems.at[i])
         for i, (src, dst) in enumerate(((wz_any, wz_ref), (wyh_any, wyh_ref), (wyl_any, wyl_ref)))
@@ -92,8 +102,7 @@
     for copy in weights:
         copy.start()
     for g in range(4):
-        part = x_ref.at[:, :, pl.ds(8 * g, 8), :]
-        pltpu.make_async_copy(part, part, sems.at[g]).wait()
+        wait_tiles(x_ref, sems, g)
 
         @pl.loop(0, slots)
         def _(s):
@@ -138,15 +147,16 @@
     anywhere = pl.BlockSpec(memory_space=pl.ANY)
     vmem = pl.BlockSpec(memory_space=pltpu.VMEM)
     rows_all = slots * 8 * quarter
-    pieces, held = pl.pallas_call(
+    pieces, token = pl.pallas_call(
         lowpass_kernel,
         in_specs=[pl.BlockSpec(memory_space=pltpu.SMEM)] + [anywhere] * 4,
-        out_specs=[vmem, vmem],
+        out_specs=[vmem, pl.BlockSpec(memory_space=pltpu.SMEM)],
         out_shape=[
             jax.ShapeDtypeStruct((16 * quarter, 128), F32),
-            jax.ShapeDtypeStruct((slots, edge, plane // 128, 128), F32),
+            jax.ShapeDtypeStruct((1,), jnp.int32),
         ],
         scratch_shapes=[
+            pltpu.VMEM((slots, edge, plane // 128, 128), F32),
             pltpu.VMEM(wz.shape, BF16),
             pltpu.VMEM(wyh.shape, BF16),
             pltpu.VMEM(wyl.shape, BF16),
@@ -158,7 +168,7 @@
         compiler_params=pltpu.CompilerParams(vmem_limit_bytes=VMEM_LARGE),
         name="lowpass",
     )(owner_counts, density, wz, wyh, wyl)
-    return pieces.reshape(2 * quarter, 8, 128), held
+    return pieces.reshape(2 * quarter, 8, 128), token
 
 
 def route_kernel(me_ref, got_any, _, send_ref, index_ref, got_ref, order_ref, count_ref, sems):
@@ -259,8 +269,8 @@
     return [fourth[i] for i in range(n)], [third[i] for i in range(n)]
 
 
-def fine_kernel(count_ref, _, x_ref, w1_ref, w2_ref, *refs, first):
-    out_ref, token_ref, l_ref, y_ref, c_ref, m_ref, d_ref, o_ref, sems = refs[-9:]
+def fine_kernel(count_ref, _, x_any, w1_ref, w2_ref, *refs, first):
+    out_ref, token_ref, x_ref, l_ref, y_ref, c_ref, m_ref, d_ref, o_ref, x_sems, sems = refs[-11:]
     slots, edge = o_ref.shape[:2]
     tiles = x_ref.shape[2]
     pairs = tiles // 2
@@ -272,6 +282,7 @@
     front = lane < 64
     inner = (lane & 63) < half
     token_ref[0] = live
+    start_tiles(x_any.at[pl.ds(first, slots)], x_ref, x_sems)
 
     def turn(value):
         return pltpu.roll(value, 64, 1)
@@ -306,10 +317,12 @@
         o_ref[s] = jnp.zeros(o_ref.shape[1:], F32)
         write(s).start()
 
-    @pl.loop(0, live)
-    def _(s):
-        for g in range(4):
-            rows = scaled_rows([x_ref[first + s, i, pl.ds(8 * g, 8), :] for i in range(edge)])
+    for g in range(4):
+        wait_tiles(x_ref, x_sems, g)
+
+        @pl.loop(0, live)
+        def _(s):
+            rows = scaled_rows([x_ref[s, i, pl.ds(8 * g, 8), :] for i in range(edge)])
             store_terms(l_ref, s * block + (g % 2) * 8 * edge, (g // 2) * 128, rows)
 
     lifted = dot(l_ref[...], w1_ref[...])
@@ -366,8 +379,9 @@
         write(s).wait()
 
 
-def fine_call(owner_counts, token, held, first, last, before=None):
-    slots, edge, tiles, _ = held.shape
+def fine_call(owner_counts, token, density, first, last, before=None):
+    slots, edge, plane = density.shape
+    tiles = plane // 128
     half = edge // 2
     pairs = tiles // 2
     count = last - first
@@ -390,19 +404,21 @@
     old = [] if before is None else [before]
     return pl.pallas_call(
         functools.partial(fine_kernel, first=first),
-        in_specs=[smem, smem, vmem, vmem, vmem] + [anywhere] * len(old),
+        in_specs=[smem, smem, anywhere, vmem, vmem] + [anywhere] * len(old),
         out_specs=[anywhere, smem],
         out_shape=[
-            jax.ShapeDtypeStruct((slots, edge, tiles * 128), F32),
+            jax.ShapeDtypeStruct(density.shape, F32),
             jax.ShapeDtypeStruct((1,), jnp.int32),
         ],
         scratch_shapes=[
+            pltpu.VMEM((count, edge, tiles, 128), F32),
             pltpu.VMEM((count * pairs * edge, 768), BF16),
             pltpu.VMEM((2, count * pairs * edge, 128), F32),
             pltpu.VMEM((16 * half, 128), F32),
             pltpu.VMEM((count * 8 * half, 768), BF16),
             pltpu.VMEM((2, count * 8 * half, 128), F32),
             pltpu.VMEM((count, edge, tiles * 128), F32),
+            pltpu.SemaphoreType.DMA((4,)),
             pltpu.SemaphoreType.DMA((count,)),
         ],
         input_output_aliases={5: 0} if old else {},
@@ -411,7 +427,7 @@
             flops=6 * count * edge * tiles * 128 * 256, bytes_accessed=2 * count * MIB, transcendentals=0
         ),
         name="fine",
-    )(owner_counts, token, held, stacked(w1), stacked(w2), *old)
+    )(owner_counts, token, density, stacked(w1), stacked(w2), *old)
 
 
 def coarse_kernel(
@@ -574,10 +590,10 @@
 def per_device(density, owner_counts):
     slots = density.shape[0]
     early = slots // 3
-    lowpass, held = lowpass_call(owner_counts, density)
-    fine, token = fine_call(owner_counts, owner_counts, held, 0, early)
+    lowpass, token = lowpass_call(owner_counts, density)
+    fine, token = fine_call(owner_counts, token, density, 0, early)
     pieces, index = exchange(lowpass, slots, token)
-    fine, _ = fine_call(owner_counts, index, held, early, slots, fine)
+    fine, _ = fine_call(owner_counts, index, density, early, slots, fine)
     return coarse_call(index, pieces, fine)
 
 

time: 57.4 us -> 49.1 us (0.86)
  local copies, waits for them, and re-layouts: 11.3 us -> 0.07 us
  Pallas kernels: 31.5 us -> 34.6 us
    unnamed x34 -> x22, local copies, waits for them, and re-layouts: 11.3 us -> 0.07 us
    pallas_call x2, Pallas kernels: 19.5 us -> 22.6 us  [fine_call(): pl.pallas_call(functools.partial(fine_kernel, first=first), in_specs=[sme...]
  transfers between devices with their start and end apart: 2 -> 2, of which waited for: 0 -> 0; matrix products, arithmetic and copies ran while one was open for 0% -> 0% of each run, Pallas kernels for 34% -> 46%
where the time goes in v6:
time: 49.1 us; the launch traced here: 48.8 us
  Pallas kernels  34.6 us (70%)
  starting transfers between devices  13.1 us (27%)
  between operations  0.95 us (2%)
    pallas_call x2, Pallas kernels, fine_call(): pl.pallas_call(functools.partial(fine_kernel, first=first), in_specs=[sme...  22.6 us
    all_to_all x1, starting transfers between devices, exchange(): got = lax.all_to_all(lowpass, AXES, 0, 0, tiled=True)  7.3 us
    all_to_all x1, starting transfers between devices, exchange(): return (lax.all_to_all(sent, AXES, 0, 0, tiled=True), index)  5.84 us
    pallas_call x1, Pallas kernels, lowpass_call(): pl.pallas_call(lowpass_kernel, in_specs=[pl.BlockSpec(memory_space=pltpu....  5.73 us
    pallas_call x1, Pallas kernels, coarse_call(): pl.pallas_call(coarse_kernel, in_specs=[pl.BlockSpec(memory_space=pltpu.S...  3.9 us
    pallas_call x1, Pallas kernels, route_call(): pl.pallas_call(route_kernel, in_specs=[pl.BlockSpec(memory_space=pltpu.SM...  2.37 us
  transfers between devices with their start and end apart: 2, of which 0 were waited for; matrix products, arithmetic and copies ran while one was open for 0% of the time, Pallas kernels for 46%

profile of v6, /device:TPU:0, one launch (start us, length us, event | category | flops | bytes accessed | tf_op | source)
XLA Modules:
  0.0 48.8 jit_solution(9234331143014636454)
XLA Ops:
  0.0 0.0 copy-start
  0.0 0.0 copy-start.1
  0.7 5.7 %lowpass.1 = (f32[256,128]{1,0:T(8,128)}, s32[1]{0:T(128)}) custom-call(s32[1]{0:T(128)S(6)} %copy.23.count_ref, f32[6,64,4096]{2,1,0:T(8,128)} %x_any.5, bf16[2,256,256]{2,1,0:T(8,128)(2,1)} %constant.39.clone.wz_any, bf16[1024,256]{1,0:T(8,128)(2,1)} %constant.40.clone.wyh_any, bf16[1024,256]{1,0:T(8,128)(2,1)} %constant.41.clone.wyl_any), custom_call_target="tpu_custom_call" | custom-call | tf_op jit(solution)/shard_map/lowpass/pallas_call | solution.py:150
  6.5 7.3 %all-to-all-start = ((f32[32,8,128]{2,1,0:T(8,128)}), f32[32,8,128]{2,1,0:T(8,128)S(1)}, u32[]{:S(2)}, u32[]{:S(2)}) async-start(f32[32,8,128]{2,1,0:T(8,128)} %bitcast.4), calls=%async_computation | async-start | bytes 262144 | tf_op jit(solution)/shard_map/all_to_all | solution.py:577
  13.8 0.0 copy-done
  13.8 0.0 copy-done.1
  13.8 8.6 %fine.2 = (f32[6,64,4096]{2,1,0:T(8,128)}, s32[1]{0:T(128)}) custom-call(s32[1]{0:T(128)S(6)} %copy.23.count_ref, s32[1]{0:T(128)} %get-tuple-element.13._, f32[6,64,4096]{2,1,0:T(8,128)} %x_any.5, bf16[768,256]{1,0:T(8,128)(2,1)S(1)} %copy-done.1, bf16[768,256]{1,0:T(8,128)(2,1)S(1)} %copy-done), custom_call_target="tpu_custom_call" | custom-call | flops 805306368 | bytes 4194304 | tf_op jit(solution)/shard_map/fine/pallas_call | solution.py:405
  22.4 0.0 all-to-all-done.got_any
  22.4 2.4 %route.1 = (f32[32,16,128]{2,1,0:T(8,128)}, s32[2]{0:T(128)S(1)}) custom-call(s32[1]{0:T(128)} %bitcast.me_ref, f32[32,8,128]{2,1,0:T(8,128)S(1)} %all-to-all-done.got_any, s32[1]{0:T(128)} %get-tuple-element.14._), custom_call_target="tpu_custom_call" | custom-call | tf_op jit(solution)/shard_map/route/pallas_call | solution.py:203
  24.8 5.8 %all-to-all-start.1 = ((f32[32,16,128]{2,1,0:T(8,128)}), f32[32,16,128]{2,1,0:T(8,128)S(1)}, u32[]{:S(2)}, u32[]{:S(2)}) async-start(f32[32,16,128]{2,1,0:T(8,128)} %get-tuple-element.16), calls=%async_computation.1 | async-start | bytes 524288 | tf_op jit(solution)/shard_map/all_to_all | solution.py:579
  30.6 0.0 copy-start.2
  30.6 0.0 copy-start.3
  30.6 0.0 copy-start.4
  30.6 0.0 copy-start.5
  30.7 0.0 copy-start.6
  30.7 0.0 copy-start.7
  30.7 0.0 copy-start.8
  30.7 0.0 copy-start.9
  30.7 0.0 copy-start.10
  30.7 14.1 %fine.3 = (f32[6,64,4096]{2,1,0:T(8,128)}, s32[1]{0:T(128)}) custom-call(s32[1]{0:T(128)S(6)} %copy.23.count_ref, s32[2]{0:T(128)S(1)} %get-tuple-element.15._.index_ref, f32[6,64,4096]{2,1,0:T(8,128)} %x_any.5, bf16[768,256]{1,0:T(8,128)(2,1)S(1)} %copy-done.1, bf16[768,256]{1,0:T(8,128)(2,1)S(1)} %copy-done, ...), custom_call_target="tpu_custom_call", output_to_operand_aliasing={{0}: (5, {})} | custom-call | flops 1610612736 | bytes 8388608 | tf_op jit(solution)/shard_map/fine/pallas_call | solution.py:405
  44.8 0.0 all-to-all-done.1
  44.8 0.0 copy-done.2
  44.8 0.0 copy-done.3
  44.8 0.0 copy-done.4
  44.8 0.0 copy-done.5
  44.8 0.0 copy-done.6
  44.8 0.0 copy-done.7
  44.9 0.0 copy-done.8
  44.9 0.0 copy-done.9
  44.9 0.0 copy-done.10
  44.9 3.9 %coarse.1 = f32[6,64,4096]{2,1,0:T(8,128)} custom-call(s32[2]{0:T(128)S(1)} %get-tuple-element.15._.index_ref, f32[512,128]{1,0:T(8,128)S(1)} %bitcast.3, bf16[32,96]{1,0:T(8,128)(2,1)S(1)} %copy-done.8, bf16[256,256]{1,0:T(8,128)(2,1)S(1)} %copy-done.7, bf16[256,256]{1,0:T(8,128)(2,1)S(1)} %copy-done.6, ...), custom_call_target="tpu_custom_call", output_to_operand_aliasing={{}: (11, {})} | custom-call | tf_op jit(solution)/shard_map/coarse/pallas_call | solution.py:556
Async XLA Ops:
  0.0 13.8 %copy-start = (bf16[768,256]{1,0:T(8,128)(2,1)S(1)}, bf16[768,256]{1,0:T(8,128)(2,1)}, u32[]{:S(2)}) copy-start(bf16[768,256]{1,0:T(8,128)(2,1)} %constant.43.clone.w2_ref) | copy-start | bytes 1179652
  0.0 13.8 %copy-start.1 = (bf16[768,256]{1,0:T(8,128)(2,1)S(1)}, bf16[768,256]{1,0:T(8,128)(2,1)}, u32[]{:S(2)}) copy-start(bf16[768,256]{1,0:T(8,128)(2,1)} %constant.42.clone.w1_ref) | copy-start | bytes 1179652
  6.5 15.9 %all-to-all-start = ((f32[32,8,128]{2,1,0:T(8,128)}), f32[32,8,128]{2,1,0:T(8,128)S(1)}, u32[]{:S(2)}, u32[]{:S(2)}) async-start(f32[32,8,128]{2,1,0:T(8,128)} %bitcast.4), calls=%async_computation | async-start | bytes 262144 | tf_op jit(solution)/shard_map/all_to_all | solution.py:577
  24.8 20.0 %all-to-all-start.1 = ((f32[32,16,128]{2,1,0:T(8,128)}), f32[32,16,128]{2,1,0:T(8,128)S(1)}, u32[]{:S(2)}, u32[]{:S(2)}) async-start(f32[32,16,128]{2,1,0:T(8,128)} %get-tuple-element.16), calls=%async_computation.1 | async-start | bytes 524288 | tf_op jit(solution)/shard_map/all_to_all | solution.py:579
  30.6 14.2 %copy-start.2 = (bf16[512,512]{1,0:T(8,128)(2,1)S(1)}, bf16[512,512]{1,0:T(8,128)(2,1)}, u32[]{:S(2)}) copy-start(bf16[512,512]{1,0:T(8,128)(2,1)} %constant.48.clone.wyl_ref) | copy-start | bytes 1572868
  30.6 14.2 %copy-start.3 = (bf16[512,512]{1,0:T(8,128)(2,1)S(1)}, bf16[512,512]{1,0:T(8,128)(2,1)}, u32[]{:S(2)}) copy-start(bf16[512,512]{1,0:T(8,128)(2,1)} %constant.47.clone.wyh_ref) | copy-start | bytes 1572868
  30.6 14.2 %copy-start.4 = (bf16[256,384]{1,0:T(8,128)(2,1)S(1)}, bf16[256,384]{1,0:T(8,128)(2,1)}, u32[]{:S(2)}) copy-start(bf16[256,384]{1,0:T(8,128)(2,1)} %constant.50.clone.w23l_ref) | copy-start | bytes 589828
  30.6 14.2 %copy-start.5 = (bf16[256,384]{1,0:T(8,128)(2,1)S(1)}, bf16[256,384]{1,0:T(8,128)(2,1)}, u32[]{:S(2)}) copy-start(bf16[256,384]{1,0:T(8,128)(2,1)} %constant.49.clone.w23h_ref) | copy-start | bytes 589828
  30.7 14.2 %copy-start.6 = (bf16[256,256]{1,0:T(8,128)(2,1)S(1)}, bf16[256,256]{1,0:T(8,128)(2,1)}, u32[]{:S(2)}) copy-start(bf16[256,256]{1,0:T(8,128)(2,1)} %constant.46.clone.wzl_ref) | copy-start | bytes 393220
  30.7 14.2 %copy-start.7 = (bf16[256,256]{1,0:T(8,128)(2,1)S(1)}, bf16[256,256]{1,0:T(8,128)(2,1)}, u32[]{:S(2)}) copy-start(bf16[256,256]{1,0:T(8,128)(2,1)} %constant.45.clone.wzh_ref) | copy-start | bytes 393220
  30.7 14.2 %copy-start.8 = (bf16[32,96]{1,0:T(8,128)(2,1)S(1)}, bf16[32,96]{1,0:T(8,128)(2,1)}, u32[]{:S(2)}) copy-start(bf16[32,96]{1,0:T(8,128)(2,1)} %constant.44.clone.wx_ref) | copy-start | bytes 18436
  30.7 14.2 %copy-start.9 = (bf16[16,48]{1,0:T(8,128)(2,1)S(1)}, bf16[16,48]{1,0:T(8,128)(2,1)}, u32[]{:S(2)}) copy-start(bf16[16,48]{1,0:T(8,128)(2,1)} %constant.52.clone.wx3_ref) | copy-start | bytes 4612
  30.7 14.2 %copy-start.10 = (bf16[16,48]{1,0:T(8,128)(2,1)S(1)}, bf16[16,48]{1,0:T(8,128)(2,1)}, u32[]{:S(2)}) copy-start(bf16[16,48]{1,0:T(8,128)(2,1)} %constant.51.clone.wx2_ref) | copy-start | bytes 4612

commit v7 on v6

--- a/solution.py
+++ b/solution.py
@@ -75,16 +75,31 @@
     return [split(jnp.concatenate(rows[m : m + 2], 0)) for m in range(0, len(rows), 2)]
 
 
+def tile_buffer(tiles, slots, edge):
+    return pltpu.VMEM((tiles, slots | 1, edge + 8, 128), F32)
+
+
 def start_tiles(src_ref, dst_ref, sems):
-    for t in range(dst_ref.shape[2]):
+    slots, edge = src_ref.shape[:2]
+    for t in range(dst_ref.shape[0]):
         pltpu.make_async_copy(
-            src_ref.at[:, :, pl.ds(t * 128, 128)], dst_ref.at[:, :, t, :], sems.at[t // 8]
+            src_ref.at[:, :, pl.ds(t * 128, 128)],
+            dst_ref.at[t, pl.ds(0, slots), pl.ds(0, edge), :],
+            sems.at[t // 8],
         ).start()
 
 
-def wait_tiles(dst_ref, sems, group):
-    part = dst_ref.at[:, :, pl.ds(8 * group, 8), :]
+def wait_tiles(src_ref, dst_ref, sems, group):
+    slots, edge = src_ref.shape[:2]
+    part = dst_ref.at[pl.ds(8 * group, 8), pl.ds(0, slots), pl.ds(0, edge), :]
     pltpu.make_async_copy(part, part, sems.at[group]).wait()
+
+
+def tile_rows(ref, slot, group, edge):
+    tiles, slots, pitch, lanes = ref.shape
+    flat = ref.reshape(tiles * slots * pitch, lanes)
+    base = 8 * group * slots * pitch + slot * pitch
+    return [flat[pl.ds(base + x, 8, stride=slots * pitch), :] for x in range(edge)]
 
 
 def lowpass_kernel(
@@ -102,11 +117,11 @@
     for copy in weights:
         copy.start()
     for g in range(4):
-        wait_tiles(x_ref, sems, g)
+        wait_tiles(x_any, x_ref, sems, g)
 
         @pl.loop(0, slots)
         def _(s):
-            rows = [x_ref[s, x, pl.ds(8 * g, 8), :] for x in range(edge)]
+            rows = tile_rows(x_ref, s, g, edge)
             rows, _ = lift(rows[0::2], rows[1::2], edge // 2, False, False)
             rows, _ = lift(rows[0::2], rows[1::2], quarter, False, False)
             for m, (high, low) in enumerate(split_rows(rows)):
@@ -156,7 +171,7 @@
             jax.ShapeDtypeStruct((1,), jnp.int32),
         ],
         scratch_shapes=[
-            pltpu.VMEM((slots, edge, plane // 128, 128), F32),
+            tile_buffer(plane // 128, slots, edge),
             pltpu.VMEM(wz.shape, BF16),
             pltpu.VMEM(wyh.shape, BF16),
             pltpu.VMEM(wyl.shape, BF16),
@@ -171,17 +186,12 @@
     return pieces.reshape(2 * quarter, 8, 128), token
 
 
-def route_kernel(me_ref, got_any, _, send_ref, index_ref, got_ref, order_ref, count_ref, sems):
+def route_kernel(me_ref, got_ref, _, send_ref, index_ref, order_ref, count_ref, sem):
     devices = got_ref.shape[0]
-    copies = [
-        pltpu.make_async_copy(got_any.at[:, 7, :], count_ref, sems.at[0]),
-        pltpu.make_async_copy(got_any, got_ref, sems.at[1]),
-    ]
-    for copy in copies:
-        copy.start()
+    copy = pltpu.make_async_copy(got_ref.at[:, 7, :], count_ref, sem)
+    copy.start()
     order_ref[...] = jnp.zeros_like(order_ref)
-    for copy in copies:
-        copy.wait()
+    copy.wait()
     start, my_start, my_count = 0, 0, 0
     starts = []
     for d in range(devices):
@@ -204,7 +214,7 @@
         route_kernel,
         in_specs=[
             pl.BlockSpec(memory_space=pltpu.SMEM),
-            pl.BlockSpec(memory_space=pl.ANY),
+            pl.BlockSpec(memory_space=pltpu.VMEM),
             pl.BlockSpec(memory_space=pltpu.SMEM),
         ],
         out_specs=[pl.BlockSpec(memory_space=pltpu.VMEM), pl.BlockSpec(memory_space=pltpu.SMEM)],
@@ -213,10 +223,9 @@
             jax.ShapeDtypeStruct((2,), jnp.int32),
         ],
         scratch_shapes=[
-            pltpu.VMEM(got.shape, F32),
             pltpu.VMEM((devices * slots + 16, 128), F32),
             pltpu.SMEM((devices, 128), F32),
-            pltpu.SemaphoreType.DMA((2,)),
+            pltpu.SemaphoreType.DMA,
         ],
         compiler_params=pltpu.CompilerParams(vmem_limit_bytes=VMEM_SMALL),
         name="route",
@@ -272,7 +281,7 @@
 def fine_kernel(count_ref, _, x_any, w1_ref, w2_ref, *refs, first):
     out_ref, token_ref, x_ref, l_ref, y_ref, c_ref, m_ref, d_ref, o_ref, x_sems, sems = refs[-11:]
     slots, edge = o_ref.shape[:2]
-    tiles = x_ref.shape[2]
+    tiles = x_ref.shape[0]
     pairs = tiles // 2
     half = edge // 2
     block = pairs * edge
@@ -282,21 +291,23 @@
     front = lane < 64
     inner = (lane & 63) < half
     token_ref[0] = live
-    start_tiles(x_any.at[pl.ds(first, slots)], x_ref, x_sems)
-
-    def turn(value):
-        return pltpu.roll(value, 64, 1)
+    x_any = x_any.at[pl.ds(first, slots)]
+    start_tiles(x_any, x_ref, x_sems)
+
+    def cross(a, b):
+        return pltpu.roll(jnp.where(front, b, a), 64, 1)
+
+    def exchange(a, b):
+        crossed = cross(a, b)
+        return jnp.where(front, a, crossed), jnp.where(front, crossed, b)
 
     def with_halo(low, high):
-        def left(values, i):
-            return jnp.where(front, values[i[0]], turn(values[i[1]]))
-
-        def right(values, i):
-            return jnp.where(front, turn(values[i[0]]), values[i[1]])
-
-        low_all = [left(low, (2, -2)), left(low, (1, -1))] + low + [right(low, (0, -1)), right(low, (1, -2))]
-        high_all = [left(high, (1, -2)), left(high, (0, -1))] + high + [right(high, (0, -2))]
-        return low_all, high_all
+        one, two = cross(low[0], low[-1]), cross(low[1], low[-2])
+        low_all = [jnp.where(front, low[2], two), jnp.where(front, low[1], one)] + low
+        low_all += [jnp.where(front, one, low[-1]), jnp.where(front, two, low[-2])]
+        one, two = cross(high[0], high[-1]), cross(high[1], high[-2])
+        high_all = [jnp.where(front, high[1], two), jnp.where(front, high[0], one)] + high
+        return low_all, high_all + [jnp.where(front, one, high[-2])]
 
     def scaled_rows(rows):
         low, high = lift(rows[0::2], rows[1::2], len(rows) // 2, False, False)
@@ -318,11 +329,11 @@
         write(s).start()
 
     for g in range(4):
-        wait_tiles(x_ref, x_sems, g)
+        wait_tiles(x_any, x_ref, x_sems, g)
 
         @pl.loop(0, live)
         def _(s):
-            rows = scaled_rows([x_ref[s, i, pl.ds(8 * g, 8), :] for i in range(edge)])
+            rows = scaled_rows(tile_rows(x_ref, s, g, edge))
             store_terms(l_ref, s * block + (g % 2) * 8 * edge, (g // 2) * 128, rows)
 
     lifted = dot(l_ref[...], w1_ref[...])
@@ -342,10 +353,10 @@
             low, high = lift(*with_halo(low, high), pairs, True, True)
             for part, values in enumerate((low, high)):
                 for t in range(pairs // 2):
-                    a, b = values[2 * t], values[2 * t + 1]
+                    a, b = exchange(values[2 * t], values[2 * t + 1])
                     at = part * pairs + t
-                    o_ref[s, rows, pl.ds(at * 128, 128)] = jnp.where(front, a, turn(b))
-                    o_ref[s, rows, pl.ds((at + pairs // 2) * 128, 128)] = jnp.where(front, turn(a), b)
+                    o_ref[s, rows, pl.ds(at * 128, 128)] = a
+                    o_ref[s, rows, pl.ds((at + pairs // 2) * 128, 128)] = b
             if r < half // 8:
                 low, high = lift(*with_halo(low[0::2], low[1::2]), 8, True, False)
                 for i in range(8):
@@ -367,10 +378,7 @@
                     base = s * corner + 64 * r + 2 * t
                     a = d_ref[u, pl.ds(base, 8, stride=8), :]
                     b = d_ref[u, pl.ds(base + 1, 8, stride=8), :]
-                    for at, value in (
-                        (u * 8 + t, jnp.where(front, a, turn(b))),
-                        (u * 8 + 4 + t, jnp.where(front, turn(a), b)),
-                    ):
+                    for at, value in zip((u * 8 + t, u * 8 + 4 + t), exchange(a, b)):
                         rows, cols = pl.ds(8 * r, 8), pl.ds(at * 128, 128)
                         o_ref[s, rows, cols] = jnp.where(inner, value, o_ref[s, rows, cols])
         write(s).start()
@@ -411,7 +419,7 @@
             jax.ShapeDtypeStruct((1,), jnp.int32),
         ],
         scratch_shapes=[
-            pltpu.VMEM((count, edge, tiles, 128), F32),
+            tile_buffer(tiles, count, edge),
             pltpu.VMEM((count * pairs * edge, 768), BF16),
             pltpu.VMEM((2, count * pairs * edge, 128), F32),
             pltpu.VMEM((16 * half, 128), F32),

time: 49.1 us -> 48.7 us (level)
    pallas_call x2, Pallas kernels: 22.6 us -> 21.6 us  [fine_call(): pl.pallas_call(functools.partial(fine_kernel, first=first), in_specs=[sme...]
    pallas_call x1, Pallas kernels: 5.73 us -> 6.32 us  [lowpass_call(): pl.pallas_call(lowpass_kernel, in_specs=[pl.BlockSpec(memory_space=pltpu....]
  transfers between devices with their start and end apart: 2 -> 2, of which waited for: 0 -> 1; matrix products, arithmetic and copies ran while one was open for 0% -> 0% of each run, Pallas kernels for 46% -> 45%
where the time goes in v7:
time: 48.7 us; the launch traced here: 48.4 us
  Pallas kernels  34.2 us (70%)
  starting transfers between devices  13 us (27%)
  between operations  0.95 us (2%)
    pallas_call x2, Pallas kernels, fine_call(): pl.pallas_call(functools.partial(fine_kernel, first=first), in_specs=[sme...  21.6 us
    all_to_all x1, starting transfers between devices, exchange(): got = lax.all_to_all(lowpass, AXES, 0, 0, tiled=True)  7.3 us
    pallas_call x1, Pallas kernels, lowpass_call(): pl.pallas_call(lowpass_kernel, in_specs=[pl.BlockSpec(memory_space=pltpu....  6.32 us
    all_to_all x1, starting transfers between devices, exchange(): return (lax.all_to_all(sent, AXES, 0, 0, tiled=True), index)  5.7 us
    pallas_call x1, Pallas kernels, coarse_call(): pl.pallas_call(coarse_kernel, in_specs=[pl.BlockSpec(memory_space=pltpu.S...  3.9 us
    pallas_call x1, Pallas kernels, route_call(): pl.pallas_call(route_kernel, in_specs=[pl.BlockSpec(memory_space=pltpu.SM...  2.35 us
  transfers between devices with their start and end apart: 2, of which 1 were waited for; matrix products, arithmetic and copies ran while one was open for 0% of the time, Pallas kernels for 45%

profile of v7, /device:TPU:0, one launch (start us, length us, event | category | flops | bytes accessed | tf_op | source)
XLA Modules:
  0.0 48.4 jit_solution(18302875860929007810)
XLA Ops:
  0.0 0.0 copy-start
  0.0 0.0 copy-start.1
  0.7 6.3 %lowpass.1 = (f32[256,128]{1,0:T(8,128)}, s32[1]{0:T(128)}) custom-call(s32[1]{0:T(128)S(6)} %copy.23.count_ref, f32[6,64,4096]{2,1,0:T(8,128)} %x_any.5, bf16[2,256,256]{2,1,0:T(8,128)(2,1)} %constant.39.clone.wz_any, bf16[1024,256]{1,0:T(8,128)(2,1)} %constant.40.clone.wyh_any, bf16[1024,256]{1,0:T(8,128)(2,1)} %constant.41.clone.wyl_any), custom_call_target="tpu_custom_call" | custom-call | tf_op jit(solution)/shard_map/lowpass/pallas_call | solution.py:165
  7.1 7.3 %all-to-all-start = ((f32[32,8,128]{2,1,0:T(8,128)}), f32[32,8,128]{2,1,0:T(8,128)S(1)}, u32[]{:S(2)}, u32[]{:S(2)}) async-start(f32[32,8,128]{2,1,0:T(8,128)} %bitcast.4), calls=%async_computation | async-start | bytes 262144 | tf_op jit(solution)/shard_map/all_to_all | solution.py:585
  14.4 0.0 copy-done
  14.4 0.0 copy-done.1
  14.4 8.2 %fine.2 = (f32[6,64,4096]{2,1,0:T(8,128)}, s32[1]{0:T(128)}) custom-call(s32[1]{0:T(128)S(6)} %copy.23.count_ref, s32[1]{0:T(128)} %get-tuple-element.13._, f32[6,64,4096]{2,1,0:T(8,128)} %x_any.5, bf16[768,256]{1,0:T(8,128)(2,1)S(1)} %copy-done.1, bf16[768,256]{1,0:T(8,128)(2,1)S(1)} %copy-done), custom_call_target="tpu_custom_call" | custom-call | flops 805306368 | bytes 4194304 | tf_op jit(solution)/shard_map/fine/pallas_call | solution.py:413
  22.6 0.1 all-to-all-done.got_ref
  22.8 2.4 %route.1 = (f32[32,16,128]{2,1,0:T(8,128)}, s32[2]{0:T(128)S(1)}) custom-call(s32[1]{0:T(128)} %bitcast.me_ref, f32[32,8,128]{2,1,0:T(8,128)S(1)} %all-to-all-done.got_ref, s32[1]{0:T(128)} %get-tuple-element.14._), custom_call_target="tpu_custom_call" | custom-call | tf_op jit(solution)/shard_map/route/pallas_call | solution.py:213
  25.1 5.7 %all-to-all-start.1 = ((f32[32,16,128]{2,1,0:T(8,128)}), f32[32,16,128]{2,1,0:T(8,128)S(1)}, u32[]{:S(2)}, u32[]{:S(2)}) async-start(f32[32,16,128]{2,1,0:T(8,128)} %get-tuple-element.16), calls=%async_computation.1 | async-start | bytes 524288 | tf_op jit(solution)/shard_map/all_to_all | solution.py:587
  30.9 0.0 copy-start.2
  30.9 0.0 copy-start.3
  30.9 0.0 copy-start.4
  30.9 0.0 copy-start.5
  30.9 0.0 copy-start.6
  30.9 0.0 copy-start.7
  30.9 0.0 copy-start.8
  30.9 0.0 copy-start.9
  31.0 0.0 copy-start.10
  31.0 13.4 %fine.3 = (f32[6,64,4096]{2,1,0:T(8,128)}, s32[1]{0:T(128)}) custom-call(s32[1]{0:T(128)S(6)} %copy.23.count_ref, s32[2]{0:T(128)S(1)} %get-tuple-element.15._.index_ref, f32[6,64,4096]{2,1,0:T(8,128)} %x_any.5, bf16[768,256]{1,0:T(8,128)(2,1)S(1)} %copy-done.1, bf16[768,256]{1,0:T(8,128)(2,1)S(1)} %copy-done, ...), custom_call_target="tpu_custom_call", output_to_operand_aliasing={{0}: (5, {})} | custom-call | flops 1610612736 | bytes 8388608 | tf_op jit(solution)/shard_map/fine/pallas_call | solution.py:413
  44.4 0.0 all-to-all-done.1
  44.4 0.0 copy-done.2
  44.4 0.0 copy-done.3
  44.4 0.0 copy-done.4
  44.4 0.0 copy-done.5
  44.4 0.0 copy-done.6
  44.4 0.0 copy-done.7
  44.4 0.0 copy-done.8
  44.5 0.0 copy-done.9
  44.5 0.0 copy-done.10
  44.5 3.9 %coarse.1 = f32[6,64,4096]{2,1,0:T(8,128)} custom-call(s32[2]{0:T(128)S(1)} %get-tuple-element.15._.index_ref, f32[512,128]{1,0:T(8,128)S(1)} %bitcast.3, bf16[32,96]{1,0:T(8,128)(2,1)S(1)} %copy-done.8, bf16[256,256]{1,0:T(8,128)(2,1)S(1)} %copy-done.7, bf16[256,256]{1,0:T(8,128)(2,1)S(1)} %copy-done.6, ...), custom_call_target="tpu_custom_call", output_to_operand_aliasing={{}: (11, {})} | custom-call | tf_op jit(solution)/shard_map/coarse/pallas_call | solution.py:564
Async XLA Ops:
  0.0 14.4 %copy-start = (bf16[768,256]{1,0:T(8,128)(2,1)S(1)}, bf16[768,256]{1,0:T(8,128)(2,1)}, u32[]{:S(2)}) copy-start(bf16[768,256]{1,0:T(8,128)(2,1)} %constant.43.clone.w2_ref) | copy-start | bytes 1179652
  0.0 14.4 %copy-start.1 = (bf16[768,256]{1,0:T(8,128)(2,1)S(1)}, bf16[768,256]{1,0:T(8,128)(2,1)}, u32[]{:S(2)}) copy-start(bf16[768,256]{1,0:T(8,128)(2,1)} %constant.42.clone.w1_ref) | copy-start | bytes 1179652
  7.1 15.7 %all-to-all-start = ((f32[32,8,128]{2,1,0:T(8,128)}), f32[32,8,128]{2,1,0:T(8,128)S(1)}, u32[]{:S(2)}, u32[]{:S(2)}) async-start(f32[32,8,128]{2,1,0:T(8,128)} %bitcast.4), calls=%async_computation | async-start | bytes 262144 | tf_op jit(solution)/shard_map/all_to_all | solution.py:585
  25.1 19.2 %all-to-all-start.1 = ((f32[32,16,128]{2,1,0:T(8,128)}), f32[32,16,128]{2,1,0:T(8,128)S(1)}, u32[]{:S(2)}, u32[]{:S(2)}) async-start(f32[32,16,128]{2,1,0:T(8,128)} %get-tuple-element.16), calls=%async_computation.1 | async-start | bytes 524288 | tf_op jit(solution)/shard_map/all_to_all | solution.py:587
  30.9 13.5 %copy-start.2 = (bf16[512,512]{1,0:T(8,128)(2,1)S(1)}, bf16[512,512]{1,0:T(8,128)(2,1)}, u32[]{:S(2)}) copy-start(bf16[512,512]{1,0:T(8,128)(2,1)} %constant.48.clone.wyl_ref) | copy-start | bytes 1572868
  30.9 13.5 %copy-start.3 = (bf16[512,512]{1,0:T(8,128)(2,1)S(1)}, bf16[512,512]{1,0:T(8,128)(2,1)}, u32[]{:S(2)}) copy-start(bf16[512,512]{1,0:T(8,128)(2,1)} %constant.47.clone.wyh_ref) | copy-start | bytes 1572868
  30.9 13.5 %copy-start.4 = (bf16[256,384]{1,0:T(8,128)(2,1)S(1)}, bf16[256,384]{1,0:T(8,128)(2,1)}, u32[]{:S(2)}) copy-start(bf16[256,384]{1,0:T(8,128)(2,1)} %constant.50.clone.w23l_ref) | copy-start | bytes 589828
  30.9 13.5 %copy-start.5 = (bf16[256,384]{1,0:T(8,128)(2,1)S(1)}, bf16[256,384]{1,0:T(8,128)(2,1)}, u32[]{:S(2)}) copy-start(bf16[256,384]{1,0:T(8,128)(2,1)} %constant.49.clone.w23h_ref) | copy-start | bytes 589828
  30.9 13.5 %copy-start.6 = (bf16[256,256]{1,0:T(8,128)(2,1)S(1)}, bf16[256,256]{1,0:T(8,128)(2,1)}, u32[]{:S(2)}) copy-start(bf16[256,256]{1,0:T(8,128)(2,1)} %constant.46.clone.wzl_ref) | copy-start | bytes 393220
  30.9 13.5 %copy-start.7 = (bf16[256,256]{1,0:T(8,128)(2,1)S(1)}, bf16[256,256]{1,0:T(8,128)(2,1)}, u32[]{:S(2)}) copy-start(bf16[256,256]{1,0:T(8,128)(2,1)} %constant.45.clone.wzh_ref) | copy-start | bytes 393220
  30.9 13.5 %copy-start.8 = (bf16[32,96]{1,0:T(8,128)(2,1)S(1)}, bf16[32,96]{1,0:T(8,128)(2,1)}, u32[]{:S(2)}) copy-start(bf16[32,96]{1,0:T(8,128)(2,1)} %constant.44.clone.wx_ref) | copy-start | bytes 18436
  30.9 13.5 %copy-start.9 = (bf16[16,48]{1,0:T(8,128)(2,1)S(1)}, bf16[16,48]{1,0:T(8,128)(2,1)}, u32[]{:S(2)}) copy-start(bf16[16,48]{1,0:T(8,128)(2,1)} %constant.52.clone.wx3_ref) | copy-start | bytes 4612
  31.0 13.5 %copy-start.10 = (bf16[16,48]{1,0:T(8,128)(2,1)S(1)}, bf16[16,48]{1,0:T(8,128)(2,1)}, u32[]{:S(2)}) copy-start(bf16[16,48]{1,0:T(8,128)(2,1)} %constant.51.clone.wx2_ref) | copy-start | bytes 4612

commit v8 on v7

--- a/solution.py
+++ b/solution.py
@@ -75,31 +75,16 @@
     return [split(jnp.concatenate(rows[m : m + 2], 0)) for m in range(0, len(rows), 2)]
 
 
-def tile_buffer(tiles, slots, edge):
-    return pltpu.VMEM((tiles, slots | 1, edge + 8, 128), F32)
-
-
 def start_tiles(src_ref, dst_ref, sems):
-    slots, edge = src_ref.shape[:2]
-    for t in range(dst_ref.shape[0]):
+    for t in range(dst_ref.shape[2]):
         pltpu.make_async_copy(
-            src_ref.at[:, :, pl.ds(t * 128, 128)],
-            dst_ref.at[t, pl.ds(0, slots), pl.ds(0, edge), :],
-            sems.at[t // 8],
+            src_ref.at[:, :, pl.ds(t * 128, 128)], dst_ref.at[:, :, t, :], sems.at[t // 8]
         ).start()
 
 
-def wait_tiles(src_ref, dst_ref, sems, group):
-    slots, edge = src_ref.shape[:2]
-    part = dst_ref.at[pl.ds(8 * group, 8), pl.ds(0, slots), pl.ds(0, edge), :]
+def wait_tiles(dst_ref, sems, group):
+    part = dst_ref.at[:, :, pl.ds(8 * group, 8), :]
     pltpu.make_async_copy(part, part, sems.at[group]).wait()
-
-
-def tile_rows(ref, slot, group, edge):
-    tiles, slots, pitch, lanes = ref.shape
-    flat = ref.reshape(tiles * slots * pitch, lanes)
-    base = 8 * group * slots * pitch + slot * pitch
-    return [flat[pl.ds(base + x, 8, stride=slots * pitch), :] for x in range(edge)]
 
 
 def lowpass_kernel(
@@ -117,11 +102,11 @@
     for copy in weights:
         copy.start()
     for g in range(4):
-        wait_tiles(x_any, x_ref, sems, g)
+        wait_tiles(x_ref, sems, g)
 
         @pl.loop(0, slots)
         def _(s):
-            rows = tile_rows(x_ref, s, g, edge)
+            rows = [x_ref[s, x, pl.ds(8 * g, 8), :] for x in range(edge)]
             rows, _ = lift(rows[0::2], rows[1::2], edge // 2, False, False)
             rows, _ = lift(rows[0::2], rows[1::2], quarter, False, False)
             for m, (high, low) in enumerate(split_rows(rows)):
@@ -171,7 +156,7 @@
             jax.ShapeDtypeStruct((1,), jnp.int32),
         ],
         scratch_shapes=[
-            tile_buffer(plane // 128, slots, edge),
+            pltpu.VMEM((slots, edge, plane // 128, 128), F32),
             pltpu.VMEM(wz.shape, BF16),
             pltpu.VMEM(wyh.shape, BF16),
             pltpu.VMEM(wyl.shape, BF16),
@@ -279,20 +264,19 @@
 
 
 def fine_kernel(count_ref, _, x_any, w1_ref, w2_ref, *refs, first):
-    out_ref, token_ref, x_ref, l_ref, y_ref, c_ref, m_ref, d_ref, o_ref, x_sems, sems = refs[-11:]
-    slots, edge = o_ref.shape[:2]
-    tiles = x_ref.shape[0]
+    out_ref, token_ref, x_buf, l_ref, y_ref, c_ref, m_ref, d_ref, sems = refs[-9:]
+    step = pl.program_id(0)
+    slot = step + first
+    edge = x_any.shape[1]
+    tiles = x_buf.shape[2]
     pairs = tiles // 2
     half = edge // 2
-    block = pairs * edge
     corner = 8 * half
-    live = jnp.clip(count_ref[0] - first, 0, slots)
+    live = slot < count_ref[0]
     lane = lax.broadcasted_iota(jnp.int32, (8, 128), 1)
     front = lane < 64
     inner = (lane & 63) < half
-    token_ref[0] = live
-    x_any = x_any.at[pl.ds(first, slots)]
-    start_tiles(x_any, x_ref, x_sems)
+    token_ref[0] = step
 
     def cross(a, b):
         return pltpu.roll(jnp.where(front, b, a), 64, 1)
@@ -320,33 +304,39 @@
             ref[place, pl.ds(256 + col, 128)] = low
             ref[place, pl.ds(512 + col, 128)] = high
 
-    def write(s):
-        return pltpu.make_async_copy(o_ref.at[s], out_ref.at[first + s], sems.at[s])
-
-    @pl.loop(live, slots)
-    def _(s):
-        o_ref[s] = jnp.zeros(o_ref.shape[1:], F32)
-        write(s).start()
-
-    for g in range(4):
-        wait_tiles(x_any, x_ref, x_sems, g)
-
-        @pl.loop(0, live)
-        def _(s):
-            rows = scaled_rows(tile_rows(x_ref, s, g, edge))
-            store_terms(l_ref, s * block + (g % 2) * 8 * edge, (g // 2) * 128, rows)
-
-    lifted = dot(l_ref[...], w1_ref[...])
-    y_ref[0] = lifted[:, :128]
-    y_ref[1] = lifted[:, 128:]
-
-    @pl.loop(0, live)
-    def _(s):
+    def fetch(which, place):
+        for t in range(tiles):
+            pltpu.make_async_copy(
+                x_any.at[which, :, pl.ds(t * 128, 128)], x_buf.at[place, :, t, :], sems.at[place]
+            ).start()
+
+    @pl.when((step == 0) & live)
+    def _():
+        fetch(slot, 0)
+
+    @pl.when((step + 1 < pl.num_programs(0)) & (slot + 1 < count_ref[0]))
+    def _():
+        fetch(slot + 1, (step + 1) % 2)
+
+    @pl.when(jnp.logical_not(live))
+    def _():
+        out_ref[...] = jnp.zeros_like(out_ref)
+
+    @pl.when(live)
+    def _():
+        x = x_buf.at[step % 2]
+        pltpu.make_async_copy(x, x, sems.at[step % 2]).wait()
+        for g in range(4):
+            rows = scaled_rows([x[i, pl.ds(8 * g, 8), :] for i in range(edge)])
+            store_terms(l_ref, (g % 2) * 8 * edge, (g // 2) * 128, rows)
+        lifted = dot(l_ref[...], w1_ref[...])
+        y_ref[0] = lifted[:, :128]
+        y_ref[1] = lifted[:, 128:]
         for r in range(edge // 8):
             rows = pl.ds(8 * r, 8)
 
             def tile(part, j):
-                return y_ref[part, pl.ds(s * block + (j // 8) * 8 * edge + 64 * r + j % 8, 8, stride=8), :]
+                return y_ref[part, pl.ds((j // 8) * 8 * edge + 64 * r + j % 8, 8, stride=8), :]
 
             low = [tile(0, j) for j in range(pairs)]
             high = [tile(1, j) for j in range(pairs)]
@@ -355,8 +345,8 @@
                 for t in range(pairs // 2):
                     a, b = exchange(values[2 * t], values[2 * t + 1])
                     at = part * pairs + t
-                    o_ref[s, rows, pl.ds(at * 128, 128)] = a
-                    o_ref[s, rows, pl.ds((at + pairs // 2) * 128, 128)] = b
+                    out_ref[0, rows, pl.ds(at * 128, 128)] = a
+                    out_ref[0, rows, pl.ds((at + pairs // 2) * 128, 128)] = b
             if r < half // 8:
                 low, high = lift(*with_halo(low[0::2], low[1::2]), 8, True, False)
                 for i in range(8):
@@ -364,27 +354,18 @@
                     c_ref[pl.ds(corner + 64 * r + i, 8, stride=8), :] = high[i]
         for u in range(2):
             rows = scaled_rows([c_ref[pl.ds(u * corner + 8 * i, 8), :] for i in range(half)])
-            store_terms(m_ref, s * corner, u * 128, rows)
-
-    lifted = dot(m_ref[...], w2_ref[...])
-    d_ref[0] = lifted[:, :128]
-    d_ref[1] = lifted[:, 128:]
-
-    @pl.loop(0, live)
-    def _(s):
+            store_terms(m_ref, 0, u * 128, rows)
+        lifted = dot(m_ref[...], w2_ref[...])
+        d_ref[0] = lifted[:, :128]
+        d_ref[1] = lifted[:, 128:]
         for u in range(2):
             for t in range(4):
                 for r in range(half // 8):
-                    base = s * corner + 64 * r + 2 * t
-                    a = d_ref[u, pl.ds(base, 8, stride=8), :]
-                    b = d_ref[u, pl.ds(base + 1, 8, stride=8), :]
+                    a = d_ref[u, pl.ds(64 * r + 2 * t, 8, stride=8), :]
+                    b = d_ref[u, pl.ds(64 * r + 2 * t + 1, 8, stride=8), :]
                     for at, value in zip((u * 8 + t, u * 8 + 4 + t), exchange(a, b)):
                         rows, cols = pl.ds(8 * r, 8), pl.ds(at * 128, 128)
-                        o_ref[s, rows, cols] = jnp.where(inner, value, o_ref[s, rows, cols])
-        write(s).start()
-
-    for s in range(slots):
-        write(s).wait()
+                        out_ref[0, rows, cols] = jnp.where(inner, value, out_ref[0, rows, cols])
 
 
 def fine_call(owner_counts, token, density, first, last, before=None):
@@ -408,31 +389,30 @@
     w2 = np.kron(np.diag([1 / SCALE, 1 / SCALE, SCALE, SCALE]), two)
     anywhere = pl.BlockSpec(memory_space=pl.ANY)
     smem = pl.BlockSpec(memory_space=pltpu.SMEM)
-    vmem = pl.BlockSpec(memory_space=pltpu.VMEM)
     old = [] if before is None else [before]
+    fixed = pl.BlockSpec((768, 256), lambda s: (0, 0))
     return pl.pallas_call(
         functools.partial(fine_kernel, first=first),
-        in_specs=[smem, smem, anywhere, vmem, vmem] + [anywhere] * len(old),
-        out_specs=[anywhere, smem],
+        grid=(count,),
+        in_specs=[smem, smem, anywhere, fixed, fixed] + [anywhere] * len(old),
+        out_specs=[pl.BlockSpec((1, edge, plane), lambda s: (s + first, 0, 0)), smem],
         out_shape=[
             jax.ShapeDtypeStruct(density.shape, F32),
             jax.ShapeDtypeStruct((1,), jnp.int32),
         ],
         scratch_shapes=[
-            tile_buffer(tiles, count, edge),
-            pltpu.VMEM((count * pairs * edge, 768), BF16),
-            pltpu.VMEM((2, count * pairs * edge, 128), F32),
+            pltpu.VMEM((2, edge, tiles, 128), F32),
+            pltpu.VMEM((pairs * edge, 768), BF16),
+            pltpu.VMEM((2, pairs * edge, 128), F32),
             pltpu.VMEM((16 * half, 128), F32),
-            pltpu.VMEM((count * 8 * half, 768), BF16),
-            pltpu.VMEM((2, count * 8 * half, 128), F32),
-            pltpu.VMEM((count, edge, tiles * 128), F32),
-            pltpu.SemaphoreType.DMA((4,)),
-            pltpu.SemaphoreType.DMA((count,)),
+            pltpu.VMEM((8 * half, 768), BF16),
+            pltpu.VMEM((2, 8 * half, 128), F32),
+            pltpu.SemaphoreType.DMA((2,)),
         ],
         input_output_aliases={5: 0} if old else {},
         compiler_params=pltpu.CompilerParams(vmem_limit_bytes=VMEM_LIMIT),
         cost_estimate=pl.CostEstimate(
-            flops=6 * count * edge * tiles * 128 * 256, bytes_accessed=2 * count * MIB, transcendentals=0
+            flops=6 * count * edge * plane * 256, bytes_accessed=2 * count * MIB, transcendentals=0
         ),
         name="fine",
     )(owner_counts, token, density, stacked(w1), stacked(w2), *old)

time: 48.7 us -> 43.7 us (0.90)
  Pallas kernels: 34.2 us -> 28.5 us
  waiting for transfers between devices: 0.15 us -> 2.72 us
  starting transfers between devices: 13 us -> 11.1 us
    pallas_call x2, Pallas kernels: 21.6 us -> 16.5 us  [fine_call(): pl.pallas_call(functools.partial(fine_kernel, first=first), grid=(count,)...]
    all_to_all x1, starting transfers between devices: 5.7 us -> 3.8 us  [exchange(): return (lax.all_to_all(sent, AXES, 0, 0, tiled=True), index)]
    all_to_all x1, waiting for transfers between devices: 0.15 us -> 2.05 us  [exchange(): got = lax.all_to_all(lowpass, AXES, 0, 0, tiled=True)]
    all_to_all x1, waiting for transfers between devices: 0.01 us -> 0.67 us  [exchange(): return (lax.all_to_all(sent, AXES, 0, 0, tiled=True), index)]
    pallas_call x1, Pallas kernels: 6.32 us -> 5.73 us  [lowpass_call(): pl.pallas_call(lowpass_kernel, in_specs=[pl.BlockSpec(memory_space=pltpu....]
  transfers between devices with their start and end apart: 2 -> 2, of which waited for: 1 -> 2; matrix products, arithmetic and copies ran while one was open for 0% -> 0% of each run, Pallas kernels for 45% -> 38%
where the time goes in v8:
time: 43.7 us; the launch traced here: 43.3 us
  Pallas kernels  28.5 us (65%)
  starting transfers between devices  11.1 us (25%)
  waiting for transfers between devices  2.72 us (6%)
  between operations  0.92 us (2%)
    pallas_call x2, Pallas kernels, fine_call(): pl.pallas_call(functools.partial(fine_kernel, first=first), grid=(count,)...  16.5 us
    all_to_all x1, starting transfers between devices, exchange(): got = lax.all_to_all(lowpass, AXES, 0, 0, tiled=True)  7.3 us
    pallas_call x1, Pallas kernels, lowpass_call(): pl.pallas_call(lowpass_kernel, in_specs=[pl.BlockSpec(memory_space=pltpu....  5.73 us
    pallas_call x1, Pallas kernels, coarse_call(): pl.pallas_call(coarse_kernel, in_specs=[pl.BlockSpec(memory_space=pltpu.S...  3.9 us
    all_to_all x1, starting transfers between devices, exchange(): return (lax.all_to_all(sent, AXES, 0, 0, tiled=True), index)  3.8 us
    pallas_call x1, Pallas kernels, route_call(): pl.pallas_call(route_kernel, in_specs=[pl.BlockSpec(memory_space=pltpu.SM...  2.35 us
    all_to_all x1, waiting for transfers between devices, exchange(): got = lax.all_to_all(lowpass, AXES, 0, 0, tiled=True)  2.05 us
  transfers between devices with their start and end apart: 2, of which 2 were waited for; matrix products, arithmetic and copies ran while one was open for 0% of the time, Pallas kernels for 38%

profile of v8, /device:TPU:0, one launch (start us, length us, event | category | flops | bytes accessed | tf_op | source)
XLA Modules:
  0.0 43.3 jit_solution(7888979511418134293)
XLA Ops:
  0.0 0.0 copy-start
  0.0 0.0 copy-start.1
  0.7 5.7 %lowpass.1 = (f32[256,128]{1,0:T(8,128)}, s32[1]{0:T(128)}) custom-call(s32[1]{0:T(128)S(6)} %copy.23.count_ref, f32[6,64,4096]{2,1,0:T(8,128)} %x_any.5, bf16[2,256,256]{2,1,0:T(8,128)(2,1)} %constant.39.clone.wz_any, bf16[1024,256]{1,0:T(8,128)(2,1)} %constant.40.clone.wyh_any, bf16[1024,256]{1,0:T(8,128)(2,1)} %constant.41.clone.wyl_any), custom_call_target="tpu_custom_call" | custom-call | tf_op jit(solution)/shard_map/lowpass/pallas_call | solution.py:150
  6.5 7.3 %all-to-all-start = ((f32[32,8,128]{2,1,0:T(8,128)}), f32[32,8,128]{2,1,0:T(8,128)S(1)}, u32[]{:S(2)}, u32[]{:S(2)}) async-start(f32[32,8,128]{2,1,0:T(8,128)} %bitcast.4), calls=%async_computation | async-start | bytes 262144 | tf_op jit(solution)/shard_map/all_to_all | solution.py:565
  13.8 0.0 copy-done
  13.8 0.0 copy-done.1
  13.8 6.3 %fine.2 = (f32[6,64,4096]{2,1,0:T(8,128)}, s32[1]{0:T(128)}) custom-call(s32[1]{0:T(128)S(6)} %copy.23.count_ref, s32[1]{0:T(128)} %get-tuple-element.13._, f32[6,64,4096]{2,1,0:T(8,128)} %x_any.5, bf16[768,256]{1,0:T(8,128)(2,1)S(1)} %copy-done.1, bf16[768,256]{1,0:T(8,128)(2,1)S(1)} %copy-done), custom_call_target="tpu_custom_call" | custom-call | flops 805306368 | bytes 4194304 | tf_op jit(solution)/shard_map/fine/pallas_call | solution.py:394
  20.1 2.0 %all-to-all-done.got_ref = f32[32,8,128]{2,1,0:T(8,128)S(1)} async-done(((f32[32,8,128]{2,1,0:T(8,128)}), f32[32,8,128]{2,1,0:T(8,128)S(1)}, u32[]{:S(2)}, u32[]{:S(2)}) %all-to-all-start) | async-done | bytes 131104 | tf_op jit(solution)/shard_map/all_to_all | solution.py:565
  22.2 2.4 %route.1 = (f32[32,16,128]{2,1,0:T(8,128)}, s32[2]{0:T(128)S(1)}) custom-call(s32[1]{0:T(128)} %bitcast.me_ref, f32[32,8,128]{2,1,0:T(8,128)S(1)} %all-to-all-done.got_ref, s32[1]{0:T(128)} %get-tuple-element.14._), custom_call_target="tpu_custom_call" | custom-call | tf_op jit(solution)/shard_map/route/pallas_call | solution.py:198
  24.5 3.8 %all-to-all-start.1 = ((f32[32,16,128]{2,1,0:T(8,128)}), f32[32,16,128]{2,1,0:T(8,128)S(1)}, u32[]{:S(2)}, u32[]{:S(2)}) async-start(f32[32,16,128]{2,1,0:T(8,128)} %get-tuple-element.16), calls=%async_computation.1 | async-start | bytes 524288 | tf_op jit(solution)/shard_map/all_to_all | solution.py:567
  28.4 0.0 copy-start.2
  28.4 0.0 copy-start.3
  28.4 0.0 copy-start.4
  28.4 0.0 copy-start.5
  28.4 0.0 copy-start.6
  28.4 0.0 copy-start.7
  28.4 0.0 copy-start.8
  28.4 0.0 copy-start.9
  28.5 0.0 copy-start.10
  28.5 10.2 %fine.3 = (f32[6,64,4096]{2,1,0:T(8,128)}, s32[1]{0:T(128)}) custom-call(s32[1]{0:T(128)S(6)} %copy.23.count_ref, s32[2]{0:T(128)S(1)} %get-tuple-element.15._.index_ref, f32[6,64,4096]{2,1,0:T(8,128)} %x_any.5, bf16[768,256]{1,0:T(8,128)(2,1)S(1)} %copy-done.1, bf16[768,256]{1,0:T(8,128)(2,1)S(1)} %copy-done, ...), custom_call_target="tpu_custom_call", output_to_operand_aliasing={{0}: (5, {})} | custom-call | flops 1610612736 | bytes 8388608 | tf_op jit(solution)/shard_map/fine/pallas_call | solution.py:394
  38.6 0.7 %all-to-all-done.1 = f32[32,16,128]{2,1,0:T(8,128)S(1)} async-done(((f32[32,16,128]{2,1,0:T(8,128)}), f32[32,16,128]{2,1,0:T(8,128)S(1)}, u32[]{:S(2)}, u32[]{:S(2)}) %all-to-all-start.1) | async-done | bytes 262176 | tf_op jit(solution)/shard_map/all_to_all | solution.py:567
  39.3 0.0 copy-done.2
  39.3 0.0 copy-done.3
  39.3 0.0 copy-done.4
  39.3 0.0 copy-done.5
  39.3 0.0 copy-done.6
  39.3 0.0 copy-done.7
  39.4 0.0 copy-done.8
  39.4 0.0 copy-done.9
  39.4 0.0 copy-done.10
  39.4 3.9 %coarse.1 = f32[6,64,4096]{2,1,0:T(8,128)} custom-call(s32[2]{0:T(128)S(1)} %get-tuple-element.15._.index_ref, f32[512,128]{1,0:T(8,128)S(1)} %bitcast.3, bf16[32,96]{1,0:T(8,128)(2,1)S(1)} %copy-done.8, bf16[256,256]{1,0:T(8,128)(2,1)S(1)} %copy-done.7, bf16[256,256]{1,0:T(8,128)(2,1)S(1)} %copy-done.6, ...), custom_call_target="tpu_custom_call", output_to_operand_aliasing={{}: (11, {})} | custom-call | tf_op jit(solution)/shard_map/coarse/pallas_call | solution.py:544
Async XLA Ops:
  0.0 13.8 %copy-start = (bf16[768,256]{1,0:T(8,128)(2,1)S(1)}, bf16[768,256]{1,0:T(8,128)(2,1)}, u32[]{:S(2)}) copy-start(bf16[768,256]{1,0:T(8,128)(2,1)} %constant.43.clone.w2_ref) | copy-start | bytes 1179652
  0.0 13.8 %copy-start.1 = (bf16[768,256]{1,0:T(8,128)(2,1)S(1)}, bf16[768,256]{1,0:T(8,128)(2,1)}, u32[]{:S(2)}) copy-start(bf16[768,256]{1,0:T(8,128)(2,1)} %constant.42.clone.w1_ref) | copy-start | bytes 1179652
  6.5 15.7 %all-to-all-start = ((f32[32,8,128]{2,1,0:T(8,128)}), f32[32,8,128]{2,1,0:T(8,128)S(1)}, u32[]{:S(2)}, u32[]{:S(2)}) async-start(f32[32,8,128]{2,1,0:T(8,128)} %bitcast.4), calls=%async_computation | async-start | bytes 262144 | tf_op jit(solution)/shard_map/all_to_all | solution.py:565
  24.5 14.8 %all-to-all-start.1 = ((f32[32,16,128]{2,1,0:T(8,128)}), f32[32,16,128]{2,1,0:T(8,128)S(1)}, u32[]{:S(2)}, u32[]{:S(2)}) async-start(f32[32,16,128]{2,1,0:T(8,128)} %get-tuple-element.16), calls=%async_computation.1 | async-start | bytes 524288 | tf_op jit(solution)/shard_map/all_to_all | solution.py:567
  28.4 11.0 %copy-start.2 = (bf16[512,512]{1,0:T(8,128)(2,1)S(1)}, bf16[512,512]{1,0:T(8,128)(2,1)}, u32[]{:S(2)}) copy-start(bf16[512,512]{1,0:T(8,128)(2,1)} %constant.48.clone.wyl_ref) | copy-start | bytes 1572868
  28.4 10.9 %copy-start.3 = (bf16[512,512]{1,0:T(8,128)(2,1)S(1)}, bf16[512,512]{1,0:T(8,128)(2,1)}, u32[]{:S(2)}) copy-start(bf16[512,512]{1,0:T(8,128)(2,1)} %constant.47.clone.wyh_ref) | copy-start | bytes 1572868
  28.4 10.9 %copy-start.4 = (bf16[256,384]{1,0:T(8,128)(2,1)S(1)}, bf16[256,384]{1,0:T(8,128)(2,1)}, u32[]{:S(2)}) copy-start(bf16[256,384]{1,0:T(8,128)(2,1)} %constant.50.clone.w23l_ref) | copy-start | bytes 589828
  28.4 10.9 %copy-start.5 = (bf16[256,384]{1,0:T(8,128)(2,1)S(1)}, bf16[256,384]{1,0:T(8,128)(2,1)}, u32[]{:S(2)}) copy-start(bf16[256,384]{1,0:T(8,128)(2,1)} %constant.49.clone.w23h_ref) | copy-start | bytes 589828
  28.4 10.9 %copy-start.6 = (bf16[256,256]{1,0:T(8,128)(2,1)S(1)}, bf16[256,256]{1,0:T(8,128)(2,1)}, u32[]{:S(2)}) copy-start(bf16[256,256]{1,0:T(8,128)(2,1)} %constant.46.clone.wzl_ref) | copy-start | bytes 393220
  28.4 10.9 %copy-start.7 = (bf16[256,256]{1,0:T(8,128)(2,1)S(1)}, bf16[256,256]{1,0:T(8,128)(2,1)}, u32[]{:S(2)}) copy-start(bf16[256,256]{1,0:T(8,128)(2,1)} %constant.45.clone.wzh_ref) | copy-start | bytes 393220
  28.4 10.9 %copy-start.8 = (bf16[32,96]{1,0:T(8,128)(2,1)S(1)}, bf16[32,96]{1,0:T(8,128)(2,1)}, u32[]{:S(2)}) copy-start(bf16[32,96]{1,0:T(8,128)(2,1)} %constant.44.clone.wx_ref) | copy-start | bytes 18436
  28.4 10.9 %copy-start.9 = (bf16[16,48]{1,0:T(8,128)(2,1)S(1)}, bf16[16,48]{1,0:T(8,128)(2,1)}, u32[]{:S(2)}) copy-start(bf16[16,48]{1,0:T(8,128)(2,1)} %constant.52.clone.wx3_ref) | copy-start | bytes 4612
  28.5 10.9 %copy-start.10 = (bf16[16,48]{1,0:T(8,128)(2,1)S(1)}, bf16[16,48]{1,0:T(8,128)(2,1)}, u32[]{:S(2)}) copy-start(bf16[16,48]{1,0:T(8,128)(2,1)} %constant.51.clone.wx2_ref) | copy-start | bytes 4612

commit v9 on v8

--- a/solution.py
+++ b/solution.py
@@ -111,13 +111,13 @@
             rows, _ = lift(rows[0::2], rows[1::2], quarter, False, False)
             for m, (high, low) in enumerate(split_rows(rows)):
                 at = pl.multiple_of(s * 8 * quarter + 16 * m, 16)
-                cols = pl.ds((g // 2) * 128, 128)
-                l_ref[g % 2, pl.ds(at, 16), cols] = high
-                l_ref[g % 2, pl.ds(rows_all + at, 16), cols] = low
+                cols = pl.ds((g % 2) * 256 + (g // 2) * 128, 128)
+                l_ref[pl.ds(at, 16), cols] = high
+                l_ref[pl.ds(rows_all + at, 16), cols] = low
 
     for copy in weights:
         copy.wait()
-    made = dot(l_ref[0], wz_ref[0]) + dot(l_ref[1], wz_ref[1])
+    made = dot(l_ref[...], wz_ref[...])
     z_ref[...] = (made[:rows_all, :128] + made[rows_all:, :128]) + made[:rows_all, 128:]
     wide = jnp.concatenate([z_ref[pl.ds(i, slots * quarter, stride=8), :] for i in range(8)], 1)
     made = times(wide, wyh_ref[...], wyl_ref[...])
@@ -138,8 +138,7 @@
     slots, edge, plane = density.shape
     quarter = edge // 4
     two_levels = pass_matrix(edge // 2)[:quarter] @ pass_matrix(edge)[: edge // 2]
-    wide = np.kron(np.eye(8), two_levels.T)
-    wz = np.stack([np.concatenate(two_terms(w), 1) for w in (wide[:256], wide[256:])])
+    wz = np.concatenate(two_terms(np.kron(np.eye(8), two_levels.T)), 1)
     i, gp, q, p = np.meshgrid(np.arange(8), np.arange(2), np.arange(2), np.arange(2), indexing="ij")
     entry = (2 * (8 * gp + i) + p + 32 * q).reshape(-1)
     wy = np.kron(two_levels.T[entry] / SQUARE, np.eye(quarter))
@@ -160,7 +159,7 @@
             pltpu.VMEM(wz.shape, BF16),
             pltpu.VMEM(wyh.shape, BF16),
             pltpu.VMEM(wyl.shape, BF16),
-            pltpu.VMEM((2, 2 * rows_all, 256), BF16),
+            pltpu.VMEM((2 * rows_all, 512), BF16),
             pltpu.VMEM((rows_all, 128), F32),
             pltpu.SemaphoreType.DMA((4,)),
             pltpu.SemaphoreType.DMA((3,)),
@@ -314,10 +313,6 @@
     def _():
         fetch(slot, 0)
 
-    @pl.when((step + 1 < pl.num_programs(0)) & (slot + 1 < count_ref[0]))
-    def _():
-        fetch(slot + 1, (step + 1) % 2)
-
     @pl.when(jnp.logical_not(live))
     def _():
         out_ref[...] = jnp.zeros_like(out_ref)
@@ -326,6 +321,14 @@
     def _():
         x = x_buf.at[step % 2]
         pltpu.make_async_copy(x, x, sems.at[step % 2]).wait()
+
+    @pl.when((step + 1 < pl.num_programs(0)) & (slot + 1 < count_ref[0]))
+    def _():
+        fetch(slot + 1, (step + 1) % 2)
+
+    @pl.when(live)
+    def _():
+        x = x_buf.at[step % 2]
         for g in range(4):
             rows = scaled_rows([x[i, pl.ds(8 * g, 8), :] for i in range(edge)])
             store_terms(l_ref, (g % 2) * 8 * edge, (g // 2) * 128, rows)

time: 43.7 us -> 43.8 us (level)
  no operation moved by 1% of the time
where the time goes in v9:
time: 43.8 us; the launch traced here: 43.4 us
  Pallas kernels  28.6 us (65%)
  starting transfers between devices  11.2 us (26%)
  waiting for transfers between devices  2.56 us (6%)
  between operations  0.92 us (2%)
    pallas_call x2, Pallas kernels, fine_call(): pl.pallas_call(functools.partial(fine_kernel, first=first), grid=(count,)...  16.6 us
    all_to_all x1, starting transfers between devices, exchange(): got = lax.all_to_all(lowpass, AXES, 0, 0, tiled=True)  7.3 us
    pallas_call x1, Pallas kernels, lowpass_call(): pl.pallas_call(lowpass_kernel, in_specs=[pl.BlockSpec(memory_space=pltpu....  5.73 us
    pallas_call x1, Pallas kernels, coarse_call(): pl.pallas_call(coarse_kernel, in_specs=[pl.BlockSpec(memory_space=pltpu.S...  3.9 us
    all_to_all x1, starting transfers between devices, exchange(): return (lax.all_to_all(sent, AXES, 0, 0, tiled=True), index)  3.88 us
    pallas_call x1, Pallas kernels, route_call(): pl.pallas_call(route_kernel, in_specs=[pl.BlockSpec(memory_space=pltpu.SM...  2.35 us
    all_to_all x1, waiting for transfers between devices, exchange(): got = lax.all_to_all(lowpass, AXES, 0, 0, tiled=True)  1.97 us
  transfers between devices with their start and end apart: 2, of which 2 were waited for; matrix products, arithmetic and copies ran while one was open for 0% of the time, Pallas kernels for 38%

profile of v9, /device:TPU:0, one launch (start us, length us, event | category | flops | bytes accessed | tf_op | source)
XLA Modules:
  0.0 43.4 jit_solution(252499252953104223)
XLA Ops:
  0.0 0.0 copy-start
  0.0 0.0 copy-start.1
  0.7 5.7 %lowpass.1 = (f32[256,128]{1,0:T(8,128)}, s32[1]{0:T(128)}) custom-call(s32[1]{0:T(128)S(6)} %copy.23.count_ref, f32[6,64,4096]{2,1,0:T(8,128)} %x_any.5, bf16[512,256]{1,0:T(8,128)(2,1)} %constant.39.clone.wz_any, bf16[1024,256]{1,0:T(8,128)(2,1)} %constant.40.clone.wyh_any, bf16[1024,256]{1,0:T(8,128)(2,1)} %constant.41.clone.wyl_any), custom_call_target="tpu_custom_call" | custom-call | tf_op jit(solution)/shard_map/lowpass/pallas_call | solution.py:149
  6.5 7.3 %all-to-all-start = ((f32[32,8,128]{2,1,0:T(8,128)}), f32[32,8,128]{2,1,0:T(8,128)S(1)}, u32[]{:S(2)}, u32[]{:S(2)}) async-start(f32[32,8,128]{2,1,0:T(8,128)} %bitcast.4), calls=%async_computation | async-start | bytes 262144 | tf_op jit(solution)/shard_map/all_to_all | solution.py:568
  13.8 0.0 copy-done
  13.8 0.0 copy-done.1
  13.8 6.4 %fine.2 = (f32[6,64,4096]{2,1,0:T(8,128)}, s32[1]{0:T(128)}) custom-call(s32[1]{0:T(128)S(6)} %copy.23.count_ref, s32[1]{0:T(128)} %get-tuple-element.13._, f32[6,64,4096]{2,1,0:T(8,128)} %x_any.5, bf16[768,256]{1,0:T(8,128)(2,1)S(1)} %copy-done.1, bf16[768,256]{1,0:T(8,128)(2,1)S(1)} %copy-done), custom_call_target="tpu_custom_call" | custom-call | flops 805306368 | bytes 4194304 | tf_op jit(solution)/shard_map/fine/pallas_call | solution.py:397
  20.2 2.0 %all-to-all-done.got_ref = f32[32,8,128]{2,1,0:T(8,128)S(1)} async-done(((f32[32,8,128]{2,1,0:T(8,128)}), f32[32,8,128]{2,1,0:T(8,128)S(1)}, u32[]{:S(2)}, u32[]{:S(2)}) %all-to-all-start) | async-done | bytes 131104 | tf_op jit(solution)/shard_map/all_to_all | solution.py:568
  22.2 2.4 %route.1 = (f32[32,16,128]{2,1,0:T(8,128)}, s32[2]{0:T(128)S(1)}) custom-call(s32[1]{0:T(128)} %bitcast.me_ref, f32[32,8,128]{2,1,0:T(8,128)S(1)} %all-to-all-done.got_ref, s32[1]{0:T(128)} %get-tuple-element.14._), custom_call_target="tpu_custom_call" | custom-call | tf_op jit(solution)/shard_map/route/pallas_call | solution.py:197
  24.5 3.9 %all-to-all-start.1 = ((f32[32,16,128]{2,1,0:T(8,128)}), f32[32,16,128]{2,1,0:T(8,128)S(1)}, u32[]{:S(2)}, u32[]{:S(2)}) async-start(f32[32,16,128]{2,1,0:T(8,128)} %get-tuple-element.16), calls=%async_computation.1 | async-start | bytes 524288 | tf_op jit(solution)/shard_map/all_to_all | solution.py:570
  28.4 0.0 copy-start.2
  28.4 0.0 copy-start.3
  28.5 0.0 copy-start.4
  28.5 0.0 copy-start.5
  28.5 0.0 copy-start.6
  28.5 0.0 copy-start.7
  28.5 0.0 copy-start.8
  28.5 0.0 copy-start.9
  28.5 0.0 copy-start.10
  28.5 10.2 %fine.3 = (f32[6,64,4096]{2,1,0:T(8,128)}, s32[1]{0:T(128)}) custom-call(s32[1]{0:T(128)S(6)} %copy.23.count_ref, s32[2]{0:T(128)S(1)} %get-tuple-element.15._.index_ref, f32[6,64,4096]{2,1,0:T(8,128)} %x_any.5, bf16[768,256]{1,0:T(8,128)(2,1)S(1)} %copy-done.1, bf16[768,256]{1,0:T(8,128)(2,1)S(1)} %copy-done, ...), custom_call_target="tpu_custom_call", output_to_operand_aliasing={{0}: (5, {})} | custom-call | flops 1610612736 | bytes 8388608 | tf_op jit(solution)/shard_map/fine/pallas_call | solution.py:397
  38.8 0.6 %all-to-all-done.1 = f32[32,16,128]{2,1,0:T(8,128)S(1)} async-done(((f32[32,16,128]{2,1,0:T(8,128)}), f32[32,16,128]{2,1,0:T(8,128)S(1)}, u32[]{:S(2)}, u32[]{:S(2)}) %all-to-all-start.1) | async-done | bytes 262176 | tf_op jit(solution)/shard_map/all_to_all | solution.py:570
  39.4 0.0 copy-done.2
  39.4 0.0 copy-done.3
  39.4 0.0 copy-done.4
  39.4 0.0 copy-done.5
  39.4 0.0 copy-done.6
  39.4 0.0 copy-done.7
  39.4 0.0 copy-done.8
  39.4 0.0 copy-done.9
  39.4 0.0 copy-done.10
  39.5 3.9 %coarse.1 = f32[6,64,4096]{2,1,0:T(8,128)} custom-call(s32[2]{0:T(128)S(1)} %get-tuple-element.15._.index_ref, f32[512,128]{1,0:T(8,128)S(1)} %bitcast.3, bf16[32,96]{1,0:T(8,128)(2,1)S(1)} %copy-done.8, bf16[256,256]{1,0:T(8,128)(2,1)S(1)} %copy-done.7, bf16[256,256]{1,0:T(8,128)(2,1)S(1)} %copy-done.6, ...), custom_call_target="tpu_custom_call", output_to_operand_aliasing={{}: (11, {})} | custom-call | tf_op jit(solution)/shard_map/coarse/pallas_call | solution.py:547
Async XLA Ops:
  0.0 13.8 %copy-start = (bf16[768,256]{1,0:T(8,128)(2,1)S(1)}, bf16[768,256]{1,0:T(8,128)(2,1)}, u32[]{:S(2)}) copy-start(bf16[768,256]{1,0:T(8,128)(2,1)} %constant.43.clone.w2_ref) | copy-start | bytes 1179652
  0.0 13.8 %copy-start.1 = (bf16[768,256]{1,0:T(8,128)(2,1)S(1)}, bf16[768,256]{1,0:T(8,128)(2,1)}, u32[]{:S(2)}) copy-start(bf16[768,256]{1,0:T(8,128)(2,1)} %constant.42.clone.w1_ref) | copy-start | bytes 1179652
  6.5 15.7 %all-to-all-start = ((f32[32,8,128]{2,1,0:T(8,128)}), f32[32,8,128]{2,1,0:T(8,128)S(1)}, u32[]{:S(2)}, u32[]{:S(2)}) async-start(f32[32,8,128]{2,1,0:T(8,128)} %bitcast.4), calls=%async_computation | async-start | bytes 262144 | tf_op jit(solution)/shard_map/all_to_all | solution.py:568
  24.5 14.8 %all-to-all-start.1 = ((f32[32,16,128]{2,1,0:T(8,128)}), f32[32,16,128]{2,1,0:T(8,128)S(1)}, u32[]{:S(2)}, u32[]{:S(2)}) async-start(f32[32,16,128]{2,1,0:T(8,128)} %get-tuple-element.16), calls=%async_computation.1 | async-start | bytes 524288 | tf_op jit(solution)/shard_map/all_to_all | solution.py:570
  28.4 11.0 %copy-start.2 = (bf16[512,512]{1,0:T(8,128)(2,1)S(1)}, bf16[512,512]{1,0:T(8,128)(2,1)}, u32[]{:S(2)}) copy-start(bf16[512,512]{1,0:T(8,128)(2,1)} %constant.48.clone.wyl_ref) | copy-start | bytes 1572868
  28.4 10.9 %copy-start.3 = (bf16[512,512]{1,0:T(8,128)(2,1)S(1)}, bf16[512,512]{1,0:T(8,128)(2,1)}, u32[]{:S(2)}) copy-start(bf16[512,512]{1,0:T(8,128)(2,1)} %constant.47.clone.wyh_ref) | copy-start | bytes 1572868
  28.5 10.9 %copy-start.4 = (bf16[256,384]{1,0:T(8,128)(2,1)S(1)}, bf16[256,384]{1,0:T(8,128)(2,1)}, u32[]{:S(2)}) copy-start(bf16[256,384]{1,0:T(8,128)(2,1)} %constant.50.clone.w23l_ref) | copy-start | bytes 589828
  28.5 10.9 %copy-start.5 = (bf16[256,384]{1,0:T(8,128)(2,1)S(1)}, bf16[256,384]{1,0:T(8,128)(2,1)}, u32[]{:S(2)}) copy-start(bf16[256,384]{1,0:T(8,128)(2,1)} %constant.49.clone.w23h_ref) | copy-start | bytes 589828
  28.5 10.9 %copy-start.6 = (bf16[256,256]{1,0:T(8,128)(2,1)S(1)}, bf16[256,256]{1,0:T(8,128)(2,1)}, u32[]{:S(2)}) copy-start(bf16[256,256]{1,0:T(8,128)(2,1)} %constant.46.clone.wzl_ref) | copy-start | bytes 393220
  28.5 10.9 %copy-start.7 = (bf16[256,256]{1,0:T(8,128)(2,1)S(1)}, bf16[256,256]{1,0:T(8,128)(2,1)}, u32[]{:S(2)}) copy-start(bf16[256,256]{1,0:T(8,128)(2,1)} %constant.45.clone.wzh_ref) | copy-start | bytes 393220
  28.5 10.9 %copy-start.8 = (bf16[32,96]{1,0:T(8,128)(2,1)S(1)}, bf16[32,96]{1,0:T(8,128)(2,1)}, u32[]{:S(2)}) copy-start(bf16[32,96]{1,0:T(8,128)(2,1)} %constant.44.clone.wx_ref) | copy-start | bytes 18436
  28.5 10.9 %copy-start.9 = (bf16[16,48]{1,0:T(8,128)(2,1)S(1)}, bf16[16,48]{1,0:T(8,128)(2,1)}, u32[]{:S(2)}) copy-start(bf16[16,48]{1,0:T(8,128)(2,1)} %constant.52.clone.wx3_ref) | copy-start | bytes 4612
  28.5 10.9 %copy-start.10 = (bf16[16,48]{1,0:T(8,128)(2,1)S(1)}, bf16[16,48]{1,0:T(8,128)(2,1)}, u32[]{:S(2)}) copy-start(bf16[16,48]{1,0:T(8,128)(2,1)} %constant.51.clone.wx2_ref) | copy-start | bytes 4612

commit v10 on v9

--- a/solution.py
+++ b/solution.py
@@ -17,6 +17,7 @@
 F32 = jnp.float32
 BF16 = jnp.bfloat16
 AXES = ("node", "dev")
+SWAPPED = ("dev", "node")
 MIB = 1 << 20
 VMEM_LIMIT = 48 * MIB
 VMEM_SMALL = 16 * MIB
@@ -170,8 +171,11 @@
     return pieces.reshape(2 * quarter, 8, 128), token
 
 
-def route_kernel(me_ref, got_ref, _, send_ref, index_ref, order_ref, count_ref, sem):
+def route_kernel(
+    me_ref, got_ref, _, send_any, index_ref, send_ref, order_ref, count_ref, sem, send_sem, *, width
+):
     devices = got_ref.shape[0]
+    place = [d % width * (devices // width) + d // width for d in range(devices)]
     copy = pltpu.make_async_copy(got_ref.at[:, 7, :], count_ref, sem)
     copy.start()
     order_ref[...] = jnp.zeros_like(order_ref)
@@ -179,37 +183,46 @@
     start, my_start, my_count = 0, 0, 0
     starts = []
     for d in range(devices):
-        count = count_ref[d, 0].astype(jnp.int32)
+        count = count_ref[place[d], 0].astype(jnp.int32)
         starts.append(start)
         my_start = jnp.where(me_ref[0] == d, start, my_start)
         my_count = jnp.where(me_ref[0] == d, count, my_count)
-        order_ref[pl.ds(start, 8), :] = got_ref[d]
+        order_ref[pl.ds(start, 8), :] = got_ref[place[d]]
         start = start + count
-    for d in range(devices):
-        at = pl.multiple_of(starts[d] // 8 * 8, 8) if d else 0
-        send_ref[d] = order_ref[pl.ds(at, 16), :]
     index_ref[0] = my_start % 8
     index_ref[1] = my_count
-
-
-def route_call(me, got, token, slots):
+    copies = []
+    for n, d in enumerate(sorted(range(devices), key=lambda d: place[d])):
+        at = pl.multiple_of(starts[d] // 8 * 8, 8) if d else 0
+        send_ref[n] = order_ref[pl.ds(at, 16), :]
+        if n % 8 == 7:
+            part = pl.ds(n - 7, 8)
+            copies.append(pltpu.make_async_copy(send_ref.at[part], send_any.at[part], send_sem.at[n // 8]))
+            copies[-1].start()
+    for copy in copies:
+        copy.wait()
+
+
+def route_call(me, got, token, slots, width):
     devices = got.shape[0]
     return pl.pallas_call(
-        route_kernel,
+        functools.partial(route_kernel, width=width),
         in_specs=[
             pl.BlockSpec(memory_space=pltpu.SMEM),
             pl.BlockSpec(memory_space=pltpu.VMEM),
             pl.BlockSpec(memory_space=pltpu.SMEM),
         ],
-        out_specs=[pl.BlockSpec(memory_space=pltpu.VMEM), pl.BlockSpec(memory_space=pltpu.SMEM)],
+        out_specs=[pl.BlockSpec(memory_space=pl.ANY), pl.BlockSpec(memory_space=pltpu.SMEM)],
         out_shape=[
             jax.ShapeDtypeStruct((devices, 16, 128), F32),
             jax.ShapeDtypeStruct((2,), jnp.int32),
         ],
         scratch_shapes=[
+            pltpu.VMEM((devices, 16, 128), F32),
             pltpu.VMEM((devices * slots + 16, 128), F32),
             pltpu.SMEM((devices, 128), F32),
             pltpu.SemaphoreType.DMA,
+            pltpu.SemaphoreType.DMA((devices // 8,)),
         ],
         compiler_params=pltpu.CompilerParams(vmem_limit_bytes=VMEM_SMALL),
         name="route",
@@ -565,9 +578,9 @@
     me = lax.axis_index(AXES)
     devices = lax.axis_size(AXES)
     if devices == lowpass.shape[0]:
-        got = lax.all_to_all(lowpass, AXES, 0, 0, tiled=True)
-        sent, index = route_call(me.reshape(1), got, token, slots)
-        return lax.all_to_all(sent, AXES, 0, 0, tiled=True), index
+        got = lax.all_to_all(lowpass, SWAPPED, 0, 0, tiled=True)
+        sent, index = route_call(me.reshape(1), got, token, slots, lax.axis_size("dev"))
+        return lax.all_to_all(sent, SWAPPED, 0, 0, tiled=True), index
     every = lax.all_gather(lowpass, AXES, axis=0)
     counts = every[:, 0, 7, 0].astype(jnp.int32)
     starts = jnp.cumsum(counts) - counts

time: 43.8 us -> 43.8 us (level)
  waiting for transfers between devices: 2.56 us -> 1.77 us
  Pallas kernels: 28.6 us -> 29.2 us
    all_to_all x2, waiting for transfers between devices: 2.56 us -> 1.77 us  [the longest x1 1.74 us: exchange(): got = lax.all_to_all(lowpass, SWAPPED, 0, 0, tiled=True)]
    pallas_call x1, Pallas kernels: 2.35 us -> 2.89 us  [route_call(): pl.pallas_call(functools.partial(route_kernel, width=width), in_specs=[pl...]
  transfers between devices with their start and end apart: 2 -> 2, of which waited for: 2 -> 1; matrix products, arithmetic and copies ran while one was open for 0% -> 0% of each run, Pallas kernels for 38% -> 38%
where the time goes in v10:
time: 43.8 us; the launch traced here: 43.3 us
  Pallas kernels  29.2 us (67%)
  starting transfers between devices  11.4 us (26%)
  waiting for transfers between devices  1.77 us (4%)
  between operations  0.93 us (2%)
    pallas_call x2, Pallas kernels, fine_call(): pl.pallas_call(functools.partial(fine_kernel, first=first), grid=(count,)...  16.6 us
    all_to_all x1, starting transfers between devices, exchange(): got = lax.all_to_all(lowpass, SWAPPED, 0, 0, tiled=True)  7.3 us
    pallas_call x1, Pallas kernels, lowpass_call(): pl.pallas_call(lowpass_kernel, in_specs=[pl.BlockSpec(memory_space=pltpu....  5.73 us
    all_to_all x1, starting transfers between devices, exchange(): return (lax.all_to_all(sent, SWAPPED, 0, 0, tiled=True), index)  4.11 us
    pallas_call x1, Pallas kernels, coarse_call(): pl.pallas_call(coarse_kernel, in_specs=[pl.BlockSpec(memory_space=pltpu.S...  3.9 us
    pallas_call x1, Pallas kernels, route_call(): pl.pallas_call(functools.partial(route_kernel, width=width), in_specs=[pl...  2.89 us
    all_to_all x1, waiting for transfers between devices, exchange(): got = lax.all_to_all(lowpass, SWAPPED, 0, 0, tiled=True)  1.74 us
  transfers between devices with their start and end apart: 2, of which 1 were waited for; matrix products, arithmetic and copies ran while one was open for 0% of the time, Pallas kernels for 38%

profile of v10, /device:TPU:0, one launch (start us, length us, event | category | flops | bytes accessed | tf_op | source)
XLA Modules:
  0.0 43.3 jit_solution(15940636168067218177)
XLA Ops:
  0.0 0.0 copy-start
  0.0 0.0 copy-start.1
  0.7 5.7 %lowpass.1 = (f32[256,128]{1,0:T(8,128)}, s32[1]{0:T(128)}) custom-call(s32[1]{0:T(128)S(6)} %copy.23.count_ref, f32[6,64,4096]{2,1,0:T(8,128)} %x_any.5, bf16[512,256]{1,0:T(8,128)(2,1)} %constant.39.clone.wz_any, bf16[1024,256]{1,0:T(8,128)(2,1)} %constant.40.clone.wyh_any, bf16[1024,256]{1,0:T(8,128)(2,1)} %constant.41.clone.wyl_any), custom_call_target="tpu_custom_call" | custom-call | tf_op jit(solution)/shard_map/lowpass/pallas_call | solution.py:150
  6.5 7.3 %all-to-all-start = ((f32[32,8,128]{2,1,0:T(8,128)}), f32[32,8,128]{2,1,0:T(8,128)S(1)}, u32[]{:S(2)}, u32[]{:S(2)}) async-start(f32[32,8,128]{2,1,0:T(8,128)} %bitcast.4), calls=%async_computation | async-start | bytes 262144 | tf_op jit(solution)/shard_map/all_to_all | solution.py:581
  13.8 0.0 copy-done
  13.8 0.0 copy-done.1
  13.8 6.4 %fine.2 = (f32[6,64,4096]{2,1,0:T(8,128)}, s32[1]{0:T(128)}) custom-call(s32[1]{0:T(128)S(6)} %copy.23.count_ref, s32[1]{0:T(128)} %get-tuple-element.13._, f32[6,64,4096]{2,1,0:T(8,128)} %x_any.5, bf16[768,256]{1,0:T(8,128)(2,1)S(1)} %copy-done.1, bf16[768,256]{1,0:T(8,128)(2,1)S(1)} %copy-done), custom_call_target="tpu_custom_call" | custom-call | flops 805306368 | bytes 4194304 | tf_op jit(solution)/shard_map/fine/pallas_call | solution.py:410
  20.2 1.7 %all-to-all-done.got_ref = f32[32,8,128]{2,1,0:T(8,128)S(1)} async-done(((f32[32,8,128]{2,1,0:T(8,128)}), f32[32,8,128]{2,1,0:T(8,128)S(1)}, u32[]{:S(2)}, u32[]{:S(2)}) %all-to-all-start) | async-done | bytes 131104 | tf_op jit(solution)/shard_map/all_to_all | solution.py:581
  22.0 2.9 %route.1 = (f32[32,16,128]{2,1,0:T(8,128)}, s32[2]{0:T(128)S(1)}) custom-call(s32[1]{0:T(128)} %bitcast.me_ref, f32[32,8,128]{2,1,0:T(8,128)S(1)} %all-to-all-done.got_ref, s32[1]{0:T(128)} %get-tuple-element.14._), custom_call_target="tpu_custom_call" | custom-call | tf_op jit(solution)/shard_map/route/pallas_call | solution.py:208
  24.9 4.1 %all-to-all-start.1 = ((f32[32,16,128]{2,1,0:T(8,128)}), f32[32,16,128]{2,1,0:T(8,128)S(1)}, u32[]{:S(2)}, u32[]{:S(2)}) async-start(f32[32,16,128]{2,1,0:T(8,128)} %get-tuple-element.16), calls=%async_computation.1 | async-start | bytes 524288 | tf_op jit(solution)/shard_map/all_to_all | solution.py:583
  29.0 0.0 copy-start.2
  29.0 0.0 copy-start.3
  29.0 0.0 copy-start.4
  29.0 0.0 copy-start.5
  29.0 0.0 copy-start.6
  29.0 0.0 copy-start.7
  29.0 0.0 copy-start.8
  29.1 0.0 copy-start.9
  29.1 0.0 copy-start.10
  29.1 10.2 %fine.3 = (f32[6,64,4096]{2,1,0:T(8,128)}, s32[1]{0:T(128)}) custom-call(s32[1]{0:T(128)S(6)} %copy.23.count_ref, s32[2]{0:T(128)S(1)} %get-tuple-element.15._.index_ref, f32[6,64,4096]{2,1,0:T(8,128)} %x_any.5, bf16[768,256]{1,0:T(8,128)(2,1)S(1)} %copy-done.1, bf16[768,256]{1,0:T(8,128)(2,1)S(1)} %copy-done, ...), custom_call_target="tpu_custom_call", output_to_operand_aliasing={{0}: (5, {})} | custom-call | flops 1610612736 | bytes 8388608 | tf_op jit(solution)/shard_map/fine/pallas_call | solution.py:410
  39.3 0.0 all-to-all-done.1
  39.4 0.0 copy-done.2
  39.4 0.0 copy-done.3
  39.4 0.0 copy-done.4
  39.4 0.0 copy-done.5
  39.4 0.0 copy-done.6
  39.4 0.0 copy-done.7
  39.4 0.0 copy-done.8
  39.4 0.0 copy-done.9
  39.4 0.0 copy-done.10
  39.4 3.9 %coarse.1 = f32[6,64,4096]{2,1,0:T(8,128)} custom-call(s32[2]{0:T(128)S(1)} %get-tuple-element.15._.index_ref, f32[512,128]{1,0:T(8,128)S(1)} %bitcast.3, bf16[32,96]{1,0:T(8,128)(2,1)S(1)} %copy-done.8, bf16[256,256]{1,0:T(8,128)(2,1)S(1)} %copy-done.7, bf16[256,256]{1,0:T(8,128)(2,1)S(1)} %copy-done.6, ...), custom_call_target="tpu_custom_call", output_to_operand_aliasing={{}: (11, {})} | custom-call | tf_op jit(solution)/shard_map/coarse/pallas_call | solution.py:560
Async XLA Ops:
  0.0 13.8 %copy-start = (bf16[768,256]{1,0:T(8,128)(2,1)S(1)}, bf16[768,256]{1,0:T(8,128)(2,1)}, u32[]{:S(2)}) copy-start(bf16[768,256]{1,0:T(8,128)(2,1)} %constant.43.clone.w2_ref) | copy-start | bytes 1179652
  0.0 13.8 %copy-start.1 = (bf16[768,256]{1,0:T(8,128)(2,1)S(1)}, bf16[768,256]{1,0:T(8,128)(2,1)}, u32[]{:S(2)}) copy-start(bf16[768,256]{1,0:T(8,128)(2,1)} %constant.42.clone.w1_ref) | copy-start | bytes 1179652
  6.5 15.5 %all-to-all-start = ((f32[32,8,128]{2,1,0:T(8,128)}), f32[32,8,128]{2,1,0:T(8,128)S(1)}, u32[]{:S(2)}, u32[]{:S(2)}) async-start(f32[32,8,128]{2,1,0:T(8,128)} %bitcast.4), calls=%async_computation | async-start | bytes 262144 | tf_op jit(solution)/shard_map/all_to_all | solution.py:581
  24.9 14.5 %all-to-all-start.1 = ((f32[32,16,128]{2,1,0:T(8,128)}), f32[32,16,128]{2,1,0:T(8,128)S(1)}, u32[]{:S(2)}, u32[]{:S(2)}) async-start(f32[32,16,128]{2,1,0:T(8,128)} %get-tuple-element.16), calls=%async_computation.1 | async-start | bytes 524288 | tf_op jit(solution)/shard_map/all_to_all | solution.py:583
  29.0 10.4 %copy-start.2 = (bf16[512,512]{1,0:T(8,128)(2,1)S(1)}, bf16[512,512]{1,0:T(8,128)(2,1)}, u32[]{:S(2)}) copy-start(bf16[512,512]{1,0:T(8,128)(2,1)} %constant.48.clone.wyl_ref) | copy-start | bytes 1572868
  29.0 10.4 %copy-start.3 = (bf16[512,512]{1,0:T(8,128)(2,1)S(1)}, bf16[512,512]{1,0:T(8,128)(2,1)}, u32[]{:S(2)}) copy-start(bf16[512,512]{1,0:T(8,128)(2,1)} %constant.47.clone.wyh_ref) | copy-start | bytes 1572868
  29.0 10.4 %copy-start.4 = (bf16[256,384]{1,0:T(8,128)(2,1)S(1)}, bf16[256,384]{1,0:T(8,128)(2,1)}, u32[]{:S(2)}) copy-start(bf16[256,384]{1,0:T(8,128)(2,1)} %constant.50.clone.w23l_ref) | copy-start | bytes 589828
  29.0 10.4 %copy-start.5 = (bf16[256,384]{1,0:T(8,128)(2,1)S(1)}, bf16[256,384]{1,0:T(8,128)(2,1)}, u32[]{:S(2)}) copy-start(bf16[256,384]{1,0:T(8,128)(2,1)} %constant.49.clone.w23h_ref) | copy-start | bytes 589828
  29.0 10.4 %copy-start.6 = (bf16[256,256]{1,0:T(8,128)(2,1)S(1)}, bf16[256,256]{1,0:T(8,128)(2,1)}, u32[]{:S(2)}) copy-start(bf16[256,256]{1,0:T(8,128)(2,1)} %constant.46.clone.wzl_ref) | copy-start | bytes 393220
  29.0 10.4 %copy-start.7 = (bf16[256,256]{1,0:T(8,128)(2,1)S(1)}, bf16[256,256]{1,0:T(8,128)(2,1)}, u32[]{:S(2)}) copy-start(bf16[256,256]{1,0:T(8,128)(2,1)} %constant.45.clone.wzh_ref) | copy-start | bytes 393220
  29.0 10.4 %copy-start.8 = (bf16[32,96]{1,0:T(8,128)(2,1)S(1)}, bf16[32,96]{1,0:T(8,128)(2,1)}, u32[]{:S(2)}) copy-start(bf16[32,96]{1,0:T(8,128)(2,1)} %constant.44.clone.wx_ref) | copy-start | bytes 18436
  29.1 10.4 %copy-start.9 = (bf16[16,48]{1,0:T(8,128)(2,1)S(1)}, bf16[16,48]{1,0:T(8,128)(2,1)}, u32[]{:S(2)}) copy-start(bf16[16,48]{1,0:T(8,128)(2,1)} %constant.52.clone.wx3_ref) | copy-start | bytes 4612
  29.1 10.4 %copy-start.10 = (bf16[16,48]{1,0:T(8,128)(2,1)S(1)}, bf16[16,48]{1,0:T(8,128)(2,1)}, u32[]{:S(2)}) copy-start(bf16[16,48]{1,0:T(8,128)(2,1)} %constant.51.clone.wx2_ref) | copy-start | bytes 4612

commit v11 on v10

--- a/solution.py
+++ b/solution.py
@@ -80,7 +80,7 @@
     for t in range(dst_ref.shape[2]):
         pltpu.make_async_copy(
             src_ref.at[:, :, pl.ds(t * 128, 128)], dst_ref.at[:, :, t, :], sems.at[t // 8]
-        ).start()
+        ).start(priority=t % 2)
 
 
 def wait_tiles(dst_ref, sems, group):
@@ -100,8 +100,8 @@
         pltpu.make_async_copy(src, dst, w_sems.at[i])
         for i, (src, dst) in enumerate(((wz_any, wz_ref), (wyh_any, wyh_ref), (wyl_any, wyl_ref)))
     ]
-    for copy in weights:
-        copy.start()
+    for i, copy in enumerate(weights):
+        copy.start(priority=i % 2)
     for g in range(4):
         wait_tiles(x_ref, sems, g)
 
@@ -171,9 +171,7 @@
     return pieces.reshape(2 * quarter, 8, 128), token
 
 
-def route_kernel(
-    me_ref, got_ref, _, send_any, index_ref, send_ref, order_ref, count_ref, sem, send_sem, *, width
-):
+def route_kernel(me_ref, got_ref, _, send_ref, index_ref, order_ref, count_ref, sem, *, width):
     devices = got_ref.shape[0]
     place = [d % width * (devices // width) + d // width for d in range(devices)]
     copy = pltpu.make_async_copy(got_ref.at[:, 7, :], count_ref, sem)
@@ -191,16 +189,9 @@
         start = start + count
     index_ref[0] = my_start % 8
     index_ref[1] = my_count
-    copies = []
-    for n, d in enumerate(sorted(range(devices), key=lambda d: place[d])):
+    for d in range(devices):
         at = pl.multiple_of(starts[d] // 8 * 8, 8) if d else 0
-        send_ref[n] = order_ref[pl.ds(at, 16), :]
-        if n % 8 == 7:
-            part = pl.ds(n - 7, 8)
-            copies.append(pltpu.make_async_copy(send_ref.at[part], send_any.at[part], send_sem.at[n // 8]))
-            copies[-1].start()
-    for copy in copies:
-        copy.wait()
+        send_ref[place[d]] = order_ref[pl.ds(at, 16), :]
 
 
 def route_call(me, got, token, slots, width):
@@ -212,17 +203,15 @@
             pl.BlockSpec(memory_space=pltpu.VMEM),
             pl.BlockSpec(memory_space=pltpu.SMEM),
         ],
-        out_specs=[pl.BlockSpec(memory_space=pl.ANY), pl.BlockSpec(memory_space=pltpu.SMEM)],
+        out_specs=[pl.BlockSpec(memory_space=pltpu.VMEM), pl.BlockSpec(memory_space=pltpu.SMEM)],
         out_shape=[
             jax.ShapeDtypeStruct((devices, 16, 128), F32),
             jax.ShapeDtypeStruct((2,), jnp.int32),
         ],
         scratch_shapes=[
-            pltpu.VMEM((devices, 16, 128), F32),
             pltpu.VMEM((devices * slots + 16, 128), F32),
             pltpu.SMEM((devices, 128), F32),
             pltpu.SemaphoreType.DMA,
-            pltpu.SemaphoreType.DMA((devices // 8,)),
         ],
         compiler_params=pltpu.CompilerParams(vmem_limit_bytes=VMEM_SMALL),
         name="route",
@@ -320,7 +309,7 @@
         for t in range(tiles):
             pltpu.make_async_copy(
                 x_any.at[which, :, pl.ds(t * 128, 128)], x_buf.at[place, :, t, :], sems.at[place]
-            ).start()
+            ).start(priority=t % 2)
 
     @pl.when((step == 0) & live)
     def _():
@@ -342,14 +331,16 @@
     @pl.when(live)
     def _():
         x = x_buf.at[step % 2]
-        for g in range(4):
-            rows = scaled_rows([x[i, pl.ds(8 * g, 8), :] for i in range(edge)])
-            store_terms(l_ref, (g % 2) * 8 * edge, (g // 2) * 128, rows)
+        @pl.loop(0, 4)
+        def _(g):
+            rows = scaled_rows([x[i, pl.ds(pl.multiple_of(8 * g, 8), 8), :] for i in range(edge)])
+            store_terms(l_ref, (g % 2) * 8 * edge, pl.multiple_of((g // 2) * 128, 128), rows)
+
         lifted = dot(l_ref[...], w1_ref[...])
         y_ref[0] = lifted[:, :128]
         y_ref[1] = lifted[:, 128:]
-        for r in range(edge // 8):
-            rows = pl.ds(8 * r, 8)
+        def second(r, deeper):
+            rows = pl.ds(pl.multiple_of(8 * r, 8), 8)
 
             def tile(part, j):
                 return y_ref[part, pl.ds((j // 8) * 8 * edge + 64 * r + j % 8, 8, stride=8), :]
@@ -363,11 +354,19 @@
                     at = part * pairs + t
                     out_ref[0, rows, pl.ds(at * 128, 128)] = a
                     out_ref[0, rows, pl.ds((at + pairs // 2) * 128, 128)] = b
-            if r < half // 8:
+            if deeper:
                 low, high = lift(*with_halo(low[0::2], low[1::2]), 8, True, False)
                 for i in range(8):
                     c_ref[pl.ds(64 * r + i, 8, stride=8), :] = low[i]
                     c_ref[pl.ds(corner + 64 * r + i, 8, stride=8), :] = high[i]
+
+        for deeper in (True, False):
+
+            @pl.loop(0, half // 16)
+            def _(q):
+                for u in range(2):
+                    second(2 * q + u + (0 if deeper else half // 8), deeper)
+
         for u in range(2):
             rows = scaled_rows([c_ref[pl.ds(u * corner + 8 * i, 8), :] for i in range(half)])
             store_terms(m_ref, 0, u * 128, rows)
@@ -463,7 +462,7 @@
         return jnp.concatenate([piece_ref[pl.ds(16 * h + i, 16, stride=32), :] for h in range(2)], 1)
 
     for s in range(slots):
-        pltpu.make_async_copy(window(s), corner_ref.at[s], corner_sem.at[s]).start()
+        pltpu.make_async_copy(window(s), corner_ref.at[s], corner_sem.at[s]).start(priority=s % 2)
 
     first = [
         [
@@ -525,7 +524,7 @@
                 old = corner_ref[s, :, pl.ds(t * 128, 128)]
                 new = jnp.where(lane < 16, near, jnp.where((lane >= 64) & (lane < 80), far, old))
                 corner_ref[s, :, pl.ds(t * 128, 128)] = new
-            pltpu.make_async_copy(corner_ref.at[s], window(s), out_sem.at[s]).start()
+            pltpu.make_async_copy(corner_ref.at[s], window(s), out_sem.at[s]).start(priority=s % 2)
 
     for s in range(slots):
 

time: 43.8 us -> 48 us (1.096)
  Pallas kernels: 29.2 us -> 33.3 us
  waiting for transfers between devices: 1.77 us -> 0.17 us
  starting transfers between devices: 11.4 us -> 13 us
    pallas_call x2, Pallas kernels: 16.6 us -> 21.3 us  [fine_call(): pl.pallas_call(functools.partial(fine_kernel, first=first), grid=(count,)...]
    all_to_all x1, waiting for transfers between devices: 1.74 us -> 0.17 us  [exchange(): got = lax.all_to_all(lowpass, SWAPPED, 0, 0, tiled=True)]
    all_to_all x1, starting transfers between devices: 4.11 us -> 5.68 us  [exchange(): return (lax.all_to_all(sent, SWAPPED, 0, 0, tiled=True), index)]
    pallas_call x1, Pallas kernels: 2.89 us -> 2.35 us  [route_call(): pl.pallas_call(functools.partial(route_kernel, width=width), in_specs=[pl...]
  transfers between devices with their start and end apart: 2 -> 2, of which waited for: 1 -> 1; matrix products, arithmetic and copies ran while one was open for 0% -> 0% of each run, Pallas kernels for 38% -> 45%
where the time goes in v11:
time: 48 us; the launch traced here: 47.5 us
  Pallas kernels  33.3 us (69%)
  starting transfers between devices  13 us (27%)
  between operations  0.95 us (2%)
    pallas_call x2, Pallas kernels, fine_call(): pl.pallas_call(functools.partial(fine_kernel, first=first), grid=(count,)...  21.3 us
    all_to_all x1, starting transfers between devices, exchange(): got = lax.all_to_all(lowpass, SWAPPED, 0, 0, tiled=True)  7.3 us
    pallas_call x1, Pallas kernels, lowpass_call(): pl.pallas_call(lowpass_kernel, in_specs=[pl.BlockSpec(memory_space=pltpu....  5.73 us
    all_to_all x1, starting transfers between devices, exchange(): return (lax.all_to_all(sent, SWAPPED, 0, 0, tiled=True), index)  5.68 us
    pallas_call x1, Pallas kernels, coarse_call(): pl.pallas_call(coarse_kernel, in_specs=[pl.BlockSpec(memory_space=pltpu.S...  3.9 us
    pallas_call x1, Pallas kernels, route_call(): pl.pallas_call(functools.partial(route_kernel, width=width), in_specs=[pl...  2.35 us
  transfers between devices with their start and end apart: 2, of which 1 were waited for; matrix products, arithmetic and copies ran while one was open for 0% of the time, Pallas kernels for 45%

profile of v11, /device:TPU:0, one launch (start us, length us, event | category | flops | bytes accessed | tf_op | source)
XLA Modules:
  0.0 47.5 jit_solution(17937390024643424944)
XLA Ops:
  0.0 0.0 copy-start
  0.0 0.0 copy-start.1
  0.7 5.7 %lowpass.1 = (f32[256,128]{1,0:T(8,128)}, s32[1]{0:T(128)}) custom-call(s32[1]{0:T(128)S(6)} %copy.23.count_ref, f32[6,64,4096]{2,1,0:T(8,128)} %x_any.5, bf16[512,256]{1,0:T(8,128)(2,1)} %constant.39.clone.wz_any, bf16[1024,256]{1,0:T(8,128)(2,1)} %constant.40.clone.wyh_any, bf16[1024,256]{1,0:T(8,128)(2,1)} %constant.41.clone.wyl_any), custom_call_target="tpu_custom_call" | custom-call | tf_op jit(solution)/shard_map/lowpass/pallas_call | solution.py:150
  6.5 7.3 %all-to-all-start = ((f32[32,8,128]{2,1,0:T(8,128)}), f32[32,8,128]{2,1,0:T(8,128)S(1)}, u32[]{:S(2)}, u32[]{:S(2)}) async-start(f32[32,8,128]{2,1,0:T(8,128)} %bitcast.4), calls=%async_computation | async-start | bytes 262144 | tf_op jit(solution)/shard_map/all_to_all | solution.py:580
  13.8 0.0 copy-done
  13.8 0.0 copy-done.1
  13.8 8.0 %fine.2 = (f32[6,64,4096]{2,1,0:T(8,128)}, s32[1]{0:T(128)}) custom-call(s32[1]{0:T(128)S(6)} %copy.23.count_ref, s32[1]{0:T(128)} %get-tuple-element.13._, f32[6,64,4096]{2,1,0:T(8,128)} %x_any.5, bf16[768,256]{1,0:T(8,128)(2,1)S(1)} %copy-done.1, bf16[768,256]{1,0:T(8,128)(2,1)S(1)} %copy-done), custom_call_target="tpu_custom_call" | custom-call | flops 805306368 | bytes 4194304 | tf_op jit(solution)/shard_map/fine/pallas_call | solution.py:409
  21.8 0.2 all-to-all-done.got_ref
  22.0 2.4 %route.1 = (f32[32,16,128]{2,1,0:T(8,128)}, s32[2]{0:T(128)S(1)}) custom-call(s32[1]{0:T(128)} %bitcast.me_ref, f32[32,8,128]{2,1,0:T(8,128)S(1)} %all-to-all-done.got_ref, s32[1]{0:T(128)} %get-tuple-element.14._), custom_call_target="tpu_custom_call" | custom-call | tf_op jit(solution)/shard_map/route/pallas_call | solution.py:199
  24.3 5.7 %all-to-all-start.1 = ((f32[32,16,128]{2,1,0:T(8,128)}), f32[32,16,128]{2,1,0:T(8,128)S(1)}, u32[]{:S(2)}, u32[]{:S(2)}) async-start(f32[32,16,128]{2,1,0:T(8,128)} %get-tuple-element.16), calls=%async_computation.1 | async-start | bytes 524288 | tf_op jit(solution)/shard_map/all_to_all | solution.py:582
  30.0 0.0 copy-start.2
  30.0 0.0 copy-start.3
  30.0 0.0 copy-start.4
  30.0 0.0 copy-start.5
  30.1 0.0 copy-start.6
  30.1 0.0 copy-start.7
  30.1 0.0 copy-start.8
  30.1 0.0 copy-start.9
  30.1 0.0 copy-start.10
  30.1 13.4 %fine.3 = (f32[6,64,4096]{2,1,0:T(8,128)}, s32[1]{0:T(128)}) custom-call(s32[1]{0:T(128)S(6)} %copy.23.count_ref, s32[2]{0:T(128)S(1)} %get-tuple-element.15._.index_ref, f32[6,64,4096]{2,1,0:T(8,128)} %x_any.5, bf16[768,256]{1,0:T(8,128)(2,1)S(1)} %copy-done.1, bf16[768,256]{1,0:T(8,128)(2,1)S(1)} %copy-done, ...), custom_call_target="tpu_custom_call", output_to_operand_aliasing={{0}: (5, {})} | custom-call | flops 1610612736 | bytes 8388608 | tf_op jit(solution)/shard_map/fine/pallas_call | solution.py:409
  43.5 0.0 all-to-all-done.1
  43.5 0.0 copy-done.2
  43.5 0.0 copy-done.3
  43.5 0.0 copy-done.4
  43.5 0.0 copy-done.5
  43.5 0.0 copy-done.6
  43.6 0.0 copy-done.7
  43.6 0.0 copy-done.8
  43.6 0.0 copy-done.9
  43.6 0.0 copy-done.10
  43.6 3.9 %coarse.1 = f32[6,64,4096]{2,1,0:T(8,128)} custom-call(s32[2]{0:T(128)S(1)} %get-tuple-element.15._.index_ref, f32[512,128]{1,0:T(8,128)S(1)} %bitcast.3, bf16[32,96]{1,0:T(8,128)(2,1)S(1)} %copy-done.8, bf16[256,256]{1,0:T(8,128)(2,1)S(1)} %copy-done.7, bf16[256,256]{1,0:T(8,128)(2,1)S(1)} %copy-done.6, ...), custom_call_target="tpu_custom_call", output_to_operand_aliasing={{}: (11, {})} | custom-call | tf_op jit(solution)/shard_map/coarse/pallas_call | solution.py:559
Async XLA Ops:
  0.0 13.8 %copy-start = (bf16[768,256]{1,0:T(8,128)(2,1)S(1)}, bf16[768,256]{1,0:T(8,128)(2,1)}, u32[]{:S(2)}) copy-start(bf16[768,256]{1,0:T(8,128)(2,1)} %constant.43.clone.w2_ref) | copy-start | bytes 1179652
  0.0 13.8 %copy-start.1 = (bf16[768,256]{1,0:T(8,128)(2,1)S(1)}, bf16[768,256]{1,0:T(8,128)(2,1)}, u32[]{:S(2)}) copy-start(bf16[768,256]{1,0:T(8,128)(2,1)} %constant.42.clone.w1_ref) | copy-start | bytes 1179652
  6.5 15.5 %all-to-all-start = ((f32[32,8,128]{2,1,0:T(8,128)}), f32[32,8,128]{2,1,0:T(8,128)S(1)}, u32[]{:S(2)}, u32[]{:S(2)}) async-start(f32[32,8,128]{2,1,0:T(8,128)} %bitcast.4), calls=%async_computation | async-start | bytes 262144 | tf_op jit(solution)/shard_map/all_to_all | solution.py:580
  24.3 19.2 %all-to-all-start.1 = ((f32[32,16,128]{2,1,0:T(8,128)}), f32[32,16,128]{2,1,0:T(8,128)S(1)}, u32[]{:S(2)}, u32[]{:S(2)}) async-start(f32[32,16,128]{2,1,0:T(8,128)} %get-tuple-element.16), calls=%async_computation.1 | async-start | bytes 524288 | tf_op jit(solution)/shard_map/all_to_all | solution.py:582
  30.0 13.5 %copy-start.2 = (bf16[512,512]{1,0:T(8,128)(2,1)S(1)}, bf16[512,512]{1,0:T(8,128)(2,1)}, u32[]{:S(2)}) copy-start(bf16[512,512]{1,0:T(8,128)(2,1)} %constant.48.clone.wyl_ref) | copy-start | bytes 1572868
  30.0 13.5 %copy-start.3 = (bf16[512,512]{1,0:T(8,128)(2,1)S(1)}, bf16[512,512]{1,0:T(8,128)(2,1)}, u32[]{:S(2)}) copy-start(bf16[512,512]{1,0:T(8,128)(2,1)} %constant.47.clone.wyh_ref) | copy-start | bytes 1572868
  30.0 13.5 %copy-start.4 = (bf16[256,384]{1,0:T(8,128)(2,1)S(1)}, bf16[256,384]{1,0:T(8,128)(2,1)}, u32[]{:S(2)}) copy-start(bf16[256,384]{1,0:T(8,128)(2,1)} %constant.50.clone.w23l_ref) | copy-start | bytes 589828
  30.0 13.5 %copy-start.5 = (bf16[256,384]{1,0:T(8,128)(2,1)S(1)}, bf16[256,384]{1,0:T(8,128)(2,1)}, u32[]{:S(2)}) copy-start(bf16[256,384]{1,0:T(8,128)(2,1)} %constant.49.clone.w23h_ref) | copy-start | bytes 589828
  30.1 13.5 %copy-start.6 = (bf16[256,256]{1,0:T(8,128)(2,1)S(1)}, bf16[256,256]{1,0:T(8,128)(2,1)}, u32[]{:S(2)}) copy-start(bf16[256,256]{1,0:T(8,128)(2,1)} %constant.46.clone.wzl_ref) | copy-start | bytes 393220
  30.1 13.5 %copy-start.7 = (bf16[256,256]{1,0:T(8,128)(2,1)S(1)}, bf16[256,256]{1,0:T(8,128)(2,1)}, u32[]{:S(2)}) copy-start(bf16[256,256]{1,0:T(8,128)(2,1)} %constant.45.clone.wzh_ref) | copy-start | bytes 393220
  30.1 13.5 %copy-start.8 = (bf16[32,96]{1,0:T(8,128)(2,1)S(1)}, bf16[32,96]{1,0:T(8,128)(2,1)}, u32[]{:S(2)}) copy-start(bf16[32,96]{1,0:T(8,128)(2,1)} %constant.44.clone.wx_ref) | copy-start | bytes 18436
  30.1 13.5 %copy-start.9 = (bf16[16,48]{1,0:T(8,128)(2,1)S(1)}, bf16[16,48]{1,0:T(8,128)(2,1)}, u32[]{:S(2)}) copy-start(bf16[16,48]{1,0:T(8,128)(2,1)} %constant.52.clone.wx3_ref) | copy-start | bytes 4612
  30.1 13.5 %copy-start.10 = (bf16[16,48]{1,0:T(8,128)(2,1)S(1)}, bf16[16,48]{1,0:T(8,128)(2,1)}, u32[]{:S(2)}) copy-start(bf16[16,48]{1,0:T(8,128)(2,1)} %constant.51.clone.wx2_ref) | copy-start | bytes 4612

commit v12 on v10

--- a/solution.py
+++ b/solution.py
@@ -105,8 +105,7 @@
     for g in range(4):
         wait_tiles(x_ref, sems, g)
 
-        @pl.loop(0, slots)
-        def _(s):
+        def first_dimension(s):
             rows = [x_ref[s, x, pl.ds(8 * g, 8), :] for x in range(edge)]
             rows, _ = lift(rows[0::2], rows[1::2], edge // 2, False, False)
             rows, _ = lift(rows[0::2], rows[1::2], quarter, False, False)
@@ -115,6 +114,13 @@
                 cols = pl.ds((g % 2) * 256 + (g // 2) * 128, 128)
                 l_ref[pl.ds(at, 16), cols] = high
                 l_ref[pl.ds(rows_all + at, 16), cols] = low
+
+        together = 3 if slots % 3 == 0 else 1
+
+        @pl.loop(0, slots // together)
+        def _(n):
+            for u in range(together):
+                first_dimension(n * together + u)
 
     for copy in weights:
         copy.wait()
@@ -171,9 +177,7 @@
     return pieces.reshape(2 * quarter, 8, 128), token
 
 
-def route_kernel(
-    me_ref, got_ref, _, send_any, index_ref, send_ref, order_ref, count_ref, sem, send_sem, *, width
-):
+def route_kernel(me_ref, got_ref, _, send_ref, index_ref, order_ref, count_ref, sem, *, width):
     devices = got_ref.shape[0]
     place = [d % width * (devices // width) + d // width for d in range(devices)]
     copy = pltpu.make_async_copy(got_ref.at[:, 7, :], count_ref, sem)
@@ -191,16 +195,9 @@
         start = start + count
     index_ref[0] = my_start % 8
     index_ref[1] = my_count
-    copies = []
-    for n, d in enumerate(sorted(range(devices), key=lambda d: place[d])):
+    for d in range(devices):
         at = pl.multiple_of(starts[d] // 8 * 8, 8) if d else 0
-        send_ref[n] = order_ref[pl.ds(at, 16), :]
-        if n % 8 == 7:
-            part = pl.ds(n - 7, 8)
-            copies.append(pltpu.make_async_copy(send_ref.at[part], send_any.at[part], send_sem.at[n // 8]))
-            copies[-1].start()
-    for copy in copies:
-        copy.wait()
+        send_ref[place[d]] = order_ref[pl.ds(at, 16), :]
 
 
 def route_call(me, got, token, slots, width):
@@ -212,17 +209,15 @@
             pl.BlockSpec(memory_space=pltpu.VMEM),
             pl.BlockSpec(memory_space=pltpu.SMEM),
         ],
-        out_specs=[pl.BlockSpec(memory_space=pl.ANY), pl.BlockSpec(memory_space=pltpu.SMEM)],
+        out_specs=[pl.BlockSpec(memory_space=pltpu.VMEM), pl.BlockSpec(memory_space=pltpu.SMEM)],
         out_shape=[
             jax.ShapeDtypeStruct((devices, 16, 128), F32),
             jax.ShapeDtypeStruct((2,), jnp.int32),
         ],
         scratch_shapes=[
-            pltpu.VMEM((devices, 16, 128), F32),
             pltpu.VMEM((devices * slots + 16, 128), F32),
             pltpu.SMEM((devices, 128), F32),
             pltpu.SemaphoreType.DMA,
-            pltpu.SemaphoreType.DMA((devices // 8,)),
         ],
         compiler_params=pltpu.CompilerParams(vmem_limit_bytes=VMEM_SMALL),
         name="route",
@@ -513,18 +508,19 @@
 
     for s in range(slots):
         pltpu.make_async_copy(window(s), corner_ref.at[s], corner_sem.at[s]).wait()
+    placed = (lane & 63) < 16
+    for s in range(slots):
+        value = block_ref[index_ref[0] + s]
+        for t in range(8):
+            tile = value[:, (t // 4) * 128 : (t // 4) * 128 + 128]
+            if t % 4:
+                tile = pltpu.roll(tile, 128 - 16 * (t % 4), 1)
+            cols = pl.ds(t * 128, 128)
+            corner_ref[s, :, cols] = jnp.where(placed, tile, corner_ref[s, :, cols])
     for s in range(slots):
 
         @pl.when(s < index_ref[1])
         def _():
-            value = block_ref[index_ref[0] + s]
-            for t in range(8):
-                tile = value[:, (t // 4) * 128 : (t // 4) * 128 + 128]
-                near = pltpu.roll(tile, (128 - 32 * (t % 4)) % 128, 1)
-                far = pltpu.roll(tile, (64 - 16 - 32 * (t % 4)) % 128, 1)
-                old = corner_ref[s, :, pl.ds(t * 128, 128)]
-                new = jnp.where(lane < 16, near, jnp.where((lane >= 64) & (lane < 80), far, old))
-                corner_ref[s, :, pl.ds(t * 128, 128)] = new
             pltpu.make_async_copy(corner_ref.at[s], window(s), out_sem.at[s]).start()
 
     for s in range(slots):
@@ -546,11 +542,13 @@
             wz[cz * 128 : cz * 128 + 128, tz * 128 : tz * 128 + 128] = np.kron(
                 eye8, m32[tz * 16 : tz * 16 + 16, cz * 16 : cz * 16 + 16].T
             )
-    w23 = np.concatenate([np.kron(m16.T, m16.T), np.kron(deep.T, deep.T)[:, :128]], 1)
+    lanes = np.arange(256).reshape(2, 4, 2, 16).transpose(0, 2, 1, 3).reshape(-1)
+    wy = np.kron(m32.T, eye16)[:, np.concatenate([lanes, 256 + lanes])]
+    w23 = np.concatenate([np.kron(m16.T, m16.T)[:, lanes], np.kron(deep.T, deep.T)[:, lanes[:128]]], 1)[lanes]
     weights = [
         left_terms(m32),
         *two_terms(wz),
-        *two_terms(np.kron(m32.T, eye16)),
+        *two_terms(wy),
         *two_terms(w23),
         left_terms(m16),
         left_terms(deep),

time: 43.8 us -> 42.8 us (0.977)
  Pallas kernels: 29.2 us -> 28.1 us
    pallas_call x1, Pallas kernels: 2.89 us -> 2.35 us  [route_call(): pl.pallas_call(functools.partial(route_kernel, width=width), in_specs=[pl...]
  transfers between devices with their start and end apart: 2 -> 2, of which waited for: 1 -> 1; matrix products, arithmetic and copies ran while one was open for 0% -> 0% of each run, Pallas kernels for 38% -> 39%
where the time goes in v12:
time: 42.8 us; the launch traced here: 42.3 us
  Pallas kernels  28.1 us (66%)
  starting transfers between devices  11.4 us (27%)
  waiting for transfers between devices  1.77 us (4%)
  between operations  0.93 us (2%)
    pallas_call x2, Pallas kernels, fine_call(): pl.pallas_call(functools.partial(fine_kernel, first=first), grid=(count,)...  16.6 us
    all_to_all x1, starting transfers between devices, exchange(): got = lax.all_to_all(lowpass, SWAPPED, 0, 0, tiled=True)  7.3 us
    pallas_call x1, Pallas kernels, lowpass_call(): pl.pallas_call(lowpass_kernel, in_specs=[pl.BlockSpec(memory_space=pltpu....  5.6 us
    all_to_all x1, starting transfers between devices, exchange(): return (lax.all_to_all(sent, SWAPPED, 0, 0, tiled=True), index)  4.11 us
    pallas_call x1, Pallas kernels, coarse_call(): pl.pallas_call(coarse_kernel, in_specs=[pl.BlockSpec(memory_space=pltpu.S...  3.55 us
    pallas_call x1, Pallas kernels, route_call(): pl.pallas_call(functools.partial(route_kernel, width=width), in_specs=[pl...  2.35 us
    all_to_all x1, waiting for transfers between devices, exchange(): got = lax.all_to_all(lowpass, SWAPPED, 0, 0, tiled=True)  1.74 us
  transfers between devices with their start and end apart: 2, of which 1 were waited for; matrix products, arithmetic and copies ran while one was open for 0% of the time, Pallas kernels for 39%

profile of v12, /device:TPU:0, one launch (start us, length us, event | category | flops | bytes accessed | tf_op | source)
XLA Modules:
  0.0 42.3 jit_solution(15257467692805189410)
XLA Ops:
  0.0 0.0 copy-start
  0.0 0.0 copy-start.1
  0.7 5.6 %lowpass.1 = (f32[256,128]{1,0:T(8,128)}, s32[1]{0:T(128)}) custom-call(s32[1]{0:T(128)S(6)} %copy.23.count_ref, f32[6,64,4096]{2,1,0:T(8,128)} %x_any.5, bf16[512,256]{1,0:T(8,128)(2,1)} %constant.39.clone.wz_any, bf16[1024,256]{1,0:T(8,128)(2,1)} %constant.40.clone.wyh_any, bf16[1024,256]{1,0:T(8,128)(2,1)} %constant.41.clone.wyl_any), custom_call_target="tpu_custom_call" | custom-call | tf_op jit(solution)/shard_map/lowpass/pallas_call | solution.py:156
  6.3 7.3 %all-to-all-start = ((f32[32,8,128]{2,1,0:T(8,128)}), f32[32,8,128]{2,1,0:T(8,128)S(1)}, u32[]{:S(2)}, u32[]{:S(2)}) async-start(f32[32,8,128]{2,1,0:T(8,128)} %bitcast.4), calls=%async_computation | async-start | bytes 262144 | tf_op jit(solution)/shard_map/all_to_all | solution.py:579
  13.7 0.0 copy-done
  13.7 0.0 copy-done.1
  13.7 6.4 %fine.2 = (f32[6,64,4096]{2,1,0:T(8,128)}, s32[1]{0:T(128)}) custom-call(s32[1]{0:T(128)S(6)} %copy.23.count_ref, s32[1]{0:T(128)} %get-tuple-element.13._, f32[6,64,4096]{2,1,0:T(8,128)} %x_any.5, bf16[768,256]{1,0:T(8,128)(2,1)S(1)} %copy-done.1, bf16[768,256]{1,0:T(8,128)(2,1)S(1)} %copy-done), custom_call_target="tpu_custom_call" | custom-call | flops 805306368 | bytes 4194304 | tf_op jit(solution)/shard_map/fine/pallas_call | solution.py:405
  20.1 1.7 %all-to-all-done.got_ref = f32[32,8,128]{2,1,0:T(8,128)S(1)} async-done(((f32[32,8,128]{2,1,0:T(8,128)}), f32[32,8,128]{2,1,0:T(8,128)S(1)}, u32[]{:S(2)}, u32[]{:S(2)}) %all-to-all-start) | async-done | bytes 131104 | tf_op jit(solution)/shard_map/all_to_all | solution.py:579
  21.8 2.4 %route.1 = (f32[32,16,128]{2,1,0:T(8,128)}, s32[2]{0:T(128)S(1)}) custom-call(s32[1]{0:T(128)} %bitcast.me_ref, f32[32,8,128]{2,1,0:T(8,128)S(1)} %all-to-all-done.got_ref, s32[1]{0:T(128)} %get-tuple-element.14._), custom_call_target="tpu_custom_call" | custom-call | tf_op jit(solution)/shard_map/route/pallas_call | solution.py:205
  24.2 4.1 %all-to-all-start.1 = ((f32[32,16,128]{2,1,0:T(8,128)}), f32[32,16,128]{2,1,0:T(8,128)S(1)}, u32[]{:S(2)}, u32[]{:S(2)}) async-start(f32[32,16,128]{2,1,0:T(8,128)} %get-tuple-element.16), calls=%async_computation.1 | async-start | bytes 524288 | tf_op jit(solution)/shard_map/all_to_all | solution.py:581
  28.3 0.0 copy-start.2
  28.3 0.0 copy-start.3
  28.3 0.0 copy-start.4
  28.3 0.0 copy-start.5
  28.3 0.0 copy-start.6
  28.4 0.0 copy-start.7
  28.4 0.0 copy-start.8
  28.4 0.0 copy-start.9
  28.4 0.0 copy-start.10
  28.4 10.2 %fine.3 = (f32[6,64,4096]{2,1,0:T(8,128)}, s32[1]{0:T(128)}) custom-call(s32[1]{0:T(128)S(6)} %copy.23.count_ref, s32[2]{0:T(128)S(1)} %get-tuple-element.15._.index_ref, f32[6,64,4096]{2,1,0:T(8,128)} %x_any.5, bf16[768,256]{1,0:T(8,128)(2,1)S(1)} %copy-done.1, bf16[768,256]{1,0:T(8,128)(2,1)S(1)} %copy-done, ...), custom_call_target="tpu_custom_call", output_to_operand_aliasing={{0}: (5, {})} | custom-call | flops 1610612736 | bytes 8388608 | tf_op jit(solution)/shard_map/fine/pallas_call | solution.py:405
  38.7 0.0 all-to-all-done.1
  38.7 0.0 copy-done.2
  38.7 0.0 copy-done.3
  38.7 0.0 copy-done.4
  38.7 0.0 copy-done.5
  38.7 0.0 copy-done.6
  38.7 0.0 copy-done.7
  38.7 0.0 copy-done.8
  38.7 0.0 copy-done.9
  38.7 0.0 copy-done.10
  38.8 3.6 %coarse.1 = f32[6,64,4096]{2,1,0:T(8,128)} custom-call(s32[2]{0:T(128)S(1)} %get-tuple-element.15._.index_ref, f32[512,128]{1,0:T(8,128)S(1)} %bitcast.3, bf16[32,96]{1,0:T(8,128)(2,1)S(1)} %copy-done.8, bf16[256,256]{1,0:T(8,128)(2,1)S(1)} %copy-done.7, bf16[256,256]{1,0:T(8,128)(2,1)S(1)} %copy-done.6, ...), custom_call_target="tpu_custom_call", output_to_operand_aliasing={{}: (11, {})} | custom-call | tf_op jit(solution)/shard_map/coarse/pallas_call | solution.py:558
Async XLA Ops:
  0.0 13.7 %copy-start = (bf16[768,256]{1,0:T(8,128)(2,1)S(1)}, bf16[768,256]{1,0:T(8,128)(2,1)}, u32[]{:S(2)}) copy-start(bf16[768,256]{1,0:T(8,128)(2,1)} %constant.43.clone.w2_ref) | copy-start | bytes 1179652
  0.0 13.7 %copy-start.1 = (bf16[768,256]{1,0:T(8,128)(2,1)S(1)}, bf16[768,256]{1,0:T(8,128)(2,1)}, u32[]{:S(2)}) copy-start(bf16[768,256]{1,0:T(8,128)(2,1)} %constant.42.clone.w1_ref) | copy-start | bytes 1179652
  6.3 15.5 %all-to-all-start = ((f32[32,8,128]{2,1,0:T(8,128)}), f32[32,8,128]{2,1,0:T(8,128)S(1)}, u32[]{:S(2)}, u32[]{:S(2)}) async-start(f32[32,8,128]{2,1,0:T(8,128)} %bitcast.4), calls=%async_computation | async-start | bytes 262144 | tf_op jit(solution)/shard_map/all_to_all | solution.py:579
  24.2 14.5 %all-to-all-start.1 = ((f32[32,16,128]{2,1,0:T(8,128)}), f32[32,16,128]{2,1,0:T(8,128)S(1)}, u32[]{:S(2)}, u32[]{:S(2)}) async-start(f32[32,16,128]{2,1,0:T(8,128)} %get-tuple-element.16), calls=%async_computation.1 | async-start | bytes 524288 | tf_op jit(solution)/shard_map/all_to_all | solution.py:581
  28.3 10.4 %copy-start.2 = (bf16[512,512]{1,0:T(8,128)(2,1)S(1)}, bf16[512,512]{1,0:T(8,128)(2,1)}, u32[]{:S(2)}) copy-start(bf16[512,512]{1,0:T(8,128)(2,1)} %constant.48.clone.wyl_ref) | copy-start | bytes 1572868
  28.3 10.4 %copy-start.3 = (bf16[512,512]{1,0:T(8,128)(2,1)S(1)}, bf16[512,512]{1,0:T(8,128)(2,1)}, u32[]{:S(2)}) copy-start(bf16[512,512]{1,0:T(8,128)(2,1)} %constant.47.clone.wyh_ref) | copy-start | bytes 1572868
  28.3 10.4 %copy-start.4 = (bf16[256,384]{1,0:T(8,128)(2,1)S(1)}, bf16[256,384]{1,0:T(8,128)(2,1)}, u32[]{:S(2)}) copy-start(bf16[256,384]{1,0:T(8,128)(2,1)} %constant.50.clone.w23l_ref) | copy-start | bytes 589828
  28.3 10.4 %copy-start.5 = (bf16[256,384]{1,0:T(8,128)(2,1)S(1)}, bf16[256,384]{1,0:T(8,128)(2,1)}, u32[]{:S(2)}) copy-start(bf16[256,384]{1,0:T(8,128)(2,1)} %constant.49.clone.w23h_ref) | copy-start | bytes 589828
  28.3 10.4 %copy-start.6 = (bf16[256,256]{1,0:T(8,128)(2,1)S(1)}, bf16[256,256]{1,0:T(8,128)(2,1)}, u32[]{:S(2)}) copy-start(bf16[256,256]{1,0:T(8,128)(2,1)} %constant.46.clone.wzl_ref) | copy-start | bytes 393220
  28.4 10.4 %copy-start.7 = (bf16[256,256]{1,0:T(8,128)(2,1)S(1)}, bf16[256,256]{1,0:T(8,128)(2,1)}, u32[]{:S(2)}) copy-start(bf16[256,256]{1,0:T(8,128)(2,1)} %constant.45.clone.wzh_ref) | copy-start | bytes 393220
  28.4 10.4 %copy-start.8 = (bf16[32,96]{1,0:T(8,128)(2,1)S(1)}, bf16[32,96]{1,0:T(8,128)(2,1)}, u32[]{:S(2)}) copy-start(bf16[32,96]{1,0:T(8,128)(2,1)} %constant.44.clone.wx_ref) | copy-start | bytes 18436
  28.4 10.4 %copy-start.9 = (bf16[16,48]{1,0:T(8,128)(2,1)S(1)}, bf16[16,48]{1,0:T(8,128)(2,1)}, u32[]{:S(2)}) copy-start(bf16[16,48]{1,0:T(8,128)(2,1)} %constant.52.clone.wx3_ref) | copy-start | bytes 4612
  28.4 10.3 %copy-start.10 = (bf16[16,48]{1,0:T(8,128)(2,1)S(1)}, bf16[16,48]{1,0:T(8,128)(2,1)}, u32[]{:S(2)}) copy-start(bf16[16,48]{1,0:T(8,128)(2,1)} %constant.51.clone.wx2_ref) | copy-start | bytes 4612

commit v13 on v12

--- a/solution.py
+++ b/solution.py
@@ -76,51 +76,50 @@
     return [split(jnp.concatenate(rows[m : m + 2], 0)) for m in range(0, len(rows), 2)]
 
 
-def start_tiles(src_ref, dst_ref, sems):
-    for t in range(dst_ref.shape[2]):
-        pltpu.make_async_copy(
-            src_ref.at[:, :, pl.ds(t * 128, 128)], dst_ref.at[:, :, t, :], sems.at[t // 8]
-        ).start()
-
-
-def wait_tiles(dst_ref, sems, group):
-    part = dst_ref.at[:, :, pl.ds(8 * group, 8), :]
-    pltpu.make_async_copy(part, part, sems.at[group]).wait()
+def tiled_view(density):
+    slots, edge, plane = density.shape
+    view = density.reshape(slots, edge // 8, 8, plane // 128, 128)
+    return jnp.transpose(view, (0, 1, 3, 2, 4))
+
+
+def tile_rows(ref, block, group, edge, tiles):
+    base = block * edge * tiles + 64 * group
+    return [ref[pl.ds(base + (x // 8) * 8 * tiles + x % 8, 8, stride=8), :] for x in range(edge)]
 
 
 def lowpass_kernel(
     count_ref, x_any, wz_any, wyh_any, wyl_any, out_ref, token_ref, x_ref, wz_ref, wyh_ref, wyl_ref, l_ref, z_ref, sems, w_sems
 ):
-    slots, edge = x_any.shape[:2]
+    slots, edge, tiles = x_any.shape[0], 8 * x_any.shape[1], x_any.shape[2]
     quarter = edge // 4
     rows_all = slots * 8 * quarter
     token_ref[0] = count_ref[0]
-    start_tiles(x_any, x_ref, sems)
+    blocks = [
+        pltpu.make_async_copy(x_any.at[n], x_ref.at[n], sems.at[n]) for n in range(slots)
+    ]
+    for copy in blocks:
+        copy.start()
+    flat = x_ref.reshape(slots * edge * tiles, 128)
     weights = [
         pltpu.make_async_copy(src, dst, w_sems.at[i])
         for i, (src, dst) in enumerate(((wz_any, wz_ref), (wyh_any, wyh_ref), (wyl_any, wyl_ref)))
     ]
     for copy in weights:
         copy.start()
-    for g in range(4):
-        wait_tiles(x_ref, sems, g)
-
-        def first_dimension(s):
-            rows = [x_ref[s, x, pl.ds(8 * g, 8), :] for x in range(edge)]
-            rows, _ = lift(rows[0::2], rows[1::2], edge // 2, False, False)
-            rows, _ = lift(rows[0::2], rows[1::2], quarter, False, False)
-            for m, (high, low) in enumerate(split_rows(rows)):
-                at = pl.multiple_of(s * 8 * quarter + 16 * m, 16)
-                cols = pl.ds((g % 2) * 256 + (g // 2) * 128, 128)
-                l_ref[pl.ds(at, 16), cols] = high
-                l_ref[pl.ds(rows_all + at, 16), cols] = low
-
-        together = 3 if slots % 3 == 0 else 1
-
-        @pl.loop(0, slots // together)
-        def _(n):
-            for u in range(together):
-                first_dimension(n * together + u)
+    for s in range(slots):
+        blocks[s].wait()
+
+        @pl.loop(0, 2)
+        def _(q):
+            for u in range(2):
+                rows = tile_rows(flat, s, 2 * q + u, edge, tiles)
+                rows, _ = lift(rows[0::2], rows[1::2], edge // 2, False, False)
+                rows, _ = lift(rows[0::2], rows[1::2], quarter, False, False)
+                for m, (high, low) in enumerate(split_rows(rows)):
+                    at = s * 8 * quarter + 16 * m
+                    cols = pl.ds(pl.multiple_of(u * 256 + q * 128, 128), 128)
+                    l_ref[pl.ds(at, 16), cols] = high
+                    l_ref[pl.ds(rows_all + at, 16), cols] = low
 
     for copy in weights:
         copy.wait()
@@ -162,18 +161,18 @@
             jax.ShapeDtypeStruct((1,), jnp.int32),
         ],
         scratch_shapes=[
-            pltpu.VMEM((slots, edge, plane // 128, 128), F32),
+            pltpu.VMEM((slots, edge // 8, plane // 128, 8, 128), F32),
             pltpu.VMEM(wz.shape, BF16),
             pltpu.VMEM(wyh.shape, BF16),
             pltpu.VMEM(wyl.shape, BF16),
             pltpu.VMEM((2 * rows_all, 512), BF16),
             pltpu.VMEM((rows_all, 128), F32),
-            pltpu.SemaphoreType.DMA((4,)),
+            pltpu.SemaphoreType.DMA((slots,)),
             pltpu.SemaphoreType.DMA((3,)),
         ],
         compiler_params=pltpu.CompilerParams(vmem_limit_bytes=VMEM_LARGE),
         name="lowpass",
-    )(owner_counts, density, wz, wyh, wyl)
+    )(owner_counts, tiled_view(density), wz, wyh, wyl)
     return pieces.reshape(2 * quarter, 8, 128), token
 
 
@@ -274,8 +273,7 @@
     out_ref, token_ref, x_buf, l_ref, y_ref, c_ref, m_ref, d_ref, sems = refs[-9:]
     step = pl.program_id(0)
     slot = step + first
-    edge = x_any.shape[1]
-    tiles = x_buf.shape[2]
+    edge, tiles = 8 * x_any.shape[1], x_any.shape[2]
     pairs = tiles // 2
     half = edge // 2
     corner = 8 * half
@@ -312,14 +310,11 @@
             ref[place, pl.ds(512 + col, 128)] = high
 
     def fetch(which, place):
-        for t in range(tiles):
-            pltpu.make_async_copy(
-                x_any.at[which, :, pl.ds(t * 128, 128)], x_buf.at[place, :, t, :], sems.at[place]
-            ).start()
+        return pltpu.make_async_copy(x_any.at[which], x_buf.at[place], sems.at[place])
 
     @pl.when((step == 0) & live)
     def _():
-        fetch(slot, 0)
+        fetch(slot, 0).start()
 
     @pl.when(jnp.logical_not(live))
     def _():
@@ -327,18 +322,17 @@
 
     @pl.when(live)
     def _():
-        x = x_buf.at[step % 2]
-        pltpu.make_async_copy(x, x, sems.at[step % 2]).wait()
+        fetch(slot, step % 2).wait()
 
     @pl.when((step + 1 < pl.num_programs(0)) & (slot + 1 < count_ref[0]))
     def _():
-        fetch(slot + 1, (step + 1) % 2)
+        fetch(slot + 1, (step + 1) % 2).start()
 
     @pl.when(live)
     def _():
-        x = x_buf.at[step % 2]
+        flat = x_buf.reshape(2 * edge * tiles, 128)
         for g in range(4):
-            rows = scaled_rows([x[i, pl.ds(8 * g, 8), :] for i in range(edge)])
+            rows = scaled_rows(tile_rows(flat, step % 2, g, edge, tiles))
             store_terms(l_ref, (g % 2) * 8 * edge, (g // 2) * 128, rows)
         lifted = dot(l_ref[...], w1_ref[...])
         y_ref[0] = lifted[:, :128]
@@ -412,7 +406,7 @@
             jax.ShapeDtypeStruct((1,), jnp.int32),
         ],
         scratch_shapes=[
-            pltpu.VMEM((2, edge, tiles, 128), F32),
+            pltpu.VMEM((2, edge // 8, tiles, 8, 128), F32),
             pltpu.VMEM((pairs * edge, 768), BF16),
             pltpu.VMEM((2, pairs * edge, 128), F32),
             pltpu.VMEM((16 * half, 128), F32),
@@ -426,7 +420,7 @@
             flops=6 * count * edge * plane * 256, bytes_accessed=2 * count * MIB, transcendentals=0
         ),
         name="fine",
-    )(owner_counts, token, density, stacked(w1), stacked(w2), *old)
+    )(owner_counts, token, tiled_view(density), stacked(w1), stacked(w2), *old)
 
 
 def coarse_kernel(

time: 42.8 us -> 42.7 us (level)
  transfers between devices with their start and end apart: 2 -> 2, of which waited for: 1 -> 2; matrix products, arithmetic and copies ran while one was open for 0% -> 0% of each run, Pallas kernels for 39% -> 39%
where the time goes in v13:
time: 42.7 us; the launch traced here: 42.4 us
  Pallas kernels  28.1 us (66%)
  starting transfers between devices  11.4 us (27%)
  waiting for transfers between devices  1.89 us (4%)
  between operations  0.92 us (2%)
    pallas_call x2, Pallas kernels, fine_call(): pl.pallas_call(functools.partial(fine_kernel, first=first), grid=(count,)...  16.5 us
    all_to_all x1, starting transfers between devices, exchange(): got = lax.all_to_all(lowpass, SWAPPED, 0, 0, tiled=True)  7.3 us
    pallas_call x1, Pallas kernels, lowpass_call(): pl.pallas_call(lowpass_kernel, in_specs=[pl.BlockSpec(memory_space=pltpu....  5.64 us
    all_to_all x1, starting transfers between devices, exchange(): return (lax.all_to_all(sent, SWAPPED, 0, 0, tiled=True), index)  4.13 us
    pallas_call x1, Pallas kernels, coarse_call(): pl.pallas_call(coarse_kernel, in_specs=[pl.BlockSpec(memory_space=pltpu.S...  3.55 us
    pallas_call x1, Pallas kernels, route_call(): pl.pallas_call(functools.partial(route_kernel, width=width), in_specs=[pl...  2.35 us
    all_to_all x1, waiting for transfers between devices, exchange(): got = lax.all_to_all(lowpass, SWAPPED, 0, 0, tiled=True)  1.72 us
  transfers between devices with their start and end apart: 2, of which 2 were waited for; matrix products, arithmetic and copies ran while one was open for 0% of the time, Pallas kernels for 39%

profile of v13, /device:TPU:0, one launch (start us, length us, event | category | flops | bytes accessed | tf_op | source)
XLA Modules:
  0.0 42.4 jit_solution(9000678080748676255)
XLA Ops:
  0.0 0.0 copy-start
  0.0 0.0 copy-start.1
  0.7 5.6 %lowpass.1 = (f32[256,128]{1,0:T(8,128)}, s32[1]{0:T(128)}) custom-call(s32[1]{0:T(128)S(6)} %copy.23.count_ref, f32[6,8,32,8,128]{4,3,2,1,0:T(8,128)} %bitcast.7, bf16[512,256]{1,0:T(8,128)(2,1)} %constant.39.clone.wz_any, bf16[1024,256]{1,0:T(8,128)(2,1)} %constant.40.clone.wyh_any, bf16[1024,256]{1,0:T(8,128)(2,1)} %constant.41.clone.wyl_any), custom_call_target="tpu_custom_call" | custom-call | tf_op jit(solution)/shard_map/lowpass/pallas_call | solution.py:155
  6.4 7.3 %all-to-all-start = ((f32[32,8,128]{2,1,0:T(8,128)}), f32[32,8,128]{2,1,0:T(8,128)S(1)}, u32[]{:S(2)}, u32[]{:S(2)}) async-start(f32[32,8,128]{2,1,0:T(8,128)} %bitcast.10), calls=%async_computation | async-start | bytes 262144 | tf_op jit(solution)/shard_map/all_to_all | solution.py:573
  13.7 0.0 copy-done
  13.7 0.0 copy-done.1
  13.7 6.4 %fine.2 = (f32[6,64,4096]{2,1,0:T(8,128)}, s32[1]{0:T(128)}) custom-call(s32[1]{0:T(128)S(6)} %copy.23.count_ref, s32[1]{0:T(128)} %get-tuple-element.13._, f32[6,8,32,8,128]{4,3,2,1,0:T(8,128)} %bitcast.8, bf16[768,256]{1,0:T(8,128)(2,1)S(1)} %copy-done.1, bf16[768,256]{1,0:T(8,128)(2,1)S(1)} %copy-done), custom_call_target="tpu_custom_call" | custom-call | flops 805306368 | bytes 4194304 | tf_op jit(solution)/shard_map/fine/pallas_call | solution.py:399
  20.2 1.7 %all-to-all-done.got_ref = f32[32,8,128]{2,1,0:T(8,128)S(1)} async-done(((f32[32,8,128]{2,1,0:T(8,128)}), f32[32,8,128]{2,1,0:T(8,128)S(1)}, u32[]{:S(2)}, u32[]{:S(2)}) %all-to-all-start) | async-done | bytes 131104 | tf_op jit(solution)/shard_map/all_to_all | solution.py:573
  21.9 2.4 %route.1 = (f32[32,16,128]{2,1,0:T(8,128)}, s32[2]{0:T(128)S(1)}) custom-call(s32[1]{0:T(128)} %bitcast.me_ref, f32[32,8,128]{2,1,0:T(8,128)S(1)} %all-to-all-done.got_ref, s32[1]{0:T(128)} %get-tuple-element.14._), custom_call_target="tpu_custom_call" | custom-call | tf_op jit(solution)/shard_map/route/pallas_call | solution.py:204
  24.2 4.1 %all-to-all-start.1 = ((f32[32,16,128]{2,1,0:T(8,128)}), f32[32,16,128]{2,1,0:T(8,128)S(1)}, u32[]{:S(2)}, u32[]{:S(2)}) async-start(f32[32,16,128]{2,1,0:T(8,128)} %get-tuple-element.16), calls=%async_computation.1 | async-start | bytes 524288 | tf_op jit(solution)/shard_map/all_to_all | solution.py:575
  28.4 0.0 copy-start.2
  28.4 0.0 copy-start.3
  28.4 0.0 copy-start.4
  28.4 0.0 copy-start.5
  28.4 0.0 copy-start.6
  28.4 0.0 copy-start.7
  28.4 0.0 copy-start.8
  28.5 0.0 copy-start.9
  28.5 0.0 copy-start.10
  28.5 10.1 %fine.3 = (f32[6,64,4096]{2,1,0:T(8,128)}, s32[1]{0:T(128)}) custom-call(s32[1]{0:T(128)S(6)} %copy.23.count_ref, s32[2]{0:T(128)S(1)} %get-tuple-element.15._.index_ref, f32[6,8,32,8,128]{4,3,2,1,0:T(8,128)} %bitcast.9, bf16[768,256]{1,0:T(8,128)(2,1)S(1)} %copy-done.1, bf16[768,256]{1,0:T(8,128)(2,1)S(1)} %copy-done, ...), custom_call_target="tpu_custom_call", output_to_operand_aliasing={{0}: (5, {})} | custom-call | flops 1610612736 | bytes 8388608 | tf_op jit(solution)/shard_map/fine/pallas_call | solution.py:399
  38.6 0.2 all-to-all-done.1
  38.8 0.0 copy-done.2
  38.8 0.0 copy-done.3
  38.8 0.0 copy-done.4
  38.8 0.0 copy-done.5
  38.8 0.0 copy-done.6
  38.8 0.0 copy-done.7
  38.8 0.0 copy-done.8
  38.8 0.0 copy-done.9
  38.8 0.0 copy-done.10
  38.8 3.6 %coarse.1 = f32[6,64,4096]{2,1,0:T(8,128)} custom-call(s32[2]{0:T(128)S(1)} %get-tuple-element.15._.index_ref, f32[512,128]{1,0:T(8,128)S(1)} %bitcast.6, bf16[32,96]{1,0:T(8,128)(2,1)S(1)} %copy-done.8, bf16[256,256]{1,0:T(8,128)(2,1)S(1)} %copy-done.7, bf16[256,256]{1,0:T(8,128)(2,1)S(1)} %copy-done.6, ...), custom_call_target="tpu_custom_call", output_to_operand_aliasing={{}: (11, {})} | custom-call | tf_op jit(solution)/shard_map/coarse/pallas_call | solution.py:552
Async XLA Ops:
  0.0 13.7 %copy-start = (bf16[768,256]{1,0:T(8,128)(2,1)S(1)}, bf16[768,256]{1,0:T(8,128)(2,1)}, u32[]{:S(2)}) copy-start(bf16[768,256]{1,0:T(8,128)(2,1)} %constant.43.clone.w2_ref) | copy-start | bytes 1179652
  0.0 13.7 %copy-start.1 = (bf16[768,256]{1,0:T(8,128)(2,1)S(1)}, bf16[768,256]{1,0:T(8,128)(2,1)}, u32[]{:S(2)}) copy-start(bf16[768,256]{1,0:T(8,128)(2,1)} %constant.42.clone.w1_ref) | copy-start | bytes 1179652
  6.4 15.5 %all-to-all-start = ((f32[32,8,128]{2,1,0:T(8,128)}), f32[32,8,128]{2,1,0:T(8,128)S(1)}, u32[]{:S(2)}, u32[]{:S(2)}) async-start(f32[32,8,128]{2,1,0:T(8,128)} %bitcast.10), calls=%async_computation | async-start | bytes 262144 | tf_op jit(solution)/shard_map/all_to_all | solution.py:573
  24.2 14.5 %all-to-all-start.1 = ((f32[32,16,128]{2,1,0:T(8,128)}), f32[32,16,128]{2,1,0:T(8,128)S(1)}, u32[]{:S(2)}, u32[]{:S(2)}) async-start(f32[32,16,128]{2,1,0:T(8,128)} %get-tuple-element.16), calls=%async_computation.1 | async-start | bytes 524288 | tf_op jit(solution)/shard_map/all_to_all | solution.py:575
  28.4 10.4 %copy-start.2 = (bf16[512,512]{1,0:T(8,128)(2,1)S(1)}, bf16[512,512]{1,0:T(8,128)(2,1)}, u32[]{:S(2)}) copy-start(bf16[512,512]{1,0:T(8,128)(2,1)} %constant.48.clone.wyl_ref) | copy-start | bytes 1572868
  28.4 10.4 %copy-start.3 = (bf16[512,512]{1,0:T(8,128)(2,1)S(1)}, bf16[512,512]{1,0:T(8,128)(2,1)}, u32[]{:S(2)}) copy-start(bf16[512,512]{1,0:T(8,128)(2,1)} %constant.47.clone.wyh_ref) | copy-start | bytes 1572868
  28.4 10.4 %copy-start.4 = (bf16[256,384]{1,0:T(8,128)(2,1)S(1)}, bf16[256,384]{1,0:T(8,128)(2,1)}, u32[]{:S(2)}) copy-start(bf16[256,384]{1,0:T(8,128)(2,1)} %constant.50.clone.w23l_ref) | copy-start | bytes 589828
  28.4 10.4 %copy-start.5 = (bf16[256,384]{1,0:T(8,128)(2,1)S(1)}, bf16[256,384]{1,0:T(8,128)(2,1)}, u32[]{:S(2)}) copy-start(bf16[256,384]{1,0:T(8,128)(2,1)} %constant.49.clone.w23h_ref) | copy-start | bytes 589828
  28.4 10.4 %copy-start.6 = (bf16[256,256]{1,0:T(8,128)(2,1)S(1)}, bf16[256,256]{1,0:T(8,128)(2,1)}, u32[]{:S(2)}) copy-start(bf16[256,256]{1,0:T(8,128)(2,1)} %constant.46.clone.wzl_ref) | copy-start | bytes 393220
  28.4 10.4 %copy-start.7 = (bf16[256,256]{1,0:T(8,128)(2,1)S(1)}, bf16[256,256]{1,0:T(8,128)(2,1)}, u32[]{:S(2)}) copy-start(bf16[256,256]{1,0:T(8,128)(2,1)} %constant.45.clone.wzh_ref) | copy-start | bytes 393220
  28.4 10.4 %copy-start.8 = (bf16[32,96]{1,0:T(8,128)(2,1)S(1)}, bf16[32,96]{1,0:T(8,128)(2,1)}, u32[]{:S(2)}) copy-start(bf16[32,96]{1,0:T(8,128)(2,1)} %constant.44.clone.wx_ref) | copy-start | bytes 18436
  28.5 10.3 %copy-start.9 = (bf16[16,48]{1,0:T(8,128)(2,1)S(1)}, bf16[16,48]{1,0:T(8,128)(2,1)}, u32[]{:S(2)}) copy-start(bf16[16,48]{1,0:T(8,128)(2,1)} %constant.52.clone.wx3_ref) | copy-start | bytes 4612
  28.5 10.3 %copy-start.10 = (bf16[16,48]{1,0:T(8,128)(2,1)S(1)}, bf16[16,48]{1,0:T(8,128)(2,1)}, u32[]{:S(2)}) copy-start(bf16[16,48]{1,0:T(8,128)(2,1)} %constant.51.clone.wx2_ref) | copy-start | bytes 4612

commit v14 on v13

--- a/solution.py
+++ b/solution.py
@@ -40,36 +40,44 @@
     return np.concatenate([low / SCALE, high * SCALE], 0)
 
 
-def two_terms(matrix):
-    matrix = np.asarray(matrix, np.float32)
-    first = matrix.astype(BF16)
-    return first, (matrix - first.astype(np.float32)).astype(BF16)
+def three_terms(matrix):
+    rest = np.asarray(matrix, np.float32)
+    terms = []
+    for _ in range(3):
+        terms.append(rest.astype(BF16))
+        rest = rest - terms[-1].astype(np.float32)
+    return terms
 
 
 def left_terms(matrix):
-    first, second = two_terms(matrix)
-    return np.concatenate([first, second, first], 1)
+    first, second, third = three_terms(matrix)
+    return np.concatenate([first, first, first, second, second, third], 1)
 
 
 def split(value):
-    first = value.astype(BF16)
-    return first, (value - first.astype(F32)).astype(BF16)
+    terms = []
+    for _ in range(3):
+        terms.append(value.astype(BF16))
+        value = value - terms[-1].astype(F32)
+    return terms
 
 
 def dot(left, right):
     return jnp.dot(left, right, preferred_element_type=F32)
 
 
-def times(value, first, second):
-    high, low = split(value)
-    both = dot(jnp.concatenate([high, low], 0), first)
+def times(value, first, second, third):
+    high, middle, low = split(value)
     count = value.shape[0]
-    return both[:count] + both[count:] + dot(high, second)
+    one = dot(jnp.concatenate([high, middle, low], 0), first)
+    two = dot(jnp.concatenate([high, middle], 0), second)
+    small = (one[2 * count :] + two[count:]) + dot(high, third)
+    return one[:count] + ((one[count : 2 * count] + two[:count]) + small)
 
 
 def times_left(terms, value):
-    high, low = split(value)
-    return dot(terms, jnp.concatenate([high, high, low], 0))
+    high, middle, low = split(value)
+    return dot(terms, jnp.concatenate([high, middle, low, high, middle, high], 0))
 
 
 def split_rows(rows):
@@ -88,7 +96,7 @@
 
 
 def lowpass_kernel(
-    count_ref, x_any, wz_any, wyh_any, wyl_any, out_ref, token_ref, x_ref, wz_ref, wyh_ref, wyl_ref, l_ref, z_ref, sems, w_sems
+    count_ref, x_any, wz_any, wy_any, out_ref, token_ref, x_ref, wz_ref, wy_ref, l_ref, z_ref, sems, w_sems
 ):
     slots, edge, tiles = x_any.shape[0], 8 * x_any.shape[1], x_any.shape[2]
     quarter = edge // 4
@@ -102,7 +110,7 @@
     flat = x_ref.reshape(slots * edge * tiles, 128)
     weights = [
         pltpu.make_async_copy(src, dst, w_sems.at[i])
-        for i, (src, dst) in enumerate(((wz_any, wz_ref), (wyh_any, wyh_ref), (wyl_any, wyl_ref)))
+        for i, (src, dst) in enumerate(((wz_any, wz_ref), (wy_any, wy_ref)))
     ]
     for copy in weights:
         copy.start()
@@ -115,18 +123,22 @@
                 rows = tile_rows(flat, s, 2 * q + u, edge, tiles)
                 rows, _ = lift(rows[0::2], rows[1::2], edge // 2, False, False)
                 rows, _ = lift(rows[0::2], rows[1::2], quarter, False, False)
-                for m, (high, low) in enumerate(split_rows(rows)):
-                    at = s * 8 * quarter + 16 * m
+                for m, terms in enumerate(split_rows(rows)):
                     cols = pl.ds(pl.multiple_of(u * 256 + q * 128, 128), 128)
-                    l_ref[pl.ds(at, 16), cols] = high
-                    l_ref[pl.ds(rows_all + at, 16), cols] = low
+                    for n, term in enumerate(terms):
+                        l_ref[pl.ds(n * rows_all + s * 8 * quarter + 16 * m, 16), cols] = term
 
     for copy in weights:
         copy.wait()
-    made = dot(l_ref[...], wz_ref[...])
-    z_ref[...] = (made[:rows_all, :128] + made[rows_all:, :128]) + made[:rows_all, 128:]
+    made = dot(l_ref[...], wz_ref[:, :256])
+    small = (made[2 * rows_all :, :128] + made[rows_all : 2 * rows_all, 128:]) + dot(
+        l_ref[pl.ds(0, rows_all), :], wz_ref[:, 256:]
+    )
+    z_ref[...] = made[:rows_all, :128] + (
+        (made[rows_all : 2 * rows_all, :128] + made[:rows_all, 128:]) + small
+    )
     wide = jnp.concatenate([z_ref[pl.ds(i, slots * quarter, stride=8), :] for i in range(8)], 1)
-    made = times(wide, wyh_ref[...], wyl_ref[...])
+    made = times(wide, wy_ref[0], wy_ref[1], wy_ref[2])
     out_ref[...] = jnp.full(out_ref.shape, count_ref[0].astype(F32))
     for slot in range(slots):
         for h in range(2):
@@ -135,26 +147,25 @@
             ]
 
 
-def stacked(matrix):
-    first, second = two_terms(matrix)
-    return np.concatenate([first, first, second], 0)
+def triple(matrix):
+    return np.stack([np.concatenate([term] * 3, 0) for term in three_terms(matrix)])
 
 
 def lowpass_call(owner_counts, density):
     slots, edge, plane = density.shape
     quarter = edge // 4
     two_levels = pass_matrix(edge // 2)[:quarter] @ pass_matrix(edge)[: edge // 2]
-    wz = np.concatenate(two_terms(np.kron(np.eye(8), two_levels.T)), 1)
+    wz = np.concatenate(three_terms(np.kron(np.eye(8), two_levels.T)), 1)
     i, gp, q, p = np.meshgrid(np.arange(8), np.arange(2), np.arange(2), np.arange(2), indexing="ij")
     entry = (2 * (8 * gp + i) + p + 32 * q).reshape(-1)
     wy = np.kron(two_levels.T[entry] / SQUARE, np.eye(quarter))
-    wyh, wyl = two_terms(wy)
+    wy = np.stack(three_terms(wy))
     anywhere = pl.BlockSpec(memory_space=pl.ANY)
     vmem = pl.BlockSpec(memory_space=pltpu.VMEM)
     rows_all = slots * 8 * quarter
     pieces, token = pl.pallas_call(
         lowpass_kernel,
-        in_specs=[pl.BlockSpec(memory_space=pltpu.SMEM)] + [anywhere] * 4,
+        in_specs=[pl.BlockSpec(memory_space=pltpu.SMEM)] + [anywhere] * 3,
         out_specs=[vmem, pl.BlockSpec(memory_space=pltpu.SMEM)],
         out_shape=[
             jax.ShapeDtypeStruct((16 * quarter, 128), F32),
@@ -163,16 +174,15 @@
         scratch_shapes=[
             pltpu.VMEM((slots, edge // 8, plane // 128, 8, 128), F32),
             pltpu.VMEM(wz.shape, BF16),
-            pltpu.VMEM(wyh.shape, BF16),
-            pltpu.VMEM(wyl.shape, BF16),
-            pltpu.VMEM((2 * rows_all, 512), BF16),
+            pltpu.VMEM(wy.shape, BF16),
+            pltpu.VMEM((3 * rows_all, 512), BF16),
             pltpu.VMEM((rows_all, 128), F32),
             pltpu.SemaphoreType.DMA((slots,)),
-            pltpu.SemaphoreType.DMA((3,)),
+            pltpu.SemaphoreType.DMA((2,)),
         ],
         compiler_params=pltpu.CompilerParams(vmem_limit_bytes=VMEM_LARGE),
         name="lowpass",
-    )(owner_counts, tiled_view(density), wz, wyh, wyl)
+    )(owner_counts, tiled_view(density), wz, wy)
     return pieces.reshape(2 * quarter, 8, 128), token
 
 
@@ -303,11 +313,10 @@
         return [v * (1.0 / SCALE) for v in low] + [v * SCALE for v in high]
 
     def store_terms(ref, row, col, rows):
-        for m, (high, low) in enumerate(split_rows(rows)):
+        for m, terms in enumerate(split_rows(rows)):
             place = pl.ds(pl.multiple_of(row + 16 * m, 16), 16)
-            ref[place, pl.ds(col, 128)] = high
-            ref[place, pl.ds(256 + col, 128)] = low
-            ref[place, pl.ds(512 + col, 128)] = high
+            for n, term in enumerate(terms):
+                ref[place, pl.ds(256 * n + col, 128)] = term
 
     def fetch(which, place):
         return pltpu.make_async_copy(x_any.at[which], x_buf.at[place], sems.at[place])
@@ -334,7 +343,8 @@
         for g in range(4):
             rows = scaled_rows(tile_rows(flat, step % 2, g, edge, tiles))
             store_terms(l_ref, (g % 2) * 8 * edge, (g // 2) * 128, rows)
-        lifted = dot(l_ref[...], w1_ref[...])
+        lifted = dot(l_ref[...], w1_ref[0]) + dot(l_ref[:, :512], w1_ref[1, :512])
+        lifted += dot(l_ref[:, :256], w1_ref[2, :256])
         y_ref[0] = lifted[:, :128]
         y_ref[1] = lifted[:, 128:]
         for r in range(edge // 8):
@@ -360,7 +370,8 @@
         for u in range(2):
             rows = scaled_rows([c_ref[pl.ds(u * corner + 8 * i, 8), :] for i in range(half)])
             store_terms(m_ref, 0, u * 128, rows)
-        lifted = dot(m_ref[...], w2_ref[...])
+        lifted = dot(m_ref[...], w2_ref[0]) + dot(m_ref[:, :512], w2_ref[1, :512])
+        lifted += dot(m_ref[:, :256], w2_ref[2, :256])
         d_ref[0] = lifted[:, :128]
         d_ref[1] = lifted[:, 128:]
         for u in range(2):
@@ -395,7 +406,7 @@
     anywhere = pl.BlockSpec(memory_space=pl.ANY)
     smem = pl.BlockSpec(memory_space=pltpu.SMEM)
     old = [] if before is None else [before]
-    fixed = pl.BlockSpec((768, 256), lambda s: (0, 0))
+    fixed = pl.BlockSpec((3, 768, 256), lambda s: (0, 0, 0))
     return pl.pallas_call(
         functools.partial(fine_kernel, first=first),
         grid=(count,),
@@ -420,19 +431,16 @@
             flops=6 * count * edge * plane * 256, bytes_accessed=2 * count * MIB, transcendentals=0
         ),
         name="fine",
-    )(owner_counts, token, tiled_view(density), stacked(w1), stacked(w2), *old)
+    )(owner_counts, token, tiled_view(density), triple(w1), triple(w2), *old)
 
 
 def coarse_kernel(
     index_ref,
     piece_ref,
     wx_ref,
-    wzh_ref,
-    wzl_ref,
-    wyh_ref,
-    wyl_ref,
-    w23h_ref,
-    w23l_ref,
+    wz_ref,
+    wy_ref,
+    w23_ref,
     wx2_ref,
     wx3_ref,
     fine_ref,
@@ -467,7 +475,7 @@
             for yh in range(2):
                 part = slice(yh * 128, yh * 128 + 128)
                 stacked.append(jnp.concatenate([first[o][cy][:, part], first[o][2 + cy][:, part]], 1))
-    lifted = times(jnp.concatenate(stacked, 0), wzh_ref[...], wzl_ref[...])
+    lifted = times(jnp.concatenate(stacked, 0), wz_ref[0], wz_ref[1], wz_ref[2])
     stacked = []
     for o in range(2):
         for tz in range(2):
@@ -477,7 +485,7 @@
                     1,
                 )
             )
-    lifted = times(jnp.concatenate(stacked, 0), wyh_ref[...], wyl_ref[...])
+    lifted = times(jnp.concatenate(stacked, 0), wy_ref[0], wy_ref[1], wy_ref[2])
     corner = []
     for o in range(2):
         for tz in range(2):
@@ -489,7 +497,7 @@
                         corner.append(value)
                     else:
                         block_ref[o * 8 + tx + 2 * ty + 4 * tz] = value
-    both = times(jnp.concatenate(corner, 0), w23h_ref[...], w23l_ref[...])
+    both = times(jnp.concatenate(corner, 0), w23_ref[0], w23_ref[1], w23_ref[2])
     depth = lax.broadcasted_iota(jnp.int32, (16, 128), 0)
     small = (depth < 8) & ((lane & 15) < 8)
     for o in range(2):
@@ -541,9 +549,9 @@
     w23 = np.concatenate([np.kron(m16.T, m16.T)[:, lanes], np.kron(deep.T, deep.T)[:, lanes[:128]]], 1)[lanes]
     weights = [
         left_terms(m32),
-        *two_terms(wz),
-        *two_terms(wy),
-        *two_terms(w23),
+        np.stack(three_terms(wz)),
+        np.stack(three_terms(wy)),
+        np.stack(three_terms(w23)),
         left_terms(m16),
         left_terms(deep),
     ]

time: 42.7 us -> 50.7 us (1.19)
  Pallas kernels: 28.1 us -> 33.7 us
  local copies, waits for them, and re-layouts: 0.07 us -> 2.43 us
  waiting for transfers between devices: 1.89 us -> 0.39 us
  starting transfers between devices: 11.4 us -> 12.8 us
    pallas_call x2, Pallas kernels: 16.5 us -> 20.4 us  [fine_call(): pl.pallas_call(functools.partial(fine_kernel, first=first), grid=(count,)...]
    unnamed x22 -> x16, local copies, waits for them, and re-layouts: 0.07 us -> 2.43 us
    all_to_all x1, waiting for transfers between devices: 1.72 us -> 0.39 us  [exchange(): got = lax.all_to_all(lowpass, SWAPPED, 0, 0, tiled=True)]
    all_to_all x1, starting transfers between devices: 4.13 us -> 5.46 us  [exchange(): return (lax.all_to_all(sent, SWAPPED, 0, 0, tiled=True), index)]
    pallas_call x1, Pallas kernels: 5.64 us -> 6.69 us  [lowpass_call(): pl.pallas_call(lowpass_kernel, in_specs=[pl.BlockSpec(memory_space=pltpu....]
    pallas_call x1, Pallas kernels: 3.55 us -> 4.23 us  [coarse_call(): pl.pallas_call(coarse_kernel, in_specs=[pl.BlockSpec(memory_space=pltpu.S...]
  transfers between devices with their start and end apart: 2 -> 2, of which waited for: 2 -> 1; matrix products, arithmetic and copies ran while one was open for 0% -> 0% of each run, Pallas kernels for 39% -> 41%
where the time goes in v14:
time: 50.7 us; the launch traced here: 50.2 us
  Pallas kernels  33.7 us (66%)
  starting transfers between devices  12.8 us (25%)
  local copies, waits for them, and re-layouts  2.43 us (5%)
  between operations  0.95 us (2%)
    pallas_call x2, Pallas kernels, fine_call(): pl.pallas_call(functools.partial(fine_kernel, first=first), grid=(count,)...  20.4 us
    all_to_all x1, starting transfers between devices, exchange(): got = lax.all_to_all(lowpass, SWAPPED, 0, 0, tiled=True)  7.3 us
    pallas_call x1, Pallas kernels, lowpass_call(): pl.pallas_call(lowpass_kernel, in_specs=[pl.BlockSpec(memory_space=pltpu....  6.69 us
    all_to_all x1, starting transfers between devices, exchange(): return (lax.all_to_all(sent, SWAPPED, 0, 0, tiled=True), index)  5.46 us
    pallas_call x1, Pallas kernels, coarse_call(): pl.pallas_call(coarse_kernel, in_specs=[pl.BlockSpec(memory_space=pltpu.S...  4.23 us
    unnamed x16, local copies, waits for them, and re-layouts  2.43 us
    pallas_call x1, Pallas kernels, route_call(): pl.pallas_call(functools.partial(route_kernel, width=width), in_specs=[pl...  2.36 us
  transfers between devices with their start and end apart: 2, of which 1 were waited for; matrix products, arithmetic and copies ran while one was open for 0% of the time, Pallas kernels for 41%

profile of v14, /device:TPU:0, one launch (start us, length us, event | category | flops | bytes accessed | tf_op | source)
XLA Modules:
  0.0 50.2 jit_solution(18118292803180217448)
XLA Ops:
  0.0 0.0 copy-start
  0.0 0.0 copy-start.1
  0.8 6.7 %lowpass.1 = (f32[256,128]{1,0:T(8,128)}, s32[1]{0:T(128)}) custom-call(s32[1]{0:T(128)S(6)} %copy.19.count_ref, f32[6,8,32,8,128]{4,3,2,1,0:T(8,128)} %bitcast.7, bf16[512,384]{1,0:T(8,128)(2,1)} %constant.31.clone.wz_any, bf16[3,1024,256]{2,1,0:T(8,128)(2,1)} %constant.32.clone.wy_any), custom_call_target="tpu_custom_call" | custom-call | tf_op jit(solution)/shard_map/lowpass/pallas_call | solution.py:166
  7.5 7.3 %all-to-all-start = ((f32[32,8,128]{2,1,0:T(8,128)}), f32[32,8,128]{2,1,0:T(8,128)S(1)}, u32[]{:S(2)}, u32[]{:S(2)}) async-start(f32[32,8,128]{2,1,0:T(8,128)} %bitcast.10), calls=%async_computation | async-start | bytes 262144 | tf_op jit(solution)/shard_map/all_to_all | solution.py:581
  14.8 0.0 copy-done
  14.8 0.0 copy-done.1
  14.8 7.8 %fine.2 = (f32[6,64,4096]{2,1,0:T(8,128)}, s32[1]{0:T(128)}) custom-call(s32[1]{0:T(128)S(6)} %copy.19.count_ref, s32[1]{0:T(128)} %get-tuple-element.13._, f32[6,8,32,8,128]{4,3,2,1,0:T(8,128)} %bitcast.8, bf16[3,768,256]{2,1,0:T(8,128)(2,1)S(1)} %copy-done.1, bf16[3,768,256]{2,1,0:T(8,128)(2,1)S(1)} %copy-done), custom_call_target="tpu_custom_call" | custom-call | flops 805306368 | bytes 4194304 | tf_op jit(solution)/shard_map/fine/pallas_call | solution.py:410
  22.6 0.4 all-to-all-done.got_ref
  23.0 2.4 %route.1 = (f32[32,16,128]{2,1,0:T(8,128)}, s32[2]{0:T(128)S(1)}) custom-call(s32[1]{0:T(128)} %bitcast.me_ref, f32[32,8,128]{2,1,0:T(8,128)S(1)} %all-to-all-done.got_ref, s32[1]{0:T(128)} %get-tuple-element.14._), custom_call_target="tpu_custom_call" | custom-call | tf_op jit(solution)/shard_map/route/pallas_call | solution.py:214
  25.4 5.5 %all-to-all-start.1 = ((f32[32,16,128]{2,1,0:T(8,128)}), f32[32,16,128]{2,1,0:T(8,128)S(1)}, u32[]{:S(2)}, u32[]{:S(2)}) async-start(f32[32,16,128]{2,1,0:T(8,128)} %get-tuple-element.16), calls=%async_computation.1 | async-start | bytes 524288 | tf_op jit(solution)/shard_map/all_to_all | solution.py:583
  30.8 0.0 copy-start.3
  30.8 0.0 copy-start.5
  30.9 0.0 copy-start.6
  30.9 0.0 copy-start.7
  30.9 12.6 %fine.3 = (f32[6,64,4096]{2,1,0:T(8,128)}, s32[1]{0:T(128)}) custom-call(s32[1]{0:T(128)S(6)} %copy.19.count_ref, s32[2]{0:T(128)S(1)} %get-tuple-element.15._.index_ref, f32[6,8,32,8,128]{4,3,2,1,0:T(8,128)} %bitcast.9, bf16[3,768,256]{2,1,0:T(8,128)(2,1)S(1)} %copy-done.1, bf16[3,768,256]{2,1,0:T(8,128)(2,1)S(1)} %copy-done, ...), custom_call_target="tpu_custom_call", output_to_operand_aliasing={{0}: (5, {})} | custom-call | flops 1610612736 | bytes 8388608 | tf_op jit(solution)/shard_map/fine/pallas_call | solution.py:410
  43.5 0.0 all-to-all-done.1
  43.5 0.0 copy-done.3
  43.5 0.0 copy-done.5
  43.6 0.0 copy-done.6
  43.6 0.0 copy-done.7
  43.6 0.0 copy-start.2
  43.6 1.4 %copy-done.2 = bf16[3,512,512]{2,1,0:T(8,128)(2,1)S(1)} copy-done((bf16[3,512,512]{2,1,0:T(8,128)(2,1)S(1)}, bf16[3,512,512]{2,1,0:T(8,128)(2,1)}, u32[]{:S(2)}) %copy-start.2) | copy-done | bytes 1572888
  45.0 0.0 copy-start.4
  45.0 1.0 %copy-done.4 = bf16[3,256,256]{2,1,0:T(8,128)(2,1)S(1)} copy-done((bf16[3,256,256]{2,1,0:T(8,128)(2,1)S(1)}, bf16[3,256,256]{2,1,0:T(8,128)(2,1)}, u32[]{:S(2)}) %copy-start.4) | copy-done | bytes 393240
  46.0 4.2 %coarse.1 = f32[6,64,4096]{2,1,0:T(8,128)} custom-call(s32[2]{0:T(128)S(1)} %get-tuple-element.15._.index_ref, f32[512,128]{1,0:T(8,128)S(1)} %bitcast.6, bf16[32,192]{1,0:T(8,128)(2,1)S(1)} %copy-done.5, bf16[3,256,256]{2,1,0:T(8,128)(2,1)S(1)} %copy-done.4, bf16[3,512,512]{2,1,0:T(8,128)(2,1)S(1)} %copy-done.2, ...), custom_call_target="tpu_custom_call", output_to_operand_aliasing={{}: (8, {})} | custom-call | tf_op jit(solution)/shard_map/coarse/pallas_call | solution.py:560
Async XLA Ops:
  0.0 14.8 %copy-start = (bf16[3,768,256]{2,1,0:T(8,128)(2,1)S(1)}, bf16[3,768,256]{2,1,0:T(8,128)(2,1)}, u32[]{:S(2)}) copy-start(bf16[3,768,256]{2,1,0:T(8,128)(2,1)} %constant.34.clone.w2_ref) | copy-start | bytes 3538948
  0.0 14.8 %copy-start.1 = (bf16[3,768,256]{2,1,0:T(8,128)(2,1)S(1)}, bf16[3,768,256]{2,1,0:T(8,128)(2,1)}, u32[]{:S(2)}) copy-start(bf16[3,768,256]{2,1,0:T(8,128)(2,1)} %constant.33.clone.w1_ref) | copy-start | bytes 3538948
  7.5 15.5 %all-to-all-start = ((f32[32,8,128]{2,1,0:T(8,128)}), f32[32,8,128]{2,1,0:T(8,128)S(1)}, u32[]{:S(2)}, u32[]{:S(2)}) async-start(f32[32,8,128]{2,1,0:T(8,128)} %bitcast.10), calls=%async_computation | async-start | bytes 262144 | tf_op jit(solution)/shard_map/all_to_all | solution.py:581
  25.4 18.2 %all-to-all-start.1 = ((f32[32,16,128]{2,1,0:T(8,128)}), f32[32,16,128]{2,1,0:T(8,128)S(1)}, u32[]{:S(2)}, u32[]{:S(2)}) async-start(f32[32,16,128]{2,1,0:T(8,128)} %get-tuple-element.16), calls=%async_computation.1 | async-start | bytes 524288 | tf_op jit(solution)/shard_map/all_to_all | solution.py:583
  30.8 12.7 %copy-start.3 = (bf16[3,256,384]{2,1,0:T(8,128)(2,1)S(1)}, bf16[3,256,384]{2,1,0:T(8,128)(2,1)}, u32[]{:S(2)}) copy-start(bf16[3,256,384]{2,1,0:T(8,128)(2,1)} %constant.38.clone.w23_ref) | copy-start | bytes 1769476
  30.8 12.7 %copy-start.5 = (bf16[32,192]{1,0:T(8,128)(2,1)S(1)}, bf16[32,192]{1,0:T(8,128)(2,1)}, u32[]{:S(2)}) copy-start(bf16[32,192]{1,0:T(8,128)(2,1)} %constant.35.clone.wx_ref) | copy-start | bytes 36868
  30.9 12.7 %copy-start.6 = (bf16[16,96]{1,0:T(8,128)(2,1)S(1)}, bf16[16,96]{1,0:T(8,128)(2,1)}, u32[]{:S(2)}) copy-start(bf16[16,96]{1,0:T(8,128)(2,1)} %constant.40.clone.wx3_ref) | copy-start | bytes 9220
  30.9 12.7 %copy-start.7 = (bf16[16,96]{1,0:T(8,128)(2,1)S(1)}, bf16[16,96]{1,0:T(8,128)(2,1)}, u32[]{:S(2)}) copy-start(bf16[16,96]{1,0:T(8,128)(2,1)} %constant.39.clone.wx2_ref) | copy-start | bytes 9220
  43.6 1.4 %copy-start.2 = (bf16[3,512,512]{2,1,0:T(8,128)(2,1)S(1)}, bf16[3,512,512]{2,1,0:T(8,128)(2,1)}, u32[]{:S(2)}) copy-start(bf16[3,512,512]{2,1,0:T(8,128)(2,1)} %constant.37.clone.wy_ref) | copy-start | bytes 4718596
  45.0 1.0 %copy-start.4 = (bf16[3,256,256]{2,1,0:T(8,128)(2,1)S(1)}, bf16[3,256,256]{2,1,0:T(8,128)(2,1)}, u32[]{:S(2)}) copy-start(bf16[3,256,256]{2,1,0:T(8,128)(2,1)} %constant.36.clone.wz_ref) | copy-start | bytes 1179652

commit v15 on v13

--- a/solution.py
+++ b/solution.py
@@ -88,7 +88,7 @@
 
 
 def lowpass_kernel(
-    count_ref, x_any, wz_any, wyh_any, wyl_any, out_ref, token_ref, x_ref, wz_ref, wyh_ref, wyl_ref, l_ref, z_ref, sems, w_sems
+    count_ref, x_any, wz_any, wy_ref, out_ref, token_ref, x_ref, wz_ref, wyh_ref, wyl_ref, l_ref, z_ref, sems, w_sem
 ):
     slots, edge, tiles = x_any.shape[0], 8 * x_any.shape[1], x_any.shape[2]
     quarter = edge // 4
@@ -100,12 +100,15 @@
     for copy in blocks:
         copy.start()
     flat = x_ref.reshape(slots * edge * tiles, 128)
-    weights = [
-        pltpu.make_async_copy(src, dst, w_sems.at[i])
-        for i, (src, dst) in enumerate(((wz_any, wz_ref), (wyh_any, wyh_ref), (wyl_any, wyl_ref)))
-    ]
-    for copy in weights:
-        copy.start()
+    weights = pltpu.make_async_copy(wz_any, wz_ref, w_sem)
+    weights.start()
+    same = lax.broadcasted_iota(jnp.int32, (16, 256), 0) == (
+        lax.broadcasted_iota(jnp.int32, (16, 256), 1) & 15
+    )
+    for k in range(edge):
+        for term, ref in enumerate((wyh_ref, wyl_ref)):
+            row = jnp.broadcast_to(wy_ref[term, pl.ds(k, 1), :], (16, 256))
+            ref[pl.ds(16 * k, 16), :] = jnp.where(same, row, 0.0).astype(BF16)
     for s in range(slots):
         blocks[s].wait()
 
@@ -121,8 +124,7 @@
                     l_ref[pl.ds(at, 16), cols] = high
                     l_ref[pl.ds(rows_all + at, 16), cols] = low
 
-    for copy in weights:
-        copy.wait()
+    weights.wait()
     made = dot(l_ref[...], wz_ref[...])
     z_ref[...] = (made[:rows_all, :128] + made[rows_all:, :128]) + made[:rows_all, 128:]
     wide = jnp.concatenate([z_ref[pl.ds(i, slots * quarter, stride=8), :] for i in range(8)], 1)
@@ -147,14 +149,14 @@
     wz = np.concatenate(two_terms(np.kron(np.eye(8), two_levels.T)), 1)
     i, gp, q, p = np.meshgrid(np.arange(8), np.arange(2), np.arange(2), np.arange(2), indexing="ij")
     entry = (2 * (8 * gp + i) + p + 32 * q).reshape(-1)
-    wy = np.kron(two_levels.T[entry] / SQUARE, np.eye(quarter))
-    wyh, wyl = two_terms(wy)
+    wy = np.repeat(two_levels.T[entry] / SQUARE, quarter, 1)
+    wy = np.stack([term.astype(np.float32) for term in two_terms(wy)])
     anywhere = pl.BlockSpec(memory_space=pl.ANY)
     vmem = pl.BlockSpec(memory_space=pltpu.VMEM)
     rows_all = slots * 8 * quarter
     pieces, token = pl.pallas_call(
         lowpass_kernel,
-        in_specs=[pl.BlockSpec(memory_space=pltpu.SMEM)] + [anywhere] * 4,
+        in_specs=[pl.BlockSpec(memory_space=pltpu.SMEM)] + [anywhere] * 2 + [vmem],
         out_specs=[vmem, pl.BlockSpec(memory_space=pltpu.SMEM)],
         out_shape=[
             jax.ShapeDtypeStruct((16 * quarter, 128), F32),
@@ -163,16 +165,16 @@
         scratch_shapes=[
             pltpu.VMEM((slots, edge // 8, plane // 128, 8, 128), F32),
             pltpu.VMEM(wz.shape, BF16),
-            pltpu.VMEM(wyh.shape, BF16),
-            pltpu.VMEM(wyl.shape, BF16),
+            pltpu.VMEM((quarter * edge, quarter * quarter), BF16),
+            pltpu.VMEM((quarter * edge, quarter * quarter), BF16),
             pltpu.VMEM((2 * rows_all, 512), BF16),
             pltpu.VMEM((rows_all, 128), F32),
             pltpu.SemaphoreType.DMA((slots,)),
-            pltpu.SemaphoreType.DMA((3,)),
+            pltpu.SemaphoreType.DMA,
         ],
         compiler_params=pltpu.CompilerParams(vmem_limit_bytes=VMEM_LARGE),
         name="lowpass",
-    )(owner_counts, tiled_view(density), wz, wyh, wyl)
+    )(owner_counts, tiled_view(density), wz, wy)
     return pieces.reshape(2 * quarter, 8, 128), token
 
 

time: 42.7 us -> 43.6 us (1.021)
  Pallas kernels: 28.1 us -> 28.9 us
    pallas_call x1, Pallas kernels: 5.64 us -> 6.53 us  [lowpass_call(): pl.pallas_call(lowpass_kernel, in_specs=[pl.BlockSpec(memory_space=pltpu....]
  transfers between devices with their start and end apart: 2 -> 2, of which waited for: 2 -> 2; matrix products, arithmetic and copies ran while one was open for 0% -> 0% of each run, Pallas kernels for 39% -> 38%
where the time goes in v15:
time: 43.6 us; the launch traced here: 43.3 us
  Pallas kernels  28.9 us (66%)
  starting transfers between devices  11.4 us (26%)
  waiting for transfers between devices  1.89 us (4%)
  between operations  0.92 us (2%)
    pallas_call x2, Pallas kernels, fine_call(): pl.pallas_call(functools.partial(fine_kernel, first=first), grid=(count,)...  16.5 us
    all_to_all x1, starting transfers between devices, exchange(): got = lax.all_to_all(lowpass, SWAPPED, 0, 0, tiled=True)  7.3 us
    pallas_call x1, Pallas kernels, lowpass_call(): pl.pallas_call(lowpass_kernel, in_specs=[pl.BlockSpec(memory_space=pltpu....  6.53 us
    all_to_all x1, starting transfers between devices, exchange(): return (lax.all_to_all(sent, SWAPPED, 0, 0, tiled=True), index)  4.13 us
    pallas_call x1, Pallas kernels, coarse_call(): pl.pallas_call(coarse_kernel, in_specs=[pl.BlockSpec(memory_space=pltpu.S...  3.55 us
    pallas_call x1, Pallas kernels, route_call(): pl.pallas_call(functools.partial(route_kernel, width=width), in_specs=[pl...  2.35 us
    all_to_all x1, waiting for transfers between devices, exchange(): got = lax.all_to_all(lowpass, SWAPPED, 0, 0, tiled=True)  1.72 us
  transfers between devices with their start and end apart: 2, of which 2 were waited for; matrix products, arithmetic and copies ran while one was open for 0% of the time, Pallas kernels for 38%

profile of v15, /device:TPU:0, one launch (start us, length us, event | category | flops | bytes accessed | tf_op | source)
XLA Modules:
  0.0 43.3 jit_solution(7455207558314448144)
XLA Ops:
  0.0 0.0 copy-start
  0.0 0.0 copy-start.1
  0.7 6.5 %lowpass.1 = (f32[256,128]{1,0:T(8,128)}, s32[1]{0:T(128)}) custom-call(s32[1]{0:T(128)S(6)} %copy.22.count_ref, f32[6,8,32,8,128]{4,3,2,1,0:T(8,128)} %bitcast.7, bf16[512,256]{1,0:T(8,128)(2,1)} %constant.37.clone.wz_any, f32[2,64,256]{2,1,0:T(8,128)} %constant.38.clone.wy_ref), custom_call_target="tpu_custom_call" | custom-call | tf_op jit(solution)/shard_map/lowpass/pallas_call | solution.py:157
  7.3 7.3 %all-to-all-start = ((f32[32,8,128]{2,1,0:T(8,128)}), f32[32,8,128]{2,1,0:T(8,128)S(1)}, u32[]{:S(2)}, u32[]{:S(2)}) async-start(f32[32,8,128]{2,1,0:T(8,128)} %bitcast.10), calls=%async_computation | async-start | bytes 262144 | tf_op jit(solution)/shard_map/all_to_all | solution.py:575
  14.6 0.0 copy-done
  14.6 0.0 copy-done.1
  14.6 6.4 %fine.2 = (f32[6,64,4096]{2,1,0:T(8,128)}, s32[1]{0:T(128)}) custom-call(s32[1]{0:T(128)S(6)} %copy.22.count_ref, s32[1]{0:T(128)} %get-tuple-element.13._, f32[6,8,32,8,128]{4,3,2,1,0:T(8,128)} %bitcast.8, bf16[768,256]{1,0:T(8,128)(2,1)S(1)} %copy-done.1, bf16[768,256]{1,0:T(8,128)(2,1)S(1)} %copy-done), custom_call_target="tpu_custom_call" | custom-call | flops 805306368 | bytes 4194304 | tf_op jit(solution)/shard_map/fine/pallas_call | solution.py:401
  21.0 1.7 %all-to-all-done.got_ref = f32[32,8,128]{2,1,0:T(8,128)S(1)} async-done(((f32[32,8,128]{2,1,0:T(8,128)}), f32[32,8,128]{2,1,0:T(8,128)S(1)}, u32[]{:S(2)}, u32[]{:S(2)}) %all-to-all-start) | async-done | bytes 131104 | tf_op jit(solution)/shard_map/all_to_all | solution.py:575
  22.7 2.4 %route.1 = (f32[32,16,128]{2,1,0:T(8,128)}, s32[2]{0:T(128)S(1)}) custom-call(s32[1]{0:T(128)} %bitcast.me_ref, f32[32,8,128]{2,1,0:T(8,128)S(1)} %all-to-all-done.got_ref, s32[1]{0:T(128)} %get-tuple-element.14._), custom_call_target="tpu_custom_call" | custom-call | tf_op jit(solution)/shard_map/route/pallas_call | solution.py:206
  25.1 4.1 %all-to-all-start.1 = ((f32[32,16,128]{2,1,0:T(8,128)}), f32[32,16,128]{2,1,0:T(8,128)S(1)}, u32[]{:S(2)}, u32[]{:S(2)}) async-start(f32[32,16,128]{2,1,0:T(8,128)} %get-tuple-element.16), calls=%async_computation.1 | async-start | bytes 524288 | tf_op jit(solution)/shard_map/all_to_all | solution.py:577
  29.3 0.0 copy-start.2
  29.3 0.0 copy-start.3
  29.3 0.0 copy-start.4
  29.3 0.0 copy-start.5
  29.3 0.0 copy-start.6
  29.3 0.0 copy-start.7
  29.3 0.0 copy-start.8
  29.3 0.0 copy-start.9
  29.4 0.0 copy-start.10
  29.4 10.1 %fine.3 = (f32[6,64,4096]{2,1,0:T(8,128)}, s32[1]{0:T(128)}) custom-call(s32[1]{0:T(128)S(6)} %copy.22.count_ref, s32[2]{0:T(128)S(1)} %get-tuple-element.15._.index_ref, f32[6,8,32,8,128]{4,3,2,1,0:T(8,128)} %bitcast.9, bf16[768,256]{1,0:T(8,128)(2,1)S(1)} %copy-done.1, bf16[768,256]{1,0:T(8,128)(2,1)S(1)} %copy-done, ...), custom_call_target="tpu_custom_call", output_to_operand_aliasing={{0}: (5, {})} | custom-call | flops 1610612736 | bytes 8388608 | tf_op jit(solution)/shard_map/fine/pallas_call | solution.py:401
  39.5 0.2 all-to-all-done.1
  39.6 0.0 copy-done.2
  39.6 0.0 copy-done.3
  39.6 0.0 copy-done.4
  39.6 0.0 copy-done.5
  39.7 0.0 copy-done.6
  39.7 0.0 copy-done.7
  39.7 0.0 copy-done.8
  39.7 0.0 copy-done.9
  39.7 0.0 copy-done.10
  39.7 3.6 %coarse.1 = f32[6,64,4096]{2,1,0:T(8,128)} custom-call(s32[2]{0:T(128)S(1)} %get-tuple-element.15._.index_ref, f32[512,128]{1,0:T(8,128)S(1)} %bitcast.6, bf16[32,96]{1,0:T(8,128)(2,1)S(1)} %copy-done.8, bf16[256,256]{1,0:T(8,128)(2,1)S(1)} %copy-done.7, bf16[256,256]{1,0:T(8,128)(2,1)S(1)} %copy-done.6, ...), custom_call_target="tpu_custom_call", output_to_operand_aliasing={{}: (11, {})} | custom-call | tf_op jit(solution)/shard_map/coarse/pallas_call | solution.py:554
Async XLA Ops:
  0.0 14.6 %copy-start = (bf16[768,256]{1,0:T(8,128)(2,1)S(1)}, bf16[768,256]{1,0:T(8,128)(2,1)}, u32[]{:S(2)}) copy-start(bf16[768,256]{1,0:T(8,128)(2,1)} %constant.40.clone.w2_ref) | copy-start | bytes 1179652
  0.0 14.6 %copy-start.1 = (bf16[768,256]{1,0:T(8,128)(2,1)S(1)}, bf16[768,256]{1,0:T(8,128)(2,1)}, u32[]{:S(2)}) copy-start(bf16[768,256]{1,0:T(8,128)(2,1)} %constant.39.clone.w1_ref) | copy-start | bytes 1179652
  7.3 15.5 %all-to-all-start = ((f32[32,8,128]{2,1,0:T(8,128)}), f32[32,8,128]{2,1,0:T(8,128)S(1)}, u32[]{:S(2)}, u32[]{:S(2)}) async-start(f32[32,8,128]{2,1,0:T(8,128)} %bitcast.10), calls=%async_computation | async-start | bytes 262144 | tf_op jit(solution)/shard_map/all_to_all | solution.py:575
  25.1 14.5 %all-to-all-start.1 = ((f32[32,16,128]{2,1,0:T(8,128)}), f32[32,16,128]{2,1,0:T(8,128)S(1)}, u32[]{:S(2)}, u32[]{:S(2)}) async-start(f32[32,16,128]{2,1,0:T(8,128)} %get-tuple-element.16), calls=%async_computation.1 | async-start | bytes 524288 | tf_op jit(solution)/shard_map/all_to_all | solution.py:577
  29.3 10.4 %copy-start.2 = (bf16[512,512]{1,0:T(8,128)(2,1)S(1)}, bf16[512,512]{1,0:T(8,128)(2,1)}, u32[]{:S(2)}) copy-start(bf16[512,512]{1,0:T(8,128)(2,1)} %constant.45.clone.wyl_ref) | copy-start | bytes 1572868
  29.3 10.4 %copy-start.3 = (bf16[512,512]{1,0:T(8,128)(2,1)S(1)}, bf16[512,512]{1,0:T(8,128)(2,1)}, u32[]{:S(2)}) copy-start(bf16[512,512]{1,0:T(8,128)(2,1)} %constant.44.clone.wyh_ref) | copy-start | bytes 1572868
  29.3 10.4 %copy-start.4 = (bf16[256,384]{1,0:T(8,128)(2,1)S(1)}, bf16[256,384]{1,0:T(8,128)(2,1)}, u32[]{:S(2)}) copy-start(bf16[256,384]{1,0:T(8,128)(2,1)} %constant.47.clone.w23l_ref) | copy-start | bytes 589828
  29.3 10.4 %copy-start.5 = (bf16[256,384]{1,0:T(8,128)(2,1)S(1)}, bf16[256,384]{1,0:T(8,128)(2,1)}, u32[]{:S(2)}) copy-start(bf16[256,384]{1,0:T(8,128)(2,1)} %constant.46.clone.w23h_ref) | copy-start | bytes 589828
  29.3 10.4 %copy-start.6 = (bf16[256,256]{1,0:T(8,128)(2,1)S(1)}, bf16[256,256]{1,0:T(8,128)(2,1)}, u32[]{:S(2)}) copy-start(bf16[256,256]{1,0:T(8,128)(2,1)} %constant.43.clone.wzl_ref) | copy-start | bytes 393220
  29.3 10.4 %copy-start.7 = (bf16[256,256]{1,0:T(8,128)(2,1)S(1)}, bf16[256,256]{1,0:T(8,128)(2,1)}, u32[]{:S(2)}) copy-start(bf16[256,256]{1,0:T(8,128)(2,1)} %constant.42.clone.wzh_ref) | copy-start | bytes 393220
  29.3 10.4 %copy-start.8 = (bf16[32,96]{1,0:T(8,128)(2,1)S(1)}, bf16[32,96]{1,0:T(8,128)(2,1)}, u32[]{:S(2)}) copy-start(bf16[32,96]{1,0:T(8,128)(2,1)} %constant.41.clone.wx_ref) | copy-start | bytes 18436
  29.3 10.3 %copy-start.9 = (bf16[16,48]{1,0:T(8,128)(2,1)S(1)}, bf16[16,48]{1,0:T(8,128)(2,1)}, u32[]{:S(2)}) copy-start(bf16[16,48]{1,0:T(8,128)(2,1)} %constant.49.clone.wx3_ref) | copy-start | bytes 4612
  29.4 10.3 %copy-start.10 = (bf16[16,48]{1,0:T(8,128)(2,1)S(1)}, bf16[16,48]{1,0:T(8,128)(2,1)}, u32[]{:S(2)}) copy-start(bf16[16,48]{1,0:T(8,128)(2,1)} %constant.48.clone.wx2_ref) | copy-start | bytes 4612

commit v16 on v13

--- a/solution.py
+++ b/solution.py
@@ -88,11 +88,10 @@
 
 
 def lowpass_kernel(
-    count_ref, x_any, wz_any, wyh_any, wyl_any, out_ref, token_ref, x_ref, wz_ref, wyh_ref, wyl_ref, l_ref, z_ref, sems, w_sems
+    count_ref, x_any, wz_any, wyh_any, wyl_any, out_ref, token_ref, x_ref, wz_ref, wyh_ref, wyl_ref, l_ref, k_ref, z_ref, sems, w_sems
 ):
     slots, edge, tiles = x_any.shape[0], 8 * x_any.shape[1], x_any.shape[2]
     quarter = edge // 4
-    rows_all = slots * 8 * quarter
     token_ref[0] = count_ref[0]
     blocks = [
         pltpu.make_async_copy(x_any.at[n], x_ref.at[n], sems.at[n]) for n in range(slots)
@@ -106,25 +105,39 @@
     ]
     for copy in weights:
         copy.start()
-    for s in range(slots):
+    part = slots // 2
+    rows_part = part * 8 * quarter
+
+    def first_dimension(s, g):
+        rows = tile_rows(flat, s, g, edge, tiles)
+        rows, _ = lift(rows[0::2], rows[1::2], edge // 2, False, False)
+        rows, _ = lift(rows[0::2], rows[1::2], quarter, False, False)
+        ref = (l_ref, k_ref)[s // part]
+        for m, (high, low) in enumerate(split_rows(rows)):
+            at = (s % part) * 8 * quarter + 16 * m
+            cols = pl.ds((g % 2) * 256 + (g // 2) * 128, 128)
+            ref[pl.ds(at, 16), cols] = high
+            ref[pl.ds(rows_part + at, 16), cols] = low
+
+    def third_dimension(ref, half):
+        made = dot(ref[...], wz_ref[...])
+        z_ref[pl.ds(half * rows_part, rows_part), :] = (
+            made[:rows_part, :128] + made[rows_part:, :128]
+        ) + made[:rows_part, 128:]
+
+    for s in range(part):
         blocks[s].wait()
-
-        @pl.loop(0, 2)
-        def _(q):
-            for u in range(2):
-                rows = tile_rows(flat, s, 2 * q + u, edge, tiles)
-                rows, _ = lift(rows[0::2], rows[1::2], edge // 2, False, False)
-                rows, _ = lift(rows[0::2], rows[1::2], quarter, False, False)
-                for m, (high, low) in enumerate(split_rows(rows)):
-                    at = s * 8 * quarter + 16 * m
-                    cols = pl.ds(pl.multiple_of(u * 256 + q * 128, 128), 128)
-                    l_ref[pl.ds(at, 16), cols] = high
-                    l_ref[pl.ds(rows_all + at, 16), cols] = low
-
+        for g in range(4):
+            first_dimension(s, g)
     for copy in weights:
         copy.wait()
-    made = dot(l_ref[...], wz_ref[...])
-    z_ref[...] = (made[:rows_all, :128] + made[rows_all:, :128]) + made[:rows_all, 128:]
+    for s in range(part, slots):
+        blocks[s].wait()
+    third_dimension(l_ref, 0)
+    for s in range(part, slots):
+        for g in range(4):
+            first_dimension(s, g)
+    third_dimension(k_ref, 1)
     wide = jnp.concatenate([z_ref[pl.ds(i, slots * quarter, stride=8), :] for i in range(8)], 1)
     made = times(wide, wyh_ref[...], wyl_ref[...])
     out_ref[...] = jnp.full(out_ref.shape, count_ref[0].astype(F32))
@@ -165,7 +178,8 @@
             pltpu.VMEM(wz.shape, BF16),
             pltpu.VMEM(wyh.shape, BF16),
             pltpu.VMEM(wyl.shape, BF16),
-            pltpu.VMEM((2 * rows_all, 512), BF16),
+            pltpu.VMEM((rows_all, 512), BF16),
+            pltpu.VMEM((rows_all, 512), BF16),
             pltpu.VMEM((rows_all, 128), F32),
             pltpu.SemaphoreType.DMA((slots,)),
             pltpu.SemaphoreType.DMA((3,)),

time: 42.7 us -> 43.1 us (level)
  no operation moved by 1% of the time
where the time goes in v16:
time: 43.1 us; the launch traced here: 42.8 us
  Pallas kernels  28.4 us (66%)
  starting transfers between devices  11.4 us (26%)
  waiting for transfers between devices  1.89 us (4%)
  between operations  0.92 us (2%)
    pallas_call x2, Pallas kernels, fine_call(): pl.pallas_call(functools.partial(fine_kernel, first=first), grid=(count,)...  16.5 us
    all_to_all x1, starting transfers between devices, exchange(): got = lax.all_to_all(lowpass, SWAPPED, 0, 0, tiled=True)  7.3 us
    pallas_call x1, Pallas kernels, lowpass_call(): pl.pallas_call(lowpass_kernel, in_specs=[pl.BlockSpec(memory_space=pltpu....  6.02 us
    all_to_all x1, starting transfers between devices, exchange(): return (lax.all_to_all(sent, SWAPPED, 0, 0, tiled=True), index)  4.13 us
    pallas_call x1, Pallas kernels, coarse_call(): pl.pallas_call(coarse_kernel, in_specs=[pl.BlockSpec(memory_space=pltpu.S...  3.55 us
    pallas_call x1, Pallas kernels, route_call(): pl.pallas_call(functools.partial(route_kernel, width=width), in_specs=[pl...  2.35 us
    all_to_all x1, waiting for transfers between devices, exchange(): got = lax.all_to_all(lowpass, SWAPPED, 0, 0, tiled=True)  1.72 us
  transfers between devices with their start and end apart: 2, of which 2 were waited for; matrix products, arithmetic and copies ran while one was open for 0% of the time, Pallas kernels for 39%

profile of v16, /device:TPU:0, one launch (start us, length us, event | category | flops | bytes accessed | tf_op | source)
XLA Modules:
  0.0 42.8 jit_solution(17038630823289280487)
XLA Ops:
  0.0 0.0 copy-start
  0.0 0.0 copy-start.1
  0.7 6.0 %lowpass.1 = (f32[256,128]{1,0:T(8,128)}, s32[1]{0:T(128)}) custom-call(s32[1]{0:T(128)S(6)} %copy.23.count_ref, f32[6,8,32,8,128]{4,3,2,1,0:T(8,128)} %bitcast.7, bf16[512,256]{1,0:T(8,128)(2,1)} %constant.39.clone.wz_any, bf16[1024,256]{1,0:T(8,128)(2,1)} %constant.40.clone.wyh_any, bf16[1024,256]{1,0:T(8,128)(2,1)} %constant.41.clone.wyl_any), custom_call_target="tpu_custom_call" | custom-call | tf_op jit(solution)/shard_map/lowpass/pallas_call | solution.py:168
  6.8 7.3 %all-to-all-start = ((f32[32,8,128]{2,1,0:T(8,128)}), f32[32,8,128]{2,1,0:T(8,128)S(1)}, u32[]{:S(2)}, u32[]{:S(2)}) async-start(f32[32,8,128]{2,1,0:T(8,128)} %bitcast.10), calls=%async_computation | async-start | bytes 262144 | tf_op jit(solution)/shard_map/all_to_all | solution.py:587
  14.1 0.0 copy-done
  14.1 0.0 copy-done.1
  14.1 6.4 %fine.2 = (f32[6,64,4096]{2,1,0:T(8,128)}, s32[1]{0:T(128)}) custom-call(s32[1]{0:T(128)S(6)} %copy.23.count_ref, s32[1]{0:T(128)} %get-tuple-element.13._, f32[6,8,32,8,128]{4,3,2,1,0:T(8,128)} %bitcast.8, bf16[768,256]{1,0:T(8,128)(2,1)S(1)} %copy-done.1, bf16[768,256]{1,0:T(8,128)(2,1)S(1)} %copy-done), custom_call_target="tpu_custom_call" | custom-call | flops 805306368 | bytes 4194304 | tf_op jit(solution)/shard_map/fine/pallas_call | solution.py:413
  20.5 1.7 %all-to-all-done.got_ref = f32[32,8,128]{2,1,0:T(8,128)S(1)} async-done(((f32[32,8,128]{2,1,0:T(8,128)}), f32[32,8,128]{2,1,0:T(8,128)S(1)}, u32[]{:S(2)}, u32[]{:S(2)}) %all-to-all-start) | async-done | bytes 131104 | tf_op jit(solution)/shard_map/all_to_all | solution.py:587
  22.2 2.4 %route.1 = (f32[32,16,128]{2,1,0:T(8,128)}, s32[2]{0:T(128)S(1)}) custom-call(s32[1]{0:T(128)} %bitcast.me_ref, f32[32,8,128]{2,1,0:T(8,128)S(1)} %all-to-all-done.got_ref, s32[1]{0:T(128)} %get-tuple-element.14._), custom_call_target="tpu_custom_call" | custom-call | tf_op jit(solution)/shard_map/route/pallas_call | solution.py:218
  24.6 4.1 %all-to-all-start.1 = ((f32[32,16,128]{2,1,0:T(8,128)}), f32[32,16,128]{2,1,0:T(8,128)S(1)}, u32[]{:S(2)}, u32[]{:S(2)}) async-start(f32[32,16,128]{2,1,0:T(8,128)} %get-tuple-element.16), calls=%async_computation.1 | async-start | bytes 524288 | tf_op jit(solution)/shard_map/all_to_all | solution.py:589
  28.7 0.0 copy-start.2
  28.8 0.0 copy-start.3
  28.8 0.0 copy-start.4
  28.8 0.0 copy-start.5
  28.8 0.0 copy-start.6
  28.8 0.0 copy-start.7
  28.8 0.0 copy-start.8
  28.8 0.0 copy-start.9
  28.8 0.0 copy-start.10
  28.9 10.1 %fine.3 = (f32[6,64,4096]{2,1,0:T(8,128)}, s32[1]{0:T(128)}) custom-call(s32[1]{0:T(128)S(6)} %copy.23.count_ref, s32[2]{0:T(128)S(1)} %get-tuple-element.15._.index_ref, f32[6,8,32,8,128]{4,3,2,1,0:T(8,128)} %bitcast.9, bf16[768,256]{1,0:T(8,128)(2,1)S(1)} %copy-done.1, bf16[768,256]{1,0:T(8,128)(2,1)S(1)} %copy-done, ...), custom_call_target="tpu_custom_call", output_to_operand_aliasing={{0}: (5, {})} | custom-call | flops 1610612736 | bytes 8388608 | tf_op jit(solution)/shard_map/fine/pallas_call | solution.py:413
  39.0 0.2 all-to-all-done.1
  39.1 0.0 copy-done.2
  39.1 0.0 copy-done.3
  39.1 0.0 copy-done.4
  39.1 0.0 copy-done.5
  39.1 0.0 copy-done.6
  39.2 0.0 copy-done.7
  39.2 0.0 copy-done.8
  39.2 0.0 copy-done.9
  39.2 0.0 copy-done.10
  39.2 3.6 %coarse.1 = f32[6,64,4096]{2,1,0:T(8,128)} custom-call(s32[2]{0:T(128)S(1)} %get-tuple-element.15._.index_ref, f32[512,128]{1,0:T(8,128)S(1)} %bitcast.6, bf16[32,96]{1,0:T(8,128)(2,1)S(1)} %copy-done.8, bf16[256,256]{1,0:T(8,128)(2,1)S(1)} %copy-done.7, bf16[256,256]{1,0:T(8,128)(2,1)S(1)} %copy-done.6, ...), custom_call_target="tpu_custom_call", output_to_operand_aliasing={{}: (11, {})} | custom-call | tf_op jit(solution)/shard_map/coarse/pallas_call | solution.py:566
Async XLA Ops:
  0.0 14.1 %copy-start = (bf16[768,256]{1,0:T(8,128)(2,1)S(1)}, bf16[768,256]{1,0:T(8,128)(2,1)}, u32[]{:S(2)}) copy-start(bf16[768,256]{1,0:T(8,128)(2,1)} %constant.43.clone.w2_ref) | copy-start | bytes 1179652
  0.0 14.1 %copy-start.1 = (bf16[768,256]{1,0:T(8,128)(2,1)S(1)}, bf16[768,256]{1,0:T(8,128)(2,1)}, u32[]{:S(2)}) copy-start(bf16[768,256]{1,0:T(8,128)(2,1)} %constant.42.clone.w1_ref) | copy-start | bytes 1179652
  6.8 15.5 %all-to-all-start = ((f32[32,8,128]{2,1,0:T(8,128)}), f32[32,8,128]{2,1,0:T(8,128)S(1)}, u32[]{:S(2)}, u32[]{:S(2)}) async-start(f32[32,8,128]{2,1,0:T(8,128)} %bitcast.10), calls=%async_computation | async-start | bytes 262144 | tf_op jit(solution)/shard_map/all_to_all | solution.py:587
  24.6 14.5 %all-to-all-start.1 = ((f32[32,16,128]{2,1,0:T(8,128)}), f32[32,16,128]{2,1,0:T(8,128)S(1)}, u32[]{:S(2)}, u32[]{:S(2)}) async-start(f32[32,16,128]{2,1,0:T(8,128)} %get-tuple-element.16), calls=%async_computation.1 | async-start | bytes 524288 | tf_op jit(solution)/shard_map/all_to_all | solution.py:589
  28.7 10.4 %copy-start.2 = (bf16[512,512]{1,0:T(8,128)(2,1)S(1)}, bf16[512,512]{1,0:T(8,128)(2,1)}, u32[]{:S(2)}) copy-start(bf16[512,512]{1,0:T(8,128)(2,1)} %constant.48.clone.wyl_ref) | copy-start | bytes 1572868
  28.8 10.4 %copy-start.3 = (bf16[512,512]{1,0:T(8,128)(2,1)S(1)}, bf16[512,512]{1,0:T(8,128)(2,1)}, u32[]{:S(2)}) copy-start(bf16[512,512]{1,0:T(8,128)(2,1)} %constant.47.clone.wyh_ref) | copy-start | bytes 1572868
  28.8 10.4 %copy-start.4 = (bf16[256,384]{1,0:T(8,128)(2,1)S(1)}, bf16[256,384]{1,0:T(8,128)(2,1)}, u32[]{:S(2)}) copy-start(bf16[256,384]{1,0:T(8,128)(2,1)} %constant.50.clone.w23l_ref) | copy-start | bytes 589828
  28.8 10.4 %copy-start.5 = (bf16[256,384]{1,0:T(8,128)(2,1)S(1)}, bf16[256,384]{1,0:T(8,128)(2,1)}, u32[]{:S(2)}) copy-start(bf16[256,384]{1,0:T(8,128)(2,1)} %constant.49.clone.w23h_ref) | copy-start | bytes 589828
  28.8 10.4 %copy-start.6 = (bf16[256,256]{1,0:T(8,128)(2,1)S(1)}, bf16[256,256]{1,0:T(8,128)(2,1)}, u32[]{:S(2)}) copy-start(bf16[256,256]{1,0:T(8,128)(2,1)} %constant.46.clone.wzl_ref) | copy-start | bytes 393220
  28.8 10.4 %copy-start.7 = (bf16[256,256]{1,0:T(8,128)(2,1)S(1)}, bf16[256,256]{1,0:T(8,128)(2,1)}, u32[]{:S(2)}) copy-start(bf16[256,256]{1,0:T(8,128)(2,1)} %constant.45.clone.wzh_ref) | copy-start | bytes 393220
  28.8 10.4 %copy-start.8 = (bf16[32,96]{1,0:T(8,128)(2,1)S(1)}, bf16[32,96]{1,0:T(8,128)(2,1)}, u32[]{:S(2)}) copy-start(bf16[32,96]{1,0:T(8,128)(2,1)} %constant.44.clone.wx_ref) | copy-start | bytes 18436
  28.8 10.3 %copy-start.9 = (bf16[16,48]{1,0:T(8,128)(2,1)S(1)}, bf16[16,48]{1,0:T(8,128)(2,1)}, u32[]{:S(2)}) copy-start(bf16[16,48]{1,0:T(8,128)(2,1)} %constant.52.clone.wx3_ref) | copy-start | bytes 4612
  28.8 10.3 %copy-start.10 = (bf16[16,48]{1,0:T(8,128)(2,1)S(1)}, bf16[16,48]{1,0:T(8,128)(2,1)}, u32[]{:S(2)}) copy-start(bf16[16,48]{1,0:T(8,128)(2,1)} %constant.51.clone.wx2_ref) | copy-start | bytes 4612
